TPU v7x, 32 devices: a whole 2x2x4 slice. The times are simulated.
32 devices in a mesh: dp: 8 (over z, x), expert: 4 (over y, core).
Axes of the slice: x: 2, y: 2, z: 4, core: 2. Of those that a mesh axis runs over, the one named last changes fastest.
Arguments:
- tokens: bfloat16 [16384, 1024], P(('dp', 'expert')), may hold values from -6 to 6
- cotangent: bfloat16 [16384, 1024], P(('dp', 'expert')), may hold values from -6 to 6
- gain_attn: float32 [1024], replicated, may hold values from 0.5 to 1.5
- w_query: bfloat16 [1024, 1024], replicated, may hold values from -0.1875 to 0.1875
- w_key: bfloat16 [1024, 1024], replicated, may hold values from -0.1875 to 0.1875
- w_value: bfloat16 [1024, 1024], replicated, may hold values from -0.1875 to 0.1875
- w_out: bfloat16 [1024, 1024], replicated, may hold values from -1.5 to 1.5
- rel_bias: float32 [32, 16], replicated, may hold values from -3 to 3
- gain_moe: float32 [1024], replicated, may hold values from 0.5 to 1.5
- w_router: bfloat16 [1024, 4], replicated, may hold values from -0.09375 to 0.09375
- w_gate: bfloat16 [4, 1024, 2816], P('expert'), may hold values from -0.1875 to 0.1875
- w_up: bfloat16 [4, 1024, 2816], P('expert'), may hold values from -0.1875 to 0.1875
- w_down: bfloat16 [4, 2816, 1024], P('expert'), may hold values from -0.4375 to 0.4375
- segments: int32 [32, 512], P(('dp', 'expert')), may hold values from 0 to 7, never falling along the last dimension, each value on 1 to 256 neighbouring positions
- routes: int32 [16384, 2], P(('dp', 'expert')), may hold values from 0 to 3, all different within a row; in each aligned block of 512 rows (0 to 511, 512 to 1023, ...) at most 320 rows name the same one
Outputs:
- layer_out: bfloat16 [16384, 1024], P(('dp', 'expert'))
- token_grad: float32 [16384, 1024], P(('dp', 'expert'))
- query_grad: float32 [1024, 1024], P(('dp', 'expert'))
- key_grad: float32 [1024, 1024], P(('dp', 'expert'))
- value_grad: float32 [1024, 1024], P(('dp', 'expert'))
- out_grad: float32 [1024, 1024], P(('dp', 'expert'))
- gain_attn_grad: float32 [1024], P(('dp', 'expert'))
- gain_moe_grad: float32 [1024], P(('dp', 'expert'))
- bias_grad: float32 [512], P(('dp', 'expert'))
- router_grad: float32 [1024, 4], P(('dp', 'expert'))
- gate_grad: float32 [4, 1024, 2816], P('expert', 'dp')
- up_grad: float32 [4, 1024, 2816], P('expert', 'dp')
- down_grad: float32 [4, 2816, 1024], P('expert', 'dp')
Inputs may be any that keep to these rules, and one draw needn't show every extreme that they name: `routes`: in each aligned block of 512 rows (the rows of one device) every expert is named by at most 320 rows, and in some blocks one expert by exactly 320; a token's two experts differ. `segments`: within each sequence the document numbers never fall; a document has at most 256 tokens, and some document exactly that many.
All inputs are finite; a program needn't handle non-finite values.
Results may differ from a plain program's by a relative error of at most 0.015.
Values may be sent and summed in bfloat16 or wider, within the bound.
No kernel may reach another device: no remote copies, remote signals or barrier semaphores. Data moves between devices by JAX's collectives and lax.ppermute only.
A program may use at most 256 MiB of HBM per device.

v0:
```python
import jax
import jax.numpy as jnp
import numpy as np
from jax import lax
from jax.sharding import PartitionSpec as P

EPS = 1e-06
HIGHEST = lax.Precision.HIGHEST


def bucket_of(relative, buckets):
    halfway = buckets // 2
    exact_span = halfway // 2
    distance = np.abs(relative)
    beyond = exact_span + (
        np.log(np.maximum(distance, 1) / exact_span)
        / np.log(128.0 / exact_span)
        * (halfway - exact_span)
    ).astype(np.int64)
    beyond = np.minimum(beyond, halfway - 1)
    return (
        (relative > 0).astype(np.int64) * halfway
        + np.where(distance < exact_span, distance, beyond)
    ).astype(np.int32)


def offset_onehot(length, buckets):
    relative = np.arange(2 * length - 1) - (length - 1)
    return (bucket_of(relative, buckets)[:, None] == np.arange(buckets)[None, :]).astype(np.float32)


def toeplitz_heads(per_offset):
    span_count = per_offset.shape[1]
    length = (span_count + 1) // 2
    padded = jnp.pad(per_offset, ((0, 0), (0, 1)))
    repeated = jnp.tile(padded, (1, length))
    window = repeated[:, length - 1 : length - 1 + length * span_count]
    return window.reshape(per_offset.shape[0], length, span_count)[:, :, :length]


def positional_scores(bias_table, onehot_table):
    offsets = jnp.dot(bias_table.T, onehot_table.T, precision=HIGHEST)
    return toeplitz_heads(offsets)


def rms_apply(values, gain_row):
    return values * lax.rsqrt(jnp.mean(values * values, axis=-1, keepdims=True) + EPS) * gain_row


def slot_numbers(route_rows, expert_count):
    flat_routes = route_rows.reshape(-1)
    marked = (flat_routes[:, None] == jnp.arange(expert_count, dtype=jnp.int32)[None, :]).astype(
        jnp.int32
    )
    before = jnp.cumsum(marked, axis=0) - marked
    return jnp.sum(before * marked, axis=1).reshape(route_rows.shape)


def geglu(gate_pre, up_pre):
    return jax.nn.gelu(gate_pre, approximate=True) * up_pre


def body(
    tokens,
    cotangent,
    gain_attn,
    w_query,
    w_key,
    w_value,
    w_out,
    rel_bias,
    gain_moe,
    w_router,
    w_gate,
    w_up,
    w_down,
    segments,
    routes,
):
    tok_rows, model_dim = tokens.shape
    head_count = rel_bias.shape[1]
    head_dim = model_dim // head_count
    expert_count = w_router.shape[1]
    capacity = 10 * tok_rows // (4 * expert_count)
    score_scale = head_dim ** (-0.5)
    start_rows = tokens.astype(jnp.float32)
    normed_attn = rms_apply(start_rows, gain_attn).astype(jnp.bfloat16)
    queries = (
        jnp.dot(normed_attn, w_query, preferred_element_type=jnp.float32)
        .astype(jnp.bfloat16)
        .reshape(tok_rows, head_count, head_dim)
    )
    keys_all = (
        jnp.dot(normed_attn, w_key, preferred_element_type=jnp.float32)
        .astype(jnp.bfloat16)
        .reshape(tok_rows, head_count, head_dim)
    )
    values_all = (
        jnp.dot(normed_attn, w_value, preferred_element_type=jnp.float32)
        .astype(jnp.bfloat16)
        .reshape(tok_rows, head_count, head_dim)
    )
    onehot_table = jnp.asarray(offset_onehot(tok_rows, rel_bias.shape[0]))
    positional = positional_scores(rel_bias, onehot_table)
    document = segments[0]
    same_doc = (document[:, None] == document[None, :])[None]

    def masked_scores():
        product = (
            jnp.einsum("qhd,khd->hqk", queries, keys_all, preferred_element_type=jnp.float32)
            * score_scale
            + positional
        )
        return jnp.where(same_doc, product, -1e30)

    scores = masked_scores()
    row_peak = jnp.max(scores, axis=-1, keepdims=True)
    log_total = row_peak + jnp.log(jnp.sum(jnp.exp(scores - row_peak), axis=-1, keepdims=True))
    weights_soft = jnp.exp(scores - log_total).astype(jnp.bfloat16)
    attended = (
        jnp.einsum("hqk,khd->qhd", weights_soft, values_all, preferred_element_type=jnp.float32)
        .astype(jnp.bfloat16)
        .reshape(tok_rows, model_dim)
    )
    middle = start_rows + jnp.dot(attended, w_out, preferred_element_type=jnp.float32)
    normed_moe = rms_apply(middle, gain_moe).astype(jnp.bfloat16)
    logits = jnp.dot(normed_moe, w_router, preferred_element_type=jnp.float32)
    chances = jax.nn.softmax(logits, axis=-1)
    chosen = (
        routes[:, :, None] == jnp.arange(expert_count, dtype=jnp.int32)[None, None, :]
    ).astype(jnp.float32)
    gate_values = jnp.sum(chances[:, None, :] * chosen, axis=-1)
    slot_index = slot_numbers(routes, expert_count)
    copies = jnp.broadcast_to(normed_moe[:, None, :], (tok_rows, 2, model_dim))
    dispatch = (
        jnp.zeros((expert_count, capacity, model_dim), jnp.bfloat16)
        .at[routes, slot_index]
        .set(copies)
    )
    arrived = lax.all_to_all(dispatch, "expert", split_axis=0, concat_axis=0, tiled=True)
    flat_rows = arrived.reshape(-1, model_dim)
    gate_pre = jnp.dot(flat_rows, w_gate[0], preferred_element_type=jnp.float32)
    up_pre = jnp.dot(flat_rows, w_up[0], preferred_element_type=jnp.float32)
    hidden = geglu(gate_pre, up_pre).astype(jnp.bfloat16)
    produced = (
        jnp.dot(hidden, w_down[0], preferred_element_type=jnp.float32)
        .astype(jnp.bfloat16)
        .reshape(arrived.shape)
    )
    returned = lax.all_to_all(produced, "expert", split_axis=0, concat_axis=0, tiled=True)
    picked = returned[routes, slot_index].astype(jnp.float32)
    layer_out = (middle + jnp.sum(gate_values[:, :, None] * picked, axis=1)).astype(jnp.bfloat16)
    grad_out = cotangent.astype(jnp.float32)
    grad_gates = jnp.sum(grad_out[:, None, :] * picked, axis=-1)
    grad_rows = (gate_values[:, :, None] * grad_out[:, None, :]).astype(jnp.bfloat16)
    grad_dispatch = (
        jnp.zeros((expert_count, capacity, model_dim), jnp.bfloat16)
        .at[routes, slot_index]
        .set(grad_rows)
    )
    arrived = lax.all_to_all(dispatch, "expert", split_axis=0, concat_axis=0, tiled=True)
    arrived_grads = lax.all_to_all(grad_dispatch, "expert", split_axis=0, concat_axis=0, tiled=True)
    leading = arrived.shape[:2]
    flat_rows = arrived.reshape(-1, model_dim)
    gate_pre = jnp.dot(flat_rows, w_gate[0], preferred_element_type=jnp.float32)
    up_pre = jnp.dot(flat_rows, w_up[0], preferred_element_type=jnp.float32)
    hidden, pullback = jax.vjp(geglu, gate_pre, up_pre)
    grad_hidden = jnp.dot(
        arrived_grads.reshape(-1, model_dim), w_down[0].T, preferred_element_type=jnp.float32
    )
    grad_gate, grad_up = pullback(grad_hidden)
    grad_gate = grad_gate.astype(jnp.bfloat16)
    grad_up = grad_up.astype(jnp.bfloat16)
    grad_in = jnp.dot(grad_gate, w_gate[0].T, preferred_element_type=jnp.float32) + jnp.dot(
        grad_up, w_up[0].T, preferred_element_type=jnp.float32
    )
    grad_in, hidden, grad_gate, grad_up = (
        grad_in.astype(jnp.bfloat16),
        hidden.astype(jnp.bfloat16),
        grad_gate,
        grad_up,
    )
    sent_back = lax.all_to_all(
        grad_in.reshape(arrived.shape), "expert", split_axis=0, concat_axis=0, tiled=True
    )
    hidden_here = hidden.reshape(leading + (-1,))
    gate_here = grad_gate.reshape(leading + (-1,))
    up_here = grad_up.reshape(leading + (-1,))
    flat_rows = arrived.reshape(-1, model_dim)
    flat_grads = arrived_grads.reshape(-1, model_dim)
    hidden_flat = hidden_here.reshape(flat_rows.shape[0], -1)
    gate_flat = gate_here.reshape(flat_rows.shape[0], -1)
    up_flat = up_here.reshape(flat_rows.shape[0], -1)
    down_term = jnp.einsum("nf,nd->fd", hidden_flat, flat_grads, preferred_element_type=jnp.float32)
    gate_term = jnp.einsum("nd,nf->df", flat_rows, gate_flat, preferred_element_type=jnp.float32)
    up_term = jnp.einsum("nd,nf->df", flat_rows, up_flat, preferred_element_type=jnp.float32)
    gate_grad, up_grad, down_grad = (
        lax.psum_scatter(
            gate_term[None].astype(jnp.bfloat16), "dp", scatter_dimension=1, tiled=True
        ).astype(jnp.float32),
        lax.psum_scatter(
            up_term[None].astype(jnp.bfloat16), "dp", scatter_dimension=1, tiled=True
        ).astype(jnp.float32),
        lax.psum_scatter(
            down_term[None].astype(jnp.bfloat16), "dp", scatter_dimension=1, tiled=True
        ).astype(jnp.float32),
    )
    grad_copies = sent_back[routes, slot_index].astype(jnp.float32)
    grad_chances = jnp.sum(grad_gates[:, :, None] * chosen, axis=1)
    grad_logits = chances * (grad_chances - jnp.sum(chances * grad_chances, axis=-1, keepdims=True))
    router_wide = w_router.astype(jnp.float32)
    grad_normed_moe = jnp.sum(grad_copies, axis=1) + jnp.dot(
        grad_logits, router_wide.T, precision=HIGHEST
    )
    router_term = jnp.dot(normed_moe.astype(jnp.float32).T, grad_logits, precision=HIGHEST)
    _, norm_pull = jax.vjp(rms_apply, middle, gain_moe)
    grad_mid_norm, gain_moe_term = norm_pull(grad_normed_moe)
    grad_middle = grad_out + grad_mid_norm
    grad_branch = grad_middle.astype(jnp.bfloat16)
    out_term = jnp.einsum("nd,ne->de", attended, grad_branch, preferred_element_type=jnp.float32)
    grad_attended = (
        jnp.dot(grad_branch, w_out.T, preferred_element_type=jnp.float32)
        .astype(jnp.bfloat16)
        .reshape(tok_rows, head_count, head_dim)
    )
    soft_again = jnp.exp(masked_scores() - log_total)
    grad_soft = jnp.einsum(
        "qhd,khd->hqk", grad_attended, values_all, preferred_element_type=jnp.float32
    )
    grad_values = jnp.einsum(
        "hqk,qhd->khd",
        soft_again.astype(jnp.bfloat16),
        grad_attended,
        preferred_element_type=jnp.float32,
    ).astype(jnp.bfloat16)
    grad_scores = (
        soft_again * (grad_soft - jnp.sum(soft_again * grad_soft, axis=-1, keepdims=True))
    ).astype(jnp.bfloat16)
    grad_queries = (
        (
            jnp.einsum("hqk,khd->qhd", grad_scores, keys_all, preferred_element_type=jnp.float32)
            * score_scale
        )
        .astype(jnp.bfloat16)
        .reshape(tok_rows, model_dim)
    )
    grad_keys = (
        (
            jnp.einsum("hqk,qhd->khd", grad_scores, queries, preferred_element_type=jnp.float32)
            * score_scale
        )
        .astype(jnp.bfloat16)
        .reshape(tok_rows, model_dim)
    )
    grad_values = grad_values.reshape(tok_rows, model_dim)

    def positional_of(bias_table):
        return positional_scores(bias_table, onehot_table)

    _, bias_pull = jax.vjp(positional_of, rel_bias)
    bias_term = bias_pull(grad_scores.astype(jnp.float32))[0]
    query_term = jnp.einsum(
        "nd,ne->de", normed_attn, grad_queries, preferred_element_type=jnp.float32
    )
    key_term = jnp.einsum("nd,ne->de", normed_attn, grad_keys, preferred_element_type=jnp.float32)
    value_term = jnp.einsum(
        "nd,ne->de", normed_attn, grad_values, preferred_element_type=jnp.float32
    )
    grad_normed_attn = (
        jnp.dot(grad_queries, w_query.T, preferred_element_type=jnp.float32)
        + jnp.dot(grad_keys, w_key.T, preferred_element_type=jnp.float32)
        + jnp.dot(grad_values, w_value.T, preferred_element_type=jnp.float32)
    )
    _, attn_pull = jax.vjp(rms_apply, start_rows, gain_attn)
    grad_start, gain_attn_term = attn_pull(grad_normed_attn)
    token_grad = grad_middle + grad_start
    dense_parts = (
        lax.psum_scatter(query_term, ("dp", "expert"), scatter_dimension=0, tiled=True),
        lax.psum_scatter(key_term, ("dp", "expert"), scatter_dimension=0, tiled=True),
        lax.psum_scatter(value_term, ("dp", "expert"), scatter_dimension=0, tiled=True),
        lax.psum_scatter(out_term, ("dp", "expert"), scatter_dimension=0, tiled=True),
        lax.psum_scatter(router_term, ("dp", "expert"), scatter_dimension=0, tiled=True),
        lax.psum_scatter(gain_attn_term, ("dp", "expert"), scatter_dimension=0, tiled=True),
        lax.psum_scatter(gain_moe_term, ("dp", "expert"), scatter_dimension=0, tiled=True),
        lax.psum_scatter(bias_term.reshape(-1), ("dp", "expert"), scatter_dimension=0, tiled=True),
    )
    return (
        layer_out,
        token_grad,
        dense_parts[0],
        dense_parts[1],
        dense_parts[2],
        dense_parts[3],
        dense_parts[5],
        dense_parts[6],
        dense_parts[7],
        dense_parts[4],
        gate_grad,
        up_grad,
        down_grad,
    )


def solution(mesh):
    in_specs = (
        P(("dp", "expert"), None),
        P(("dp", "expert"), None),
        P(),
        P(),
        P(),
        P(),
        P(),
        P(),
        P(),
        P(),
        P("expert", None, None),
        P("expert", None, None),
        P("expert", None, None),
        P(("dp", "expert"), None),
        P(("dp", "expert"), None),
    )
    out_specs = (
        P(("dp", "expert"), None),
        P(("dp", "expert"), None),
        P(("dp", "expert"), None),
        P(("dp", "expert"), None),
        P(("dp", "expert"), None),
        P(("dp", "expert"), None),
        P(("dp", "expert")),
        P(("dp", "expert")),
        P(("dp", "expert")),
        P(("dp", "expert"), None),
        P("expert", "dp", None),
        P("expert", "dp", None),
        P("expert", "dp", None),
    )
    return jax.shard_map(body, mesh=mesh, in_specs=in_specs, out_specs=out_specs, check_vma=False)
```

profile of v0, /device:TPU:0, one launch (start us, length us, event | category | flops | bytes accessed | tf_op | source)
XLA Modules:
  0.0 1482.4 jit_solution(8487545132882193816)
XLA Ops:
  39.5 39.7 %copy.184 = f32[2,8,512,1024]{3,1,2,0:T(8,128)} copy(f32[2,8,512,1024]{3,2,1,0:T(8,128)S(1)} %bitcast.130) | data formatting | bytes 67108864
  79.2 25.5 %slice.21 = f32[16,523776]{1,0:T(8,128)} slice(f32[16,524288]{1,0:T(8,128)} %bitcast.132), slice={[0:16], [511:524287]} | slice | bytes 67043328 | tf_op jit(solution)/shard_map/slice | solution.py:37
  104.7 51.2 %reshape.229 = f32[16,512,1023]{2,1,0:T(8,128)} reshape(f32[16,523776]{1,0:T(8,128)} %slice.21) | data formatting | bytes 67043328 | tf_op jit(solution)/shard_map/reshape | solution.py:38
  167.5 17.6 %copy.182 = f32[16,512,512]{1,2,0:T(8,128)} copy(f32[16,512,512]{2,1,0:T(8,128)} %slice.22) | data formatting | bytes 33554432
  185.1 15.3 %fusion.71 = (f32[16,512]{1,0:T(8,128)S(1)}, f32[16,512,512]{1,2,0:T(8,128)}) fusion(f32[16,512,512]{1,2,0:T(8,128)} %copy.182, bf16[512,16,64]{0,2,1:T(8,128)(2,1)} %bitcast.139, bf16[512,16,64]{0,2,1:T(8,128)(2,1)} %bitcast.133, pred[512,512]{0,1:T(8,128)(4,1)S(1)} %broadcast_compare_fusion), kind=kOutput, calls=%fused_computation.123 | convolution fusion | flops 553639936 | bytes 35946496 | tf_op jit(solution)/shard_map/qhd,khd->hqk/dot_general | solution.py:110
  259.5 12.1 all-to-all-done
  276.6 13.8 fusion.14
  290.5 17.5 %all-to-all-done.2 = bf16[4,320,1024]{2,1,0:T(8,128)(2,1)} async-done(((bf16[4,320,1024]{2,1,0:T(8,128)(2,1)}), bf16[4,320,1024]{2,1,0:T(8,128)(2,1)}, u32[]{:S(2)}, u32[]{:S(2)}) %all-to-all-start.2) | async-done | bytes 2621472 | tf_op jit(solution)/shard_map/all_to_all | solution.py:162
  308.0 13.9 fusion.8
  321.9 26.8 %fusion.6 = (bf16[1280,2816]{1,0:T(8,128)(2,1)}, bf16[1280,2816]{1,0:T(8,128)(2,1)}, bf16[1280,2816]{1,0:T(8,128)(2,1)}) fusion(f32[1280,2816]{1,0:T(8,128)} %fusion.8, f32[1280,2816]{1,0:T(8,128)} %fusion.14, bf16[1280,1024]{1,0:T(8,128)(2,1)} %bitcast.10, bf16[1,1024,2816]{2,1,0:T(8,128)(2,1)} %param.26), kind=kOutput, calls=%fused_computation.19 | convolution fusion | flops 7475691520 | bytes 58851328 | tf_op jit(solution)/shard_map/dot_general | solution.py:142
  348.7 12.8 fusion.22
  368.2 29.3 %all-to-all-done.1 = bf16[4,320,1024]{2,1,0:T(8,128)(2,1)} async-done(((bf16[4,320,1024]{2,1,0:T(8,128)(2,1)}), bf16[4,320,1024]{2,1,0:T(8,128)(2,1)}, u32[]{:S(2)}, u32[]{:S(2)}) %all-to-all-start.1) | async-done | bytes 2621472 | tf_op jit(solution)/shard_map/all_to_all | solution.py:150
  397.6 20.9 %gather_fusion = bf16[1024,1024]{1,0:T(8,128)(2,1)} fusion(bf16[4,320,1024]{2,1,0:T(8,128)(2,1)} %all-to-all-done.1, s32[1024]{0:T(1024)S(1)} %reshape.255), kind=kCustom, calls=%fused_computation | custom fusion | bytes 4202496 | tf_op jit(solution)/shard_map/gather | solution.py:151
  437.6 12.4 convert_bitcast_fusion
  450.1 13.2 convert_bitcast_fusion.2
  463.4 13.0 convert_bitcast_fusion.1
  476.4 11.6 fusion.12
  488.0 11.7 add_convert_fusion
  499.7 36.3 %all_to_all.21 = bf16[4,320,1024]{2,1,0:T(8,128)(2,1)} all-to-all(bf16[4,320,1024]{2,1,0:T(8,128)(2,1)S(1)} %bitcast.150), channel_id=1, replica_groups=mesh['dp'=8,'expert'=4] {'expert'}, dimensions={0} | all-to-all | bytes 5242880 | tf_op jit(solution)/shard_map/all_to_all | solution.py:183
  536.0 20.9 %gather_fusion.1 = bf16[1024,1024]{1,0:T(8,128)(2,1)} fusion(bf16[4,320,1024]{2,1,0:T(8,128)(2,1)} %all_to_all.21, s32[1024]{0:T(1024)S(1)} %reshape.255), kind=kCustom, calls=%fused_computation.1 | custom fusion | bytes 4202496 | tf_op jit(solution)/shard_map/gather | solution.py:208
  599.7 11.9 multiply_reduce_fusion
  611.6 12.1 multiply_convert_fusion
  631.4 12.6 copy.183
  653.5 36.9 %reshape.241 = bf16[16,523776]{1,0:T(8,128)(2,1)} reshape(bf16[16,512,1023]{2,1,0:T(8,128)(2,1)} %pad.18.clone) | data formatting | bytes 33521664 | tf_op jit(solution)/shard_map/transpose(jvp())/reshape | solution.py:38
  710.2 35.7 %copy.186 = f32[2,8,512,1024]{3,2,1,0:T(8,128)} copy(f32[2,8,512,1024]{3,1,2,0:T(8,128)S(1)} %bitcast.131) | data formatting | bytes 67108864
  745.9 12.2 bitcast_reduce_fusion
  767.0 44.0 %all-reduce.6 = (f32[1024]{0:T(1024)S(1)}, f32[1024]{0:T(1024)S(1)}, f32[512]{0:T(512)S(1)}) all-reduce(f32[1024]{0:T(1024)S(1)} %get-tuple-element.17, f32[1024]{0:T(1024)S(1)} %get-tuple-element.13, f32[512]{0:T(512)S(1)} %reshape.244), channel_id=6, replica_groups=mesh['dp'=8,'expert'=4] {'dp','expert'}, use_global_device_ids=true, to_apply=%region_25.26.clone | all-reduce | flops 2560 | bytes 20480
  822.9 89.3 %reduce-scatter.21.cloned.1.call-done = bf16[1,128,2816]{2,1,0:T(8,128)(2,1)} async-done(((bf16[1,1024,2816]{2,1,0:T(8,128)(2,1)}), bf16[1,128,2816]{2,1,0:T(8,128)(2,1)}) %reduce-scatter.21.cloned.1.call-update) | async-done | bytes 720912 | tf_op jit(solution)/shard_map/reduce_scatter | solution.py:201
  914.4 141.3 %reduce-scatter.17.cloned.1.call-done = f32[32,1024]{1,0:T(8,128)} async-done(((f32[1024,1024]{1,0:T(8,128)}), f32[32,1024]{1,0:T(8,128)}) %reduce-scatter.17.cloned.1.call-update) | async-done | bytes 131088 | tf_op jit(solution)/shard_map/reduce_scatter | solution.py:281
  1055.7 139.7 %reduce-scatter.15.cloned.1.call-done = f32[32,1024]{1,0:T(8,128)} async-done(((f32[1024,1024]{1,0:T(8,128)}), f32[32,1024]{1,0:T(8,128)}) %reduce-scatter.15.cloned.1.call-update) | async-done | bytes 131088 | tf_op jit(solution)/shard_map/reduce_scatter | solution.py:280
  1195.4 139.8 %reduce-scatter.13.cloned.1.call-done = f32[32,1024]{1,0:T(8,128)} async-done(((f32[1024,1024]{1,0:T(8,128)}), f32[32,1024]{1,0:T(8,128)}) %reduce-scatter.13.cloned.1.call-update) | async-done | bytes 131088 | tf_op jit(solution)/shard_map/reduce_scatter | solution.py:279
  1335.2 139.9 %reduce-scatter.11.cloned.1.call-done = f32[32,1024]{1,0:T(8,128)} async-done(((f32[1024,1024]{1,0:T(8,128)}), f32[32,1024]{1,0:T(8,128)}) %reduce-scatter.11.cloned.1.call-update) | async-done | bytes 131088 | tf_op jit(solution)/shard_map/reduce_scatter | solution.py:278
  (193 shorter events, 236.2 us)
Async XLA Ops:
  7.2 21.8 %copy-start = (bf16[1024,1024]{1,0:T(8,128)(2,1)S(1)}, bf16[1024,1024]{1,0:T(8,128)(2,1)}, u32[]{:S(2)}) copy-start(bf16[1024,1024]{1,0:T(8,128)(2,1)} %param.21) | copy-start | bytes 6291460
  7.2 9.5 copy-start.5
  7.2 9.2 copy-start.39
  7.2 9.5 copy-start.35
  10.8 18.1 %copy-start.33 = (f32[512]{0:T(512)}, f32[512]{0:T(512)S(1)}, u32[]{:S(2)}) copy-start(f32[512]{0:T(512)S(1)} %fusion.59) | copy-start | bytes 6148
  29.0 4.6 copy-start.38
  200.4 8.4 copy-start.10
  208.8 8.7 copy-start.20
  208.8 8.7 copy-start.17
  235.0 36.6 %all-to-all-start = ((bf16[4,320,1024]{2,1,0:T(8,128)(2,1)}), bf16[4,320,1024]{2,1,0:T(8,128)(2,1)}, u32[]{:S(2)}, u32[]{:S(2)}) async-start(bf16[4,320,1024]{2,1,0:T(8,128)(2,1)} %bitcast.137), calls=%async_computation | async-start | bytes 5242880 | tf_op jit(solution)/shard_map/all_to_all | solution.py:140
  271.7 36.3 %all-to-all-start.2 = ((bf16[4,320,1024]{2,1,0:T(8,128)(2,1)}), bf16[4,320,1024]{2,1,0:T(8,128)(2,1)}, u32[]{:S(2)}, u32[]{:S(2)}) async-start(bf16[4,320,1024]{2,1,0:T(8,128)(2,1)} %bitcast.138), calls=%async_computation.2 | async-start | bytes 5242880 | tf_op jit(solution)/shard_map/all_to_all | solution.py:162
  361.5 4.7 copy-start.37
  361.5 36.1 %all-to-all-start.1 = ((bf16[4,320,1024]{2,1,0:T(8,128)(2,1)}), bf16[4,320,1024]{2,1,0:T(8,128)(2,1)}, u32[]{:S(2)}, u32[]{:S(2)}) async-start(bf16[4,320,1024]{2,1,0:T(8,128)(2,1)} %bitcast.149), calls=%async_computation.1 | async-start | bytes 5242880 | tf_op jit(solution)/shard_map/all_to_all | solution.py:150
  366.2 450.6 %reduce-scatter.25.cloned.1.call-start = ((), (), s32[]{:S(2)}) async-start(), calls=%async_computation.19 | async-start | bytes 540672
  437.6 380.6 %reduce-scatter.23.cloned.1.call-start = ((), (), s32[]{:S(2)}) async-start(), calls=%async_computation.18 | async-start | bytes 6488064 | tf_op jit(solution)/shard_map/reduce_scatter | solution.py:204
  450.1 370.5 %reduce-scatter.19.cloned.1.call-start = ((), (), s32[]{:S(2)}) async-start(), calls=%async_computation.16 | async-start | bytes 6488064 | tf_op jit(solution)/shard_map/reduce_scatter | solution.py:198
  463.3 448.8 %reduce-scatter.21.cloned.1.call-start = ((), (), s32[]{:S(2)}) async-start(), calls=%async_computation.17 | async-start | bytes 6488064 | tf_op jit(solution)/shard_map/reduce_scatter | solution.py:201
  476.4 579.4 %reduce-scatter.17.cloned.1.call-start = ((), (), s32[]{:S(2)}) async-start(), calls=%async_computation.15 | async-start | bytes 4325376 | tf_op jit(solution)/shard_map/reduce_scatter | solution.py:281
  562.4 8.5 copy-start.24
  562.4 8.5 copy-start.26
  562.4 8.5 copy-start.28
  570.9 4.0 copy-start.3
  581.1 5.1 copy-start.21
  581.1 614.3 %reduce-scatter.15.cloned.1.call-start = ((), (), s32[]{:S(2)}) async-start(), calls=%async_computation.14 | async-start | bytes 4325376 | tf_op jit(solution)/shard_map/reduce_scatter | solution.py:280
  586.2 10.0 copy-start.6
  586.2 10.0 copy-start.34
  586.2 10.0 copy-start.36
  599.7 735.6 %reduce-scatter.13.cloned.1.call-start = ((), (), s32[]{:S(2)}) async-start(), calls=%async_computation.13 | async-start | bytes 4325376 | tf_op jit(solution)/shard_map/reduce_scatter | solution.py:279
  611.6 12.1 copy-start.9
  631.4 843.7 %reduce-scatter.11.cloned.1.call-start = ((), (), s32[]{:S(2)}) async-start(), calls=%async_computation.12 | async-start | bytes 4325376 | tf_op jit(solution)/shard_map/reduce_scatter | solution.py:278
  745.9 12.2 copy-start.16
  763.9 48.8 %copy-start.30 = (f32[512]{0:T(512)S(1)}, f32[512]{0:T(512)}, u32[]{:S(2)}) copy-start(f32[512]{0:T(512)} %copy-done.29) | copy-start | bytes 6148
  (20 other events, 44.0 us)
Sparse Core Ops, SparseCore 0:
  437.7 135.8 reduce-scatter.24
  577.7 105.8 reduce-scatter.22
  687.6 110.4 reduce-scatter.18
  802.1 109.9 reduce-scatter.20
  914.9 140.7 reduce-scatter.16
  1058.5 136.8 reduce-scatter.14
  1198.4 136.8 reduce-scatter.12
  1338.2 136.8 reduce-scatter.10
where the time goes:
time: 1490 us; the launch traced here: 1480 us
  waiting for transfers between devices  709 us (48%)
  local copies, waits for them, and re-layouts  347 us (23%)
  matrix products  227 us (15%)
  other arithmetic  89 us (6%)
  blocking collectives  80.2 us (5%)
  between operations  15.3 us (1%)
    reduce_scatter x1, waiting for transfers between devices, body(): lax.psum_scatter(out_term, ('dp', 'expert'), scatter_dimension=0, tiled=T...  141 us
    reduce_scatter x1, waiting for transfers between devices, body(): lax.psum_scatter(query_term, ('dp', 'expert'), scatter_dimension=0, tiled...  140 us
    reduce_scatter x1, waiting for transfers between devices, body(): lax.psum_scatter(key_term, ('dp', 'expert'), scatter_dimension=0, tiled=T...  140 us
    reduce_scatter x1, waiting for transfers between devices, body(): lax.psum_scatter(value_term, ('dp', 'expert'), scatter_dimension=0, tiled...  140 us
    unnamed x95, local copies, waits for them, and re-layouts  132 us
    reduce_scatter x1, waiting for transfers between devices, body(): lax.psum_scatter(up_term[None].astype(jnp.bfloat16), 'dp', scatter_dimens...  89.3 us
    reshape x2, local copies, waits for them, and re-layouts, toeplitz_heads(): window.reshape(per_offset.shape[0], length, span_count)[:, :, :length]  88.1 us
    unnamed x1, blocking collectives  44 us
  transfers between devices with their start and end apart: 11, of which 8 were waited for; matrix products, arithmetic and copies ran while one was open for 23% of the time, Pallas kernels for 0%

commit v1 on v0

v1 whole, which is shorter than its diff:
```python
import functools

import jax
import jax.numpy as jnp
import numpy as np
from jax import lax
from jax.experimental import pallas as pl
from jax.experimental.pallas import tpu as pltpu
from jax.sharding import PartitionSpec as P

EPS = 1e-06
HIGHEST = lax.Precision.HIGHEST
LANES = 128
BAND = 4 * LANES
HEAD_GROUP = 4
TAIL = 16
FAR = -1e30
BF = jnp.bfloat16
F32 = jnp.float32
VMEM_LIMIT = 56 * 1024 * 1024


def bucket_of(relative, buckets):
    halfway = buckets // 2
    exact_span = halfway // 2
    distance = np.abs(relative)
    beyond = exact_span + (
        np.log(np.maximum(distance, 1) / exact_span)
        / np.log(128.0 / exact_span)
        * (halfway - exact_span)
    ).astype(np.int64)
    beyond = np.minimum(beyond, halfway - 1)
    return (
        (relative > 0).astype(np.int64) * halfway
        + np.where(distance < exact_span, distance, beyond)
    ).astype(np.int32)


def band_onehot(length, buckets):
    place = np.arange(BAND)
    relative = np.where(place <= 3 * LANES, LANES - place, BAND + LANES - place)
    table = (bucket_of(relative, buckets)[None, :] == np.arange(buckets)[:, None]).astype(np.float32)
    table[:, 3 * LANES] = 0.0
    far = np.arange(LANES, length)
    assert np.all(bucket_of(far, buckets) == bucket_of(far, buckets)[0])
    assert np.all(bucket_of(-far, buckets) == bucket_of(-far, buckets)[0])
    return table


FAR_AFTER = 3 * LANES + 1
FAR_BEFORE = 3 * LANES - 1


def dot(a, b):
    return lax.dot_general(a, b, (((1,), (0,)), ((), ())), preferred_element_type=F32)


def dot_nt(a, b):
    return lax.dot_general(a, b, (((1,), (1,)), ((), ())), preferred_element_type=F32)


def dot_tn(a, b):
    return lax.dot_general(a, b, (((0,), (0,)), ((), ())), preferred_element_type=F32)


def split3(value):
    hi = value.astype(BF)
    rest = value - hi.astype(F32)
    mid = rest.astype(BF)
    low = (rest - mid.astype(F32)).astype(BF)
    return hi, mid, low


def rms_scale(value):
    return lax.rsqrt(jnp.mean(value * value, axis=-1, keepdims=True) + EPS)


def params(**kw):
    return pltpu.CompilerParams(vmem_limit_bytes=VMEM_LIMIT, **kw)


COST_SCALE = 0.05


def cost_us(time):
    return pl.CostEstimate(flops=int(time * 1.15e9 * COST_SCALE), bytes_accessed=100000, transcendentals=0)


def call(kernel, args, in_specs, **kw):
    return pl.pallas_call(kernel, in_specs=list(in_specs), compiler_params=params(), **kw)(*args)


def whole_specs(args):
    return [const_spec(a.shape) for a in args]


def const_spec(shape):
    return pl.BlockSpec(shape, lambda *_: (0,) * len(shape))


def selector(code_row, rows):
    place = lax.broadcasted_iota(jnp.int32, (rows, code_row.shape[1]), 0)
    return jnp.where(place == code_row, 1.0, 0.0).astype(BF)


def selector_t(code_column, rows):
    place = lax.broadcasted_iota(jnp.int32, (code_column.shape[0], rows), 1)
    return jnp.where(place == code_column, 1.0, 0.0).astype(BF)


def cot_dispatch_kernel(cot_ref, code_ref, *outs):
    cap = outs[0].shape[0]
    cot = cot_ref[...]
    for m, out in enumerate(outs):
        out[...] = dot(selector(code_ref[m : m + 1, :], cap), cot).astype(BF)


def cot_dispatch(cot, code, experts, cap):
    rows, width = cot.shape
    return pl.pallas_call(
        cot_dispatch_kernel,
        out_shape=[jax.ShapeDtypeStruct((cap, width), BF)] * experts,
        compiler_params=params(),
        cost_estimate=cost_us(3.6),
        name="cot_dispatch",
    )(cot, code)


def band_of(row):
    return pltpu.roll(jnp.broadcast_to(row, (LANES, BAND)), 0, 1, stride=1, stride_axis=0)


def diagonal_sums(skewed):
    eight = skewed[0:8]
    for start in range(8, LANES, 8):
        eight = eight + pltpu.roll(skewed[start : start + 8], BAND - start, 1)
    total = eight[0:1]
    for row in range(1, 8):
        total = total + pltpu.roll(eight[row : row + 1], BAND - row, 1)
    return total


def bias_column(band, row, q_block, k_blocks):
    pieces = []
    for k_block in range(k_blocks):
        d = k_block - q_block
        if d > 1:
            pieces.append(jnp.broadcast_to(row[:, FAR_AFTER : FAR_AFTER + 1], (LANES, LANES)))
        elif d < -1:
            pieces.append(jnp.broadcast_to(row[:, FAR_BEFORE : FAR_BEFORE + 1], (LANES, LANES)))
        else:
            pieces.append(band[:, LANES * (1 - d) : LANES * (2 - d)])
    return jnp.concatenate(pieces, axis=0)


def only_rows(value, h, head_dim):
    mine = value[h * head_dim : (h + 1) * head_dim]
    none = jnp.zeros_like(mine)
    return jnp.concatenate([mine, none] if h % 2 == 0 else [none, mine], axis=0)


def attn_fwd_kernel(
    tok_ref, gain_a_ref, wq_ref, wk_ref, wv_ref, wo_ref, woff_ref, segc_ref, segr_ref, gain_m_ref, wr_ref, code_ref,
    qs_ref, k_ref, v_ref, att_ref, lse_ref, mid_ref, nm_ref, ch_ref, *rest,
    experts, head_dim,
):
    disp_refs, (n_scr, mask_scr) = rest[:-2], rest[-2:]
    step = pl.program_id(0)
    rows = tok_ref.shape[0]
    blocks = rows // LANES

    @pl.when(step == 0)
    def _():
        start = tok_ref[...].astype(F32)
        n_scr[...] = (start * rms_scale(start) * gain_a_ref[...]).astype(BF)
        mid_ref[...] = start
        mask_scr[...] = jnp.where(segc_ref[...] == segr_ref[...], 0.0, FAR)

    normed = n_scr[...]
    queries = dot(normed, wq_ref[...]).astype(BF)
    scaled = (queries.astype(F32) * head_dim ** (-0.5)).astype(BF)
    keys = dot(normed, wk_ref[...]).astype(BF)
    values = dot(normed, wv_ref[...]).astype(BF)
    qs_ref[...] = scaled
    k_ref[...] = keys
    v_ref[...] = values
    q_t = scaled.T
    v_t = values.T
    heads_t = []
    for h in range(HEAD_GROUP):
        row = woff_ref[0, h : h + 1, :]
        band = band_of(row)
        pair = slice(LANES * (h // 2), LANES * (h // 2 + 1))
        k_pair = keys[:, pair]
        q_only = only_rows(q_t, h, head_dim)
        v_h = v_t[h * head_dim : (h + 1) * head_dim]
        pieces = []
        for b in range(blocks):
            lanes = slice(b * LANES, (b + 1) * LANES)
            s = dot(k_pair, q_only[:, lanes]) + bias_column(band, row, b, blocks) + mask_scr[:, lanes]
            peak = jnp.max(s, axis=0, keepdims=True)
            p = jnp.exp(s - peak)
            total = jnp.sum(p, axis=0, keepdims=True)
            pieces.append(dot(v_h, p.astype(BF)) * (1.0 / total))
            lse_ref[0, h : h + 1, lanes] = peak + jnp.log(total)
        heads_t.append(jnp.concatenate(pieces, axis=1))
    att = jnp.concatenate(heads_t, axis=0).T.astype(BF)
    att_ref[...] = att
    mid_ref[...] += dot(att, wo_ref[...])

    @pl.when(step == pl.num_programs(0) - 1)
    def _():
        mid = mid_ref[...]
        nm = (mid * rms_scale(mid) * gain_m_ref[...]).astype(BF)
        nm_ref[...] = nm
        logits = dot_nt(wr_ref[...], nm)
        live = lax.broadcasted_iota(jnp.int32, logits.shape, 0) < experts
        logits = jnp.where(live, logits, FAR)
        raised = jnp.exp(logits - jnp.max(logits, axis=0, keepdims=True))
        chances = raised / jnp.sum(raised, axis=0, keepdims=True)
        ch_ref[...] = chances
        hi = chances.astype(BF)
        low = (chances - hi.astype(F32)).astype(BF)
        both = jnp.concatenate([hi, low], axis=0)
        cap = disp_refs[0].shape[0] - TAIL
        cap_lanes = -(-cap // LANES) * LANES
        lane_row = lax.broadcasted_iota(jnp.int32, (TAIL, cap_lanes), 0)
        for m, out in enumerate(disp_refs):
            chosen = selector(code_ref[m : m + 1, :], cap_lanes)
            out[0:cap, :] = dot(chosen[:cap], nm).astype(BF)
            gates = dot_nt(both, chosen)
            packed = jnp.where(lane_row == 0, gates[m : m + 1], jnp.where(lane_row == 1, gates[TAIL + m : TAIL + m + 1], 0.0))
            out[cap:, :] = jnp.zeros((TAIL, out.shape[1]), BF)
            out[cap:, 0:cap_lanes] = packed.astype(BF)


def attn_fwd(tokens, gain_attn, w_query, w_key, w_value, w_out, woff, seg, gain_moe, wr_t, code, experts, cap):
    rows, width = tokens.shape
    groups = woff.shape[0]
    cols = width // groups
    col_block = pl.BlockSpec((rows, cols), lambda g: (0, g))
    weight_block = pl.BlockSpec((width, cols), lambda g: (0, g))
    head_dim = cols // HEAD_GROUP
    wide = jax.ShapeDtypeStruct((rows, width), BF)
    return pl.pallas_call(
        functools.partial(attn_fwd_kernel, experts=experts, head_dim=head_dim),
        grid=(groups,),
        in_specs=[
            const_spec((rows, width)),
            const_spec((1, width)),
            weight_block,
            weight_block,
            weight_block,
            pl.BlockSpec((cols, width), lambda g: (g, 0)),
            pl.BlockSpec((1, HEAD_GROUP, BAND), lambda g: (g, 0, 0)),
            const_spec((rows, 1)),
            const_spec((1, rows)),
            const_spec((1, width)),
            const_spec((TAIL, width)),
            const_spec(code.shape),
        ],
        out_specs=[
            col_block,
            col_block,
            col_block,
            col_block,
            pl.BlockSpec((1, HEAD_GROUP, rows), lambda g: (g, 0, 0)),
            const_spec((rows, width)),
            const_spec((rows, width)),
            const_spec((TAIL, rows)),
        ]
        + [const_spec((cap + TAIL, width))] * experts,
        out_shape=[
            wide,
            wide,
            wide,
            wide,
            jax.ShapeDtypeStruct((groups, HEAD_GROUP, rows), F32),
            jax.ShapeDtypeStruct((rows, width), F32),
            wide,
            jax.ShapeDtypeStruct((TAIL, rows), F32),
        ]
        + [jax.ShapeDtypeStruct((cap + TAIL, width), BF)] * experts,
        scratch_shapes=[pltpu.VMEM((rows, width), BF), pltpu.VMEM((rows, rows), F32)],
        compiler_params=params(),
        cost_estimate=cost_us(31),
        name="attn_fwd",
    )(
        tokens, gain_attn[None], w_query, w_key, w_value, w_out, woff, seg.reshape(rows, 1), seg.reshape(1, rows),
        gain_moe[None], wr_t, code,
    )


def gelu_parts(gate):
    c0 = np.float32(np.sqrt(2.0 / np.pi))
    c1 = np.float32(0.044715)
    square = gate * gate
    t = jnp.tanh(c0 * gate * (1.0 + c1 * square))
    half = 0.5 * (1.0 + t)
    value = gate * half
    slope = half + 0.5 * gate * (1.0 - t * t) * (c0 * (1.0 + 3.0 * c1 * square))
    return value, slope


def column_of(packed, cap):
    total = jnp.sum(packed.astype(F32), axis=0, keepdims=True)
    row = lax.broadcasted_iota(jnp.int32, (cap, cap), 0)
    lane = lax.broadcasted_iota(jnp.int32, (cap, cap), 1)
    return jnp.sum(jnp.where(row == lane, total, 0.0), axis=1, keepdims=True)


FF_BLOCK = 256


def cot_hidden_kernel(*refs):
    c_refs, wd_ref, out_ref, c_scr = refs[:-3], refs[-3], refs[-2], refs[-1]
    cap = c_refs[0].shape[0]

    @pl.when(pl.program_id(0) == 0)
    def _():
        for m, c_ref in enumerate(c_refs):
            c_scr[m * cap : (m + 1) * cap, :] = c_ref[...]

    out_ref[...] = dot_nt(c_scr[...], wd_ref[0]).astype(BF)


def cot_hidden(cs, w_down):
    experts = len(cs)
    cap, width = cs[0].shape
    rows, ff = experts * cap, w_down.shape[1]
    return call(
        cot_hidden_kernel,
        (*cs, w_down),
        whole_specs(cs) + [pl.BlockSpec((1, FF_BLOCK, width), lambda f: (0, f, 0))],
        grid=(ff // FF_BLOCK,),
        out_specs=pl.BlockSpec((rows, FF_BLOCK), lambda f: (0, f)),
        out_shape=jax.ShapeDtypeStruct((rows, ff), BF),
        scratch_shapes=[pltpu.VMEM((rows, width), BF)],
        cost_estimate=cost_us(14.7),
        name="cot_hidden",
    )


def expert_first(place_ref, x_refs, c_refs, x_ref, xt_ref, gate_ref, gc_ref):
    cap = c_refs[0].shape[0]
    for m, (x_part, c_part) in enumerate(zip(x_refs, c_refs)):
        part = slice(m * cap, (m + 1) * cap)
        x_ref[part, :] = x_part[0:cap, :]
        gate = column_of(x_part[cap:, 0:cap], cap)
        gate_ref[part, :] = jnp.broadcast_to(gate, (cap, LANES))
        gc_ref[part, :] = (c_part[...].astype(F32) * gate).astype(BF)
    flipped = x_ref[...].T
    owners = place_ref.shape[0]
    rows = flipped.shape[0] // owners
    for b in range(owners):
        at = pl.multiple_of(place_ref[b] * rows, rows)
        xt_ref[pl.ds(at, rows), :] = flipped[b * rows : (b + 1) * rows]


ROW_BLOCK = 320


def expert_a_kernel(*refs, experts, second_first):
    step = pl.program_id(0)
    if experts:
        place_ref, x_parts, c_parts = refs[0], refs[1 : 1 + experts], refs[1 + experts : 1 + 2 * experts]
        gh_ref, wg_ref, wu_ref = refs[1 + 2 * experts : 4 + 2 * experts]
        x_ref, xt_ref, gate_ref, gc_ref = refs[4 + 2 * experts : 8 + 2 * experts]

        @pl.when(step == 0)
        def _():
            expert_first(place_ref, x_parts, c_parts, x_ref, xt_ref, gate_ref, gc_ref)

    else:
        x_ref, xt_ref, gate_ref, gh_ref, wg_ref, wu_ref = refs[:6]
    keep_ref, send_ref, sc_ref, hid_ref, hidt_ref, gg_ref, gu_ref = refs[-7:]

    @pl.when(step == 0)
    def _():
        sc_ref[...] = jnp.zeros_like(sc_ref)

    wg, wu = wg_ref[0], wu_ref[0]
    width = wg.shape[1]
    for start in range(0, x_ref.shape[0], ROW_BLOCK):
        part = slice(start, start + ROW_BLOCK)
        x = x_ref[part, :]
        gate_pre = dot(x, wg)
        up_pre = dot(x, wu)
        grad = gh_ref[part, :].astype(F32)
        act, slope = gelu_parts(gate_pre)
        hidden = act * up_pre
        hid_ref[part, :] = hidden.astype(BF)
        product = hidden * grad
        folded = product[:, 0:LANES]
        for i in range(1, width // LANES):
            folded = folded + product[:, i * LANES : (i + 1) * LANES]
        sc_ref[part, :] += folded
        grad = grad * gate_ref[part, 0:1]
        gg_ref[part, :] = (slope * up_pre * grad).astype(BF)
        gu_ref[part, :] = (act * grad).astype(BF)
    hidt_ref[...] = hid_ref[...].T
    xt = xt_ref[...]
    cut = xt.shape[0] // 4
    for i, grad_ref in enumerate((gg_ref, gu_ref)):
        term = dot(xt, grad_ref[...]).astype(BF)
        for q in range(4):
            upper, lower = (q % 2, q // 2) if second_first else (q // 2, q % 2)
            (send_ref if upper else keep_ref)[i, lower * cut : (lower + 1) * cut] = term[q * cut : (q + 1) * cut]


def expert_a(source, gh, w_gate, w_up, first, count, second_first, filled=()):
    opening = len(source[1]) if isinstance(source[1], (list, tuple)) else 0
    rows, ff = gh.shape
    width = w_gate.shape[1]
    span = count * FF_BLOCK
    col_weight = pl.BlockSpec((1, width, FF_BLOCK), lambda f: (0, 0, first + f))
    out_block = pl.BlockSpec((rows, FF_BLOCK), lambda f: (0, first + f))
    wide = jax.ShapeDtypeStruct((rows, ff), BF)
    tall = jax.ShapeDtypeStruct((ff, rows), BF)
    term = jax.ShapeDtypeStruct((2, width // 2, span), BF)
    term_block = pl.BlockSpec((2, width // 2, FF_BLOCK), lambda f: (0, 0, f))
    if opening:
        place, xs, cs = source
        args = (place, *xs, *cs)
        specs = [pl.BlockSpec(memory_space=pltpu.SMEM)] + whole_specs(xs) + whole_specs(cs)
        shared = [
            jax.ShapeDtypeStruct((rows, width), BF),
            jax.ShapeDtypeStruct((width, rows), BF),
            jax.ShapeDtypeStruct((rows, LANES), F32),
            jax.ShapeDtypeStruct((rows, width), BF),
        ]
    else:
        args = tuple(source)
        specs = whole_specs(source)
        shared = []
    args = (*args, gh, w_gate, w_up)
    used = len(args)
    first_filled = len(shared) + 3

    def run(*refs):
        expert_a_kernel(*refs[:used], *refs[used + len(filled) :], experts=opening, second_first=second_first)

    return pl.pallas_call(
        run,
        grid=(count,),
        in_specs=specs
        + [out_block, col_weight, col_weight]
        + [pl.BlockSpec(memory_space=pl.ANY)] * len(filled),
        out_specs=whole_specs(shared)
        + [term_block, term_block, const_spec((rows, LANES)), out_block]
        + [pl.BlockSpec((FF_BLOCK, rows), lambda f: (first + f, 0)), out_block, out_block],
        out_shape=shared + [term, term, jax.ShapeDtypeStruct((rows, LANES), F32), wide, tall, wide, wide],
        input_output_aliases={used + i: first_filled + i for i in range(len(filled))},
        compiler_params=params(),
        cost_estimate=cost_us(5.4 * count),
        name="expert_grads",
    )(*args, *filled)


def expert_b_kernel(gg_ref, gu_ref, *refs, cap):
    sc_refs, (wg_ref, wu_ref, out_ref, acc) = refs[:-4], refs[-4:]
    part_sum = dot_nt(gg_ref[...], wg_ref[0]) + dot_nt(gu_ref[...], wu_ref[0])
    step, block = pl.program_id(0), pl.program_id(1)

    @pl.when(step == 0)
    def _():
        acc[block] = part_sum

    @pl.when(step == pl.num_programs(0) - 1)
    def _():
        total = acc[block] + part_sum
        row = lax.broadcasted_iota(jnp.int32, (cap, cap), 0)
        lane = lax.broadcasted_iota(jnp.int32, (cap, cap), 1)
        place = lax.broadcasted_iota(jnp.int32, (TAIL, cap), 0)
        for at in range(total.shape[0] // cap):
            part = slice(at * cap, (at + 1) * cap)
            out_ref[at, 0:cap, :] = total[part].astype(BF)
            folded = sc_refs[0][part, :]
            for other in sc_refs[1:]:
                folded = folded + other[part, :]
            column = jnp.sum(folded, axis=1, keepdims=True)
            flat = jnp.sum(jnp.where(row == lane, column, 0.0), axis=0, keepdims=True)
            hi, mid, low = split3(flat)
            packed = jnp.where(
                place == 0, hi.astype(F32), jnp.where(place == 1, mid.astype(F32), jnp.where(place == 2, low.astype(F32), 0.0))
            )
            out_ref[at, cap : cap + TAIL, :] = jnp.zeros((TAIL, total.shape[1]), BF)
            out_ref[at, cap : cap + TAIL, 0:cap] = packed.astype(BF)


def expert_b(gg, gu, scs, w_gate, w_up, experts, upper):
    rows, ff = gg.shape
    width = w_gate.shape[1]
    cap = rows // experts
    blocks = rows // 2 // ROW_BLOCK
    first = blocks if upper else 0
    cut = ff // 2
    grads = pl.BlockSpec((ROW_BLOCK, cut), lambda k, m: (first + m, k))
    sums = pl.BlockSpec((ROW_BLOCK, LANES), lambda k, m: (first + m, 0))
    weight = pl.BlockSpec((1, width, cut), lambda k, m: (0, 0, k))
    return call(
        functools.partial(expert_b_kernel, cap=cap),
        (gg, gu, *scs, w_gate, w_up),
        [grads, grads] + [sums] * len(scs) + [weight, weight],
        grid=(2, blocks),
        out_specs=pl.BlockSpec((ROW_BLOCK // cap, cap + TAIL, width), lambda k, m: (m, 0, 0)),
        out_shape=jax.ShapeDtypeStruct((experts // 2, cap + TAIL, width), BF),
        scratch_shapes=[pltpu.VMEM((blocks, ROW_BLOCK, width), F32)],
        cost_estimate=cost_us(16),
        name="expert_input_grad",
    )


def down_kernel(place_a_ref, place_b_ref, hidt_ref, gc_ref, *outs):
    ff, half = outs[0].shape
    shard = ff // place_a_ref.shape[0]
    size = int(np.gcd(shard, 32))
    rows = hidt_ref.shape[0]
    step = pl.program_id(0)
    total = dot(hidt_ref[...], gc_ref[...]).astype(BF)
    for i in range(rows // size):
        row = step * rows + i * size
        owner = row // shard
        piece = total[i * size : (i + 1) * size]
        for out, place_ref, cols in ((outs[0], place_a_ref, piece[:, :half]), (outs[1], place_b_ref, piece[:, half:])):
            at = place_ref[owner] * shard + (row - owner * shard)
            out[pl.ds(pl.multiple_of(at, size), size), :] = cols


def down_grads(hid_t, grad_cots, place_a, place_b):
    rows, width = grad_cots.shape
    ff = hid_t.shape[0]
    table = pl.BlockSpec(memory_space=pltpu.SMEM)
    half = jax.ShapeDtypeStruct((ff, width // 2), BF)
    return call(
        down_kernel,
        (place_a, place_b, hid_t, grad_cots),
        [table, table, pl.BlockSpec((ff // 4, rows), lambda f: (f, 0)), const_spec((rows, width))],
        grid=(4,),
        out_specs=[const_spec(half.shape)] * 2,
        out_shape=[half] * 2,
        cost_estimate=cost_us(13),
        name="down_grads",
    )


def produced_kernel(me_ref, hid_ref, wd_ref, out_ref):
    del me_ref
    out_ref[0] = dot(hid_ref[...], wd_ref[0]).astype(BF)


def produced_rows(me, hid, w_down, experts):
    rows, ff = hid.shape
    width = w_down.shape[2]
    cap = rows // experts
    return pl.pallas_call(
        produced_kernel,
        grid_spec=pltpu.PrefetchScalarGridSpec(
            num_scalar_prefetch=1,
            grid=(experts,),
            in_specs=[
                pl.BlockSpec((cap, ff), lambda m, me_ref: (m, 0)),
                pl.BlockSpec(w_down.shape, lambda m, me_ref: (0, 0, 0)),
            ],
            out_specs=pl.BlockSpec((1, cap, width), lambda m, me_ref: (m ^ me_ref[0], 0, 0)),
        ),
        out_shape=jax.ShapeDtypeStruct((experts, cap, width), BF),
        compiler_params=params(),
        cost_estimate=cost_us(2000),
        name="produced_rows",
    )(me.reshape(1).astype(jnp.int32), hid, w_down)


def layer_out_kernel(mid_ref, ch_ref, code_ref, parts_ref, out_ref):
    cap = parts_ref.shape[1]
    total = mid_ref[...]
    for e in range(parts_ref.shape[0]):
        picked = dot(selector_t(code_ref[:, e : e + 1], cap), parts_ref[e])
        total = total + ch_ref[:, e : e + 1] * picked
    out_ref[...] = total.astype(BF)


def distinct(slots):
    arrays = []
    found = []
    for array, index in slots:
        which = next((i for i, other in enumerate(arrays) if other is array), None)
        if which is None:
            which = len(arrays)
            arrays.append(array)
        found.append((which, index))
    return arrays, found


def layer_output(middle, chances_t, code_t, returned):
    rows, width = middle.shape
    return call(
        layer_out_kernel,
        (middle, chances_t, code_t, returned),
        [pl.BlockSpec(memory_space=pltpu.VMEM)] * 4,
        out_shape=jax.ShapeDtypeStruct((rows, width), BF),
        cost_estimate=cost_us(2000),
        name="layer_output",
    )


def moe_bwd_kernel(
    place_ref, cot_ref, mid_ref, gain_ref, nm_ref, ch_ref, wr_ref, code_ref, codet_ref, att_ref, wo_ref, *refs, places
):
    gmid_ref, ga_ref, keep_ref, send_ref, gain_o_ref, router_o_ref, att_scr = refs[-7:]
    experts = len(places)
    cap = refs[0].shape[1] - TAIL
    rows = cot_ref.shape[0]
    grad = jnp.zeros(mid_ref.shape, F32)
    gate_rows = []
    for m, (which, index) in enumerate(places):
        grad = grad + dot(selector_t(codet_ref[:, m : m + 1], cap), refs[which][index, 0:cap, :])
        picked = dot(refs[which][index, cap : cap + TAIL, 0:cap], selector(code_ref[m : m + 1, :], cap))
        gate_rows.append(jnp.sum(picked, axis=0, keepdims=True))
    gate_rows.append(jnp.zeros((TAIL - experts, rows), F32))
    grad_chances = jnp.concatenate(gate_rows, axis=0)
    chances = ch_ref[...]
    grad_logits = chances * (grad_chances - jnp.sum(chances * grad_chances, axis=0, keepdims=True))
    pieces = jnp.concatenate(split3(grad_logits), axis=0)
    wr = wr_ref[...]
    grad = grad + dot_tn(pieces, jnp.concatenate([wr, wr, wr], axis=0))
    router = dot(pieces, nm_ref[...])
    router_o_ref[...] = router[0:TAIL] + router[TAIL : 2 * TAIL] + router[2 * TAIL : 3 * TAIL]
    mid = mid_ref[...]
    scale = rms_scale(mid)
    unit = mid * scale
    gain_o_ref[...] = jnp.sum(grad * unit, axis=0, keepdims=True)
    scaled = grad * gain_ref[...]
    grad_mid = cot_ref[...].astype(F32) + scale * (scaled - unit * jnp.mean(scaled * unit, axis=-1, keepdims=True))
    gmid_ref[...] = grad_mid
    branch = grad_mid.astype(BF)
    ga_ref[...] = dot_nt(branch, wo_ref[...]).astype(BF)
    sort_rows(place_ref, att_ref[...].astype(F32).T, att_scr)
    half = att_scr.shape[0] // 2
    term = dot(att_scr[...].astype(BF), branch).astype(BF)
    keep_ref[0] = term[:half]
    send_ref[0] = term[half:]


def sort_rows(place_ref, value, out_ref):
    owners = place_ref.shape[0]
    rows = value.shape[0] // owners
    for b in range(owners):
        out_ref[pl.ds(pl.multiple_of(place_ref[b] * rows, rows), rows), :] = value[b * rows : (b + 1) * rows]


def moe_bwd(place, cot, middle, gain_moe, normed_moe, chances, wr_t, code, code_t, attended, w_out, slots):
    rows, width = cot.shape
    arrays, found = distinct(slots)
    args = (cot, middle, gain_moe[None], normed_moe, chances, wr_t, code, code_t, attended, w_out, *arrays)
    half = jax.ShapeDtypeStruct((1, width // 2, width), BF)
    return call(
        functools.partial(moe_bwd_kernel, places=found),
        (place, *args),
        [pl.BlockSpec(memory_space=pltpu.SMEM)] + [pl.BlockSpec(memory_space=pltpu.VMEM)] * len(args),
        out_shape=[
            jax.ShapeDtypeStruct((rows, width), F32),
            jax.ShapeDtypeStruct((rows, width), BF),
            half,
            half,
            jax.ShapeDtypeStruct((1, width), F32),
            jax.ShapeDtypeStruct((TAIL, width), F32),
        ],
        scratch_shapes=[pltpu.VMEM((width, rows), F32)],
        cost_estimate=cost_us(11.5),
        name="moe_bwd",
    )


def attn_bwd_kernel(
    qs_ref, k_ref, v_ref, ga_ref, lse_ref, woff_ref, segc_ref, segr_ref,
    dq_ref, dk_ref, dv_ref, dwoff_ref, mask_scr, p_scr, ds_scr,
    *, head_dim,
):
    rows = qs_ref.shape[0]
    blocks = rows // LANES

    @pl.when(pl.program_id(0) == 0)
    def _():
        mask_scr[...] = jnp.where(segc_ref[...] == segr_ref[...], 0.0, FAR)

    scaled, keys, values, grads = qs_ref[...], k_ref[...], v_ref[...], ga_ref[...]
    q_t, g_t, k_t = scaled.T, grads.T, keys.T
    low_half = lax.broadcasted_iota(jnp.int32, (rows, LANES), 1) < head_dim
    dq_t, dk_parts, dv_parts = [], [], []
    lane = lax.broadcasted_iota(jnp.int32, (1, BAND), 1)
    for h in range(HEAD_GROUP):
        row = woff_ref[0, h : h + 1, :]
        band = band_of(row)
        pair = slice(LANES * (h // 2), LANES * (h // 2 + 1))
        k_pair, v_pair = keys[:, pair], values[:, pair]
        q_only, g_only = only_rows(q_t, h, head_dim), only_rows(g_t, h, head_dim)
        tiles = {}
        for b in range(blocks):
            lanes = slice(b * LANES, (b + 1) * LANES)
            s = dot(k_pair, q_only[:, lanes]) + bias_column(band, row, b, blocks) + mask_scr[:, lanes]
            p = jnp.exp(s - lse_ref[0, h : h + 1, lanes])
            dp = dot(v_pair, g_only[:, lanes])
            ds = p * (dp - jnp.sum(p * dp, axis=0, keepdims=True))
            p_scr[:, lanes] = p.astype(BF)
            ds_scr[:, lanes] = ds.astype(BF)
            for k_block in range(blocks):
                d = max(-2, min(2, k_block - b))
                tile = ds[k_block * LANES : (k_block + 1) * LANES]
                tiles[d] = tiles[d] + tile if d in tiles else tile
        skewed = jnp.concatenate([tiles[1], tiles[0], tiles[-1], jnp.zeros_like(tiles[0])], axis=1)
        offsets = diagonal_sums(skewed)
        offsets = offsets + jnp.where(lane == FAR_AFTER, jnp.sum(tiles[2]), 0.0)
        offsets = offsets + jnp.where(lane == FAR_BEFORE, jnp.sum(tiles[-2]), 0.0)
        dwoff_ref[0, h : h + 1, :] = offsets
        p_all, ds_all = p_scr[...], ds_scr[...]
        dv_parts.append(dot(p_all, grads[:, pair]))
        dk_parts.append(dot(ds_all, scaled[:, pair]))
        dq_t.append(dot(k_t[h * head_dim : (h + 1) * head_dim], ds_all))
    dq = jnp.concatenate(dq_t, axis=0).T * head_dim ** (-0.5)
    dq_ref[...] = dq.astype(BF)
    for i in range(HEAD_GROUP // 2):
        pair = slice(LANES * i, LANES * (i + 1))
        dk_ref[:, pair] = jnp.where(low_half, dk_parts[2 * i], dk_parts[2 * i + 1]).astype(BF)
        dv_ref[:, pair] = jnp.where(low_half, dv_parts[2 * i], dv_parts[2 * i + 1]).astype(BF)


def attn_bwd(scaled, keys, values, grad_att, lse, woff, seg):
    rows, width = scaled.shape
    groups = woff.shape[0]
    cols = width // groups
    col_block = pl.BlockSpec((rows, cols), lambda g: (0, g))
    wide = jax.ShapeDtypeStruct((rows, width), BF)
    return call(
        functools.partial(attn_bwd_kernel, head_dim=cols // HEAD_GROUP),
        (scaled, keys, values, grad_att, lse, woff, seg.reshape(rows, 1), seg.reshape(1, rows)),
        [
            col_block,
            col_block,
            col_block,
            col_block,
            pl.BlockSpec((1, HEAD_GROUP, rows), lambda g: (g, 0, 0)),
            pl.BlockSpec((1, HEAD_GROUP, BAND), lambda g: (g, 0, 0)),
            const_spec((rows, 1)),
            const_spec((1, rows)),
        ],
        grid=(groups,),
        out_specs=[col_block, col_block, col_block, pl.BlockSpec((1, HEAD_GROUP, BAND), lambda g: (g, 0, 0))],
        out_shape=[wide, wide, wide, jax.ShapeDtypeStruct((groups, HEAD_GROUP, BAND), F32)],
        scratch_shapes=[
            pltpu.VMEM((rows, rows), F32),
            pltpu.VMEM((rows, rows), BF),
            pltpu.VMEM((rows, rows), BF),
        ],
        cost_estimate=cost_us(2000),
        name="attn_bwd",
    )


def dense_bwd_kernel(
    pq_ref, pk_ref, pv_ref, tok_ref, gain_ref, gmid_ref, dq_ref, dk_ref, dv_ref, wq_ref, wk_ref, wv_ref,
    tg_ref, keep_ref, send_ref, gain_o_ref, sort_scr, nt_scr, acc,
):
    step = pl.program_id(0)

    @pl.when(step == 0)
    def _():
        start = tok_ref[...].astype(F32)
        normed_t = (start * rms_scale(start) * gain_ref[...]).T
        for i, place_ref in enumerate((pq_ref, pk_ref, pv_ref)):
            sort_rows(place_ref, normed_t, sort_scr)
            nt_scr[i] = sort_scr[...].astype(BF)
        acc[...] = jnp.zeros_like(acc)

    total = acc[...]
    half = keep_ref.shape[1]
    for i, (d_ref, w_ref) in enumerate(((dq_ref, wq_ref), (dk_ref, wk_ref), (dv_ref, wv_ref))):
        part = d_ref[...]
        term = dot(nt_scr[i], part).astype(BF)
        keep_ref[i] = term[:half]
        send_ref[i] = term[half:]
        total = total + dot_nt(part, w_ref[...])
    acc[...] = total

    @pl.when(step == pl.num_programs(0) - 1)
    def _():
        grad = acc[...]
        start = tok_ref[...].astype(F32)
        scale = rms_scale(start)
        unit = start * scale
        gain_o_ref[...] = jnp.sum(grad * unit, axis=0, keepdims=True)
        scaled = grad * gain_ref[...]
        tg_ref[...] = gmid_ref[...] + scale * (scaled - unit * jnp.mean(scaled * unit, axis=-1, keepdims=True))


def dense_bwd(places, tokens, gain_attn, grad_mid, dq, dk, dv, w_query, w_key, w_value):
    rows, width = tokens.shape
    cols = 256
    col_block = pl.BlockSpec((rows, cols), lambda g: (0, g))
    weight_block = pl.BlockSpec((width, cols), lambda g: (0, g))
    term = jax.ShapeDtypeStruct((3, width // 2, width), BF)
    term_block = pl.BlockSpec((3, width // 2, cols), lambda g: (0, 0, g))
    return call(
        dense_bwd_kernel,
        (*places, tokens, gain_attn[None], grad_mid, dq, dk, dv, w_query, w_key, w_value),
        [pl.BlockSpec(memory_space=pltpu.SMEM)] * 3
        + [const_spec((rows, width)), const_spec((1, width)), const_spec((rows, width))]
        + [col_block] * 3
        + [weight_block] * 3,
        grid=(width // cols,),
        out_specs=[const_spec((rows, width)), term_block, term_block, const_spec((1, width))],
        out_shape=[jax.ShapeDtypeStruct((rows, width), F32), term, term, jax.ShapeDtypeStruct((1, width), F32)],
        scratch_shapes=[
            pltpu.VMEM((width, rows), F32),
            pltpu.VMEM((3, width, rows), BF),
            pltpu.VMEM((rows, width), F32),
        ],
        cost_estimate=cost_us(15.5),
        name="dense_bwd",
    )


def bits_of(size):
    return size.bit_length() - 1


def swap(value, axis, size, mask):
    return lax.ppermute(value, axis, [(i, i ^ mask) for i in range(size)])


def exchange(parts, axis, size, name):
    with jax.named_scope(name):
        return [part if m == 0 else swap(part, axis, size, m) for m, part in enumerate(parts)]


def pick(value, index, axis):
    return lax.dynamic_index_in_dim(value, index, axis, keepdims=False)


class Order:
    def __init__(self, token):
        self.token = token

    def enter(self, tree):
        tree, self.token = lax.optimization_barrier((tree, self.token))
        return tree

    leave = enter


def places(me, bits, order):
    key = jnp.arange(1 << bits, dtype=jnp.int32) ^ me
    place = jnp.zeros_like(key)
    for bit in order:
        place = place * 2 + ((key >> bit) & 1)
    return place


class Halving:
    def __init__(self, order, keep, send, dim, route, name):
        self.order, self.keep, self.to_send, self.dim, self.route, self.name = order, keep, send, dim, list(route), name
        self.got = None

    def start(self):
        axis, size, bit = self.route[0]
        with jax.named_scope(f"{self.name}_{axis}{1 << bit}"):
            value = self.order.enter(self.keep if self.to_send is None else self.to_send)
            self.got = swap(value, axis, size, 1 << bit)


def fold_kernel(*refs, cuts):
    pairs, outs = refs[: 2 * len(cuts)], list(refs[2 * len(cuts) :])
    for i, (dim, last) in enumerate(cuts):
        keep, got = pairs[2 * i][...].astype(F32), pairs[2 * i + 1][...].astype(F32)
        total = keep + got
        if last:
            outs.pop(0)[...] = total
            continue
        rows = total.shape[dim] // 2
        for start in (0, rows):
            outs.pop(0)[...] = lax.slice_in_dim(total, start, start + rows, axis=dim).astype(BF)


def fold(*units, cost=3):
    order = units[0].order
    args, cuts, shapes = [], [], []
    for unit in units:
        unit.route.pop(0)
        got = order.leave(unit.got)
        args += [unit.keep, got]
        whole = unit.to_send is None
        last = whole or not unit.route
        cuts.append((unit.dim, last))
        if last:
            shapes.append(jax.ShapeDtypeStruct(got.shape, F32))
        else:
            shape = list(got.shape)
            shape[unit.dim] //= 2
            shapes += [jax.ShapeDtypeStruct(tuple(shape), BF)] * 2
    args = order.enter(args)
    outs = list(
        call(
            functools.partial(fold_kernel, cuts=cuts),
            args,
            [pl.BlockSpec(memory_space=pltpu.VMEM)] * len(args),
            out_shape=shapes,
            cost_estimate=cost_us(cost),
            name="fold",
        )
    )
    outs = order.leave(outs)
    for unit, (_, last) in zip(units, cuts):
        unit.keep = outs.pop(0)
        if not last:
            unit.to_send = outs.pop(0)
        if unit.route:
            unit.start()


def fold_first_kernel(*refs, groups):
    pairs, outs = refs[: -2 * len(groups)], refs[-2 * len(groups) :]
    for i, members in enumerate(groups):
        for at, (array, index) in enumerate(members):
            total = pairs[2 * array][index].astype(F32) + pairs[2 * array + 1][index].astype(F32)
            rows = total.shape[0] // 2
            outs[2 * i][at] = total[:rows].astype(BF)
            outs[2 * i + 1][at] = total[rows:].astype(BF)


def fold_first(pairs, groups):
    args = [v for pair in pairs for v in pair]
    _, rows, width = args[0].shape
    shapes = [jax.ShapeDtypeStruct((len(members), rows // 2, width), BF) for members in groups for _ in range(2)]
    return call(
        functools.partial(fold_first_kernel, groups=groups),
        args,
        [pl.BlockSpec(memory_space=pltpu.VMEM)] * len(args),
        out_shape=shapes,
        cost_estimate=cost_us(5),
        name="fold_first",
    )


class Return:
    def __init__(self, order, high, axis, size, name):
        self.order, self.axis, self.size, self.name = order, axis, size, name
        self.slots = [None] * size
        self.bit = bits_of(size) - 1
        self.start(high)

    def low(self, value):
        for i in range(value.shape[0]):
            self.slots[i] = (value, i)

    def moving(self):
        return [m for m in range(self.size) if (m >> self.bit) & 1]

    def start(self, value):
        with jax.named_scope(f"{self.name}{1 << self.bit}"):
            self.got = swap(self.order.enter(value), self.axis, self.size, 1 << self.bit)

    def fold(self):
        got = self.order.leave(self.got)
        for i, m in enumerate(self.moving()):
            self.slots[m] = (got, i)
        self.bit -= 1
        if self.bit >= 0:
            self.start(jnp.stack([self.slots[m][0][self.slots[m][1]] for m in self.moving()]))

    def finish(self):
        while self.bit >= 0:
            self.fold()
        return self.slots


def body(
    tokens,
    cotangent,
    gain_attn,
    w_query,
    w_key,
    w_value,
    w_out,
    rel_bias,
    gain_moe,
    w_router,
    w_gate,
    w_up,
    w_down,
    segments,
    routes,
    *,
    dp_size,
    ep_size,
):
    rows, width = tokens.shape
    buckets, heads = rel_bias.shape
    experts = w_router.shape[1]
    cap = 10 * rows // (4 * experts)
    ff = w_gate.shape[2]
    me = lax.axis_index("expert")

    onehot = jnp.asarray(band_onehot(rows, buckets))
    woff = jnp.dot(rel_bias.T, onehot, precision=HIGHEST).reshape(heads // HEAD_GROUP, HEAD_GROUP, BAND)
    order = jnp.arange(experts, dtype=jnp.int32) ^ me
    named = jnp.any(routes[None, :, :] == order[:, None, None], axis=-1)
    marks = named.astype(BF)
    before = jnp.asarray(np.triu(np.ones((rows, rows), np.float32), 1)).astype(BF)
    slots = jnp.dot(marks, before, preferred_element_type=F32).astype(jnp.int32)
    code = jnp.where(named, slots, -1)
    code_t = code.T
    by_index = routes[None, :, :] == jnp.arange(experts, dtype=jnp.int32)[:, None, None]
    by_index = jnp.any(by_index, axis=-1)
    slots_by_index = jnp.dot(by_index.astype(BF), before, preferred_element_type=F32).astype(jnp.int32)
    code_by_index_t = jnp.where(by_index, slots_by_index, -1).T
    in_order = (order[:, None] == jnp.arange(experts, dtype=jnp.int32)[None, :]).astype(BF)
    wr_t = jnp.dot(in_order, w_router.T, preferred_element_type=F32).astype(BF)
    wr_t = jnp.pad(wr_t, ((0, TAIL - experts), (0, 0)))

    dp_bits, ep_bits = bits_of(dp_size), bits_of(ep_size)
    dp_me = lax.axis_index("dp")
    dp_order = list(range(dp_bits))
    z_order = [1, 0] + dp_order[2:]
    place_x = places(dp_me, dp_bits, dp_order)
    place_z = places(dp_me, dp_bits, z_order)

    def dp_route(bits):
        return [("dp", dp_size, b) for b in bits]

    dp_part = [ep_bits + b for b in dp_order]
    ep_part = list(range(1, ep_bits))
    q_bits = [0] + ep_part + dp_part
    k_bits = [0] + dp_part + ep_part
    whole_me = dp_me * ep_size + me

    def route(bits):
        return [("expert", ep_size, b) if b < ep_bits else ("dp", dp_size, b - ep_bits) for b in bits]

    place_q, place_k = [places(whole_me, dp_bits + ep_bits, bits) for bits in (q_bits, k_bits)]

    cot_blocks = cot_dispatch(cotangent, code, experts, cap)
    order = Order((routes[0, :1] < 0).astype(F32))
    cots = exchange(cot_blocks, "expert", ep_size, "cot_rows")
    scaled, keys, values, attended, lse, middle, normed_moe, chances, *sent = attn_fwd(
        tokens, gain_attn, w_query, w_key, w_value, w_out, woff, segments, gain_moe, wr_t, code, experts, cap
    )
    sent, cots = order.enter((sent, cots))
    xs = exchange(sent, "expert", ep_size, "token_rows")
    grad_hidden = order.leave(cot_hidden(cots, w_down))

    blocks = ff // FF_BLOCK
    counts = [blocks // 3, blocks // 3 + 1]
    counts.append(blocks - sum(counts))
    starts = [sum(counts[:i]) for i in range(len(counts))]
    scs, units = [], []

    def expert_part(i, source, filled=()):
        *shared, keep, send, sc, hid, hid_t, gg, gu = order.leave(
            expert_a(order.enter(source), grad_hidden, w_gate, w_up, starts[i], counts[i], i == 0, filled)
        )
        scs.append(sc)
        units.append(Halving(order, keep, send, 1, dp_route(z_order if i == 0 else dp_order), f"gate_up{i}"))
        return shared, (hid, hid_t, gg, gu)

    (x_all, x_t, gate_all, grad_cots), filled = expert_part(0, (place_x, xs, cots))
    units[0].start()
    _, filled = expert_part(1, (x_all, x_t, gate_all), filled)
    units[1].start()
    _, (hid, hid_t, gg, gu) = expert_part(2, (x_all, x_t, gate_all), filled)
    fold(units[0])
    units[2].to_send = order.enter(units[2].to_send)
    back_high = order.leave(expert_b(order.enter(gg), gu, scs, w_gate, w_up, experts, True))
    backs = Return(order, back_high, "expert", ep_size, "grad_rows")
    back_low = order.leave(expert_b(order.enter(gg), gu, scs, w_gate, w_up, experts, False))
    backs.low(back_low)
    units[2].start()
    down_halves = order.leave(down_grads(order.enter(hid_t), grad_cots, place_z, place_x))
    down_units = [
        Halving(order, half[: ff // 2], half[ff // 2 :], 0, dp_route(bits), f"down{i}")
        for i, (half, bits) in enumerate(zip(down_halves, (z_order, dp_order)))
    ]
    fold(units[0], units[1])
    backs.fold()
    produced = order.leave(produced_rows(me, order.enter(hid), w_down, experts))
    backs.finish()
    down_units[0].start()
    grad_mid, grad_att, out_keep, out_send, gain_moe_term, router_term = order.leave(
        moe_bwd(place_q, cotangent, middle, gain_moe, normed_moe, chances, wr_t, code, code_t, attended, w_out, backs.slots)
    )
    fold(units[0])
    out_unit = Halving(order, out_keep, out_send, 1, route(q_bits)[:1], "out")
    out_unit.start()
    with jax.named_scope("produced_back"):
        returned = lax.all_to_all(order.enter(produced), "expert", 0, 0, tiled=True)
    dq, dk, dv, dwoff = order.leave(attn_bwd(scaled, keys, values, order.enter(grad_att), lse, woff, segments))
    out_got = order.leave(out_unit.got)
    fold(units[1], units[2])
    down_units[1].start()
    token_grad, qkv_keep, qkv_send, gain_attn_term = order.leave(
        dense_bwd((place_q, place_k, place_k), tokens, gain_attn, grad_mid, order.enter(dq), dk, dv, w_query, w_key, w_value)
    )
    qkv = Halving(order, qkv_keep, qkv_send, 1, route(q_bits)[:1], "qkv")
    qkv.start()
    fold(units[1], units[2], down_units[0], cost=2000)
    bias_term = jnp.dot(onehot, dwoff.reshape(heads, BAND).T, precision=HIGHEST)
    router_term = jnp.dot(router_term[:experts].T, in_order.astype(F32), precision=HIGHEST)
    devices = dp_size * ep_size
    share = width // devices
    small = jnp.concatenate(
        [
            router_term.reshape(devices, -1),
            gain_attn_term.reshape(devices, -1),
            gain_moe_term.reshape(devices, -1),
            bias_term.reshape(devices, -1),
        ],
        axis=1,
    )
    with jax.named_scope("small_sums"):
        small = lax.all_to_all(order.enter(small), ("dp", "expert"), 0, 0, tiled=True)
    got = order.leave(qkv.got)
    halves = order.leave(
        fold_first([order.enter((out_keep, out_got)), (qkv_keep, got)], [[(0, 0), (1, 0)], [(1, 1), (1, 2)]])
    )
    dense = [
        Halving(order, halves[2 * i], halves[2 * i + 1], 1, route(bits)[1:], name)
        for i, (bits, name) in enumerate(((q_bits, "out_q"), (k_bits, "k_v")))
    ]
    for unit in dense:
        unit.start()
    returned = order.leave(returned)
    chances_by_index = jnp.stack([pick(chances, me ^ e, 0) for e in range(experts)], axis=1)
    layer_out = order.leave(layer_output(middle, chances_by_index, code_by_index_t, order.enter(returned)))
    fold(units[2], down_units[1], cost=2000)
    fold(down_units[0], *dense)
    fold(down_units[1], *dense)
    rest = units + down_units + dense
    while any(unit.route for unit in rest):
        fold(*[unit for unit in rest if unit.route])
    small_sum = jnp.sum(order.leave(small), axis=0) + order.token

    terms = [unit.keep for unit in units]
    gate_grad = jnp.concatenate([term[0] for term in terms], axis=1)[None]
    up_grad = jnp.concatenate([term[1] for term in terms], axis=1)[None]
    down_grad = jnp.concatenate([unit.keep for unit in down_units], axis=1)[None]
    n_router = width * experts // devices
    n_gain = width // devices
    router_grad = small_sum[:n_router].reshape(share, experts)
    gain_attn_grad = small_sum[n_router : n_router + n_gain]
    gain_moe_grad = small_sum[n_router + n_gain : n_router + 2 * n_gain]
    bias_grad = small_sum[n_router + 2 * n_gain :]
    return (
        layer_out,
        token_grad,
        dense[0].keep[1],
        dense[1].keep[0],
        dense[1].keep[1],
        dense[0].keep[0],
        gain_attn_grad,
        gain_moe_grad,
        bias_grad,
        router_grad,
        gate_grad,
        up_grad,
        down_grad,
    )


def solution(mesh):
    in_specs = (
        P(("dp", "expert"), None),
        P(("dp", "expert"), None),
        P(),
        P(),
        P(),
        P(),
        P(),
        P(),
        P(),
        P(),
        P("expert", None, None),
        P("expert", None, None),
        P("expert", None, None),
        P(("dp", "expert"), None),
        P(("dp", "expert"), None),
    )
    out_specs = (
        P(("dp", "expert"), None),
        P(("dp", "expert"), None),
        P(("dp", "expert"), None),
        P(("dp", "expert"), None),
        P(("dp", "expert"), None),
        P(("dp", "expert"), None),
        P(("dp", "expert")),
        P(("dp", "expert")),
        P(("dp", "expert")),
        P(("dp", "expert"), None),
        P("expert", "dp", None),
        P("expert", "dp", None),
        P("expert", "dp", None),
    )
    run = functools.partial(body, dp_size=mesh.shape["dp"], ep_size=mesh.shape["expert"])
    return jax.shard_map(run, mesh=mesh, in_specs=in_specs, out_specs=out_specs, check_vma=False)
```

time: 1490 us -> 469 us (0.31)
  waiting for transfers between devices: 709 us -> 118 us
  local copies, waits for them, and re-layouts: 347 us -> 31.4 us
  Pallas kernels: 0 us -> 261 us
  matrix products: 227 us -> 2.71 us
  blocking collectives: 80.2 us -> 0 us
  other arithmetic: 89 us -> 9.57 us
  starting transfers between devices: 14.5 us -> 35.3 us
    reduce_scatter x7 -> x0, waiting for transfers between devices: 650 us -> none  [the longest x1 141 us: body(): lax.psum_scatter(out_term, ('dp', 'expert'), scatter_dimension=0, tiled=T...]
    pallas_call x0 -> x25, Pallas kernels: none -> 261 us  [the longest x19 151 us: call(): pl.pallas_call(kernel, in_specs=list(in_specs), compiler_params=params(),...]
    dot_general x31 -> x6, matrix products: 225 us -> 2.71 us  [the longest x1 1.39 us: body(): slots = jnp.dot(marks, before, preferred_element_type=F32).astype(jnp.int32)]
    unnamed x95 -> x92, local copies, waits for them, and re-layouts: 132 us -> 11.9 us
    ppermute x0 -> x33, waiting for transfers between devices: none -> 118 us  [swap(): return lax.ppermute(value, axis, [(i, i ^ mask) for i in range(size)])]
    reshape x5 -> x6, local copies, waits for them, and re-layouts: 88.5 us -> 1.91 us  [the longest x1 0.86 us: attn_fwd(): seg.reshape(rows, 1)]
    all_to_all x3 -> x2, waiting for transfers between devices: 59 us -> 0.01 us  [the longest x1 0.01 us: body(): returned = lax.all_to_all(order.enter(produced), 'expert', 0, 0, tiled=True)]
    unnamed x1 -> x0, blocking collectives: 44 us -> none
  transfers between devices with their start and end apart: 11 -> 35, of which waited for: 8 -> 12; matrix products, arithmetic and copies ran while one was open for 23% -> 5% of each run, Pallas kernels for 0% -> 51%
where the time goes in v1:
time: 469 us; the launch traced here: 461 us
  Pallas kernels  261 us (56%)
  waiting for transfers between devices  118 us (25%)
  starting transfers between devices  35.3 us (8%)
  local copies, waits for them, and re-layouts  31.4 us (7%)
  other arithmetic  9.57 us (2%)
    pallas_call x19, Pallas kernels, call(): pl.pallas_call(kernel, in_specs=list(in_specs), compiler_params=params(),...  151 us
    ppermute x33, waiting for transfers between devices, swap(): return lax.ppermute(value, axis, [(i, i ^ mask) for i in range(size)])  118 us
    pallas_call x3, Pallas kernels, expert_a(): pl.pallas_call(run, grid=(count,), in_specs=specs + [out_block, col_weigh...  62.8 us
    pallas_call x1, Pallas kernels, attn_fwd(): pl.pallas_call(functools.partial(attn_fwd_kernel, experts=experts, head_d...  31.2 us
    ppermute x33, starting transfers between devices, swap(): return lax.ppermute(value, axis, [(i, i ^ mask) for i in range(size)])  27.7 us
    pallas_call x1, Pallas kernels, produced_rows(): pl.pallas_call(produced_kernel, grid_spec=pltpu.PrefetchScalarGridSpec(nu...  12.6 us
    unnamed x92, local copies, waits for them, and re-layouts  11.9 us
  transfers between devices with their start and end apart: 35, of which 12 were waited for; matrix products, arithmetic and copies ran while one was open for 5% of the time, Pallas kernels for 51%

profile of v1, /device:TPU:0, one launch (start us, length us, event | category | flops | bytes accessed | tf_op | source)
XLA Modules:
  0.0 460.8 jit_solution(6111516117621331176)
XLA Ops:
  3.8 3.6 cot_dispatch.1
  14.9 31.2 %attn_fwd.1 = (bf16[512,1024]{1,0:T(8,128)(2,1)}, bf16[512,1024]{1,0:T(8,128)(2,1)}, bf16[512,1024]{1,0:T(8,128)(2,1)}, bf16[512,1024]{1,0:T(8,128)(2,1)}, f32[4...) custom-call(bf16[512,1024]{1,0:T(8,128)(2,1)} %tok_ref.3, ...), custom_call_target="tpu_custom_call" | custom-call | flops 1782499968 | bytes 100000 | tf_op jit(solution)/shard_map/attn_fwd/pallas_call | solution.py:245
  48.8 14.8 %cot_hidden.1.refs_9_.refs_3_ = bf16[1280,2816]{1,0:T(8,128)(2,1)} custom-call(bf16[320,1024]{1,0:T(8,128)(2,1)} %get-tuple-element.463.refs_0_.refs_5_, bf16[320,1024]{1,0:T(8,128)(2,1)} %copy-done.7, bf16[320,1024]{1,0:T(8,128)(2,1)} %copy-done.8, bf16[320,1024]{1,0:T(8,128)(2,1)} %copy-done.9, bf16[1,2816,1024]{2,1,0:T(8,128)(2,1)} %wd_ref.1), custom_call_target="tpu_custom_call" | custom-call | flops 845249984 | bytes 100000 | tf_op jit(solution)/shard_map/cot_hidden/pallas_call | solution.py:90
  64.8 13.7 %collective-permute-done.5.refs_4_ = bf16[336,1024]{1,0:T(8,128)(2,1)} collective-permute-done((bf16[336,1024]{1,0:T(8,128)(2,1)}, bf16[336,1024]{1,0:T(8,128)(2,1)}, u32[]{:S(2)}, u32[]{:S(2)}) %collective-permute-start.5) | collective-permute-done | bytes 688160 | tf_op jit(solution)/shard_map/token_rows/ppermute | solution.py:828
  78.6 19.8 %expert_grads.3 = (bf16[1280,1024]{1,0:T(8,128)(2,1)}, bf16[1024,1280]{1,0:T(8,128)(2,1)}, f32[1280,128]{1,0:T(8,128)}, bf16[1280,1024]{1,0:T(8,128)(2,1)}, bf16...) custom-call(s32[8]{0:T(128)} %multiply_add_fusion.3.refs_0_.place_b_, ...), custom_call_target="tpu_custom_call" | custom-call | flops 931500032 | bytes 100000 | tf_op jit(solution)/shard_map/expert_grads/pallas_call | solution.py:443
  100.0 21.5 %expert_grads.4 = (bf16[2,512,1024]{2,1,0:T(8,128)(2,1)}, bf16[2,512,1024]{2,1,0:T(8,128)(2,1)}, f32[1280,128]{1,0:T(8,128)}, bf16[1280,2816]{1,0:T(8,128)(2,1)}...) custom-call(bf16[1280,1024]{1,0:T(8,128)(2,1)} %get-tuple-element.50, ...), custom_call_target="tpu_custom_call", output_to_operand_aliasing={{3}: (6, {}), {4}: (7, {}), {5}: (8, {}), {6}: (9, {})} | custom-call | flops 1242000000 | bytes 100000 | tf_op jit(solution)/shard_map/expert_grads/pallas_call | solution.py:443
  123.0 21.5 %expert_grads.5 = (bf16[2,512,1024]{2,1,0:T(8,128)(2,1)}, bf16[2,512,1024]{2,1,0:T(8,128)(2,1)}, f32[1280,128]{1,0:T(8,128)}, bf16[1280,2816]{1,0:T(8,128)(2,1)}...) custom-call(bf16[1280,1024]{1,0:T(8,128)(2,1)} %get-tuple-element.50, ...), custom_call_target="tpu_custom_call", output_to_operand_aliasing={{3}: (6, {}), {4}: (7, {}), {5}: (8, {}), {6}: (9, {})} | custom-call | flops 1242000000 | bytes 100000 | tf_op jit(solution)/shard_map/expert_grads/pallas_call | solution.py:443
  148.9 15.7 %expert_input_grad.2 = bf16[2,336,1024]{2,1,0:T(8,128)(2,1)} custom-call(bf16[1280,2816]{1,0:T(8,128)(2,1)} %get-tuple-element.543.gg_ref, bf16[1280,2816]{1,0:T(8,128)(2,1)} %get-tuple-element.537.gu_ref, f32[1280,128]{1,0:T(8,128)} %get-tuple-element.538.refs_0_, f32[1280,128]{1,0:T(8,128)} %get-tuple-element.539.refs_1_, ...), custom_call_target="tpu_custom_call" | custom-call | flops 920000000 | bytes 100000 | tf_op jit(solution)/shard_map/expert_input_grad/pallas_call | solution.py:90
  170.5 15.4 %expert_input_grad.3.refs_0_ = bf16[2,336,1024]{2,1,0:T(8,128)(2,1)} custom-call(bf16[1280,2816]{1,0:T(8,128)(2,1)} %get-tuple-element.543.gg_ref, bf16[1280,2816]{1,0:T(8,128)(2,1)} %get-tuple-element.537.gu_ref, f32[1280,128]{1,0:T(8,128)} %get-tuple-element.538.refs_0_, f32[1280,128]{1,0:T(8,128)} %get-tuple-element.539.refs_1_, ...), custom_call_target="tpu_custom_call" | custom-call | flops 920000000 | bytes 100000 | tf_op jit(solution)/shard_map/expert_input_grad/pallas_call | solution.py:90
  185.9 12.9 %down_grads.1 = (bf16[2816,512]{1,0:T(8,128)(2,1)}, bf16[2816,512]{1,0:T(8,128)(2,1)}) custom-call(s32[8]{0:T(128)} %multiply_add_fusion.2.place_a_ref, s32[8]{0:T(128)} %multiply_add_fusion.3.refs_0_.place_b_ref, bf16[2816,1280]{1,0:T(8,128)(2,1)} %get-tuple-element.553.hidt_ref, bf16[1280,1024]{1,0:T(8,128)(2,1)} %get-tuple-element.554.gc_ref), custom_call_target="tpu_custom_call" | custom-call | flops 747500032 | bytes 100000 | tf_op jit(solution)/shard_map/down_grads/pallas_call | solution.py:90
  200.2 3.6 fusion.8
  204.7 4.5 fold.11
  212.5 12.6 %produced_rows.1 = bf16[4,320,1024]{2,1,0:T(8,128)(2,1)} custom-call(s32[1]{0:T(128)} %bitcast.9.me_ref, bf16[1280,2816]{1,0:T(8,128)(2,1)} %get-tuple-element.582.hid_ref, bf16[1,2816,1024]{2,1,0:T(8,128)(2,1)} %wd_ref.1), custom_call_target="tpu_custom_call" | custom-call | flops 115000000512 | bytes 100000 | tf_op jit(solution)/shard_map/produced_rows/pallas_call | solution.py:556
  226.2 11.7 %moe_bwd.1 = (f32[512,1024]{1,0:T(8,128)}, bf16[512,1024]{1,0:T(8,128)(2,1)}, bf16[1,512,1024]{2,1,0:T(8,128)(2,1)}, bf16[1,512,1024]{2,1,0:T(8,128)(2,1)}, f32[1,1024]{1,0:T(1,128)}, /*index=5*/f32[16,1024]{1,0:T(8,128)}) custom-call(s32[32]{0:T(128)} %get-tuple-element.951.place_ref.pq_ref, bf16[512,1024]{1,0:T(8,128)(2,1)} %cot_ref.3, ...), custom_call_target="tpu_custom_call" | custom-call | flops 661249984 | bytes 100000 | tf_op jit(solution)/shard_map/moe_bwd/pallas_call | solution.py:90
  241.0 17.8 %attn_bwd.1 = (bf16[512,1024]{1,0:T(8,128)(2,1)}, bf16[512,1024]{1,0:T(8,128)(2,1)}, bf16[512,1024]{1,0:T(8,128)(2,1)}, f32[4,4,512]{2,1,0:T(4,128)}) custom-call(bf16[512,1024]{1,0:T(8,128)(2,1)} %get-tuple-element.613.qs_ref, bf16[512,1024]{1,0:T(8,128)(2,1)} %get-tuple-element.614.k_ref, bf16[512,1024]{1,0:T(8,128)(2,1)} %get-tuple-element.615.v_ref, ...), custom_call_target="tpu_custom_call" | custom-call | flops 115000000512 | bytes 100000 | tf_op jit(solution)/shard_map/attn_bwd/pallas_call | solution.py:90
  260.5 5.0 %fold.13 = (bf16[2,128,1024]{2,1,0:T(8,128)(2,1)}, bf16[2,128,1024]{2,1,0:T(8,128)(2,1)}, bf16[2,256,1024]{2,1,0:T(8,128)(2,1)}, bf16[2,256,1024]{2,1,0:T(8,128)(2,1)}) custom-call(bf16[2,256,1024]{2,1,0:T(8,128)(2,1)} %get-tuple-element.639.refs_0_, bf16[2,256,1024]{2,1,0:T(8,128)(2,1)} %collective-permute-done.13.refs_1_, ...), custom_call_target="tpu_custom_call" | custom-call | flops 172500000 | bytes 100000 | tf_op jit(solution)/shard_map/fold/pallas_call | solution.py:90
  270.9 4.0 all-to-all-start
  275.9 15.5 %dense_bwd.1 = (f32[512,1024]{1,0:T(8,128)}, bf16[3,512,1024]{2,1,0:T(8,128)(2,1)}, bf16[3,512,1024]{2,1,0:T(8,128)(2,1)}, f32[1,1024]{1,0:T(1,128)}) custom-call(s32[32]{0:T(128)} %get-tuple-element.951.place_ref.pq_ref, s32[32]{0:T(128)} %get-tuple-element.950.pk_ref.pv_ref, s32[32]{0:T(128)} %get-tuple-element.950.pk_ref.pv_ref, ...), custom_call_target="tpu_custom_call" | custom-call | flops 891249984 | bytes 100000 | tf_op jit(solution)/shard_map/dense_bwd/pallas_call | solution.py:90
  293.9 31.9 %collective-permute-done.16.refs_1_ = bf16[2,128,1024]{2,1,0:T(8,128)(2,1)} collective-permute-done((bf16[2,128,1024]{2,1,0:T(8,128)(2,1)}, bf16[2,128,1024]{2,1,0:T(8,128)(2,1)}, u32[]{:S(2)}, u32[]{:S(2)}) %collective-permute-start.16) | collective-permute-done | bytes 524320 | tf_op jit(solution)/shard_map/gate_up1_dp4/ppermute | solution.py:828
  326.7 4.7 %fold.14 = (f32[2,128,1024]{2,1,0:T(8,128)}, bf16[2,128,1024]{2,1,0:T(8,128)(2,1)}, bf16[2,128,1024]{2,1,0:T(8,128)(2,1)}, bf16[704,512]{1,0:T(8,128)(2,1)}, bf16[704,512]{1,0:T(8,128)(2,1)}) custom-call(bf16[2,128,1024]{2,1,0:T(8,128)(2,1)} %get-tuple-element.681.refs_0_, bf16[2,128,1024]{2,1,0:T(8,128)(2,1)} %collective-permute-done.16.refs_1_, ...), custom_call_target="tpu_custom_call" | custom-call | flops 115000000512 | bytes 100000 | tf_op jit(solution)/shard_map/fold/pallas_call | solution.py:90
  336.7 5.7 %fold_first.1 = (bf16[2,256,1024]{2,1,0:T(8,128)(2,1)}, bf16[2,256,1024]{2,1,0:T(8,128)(2,1)}, bf16[2,256,1024]{2,1,0:T(8,128)(2,1)}, bf16[2,256,1024]{2,1,0:T(8,128)(2,1)}) custom-call(bf16[1,512,1024]{2,1,0:T(8,128)(2,1)} %get-tuple-element.700.refs_0_, bf16[1,512,1024]{2,1,0:T(8,128)(2,1)} %copy-done.20, ...), custom_call_target="tpu_custom_call" | custom-call | flops 287500000 | bytes 100000 | tf_op jit(solution)/shard_map/fold_first/pallas_call | solution.py:90
  342.5 3.6 all-to-all-start.1
  346.1 6.0 %layer_output.1 = bf16[512,1024]{1,0:T(8,128)(2,1)} custom-call(f32[512,1024]{1,0:T(8,128)} %get-tuple-element.438.mid_ref, f32[512,4]{1,0:T(8,128)} %copy.101.ch_ref, s32[512,4]{1,0:T(8,128)} %bitcast.58, bf16[4,320,1024]{2,1,0:T(8,128)(2,1)} %copy-done.6), custom_call_target="tpu_custom_call" | custom-call | flops 115000000512 | bytes 100000 | tf_op jit(solution)/shard_map/layer_output/pallas_call | solution.py:90
  352.1 5.2 %collective-permute-done.20.refs_1_ = bf16[2,128,1024]{2,1,0:T(8,128)(2,1)S(1)} collective-permute-done((bf16[2,128,1024]{2,1,0:T(8,128)(2,1)}, bf16[2,128,1024]{2,1,0:T(8,128)(2,1)S(1)}, u32[]{:S(2)}, u32[]{:S(2)}) %collective-permute-start.20) | collective-permute-done | bytes 524320 | tf_op jit(solution)/shard_map/gate_up2_dp4/ppermute | solution.py:828
  358.3 3.8 fold.15
  362.9 19.7 %collective-permute-done.22.refs_3_ = bf16[2,256,1024]{2,1,0:T(8,128)(2,1)S(1)} collective-permute-done((bf16[2,256,1024]{2,1,0:T(8,128)(2,1)}, bf16[2,256,1024]{2,1,0:T(8,128)(2,1)S(1)}, u32[]{:S(2)}, u32[]{:S(2)}) %collective-permute-start.22) | collective-permute-done | bytes 1048608 | tf_op jit(solution)/shard_map/out_q_expert2/ppermute | solution.py:828
  384.6 4.3 fold.16
  391.5 10.6 %collective-permute-done.26.refs_3_ = bf16[2,128,1024]{2,1,0:T(8,128)(2,1)S(1)} collective-permute-done((bf16[2,128,1024]{2,1,0:T(8,128)(2,1)}, bf16[2,128,1024]{2,1,0:T(8,128)(2,1)S(1)}, u32[]{:S(2)}, u32[]{:S(2)}) %collective-permute-start.26) | collective-permute-done | bytes 524320 | tf_op jit(solution)/shard_map/out_q_dp1/ppermute | solution.py:828
  402.1 8.0 %collective-permute-done.27.refs_5_ = bf16[2,128,1024]{2,1,0:T(8,128)(2,1)S(1)} collective-permute-done((bf16[2,128,1024]{2,1,0:T(8,128)(2,1)}, bf16[2,128,1024]{2,1,0:T(8,128)(2,1)S(1)}, u32[]{:S(2)}, u32[]{:S(2)}) %collective-permute-start.27) | collective-permute-done | bytes 524320 | tf_op jit(solution)/shard_map/k_v_dp2/ppermute | solution.py:828
  418.3 17.6 %collective-permute-done.28.refs_3_ = bf16[352,512]{1,0:T(8,128)(2,1)S(1)} collective-permute-done((bf16[352,512]{1,0:T(8,128)(2,1)}, bf16[352,512]{1,0:T(8,128)(2,1)S(1)}, u32[]{:S(2)}, u32[]{:S(2)}) %collective-permute-start.28) | collective-permute-done | bytes 360480 | tf_op jit(solution)/shard_map/down1_dp4/ppermute | solution.py:828
  436.0 5.5 %collective-permute-done.30.refs_7_ = bf16[2,64,1024]{2,1,0:T(8,128)(2,1)S(1)} collective-permute-done((bf16[2,64,1024]{2,1,0:T(8,128)(2,1)}, bf16[2,64,1024]{2,1,0:T(8,128)(2,1)S(1)}, u32[]{:S(2)}, u32[]{:S(2)}) %collective-permute-start.30) | collective-permute-done | bytes 262176 | tf_op jit(solution)/shard_map/k_v_dp4/ppermute | solution.py:828
  448.1 3.7 collective-permute-done.31.refs_1_
  (205 shorter events, 83.5 us)
Async XLA Ops:
  7.4 38.7 %collective-permute-start = (bf16[320,1024]{1,0:T(8,128)(2,1)}, bf16[320,1024]{1,0:T(8,128)(2,1)S(1)}, u32[]{:S(2)}, u32[]{:S(2)}) collective-permute-start(bf16[320,1024]{1,0:T(8,128)(2,1)} %get-tuple-element.445), channel_id=1, source_target_pairs={{0,1},{1,0},{2,3},{3,2},{4,5},{5,4},{6,7},{7,6},{8,9},{9,8},{10,11... | collective-permute-start | bytes 1966088 | tf_op jit(solution)/shard_map/cot_rows/ppermute | solution.py:828
  7.9 38.2 %collective-permute-start.1 = (bf16[320,1024]{1,0:T(8,128)(2,1)}, bf16[320,1024]{1,0:T(8,128)(2,1)S(1)}, u32[]{:S(2)}, u32[]{:S(2)}) collective-permute-start(bf16[320,1024]{1,0:T(8,128)(2,1)} %get-tuple-element.446), channel_id=1, source_target_pairs={{0,2},{1,3},{2,0},{3,1},{4,6},{5,7},{6,4},{7,5},{8,10},{9,11},{10,... | collective-permute-start | bytes 1966088 | tf_op jit(solution)/shard_map/cot_rows/ppermute | solution.py:828
  10.5 35.7 %collective-permute-start.2 = (bf16[320,1024]{1,0:T(8,128)(2,1)}, bf16[320,1024]{1,0:T(8,128)(2,1)S(1)}, u32[]{:S(2)}, u32[]{:S(2)}) collective-permute-start(bf16[320,1024]{1,0:T(8,128)(2,1)} %get-tuple-element.447), channel_id=1, source_target_pairs={{0,3},{1,2},{2,1},{3,0},{4,7},{5,6},{6,5},{7,4},{8,11},{9,10},{10,... | collective-permute-start | bytes 1966088 | tf_op jit(solution)/shard_map/cot_rows/ppermute | solution.py:828
  46.2 17.5 %collective-permute-start.3 = (bf16[336,1024]{1,0:T(8,128)(2,1)}, bf16[336,1024]{1,0:T(8,128)(2,1)S(1)}, u32[]{:S(2)}, u32[]{:S(2)}) collective-permute-start(bf16[336,1024]{1,0:T(8,128)(2,1)} %get-tuple-element.449), channel_id=1, source_target_pairs={{0,1},{1,0},{2,3},{3,2},{4,5},{5,4},{6,7},{7,6},{8,9},{9,8},{10,11... | collective-permute-start | bytes 2064392 | tf_op jit(solution)/shard_map/token_rows/ppermute | solution.py:828
  46.4 18.5 %collective-permute-start.4 = (bf16[336,1024]{1,0:T(8,128)(2,1)}, bf16[336,1024]{1,0:T(8,128)(2,1)S(1)}, u32[]{:S(2)}, u32[]{:S(2)}) collective-permute-start(bf16[336,1024]{1,0:T(8,128)(2,1)} %get-tuple-element.450), channel_id=1, source_target_pairs={{0,2},{1,3},{2,0},{3,1},{4,6},{5,7},{6,4},{7,5},{8,10},{9,11},{10,... | collective-permute-start | bytes 2064392 | tf_op jit(solution)/shard_map/token_rows/ppermute | solution.py:828
  48.3 30.3 %collective-permute-start.5 = (bf16[336,1024]{1,0:T(8,128)(2,1)}, bf16[336,1024]{1,0:T(8,128)(2,1)}, u32[]{:S(2)}, u32[]{:S(2)}) collective-permute-start(bf16[336,1024]{1,0:T(8,128)(2,1)} %get-tuple-element.451), channel_id=1, source_target_pairs={{0,3},{1,2},{2,1},{3,0},{4,7},{5,6},{6,5},{7,4},{8,11},{9,10},{10,... | collective-permute-start | bytes 2064392 | tf_op jit(solution)/shard_map/token_rows/ppermute | solution.py:828
  98.4 46.1 %collective-permute-start.6 = (bf16[2,512,768]{2,1,0:T(8,128)(2,1)}, bf16[2,512,768]{2,1,0:T(8,128)(2,1)S(1)}, u32[]{:S(2)}, u32[]{:S(2)}) collective-permute-start(bf16[2,512,768]{2,1,0:T(8,128)(2,1)} %get-tuple-element.523), channel_id=1, source_target_pairs={{0,8},{4,12},{8,0},{12,4},{16,24},{20,28},{24,16},{28,20},{1,9},{5... | collective-permute-start | bytes 4718600 | tf_op jit(solution)/shard_map/gate_up0_dp2/ppermute | solution.py:828
  121.5 82.3 %collective-permute-start.9 = (bf16[2,512,1024]{2,1,0:T(8,128)(2,1)}, bf16[2,512,1024]{2,1,0:T(8,128)(2,1)}, u32[]{:S(2)}, u32[]{:S(2)}) collective-permute-start(bf16[2,512,1024]{2,1,0:T(8,128)(2,1)} %get-tuple-element.561), channel_id=1, source_target_pairs={{0,4},{4,0},{8,12},{12,8},{16,20},{20,16},{24,28},{28,24},{1,5},{5... | collective-permute-start | bytes 6291464 | tf_op jit(solution)/shard_map/gate_up1_dp1/ppermute | solution.py:828
  164.6 47.6 %collective-permute-start.7 = (bf16[2,336,1024]{2,1,0:T(8,128)(2,1)}, bf16[2,336,1024]{2,1,0:T(8,128)(2,1)S(1)}, u32[]{:S(2)}, u32[]{:S(2)}) collective-permute-start(bf16[2,336,1024]{2,1,0:T(8,128)(2,1)} %expert_input_grad.2), channel_id=1, source_target_pairs={{0,2},{1,3},{2,0},{3,1},{4,6},{5,7},{6,4},{7,5},{8,10},{9,11},{10,... | collective-permute-start | bytes 4128776 | tf_op jit(solution)/shard_map/grad_rows2/ppermute | solution.py:828
  167.7 36.1 %collective-permute-start.8 = (bf16[2,256,768]{2,1,0:T(8,128)(2,1)S(1)}, bf16[2,256,768]{2,1,0:T(8,128)(2,1)S(1)}, u32[]{:S(2)}, u32[]{:S(2)}) collective-permute-start(bf16[2,256,768]{2,1,0:T(8,128)(2,1)S(1)} %copy-done.39), channel_id=1, source_target_pairs={{0,4},{4,0},{8,12},{12,8},{16,20},{20,16},{24,28},{28,24},{1,5},{5... | collective-permute-start | bytes 2359304 | tf_op jit(solution)/shard_map/gate_up0_dp1/ppermute | solution.py:828
  198.8 61.8 %collective-permute-start.14 = (bf16[2,512,1024]{2,1,0:T(8,128)(2,1)}, bf16[2,512,1024]{2,1,0:T(8,128)(2,1)}, u32[]{:S(2)}, u32[]{:S(2)}) collective-permute-start(bf16[2,512,1024]{2,1,0:T(8,128)(2,1)} %get-tuple-element.635), channel_id=1, source_target_pairs={{0,4},{4,0},{8,12},{12,8},{16,20},{20,16},{24,28},{28,24},{1,5},{5... | collective-permute-start | bytes 6291464 | tf_op jit(solution)/shard_map/gate_up2_dp1/ppermute | solution.py:828
  209.2 28.8 %collective-permute-start.11 = (bf16[2,128,768]{2,1,0:T(8,128)(2,1)}, bf16[2,128,768]{2,1,0:T(8,128)(2,1)S(1)}, u32[]{:S(2)}, u32[]{:S(2)}) collective-permute-start(bf16[2,128,768]{2,1,0:T(8,128)(2,1)} %get-tuple-element.601), channel_id=1, source_target_pairs={{0,16},{4,20},{8,24},{12,28},{16,0},{20,4},{24,8},{28,12},{1,17},{... | collective-permute-start | bytes 1179656 | tf_op jit(solution)/shard_map/gate_up0_dp4/ppermute | solution.py:828
  211.8 48.8 %collective-permute-start.13 = (bf16[2,256,1024]{2,1,0:T(8,128)(2,1)}, bf16[2,256,1024]{2,1,0:T(8,128)(2,1)}, u32[]{:S(2)}, u32[]{:S(2)}) collective-permute-start(bf16[2,256,1024]{2,1,0:T(8,128)(2,1)} %get-tuple-element.631), channel_id=1, source_target_pairs={{0,8},{4,12},{8,0},{12,4},{16,24},{20,28},{24,16},{28,20},{1,9},{5... | collective-permute-start | bytes 3145736 | tf_op jit(solution)/shard_map/gate_up1_dp2/ppermute | solution.py:828
  240.8 19.8 %collective-permute-start.12 = (bf16[1,512,1024]{2,1,0:T(8,128)(2,1)}, bf16[1,512,1024]{2,1,0:T(8,128)(2,1)S(1)}, u32[]{:S(2)}, u32[]{:S(2)}) collective-permute-start(bf16[1,512,1024]{2,1,0:T(8,128)(2,1)} %get-tuple-element.612), channel_id=1, source_target_pairs={{0,1},{1,0},{2,3},{3,2},{4,5},{5,4},{6,7},{7,6},{8,9},{9,8},{10,11... | collective-permute-start | bytes 3145736 | tf_op jit(solution)/shard_map/out_expert1/ppermute | solution.py:828
  258.9 67.8 %collective-permute-start.18 = (bf16[1408,512]{1,0:T(8,128)(2,1)}, bf16[1408,512]{1,0:T(8,128)(2,1)}, u32[]{:S(2)}, u32[]{:S(2)}) collective-permute-start(bf16[1408,512]{1,0:T(8,128)(2,1)} %get-tuple-element.677), channel_id=1, source_target_pairs={{0,8},{4,12},{8,0},{12,4},{16,24},{20,28},{24,16},{28,20},{1,9},{5... | collective-permute-start | bytes 4325384 | tf_op jit(solution)/shard_map/down0_dp2/ppermute | solution.py:828
  265.6 61.1 %collective-permute-start.17 = (bf16[2,256,1024]{2,1,0:T(8,128)(2,1)}, bf16[2,256,1024]{2,1,0:T(8,128)(2,1)}, u32[]{:S(2)}, u32[]{:S(2)}) collective-permute-start(bf16[2,256,1024]{2,1,0:T(8,128)(2,1)} %get-tuple-element.674), channel_id=1, source_target_pairs={{0,8},{4,12},{8,0},{12,4},{16,24},{20,28},{24,16},{28,20},{1,9},{5... | collective-permute-start | bytes 3145736 | tf_op jit(solution)/shard_map/gate_up2_dp2/ppermute | solution.py:828
  268.8 57.0 %collective-permute-start.16 = (bf16[2,128,1024]{2,1,0:T(8,128)(2,1)}, bf16[2,128,1024]{2,1,0:T(8,128)(2,1)}, u32[]{:S(2)}, u32[]{:S(2)}) collective-permute-start(bf16[2,128,1024]{2,1,0:T(8,128)(2,1)} %get-tuple-element.670), channel_id=1, source_target_pairs={{0,16},{4,20},{8,24},{12,28},{16,0},{20,4},{24,8},{28,12},{1,17},{... | collective-permute-start | bytes 1572872 | tf_op jit(solution)/shard_map/gate_up1_dp4/ppermute | solution.py:828
  270.9 71.5 %all-to-all-start = ((bf16[4,320,1024]{2,1,0:T(8,128)(2,1)}), bf16[4,320,1024]{2,1,0:T(8,128)(2,1)S(1)}, u32[]{:S(2)}, u32[]{:S(2)}) async-start(bf16[4,320,1024]{2,1,0:T(8,128)(2,1)} %produced_rows.1), calls=%async_computation | async-start | bytes 5242880 | tf_op jit(solution)/shard_map/produced_back/all_to_all | solution.py:1094
  292.9 42.2 %collective-permute-start.15 = (bf16[3,512,1024]{2,1,0:T(8,128)(2,1)}, bf16[3,512,1024]{2,1,0:T(8,128)(2,1)S(1)}, u32[]{:S(2)}, u32[]{:S(2)}) collective-permute-start(bf16[3,512,1024]{2,1,0:T(8,128)(2,1)} %get-tuple-element.664), channel_id=1, source_target_pairs={{0,1},{1,0},{2,3},{3,2},{4,5},{5,4},{6,7},{7,6},{8,9},{9,8},{10,11... | collective-permute-start | bytes 9437192 | tf_op jit(solution)/shard_map/qkv_expert1/ppermute | solution.py:828
  293.3 63.9 %collective-permute-start.21 = (bf16[1408,512]{1,0:T(8,128)(2,1)}, bf16[1408,512]{1,0:T(8,128)(2,1)}, u32[]{:S(2)}, u32[]{:S(2)}) collective-permute-start(bf16[1408,512]{1,0:T(8,128)(2,1)} %get-tuple-element.724), channel_id=1, source_target_pairs={{0,4},{4,0},{8,12},{12,8},{16,20},{20,16},{24,28},{28,24},{1,5},{5... | collective-permute-start | bytes 4325384 | tf_op jit(solution)/shard_map/down1_dp1/ppermute | solution.py:828
  331.4 25.9 %collective-permute-start.20 = (bf16[2,128,1024]{2,1,0:T(8,128)(2,1)}, bf16[2,128,1024]{2,1,0:T(8,128)(2,1)S(1)}, u32[]{:S(2)}, u32[]{:S(2)}) collective-permute-start(bf16[2,128,1024]{2,1,0:T(8,128)(2,1)} %get-tuple-element.721), channel_id=1, source_target_pairs={{0,16},{4,20},{8,24},{12,28},{16,0},{20,4},{24,8},{28,12},{1,17},{... | collective-permute-start | bytes 1572872 | tf_op jit(solution)/shard_map/gate_up2_dp4/ppermute | solution.py:828
  333.9 29.1 %collective-permute-start.19 = (bf16[704,512]{1,0:T(8,128)(2,1)}, bf16[704,512]{1,0:T(8,128)(2,1)}, u32[]{:S(2)}, u32[]{:S(2)}) collective-permute-start(bf16[704,512]{1,0:T(8,128)(2,1)} %get-tuple-element.719), channel_id=1, source_target_pairs={{0,4},{4,0},{8,12},{12,8},{16,20},{20,16},{24,28},{28,24},{1,5},{5... | collective-permute-start | bytes 2162696 | tf_op jit(solution)/shard_map/down0_dp1/ppermute | solution.py:828
  342.5 19.7 %all-to-all-start.1 = ((f32[32,1,208]{2,1,0:T(1,128)}), f32[32,1,208]{2,1,0:T(1,128)}, u32[]{:S(2)}, u32[]{:S(2)}) async-start(f32[32,1,208]{2,1,0:T(1,128)} %copy.102), calls=%async_computation.1 | async-start | bytes 65536 | tf_op jit(solution)/shard_map/small_sums/all_to_all | solution.py:1119
  357.3 25.4 %collective-permute-start.22 = (bf16[2,256,1024]{2,1,0:T(8,128)(2,1)}, bf16[2,256,1024]{2,1,0:T(8,128)(2,1)S(1)}, u32[]{:S(2)}, u32[]{:S(2)}) collective-permute-start(bf16[2,256,1024]{2,1,0:T(8,128)(2,1)} %get-tuple-element.741), channel_id=1, source_target_pairs={{0,2},{1,3},{2,0},{3,1},{4,6},{5,7},{6,4},{7,5},{8,10},{9,11},{10,... | collective-permute-start | bytes 3145736 | tf_op jit(solution)/shard_map/out_q_expert2/ppermute | solution.py:828
  357.8 25.0 %collective-permute-start.23 = (bf16[2,256,1024]{2,1,0:T(8,128)(2,1)}, bf16[2,256,1024]{2,1,0:T(8,128)(2,1)S(1)}, u32[]{:S(2)}, u32[]{:S(2)}) collective-permute-start(bf16[2,256,1024]{2,1,0:T(8,128)(2,1)} %get-tuple-element.745), channel_id=1, source_target_pairs={{0,4},{4,0},{8,12},{12,8},{16,20},{20,16},{24,28},{28,24},{1,5},{5... | collective-permute-start | bytes 3145736 | tf_op jit(solution)/shard_map/k_v_dp1/ppermute | solution.py:828
  362.1 28.9 %collective-permute-start.25 = (bf16[704,512]{1,0:T(8,128)(2,1)}, bf16[704,512]{1,0:T(8,128)(2,1)}, u32[]{:S(2)}, u32[]{:S(2)}) collective-permute-start(bf16[704,512]{1,0:T(8,128)(2,1)} %get-tuple-element.767), channel_id=1, source_target_pairs={{0,8},{4,12},{8,0},{12,4},{16,24},{20,28},{24,16},{28,20},{1,9},{5... | collective-permute-start | bytes 2162696 | tf_op jit(solution)/shard_map/down1_dp2/ppermute | solution.py:828
  388.8 13.3 %collective-permute-start.26 = (bf16[2,128,1024]{2,1,0:T(8,128)(2,1)}, bf16[2,128,1024]{2,1,0:T(8,128)(2,1)S(1)}, u32[]{:S(2)}, u32[]{:S(2)}) collective-permute-start(bf16[2,128,1024]{2,1,0:T(8,128)(2,1)} %get-tuple-element.775), channel_id=1, source_target_pairs={{0,4},{4,0},{8,12},{12,8},{16,20},{20,16},{24,28},{28,24},{1,5},{5... | collective-permute-start | bytes 1572872 | tf_op jit(solution)/shard_map/out_q_dp1/ppermute | solution.py:828
  389.5 20.7 %collective-permute-start.27 = (bf16[2,128,1024]{2,1,0:T(8,128)(2,1)}, bf16[2,128,1024]{2,1,0:T(8,128)(2,1)S(1)}, u32[]{:S(2)}, u32[]{:S(2)}) collective-permute-start(bf16[2,128,1024]{2,1,0:T(8,128)(2,1)} %get-tuple-element.779), channel_id=1, source_target_pairs={{0,8},{4,12},{8,0},{12,4},{16,24},{20,28},{24,16},{28,20},{1,9},{5... | collective-permute-start | bytes 1572872 | tf_op jit(solution)/shard_map/k_v_dp2/ppermute | solution.py:828
  391.0 27.3 %collective-permute-start.24 = (bf16[352,512]{1,0:T(8,128)(2,1)S(1)}, bf16[352,512]{1,0:T(8,128)(2,1)S(1)}, u32[]{:S(2)}, u32[]{:S(2)}) collective-permute-start(bf16[352,512]{1,0:T(8,128)(2,1)S(1)} %copy-done.41), channel_id=1, source_target_pairs={{0,16},{4,20},{8,24},{12,28},{16,0},{20,4},{24,8},{28,12},{1,17},{... | collective-permute-start | bytes 1081352 | tf_op jit(solution)/shard_map/down0_dp4/ppermute | solution.py:828
  414.2 21.7 %collective-permute-start.28 = (bf16[352,512]{1,0:T(8,128)(2,1)}, bf16[352,512]{1,0:T(8,128)(2,1)S(1)}, u32[]{:S(2)}, u32[]{:S(2)}) collective-permute-start(bf16[352,512]{1,0:T(8,128)(2,1)} %get-tuple-element.805), channel_id=1, source_target_pairs={{0,16},{4,20},{8,24},{12,28},{16,0},{20,4},{24,8},{28,12},{1,17},{... | collective-permute-start | bytes 1081352 | tf_op jit(solution)/shard_map/down1_dp4/ppermute | solution.py:828
  414.2 21.7 %collective-permute-start.29 = (bf16[2,64,1024]{2,1,0:T(8,128)(2,1)}, bf16[2,64,1024]{2,1,0:T(8,128)(2,1)S(1)}, u32[]{:S(2)}, u32[]{:S(2)}) collective-permute-start(bf16[2,64,1024]{2,1,0:T(8,128)(2,1)} %get-tuple-element.809), channel_id=1, source_target_pairs={{0,8},{4,12},{8,0},{12,4},{16,24},{20,28},{24,16},{28,20},{1,9},{5... | collective-permute-start | bytes 786440 | tf_op jit(solution)/shard_map/out_q_dp2/ppermute | solution.py:828
  414.2 27.2 %collective-permute-start.30 = (bf16[2,64,1024]{2,1,0:T(8,128)(2,1)}, bf16[2,64,1024]{2,1,0:T(8,128)(2,1)S(1)}, u32[]{:S(2)}, u32[]{:S(2)}) collective-permute-start(bf16[2,64,1024]{2,1,0:T(8,128)(2,1)} %get-tuple-element.813), channel_id=1, source_target_pairs={{0,16},{4,20},{8,24},{12,28},{16,0},{20,4},{24,8},{28,12},{1,17},{... | collective-permute-start | bytes 786440 | tf_op jit(solution)/shard_map/k_v_dp4/ppermute | solution.py:828
  (49 other events, 385.0 us)

commit v2 on v1

v2 whole, which is shorter than its diff:
```python
import functools

import jax
import jax.numpy as jnp
import numpy as np
from jax import lax
from jax.experimental import pallas as pl
from jax.experimental.pallas import tpu as pltpu
from jax.sharding import PartitionSpec as P

EPS = 1e-06
HIGHEST = lax.Precision.HIGHEST
LANES = 128
BAND = 4 * LANES
HEAD_GROUP = 4
TAIL = 16
FAR = -1e30
BF = jnp.bfloat16
F32 = jnp.float32
VMEM_LIMIT = 56 * 1024 * 1024


def bucket_of(relative, buckets):
    halfway = buckets // 2
    exact_span = halfway // 2
    distance = np.abs(relative)
    beyond = exact_span + (
        np.log(np.maximum(distance, 1) / exact_span)
        / np.log(128.0 / exact_span)
        * (halfway - exact_span)
    ).astype(np.int64)
    beyond = np.minimum(beyond, halfway - 1)
    return (
        (relative > 0).astype(np.int64) * halfway
        + np.where(distance < exact_span, distance, beyond)
    ).astype(np.int32)


def band_onehot(length, buckets):
    place = np.arange(BAND)
    relative = np.where(place <= 3 * LANES, LANES - place, BAND + LANES - place)
    table = (bucket_of(relative, buckets)[None, :] == np.arange(buckets)[:, None]).astype(np.float32)
    table[:, 3 * LANES] = 0.0
    far = np.arange(LANES, length)
    assert np.all(bucket_of(far, buckets) == bucket_of(far, buckets)[0])
    assert np.all(bucket_of(-far, buckets) == bucket_of(-far, buckets)[0])
    return table


FAR_AFTER = 3 * LANES + 1
FAR_BEFORE = 3 * LANES - 1


def dot(a, b):
    return lax.dot_general(a, b, (((1,), (0,)), ((), ())), preferred_element_type=F32)


def dot_nt(a, b):
    return lax.dot_general(a, b, (((1,), (1,)), ((), ())), preferred_element_type=F32)


def dot_tn(a, b):
    return lax.dot_general(a, b, (((0,), (0,)), ((), ())), preferred_element_type=F32)


def split3(value):
    hi = value.astype(BF)
    rest = value - hi.astype(F32)
    mid = rest.astype(BF)
    low = (rest - mid.astype(F32)).astype(BF)
    return hi, mid, low


def rms_scale(value):
    return lax.rsqrt(jnp.mean(value * value, axis=-1, keepdims=True) + EPS)


def params(**kw):
    return pltpu.CompilerParams(vmem_limit_bytes=VMEM_LIMIT, **kw)


TIMES = {
    ("attn_second", 0): 25.0,
    ("fold", 2): 2.0,
    ("norm_bwd", 0): 7.0,
    ("fold", 6): 40.0,
}


TURNS = {}


def estimate(name):
    turn = TURNS.get(name, 0)
    TURNS[name] = turn + 1
    time = TIMES.get((name, turn), 1.0)
    return pl.CostEstimate(flops=int(time * 1.15e9), bytes_accessed=100000, transcendentals=0)


def call(kernel, args, in_specs, **kw):
    return pl.pallas_call(kernel, in_specs=list(in_specs), compiler_params=params(), **kw)(*args)


def whole_specs(args):
    return [const_spec(a.shape) for a in args]


def const_spec(shape):
    return pl.BlockSpec(shape, lambda *_: (0,) * len(shape))


def selector(code_row, rows):
    place = lax.broadcasted_iota(jnp.int32, (rows, code_row.shape[1]), 0)
    return jnp.where(place == code_row, 1.0, 0.0).astype(BF)


def selector_t(code_column, rows):
    place = lax.broadcasted_iota(jnp.int32, (code_column.shape[0], rows), 1)
    return jnp.where(place == code_column, 1.0, 0.0).astype(BF)


def band_of(row):
    return pltpu.roll(jnp.broadcast_to(row, (LANES, BAND)), 0, 1, stride=1, stride_axis=0)


def diagonal_sums(skewed):
    eight = skewed[0:8]
    for start in range(8, LANES, 8):
        eight = eight + pltpu.roll(skewed[start : start + 8], BAND - start, 1)
    total = eight[0:1]
    for row in range(1, 8):
        total = total + pltpu.roll(eight[row : row + 1], BAND - row, 1)
    return total


def bias_block(band, row, first, count, k_blocks):
    far = [jnp.broadcast_to(row[:, at : at + 1], (LANES, LANES)) for at in (FAR_BEFORE, FAR_AFTER)]
    columns = []
    for q_block in range(first, first + count):
        pieces = []
        for k_block in range(k_blocks):
            d = k_block - q_block
            pieces.append(far[1] if d > 1 else far[0] if d < -1 else band[:, LANES * (1 - d) : LANES * (2 - d)])
        columns.append(jnp.concatenate(pieces, axis=0))
    return jnp.concatenate(columns, axis=1)


def only_rows(value, h, head_dim):
    mine = value[h * head_dim : (h + 1) * head_dim]
    none = jnp.zeros_like(mine)
    return jnp.concatenate([mine, none] if h % 2 == 0 else [none, mine], axis=0)


def attend(scaled, keys, values, woff_ref, mask, first, head_dim):
    count = scaled.shape[0] // LANES
    q_t, v_t = scaled.T, values.T
    heads_t, totals = [], []
    for h in range(HEAD_GROUP):
        row = woff_ref[0, h : h + 1, :]
        bias = bias_block(band_of(row), row, first, count, keys.shape[0] // LANES)
        k_pair = keys[:, LANES * (h // 2) : LANES * (h // 2 + 1)]
        s = dot(k_pair, only_rows(q_t, h, head_dim)) + bias + mask
        peak = jnp.max(s, axis=0, keepdims=True)
        p = jnp.exp(s - peak)
        total = jnp.sum(p, axis=0, keepdims=True)
        heads_t.append(dot(v_t[h * head_dim : (h + 1) * head_dim], p.astype(BF)) * (1.0 / total))
        totals.append(peak + jnp.log(total))
    return jnp.concatenate(heads_t, axis=0).T.astype(BF), jnp.concatenate(totals, axis=0)


def route_rows(mid, gain_ref, wr_ref, experts, nm_ref, ch_ref, payload_ref):
    rows = mid.shape[0]
    nm = (mid * rms_scale(mid) * gain_ref[...]).astype(BF)
    nm_ref[...] = nm
    router = jnp.concatenate([wr_ref[...].astype(F32).T, jnp.zeros((TAIL - experts, nm.shape[1]), F32)], axis=0)
    logits = dot_nt(router.astype(BF), nm)
    live = lax.broadcasted_iota(jnp.int32, logits.shape, 0) < experts
    logits = jnp.where(live, logits, FAR)
    raised = jnp.exp(logits - jnp.max(logits, axis=0, keepdims=True))
    chances = raised / jnp.sum(raised, axis=0, keepdims=True)
    ch_ref[...] = chances
    hi = chances.astype(BF).astype(F32)
    both = jnp.concatenate([hi[: TAIL // 2], (chances - hi)[: TAIL // 2]], axis=0)
    payload_ref[0:rows, :] = nm
    payload_ref[rows:, :] = jnp.concatenate([both, jnp.zeros((TAIL, nm.shape[1] - rows), F32)], axis=1).astype(BF)


def segment_mask(seg_ref, first, count):
    seg = seg_ref[...].astype(F32)
    column = jnp.broadcast_to(seg, (8, seg.shape[1])).T[:, 0:1]
    return jnp.where(column == seg[:, first : first + count], 0.0, FAR)


def attn_first_kernel(
    tok_ref, gain_a_ref, wq_ref, wk_ref, wv_ref, wo_ref, bias_ref, onehot_ref, seg_ref, gain_m_ref, wr_ref,
    qs_ref, k_ref, v_ref, woff_ref, token_ref, att_ref, lse_ref, mid_ref, nm_ref, ch_ref, payload_ref,
    n_scr, mask_scr, woff_scr,
    *, experts, head_dim,
):
    step = pl.program_id(0)
    rows = att_ref.shape[0]

    @pl.when(step == 0)
    def _():
        start = tok_ref[...].astype(F32)
        n_scr[...] = (start * rms_scale(start) * gain_a_ref[...]).astype(BF)
        mid_ref[...] = start[:rows]
        mask_scr[...] = segment_mask(seg_ref, 0, rows)
        token_ref[...] = jnp.where(seg_ref[:, 0:LANES] < 0, 1.0, 0.0)
        table = onehot_ref[...]
        offsets = sum(dot_tn(part, table) for part in split3(bias_ref[...]))
        for g in range(woff_scr.shape[0]):
            woff_scr[g] = offsets[g * HEAD_GROUP : (g + 1) * HEAD_GROUP]

    woff_ref[0] = woff_scr[step]

    normed = n_scr[...]
    scaled = (dot(normed, wq_ref[...]).astype(BF).astype(F32) * head_dim ** (-0.5)).astype(BF)
    keys = dot(normed, wk_ref[...]).astype(BF)
    values = dot(normed, wv_ref[...]).astype(BF)
    qs_ref[...] = scaled
    k_ref[...] = keys
    v_ref[...] = values
    att, totals = attend(scaled[:rows], keys, values, woff_ref, mask_scr[...], 0, head_dim)
    att_ref[...] = att
    lse_ref[0] = totals
    mid_ref[...] += dot(att, wo_ref[...])

    @pl.when(step == pl.num_programs(0) - 1)
    def _():
        route_rows(mid_ref[...], gain_m_ref, wr_ref, experts, nm_ref, ch_ref, payload_ref)


def attn_second_kernel(
    tok_ref, qs_ref, k_ref, v_ref, wo_ref, woff_ref, seg_ref, gain_m_ref, wr_ref, *refs, experts, head_dim
):
    att_ref, lse_ref, mid_ref, nm_ref, ch_ref, payload_ref, mask_scr = refs[-7:]
    step = pl.program_id(0)
    rows = att_ref.shape[0]

    @pl.when(step == 0)
    def _():
        mid_ref[...] = tok_ref[...].astype(F32)
        mask_scr[...] = segment_mask(seg_ref, rows, rows)

    att, totals = attend(qs_ref[...], k_ref[...], v_ref[...], woff_ref, mask_scr[...], rows // LANES, head_dim)
    att_ref[...] = att
    lse_ref[0] = totals
    mid_ref[...] += dot(att, wo_ref[...])

    @pl.when(step == pl.num_programs(0) - 1)
    def _():
        route_rows(mid_ref[...], gain_m_ref, wr_ref, experts, nm_ref, ch_ref, payload_ref)


def attn_halves(rows, width, groups, half):
    cols, part = width // groups, rows // 2
    wide = jax.ShapeDtypeStruct((rows, width), BF)
    shapes = [
        wide,
        jax.ShapeDtypeStruct((groups, HEAD_GROUP, rows), F32),
        jax.ShapeDtypeStruct((rows, width), F32),
        wide,
        jax.ShapeDtypeStruct((TAIL, rows), F32),
        jax.ShapeDtypeStruct((part + TAIL, width), BF),
    ]
    specs = [
        pl.BlockSpec((part, cols), lambda g: (half, g)),
        pl.BlockSpec((1, HEAD_GROUP, part), lambda g: (g, 0, half)),
        pl.BlockSpec((part, width), lambda g: (half, 0)),
        pl.BlockSpec((part, width), lambda g: (half, 0)),
        pl.BlockSpec((TAIL, part), lambda g: (0, half)),
        const_spec((part + TAIL, width)),
    ]
    return shapes, specs


def attn_first(tokens, gain_attn, w_query, w_key, w_value, w_out, rel_bias, seg, gain_moe, w_router):
    rows, width = tokens.shape
    buckets, heads = rel_bias.shape
    experts = w_router.shape[1]
    groups = heads // HEAD_GROUP
    cols, part = width // groups, rows // 2
    weight_block = pl.BlockSpec((width, cols), lambda g: (0, g))
    shapes, specs = attn_halves(rows, width, groups, 0)
    wide = jax.ShapeDtypeStruct((rows, width), BF)
    return call(
        functools.partial(attn_first_kernel, experts=experts, head_dim=cols // HEAD_GROUP),
        (tokens, gain_attn[None], w_query, w_key, w_value, w_out, rel_bias, jnp.asarray(band_onehot(rows, buckets)).astype(BF),
         seg, gain_moe[None], w_router),
        [
            const_spec((rows, width)),
            const_spec((1, width)),
            weight_block,
            weight_block,
            weight_block,
            pl.BlockSpec((cols, width), lambda g: (g, 0)),
            const_spec(rel_bias.shape),
            const_spec((buckets, BAND)),
            const_spec(seg.shape),
            const_spec((1, width)),
            const_spec(w_router.shape),
        ],
        grid=(groups,),
        out_specs=[pl.BlockSpec((rows, cols), lambda g: (0, g))] * 3
        + [pl.BlockSpec((1, HEAD_GROUP, BAND), lambda g: (g, 0, 0)), const_spec((1, LANES))]
        + specs,
        out_shape=[wide] * 3
        + [jax.ShapeDtypeStruct((groups, HEAD_GROUP, BAND), F32), jax.ShapeDtypeStruct((1, LANES), F32)]
        + shapes,
        scratch_shapes=[
            pltpu.VMEM((rows, width), BF),
            pltpu.VMEM((rows, part), F32),
            pltpu.VMEM((groups, HEAD_GROUP, BAND), F32),
        ],
        cost_estimate=estimate("attn_first"),
        name="attn_first",
    )


def attn_second(tokens, scaled, keys, values, w_out, woff, seg, gain_moe, w_router, filled):
    rows, width = tokens.shape
    experts = w_router.shape[1]
    groups = woff.shape[0]
    cols, part = width // groups, rows // 2
    col_block = pl.BlockSpec((rows, cols), lambda g: (0, g))
    shapes, specs = attn_halves(rows, width, groups, 1)
    args = (tokens, scaled, keys, values, w_out, woff, seg, gain_moe[None], w_router)
    return call(
        functools.partial(attn_second_kernel, experts=experts, head_dim=cols // HEAD_GROUP),
        (*args, *filled),
        [
            pl.BlockSpec((part, width), lambda g: (1, 0)),
            pl.BlockSpec((part, cols), lambda g: (1, g)),
            col_block,
            col_block,
            pl.BlockSpec((cols, width), lambda g: (g, 0)),
            pl.BlockSpec((1, HEAD_GROUP, BAND), lambda g: (g, 0, 0)),
            const_spec(seg.shape),
            const_spec((1, width)),
            const_spec(w_router.shape),
        ]
        + [pl.BlockSpec(memory_space=pl.ANY)] * len(filled),
        grid=(groups,),
        out_specs=specs,
        out_shape=shapes,
        scratch_shapes=[pltpu.VMEM((rows, part), F32)],
        input_output_aliases={len(args) + i: i for i in range(len(filled))},
        cost_estimate=estimate("attn_second"),
        name="attn_second",
    )


def gelu_parts(gate):
    c0 = np.float32(np.sqrt(2.0 / np.pi))
    c1 = np.float32(0.044715)
    square = gate * gate
    t = jnp.tanh(c0 * gate * (1.0 + c1 * square))
    half = 0.5 * (1.0 + t)
    value = gate * half
    slope = half + 0.5 * gate * (1.0 - t * t) * (c0 * (1.0 + 3.0 * c1 * square))
    return value, slope


FF_BLOCK = 256


def cot_hidden_kernel(*refs, experts):
    code_ref, cot_refs, wd_ref = refs[0], refs[1 : 1 + experts], refs[1 + experts]
    out_ref, rows_ref = refs[2 + experts :]

    @pl.when(pl.program_id(0) == 0)
    def _():
        cap = rows_ref.shape[0] // experts
        for m, cot_ref in enumerate(cot_refs):
            rows_ref[m * cap : (m + 1) * cap, :] = dot(selector(code_ref[m : m + 1, :], cap), cot_ref[...]).astype(BF)

    out_ref[...] = dot_nt(rows_ref[...], wd_ref[0]).astype(BF)


def cot_hidden(code, cots, w_down, cap, count):
    experts = len(cots)
    width = cots[0].shape[1]
    rows = experts * cap
    return call(
        functools.partial(cot_hidden_kernel, experts=experts),
        (code, *cots, w_down),
        whole_specs((code, *cots)) + [pl.BlockSpec((1, FF_BLOCK, width), lambda f: (0, f, 0))],
        grid=(count,),
        out_specs=[pl.BlockSpec((rows, FF_BLOCK), lambda f: (0, f)), const_spec((rows, width))],
        out_shape=[jax.ShapeDtypeStruct((rows, count * FF_BLOCK), BF), jax.ShapeDtypeStruct((rows, width), BF)],
        cost_estimate=estimate("cot_hidden"),
        name="cot_hidden",
    )


def cot_hidden_more_kernel(rows_ref, wd_ref, out_ref):
    out_ref[...] = dot_nt(rows_ref[...], wd_ref[0]).astype(BF)


def cot_hidden_more(cot_rows, w_down, first):
    rows, width = cot_rows.shape
    count = w_down.shape[1] // FF_BLOCK - first
    return call(
        cot_hidden_more_kernel,
        (cot_rows, w_down),
        [const_spec((rows, width)), pl.BlockSpec((1, FF_BLOCK, width), lambda f: (0, first + f, 0))],
        grid=(count,),
        out_specs=pl.BlockSpec((rows, FF_BLOCK), lambda f: (0, f)),
        out_shape=jax.ShapeDtypeStruct((rows, count * FF_BLOCK), BF),
        cost_estimate=estimate("cot_hidden_more"),
        name="cot_hidden_more",
    )


ROW_BLOCK = 320


def expert_first(me_ref, place_ref, code_ref, payloads, cot_ref, x_ref, xt_ref, gate_ref, gc_ref):
    experts = len(payloads) // 2
    cap = x_ref.shape[0] // experts
    part = payloads[0].shape[0] - TAIL
    row = lax.broadcasted_iota(jnp.int32, (TAIL, part), 0)
    mine = jnp.logical_or(row == me_ref[0], row == me_ref[0] + TAIL // 2)
    for m in range(experts):
        chosen = selector(code_ref[m : m + 1, :], cap)
        place = slice(m * cap, (m + 1) * cap)
        total = jnp.zeros((cap, x_ref.shape[1]), F32)
        gate = jnp.zeros((cap, 1), F32)
        for i in range(2):
            payload = payloads[2 * m + i]
            part_chosen = chosen[:, i * part : (i + 1) * part]
            total = total + dot(part_chosen, payload[0:part, :])
            chances = jnp.sum(jnp.where(mine, payload[part:, 0:part].astype(F32), 0.0), axis=0, keepdims=True)
            gate = gate + jnp.sum(part_chosen.astype(F32) * chances, axis=1, keepdims=True)
        x_ref[place, :] = total.astype(BF)
        gate_ref[place, :] = jnp.broadcast_to(gate, (cap, LANES))
        gc_ref[place, :] = (cot_ref[place, :].astype(F32) * gate).astype(BF)
    flipped = x_ref[...].T
    owners = place_ref.shape[0]
    rows = flipped.shape[0] // owners
    for b in range(owners):
        at = pl.multiple_of(place_ref[b] * rows, rows)
        xt_ref[pl.ds(at, rows), :] = flipped[b * rows : (b + 1) * rows]


def expert_a_kernel(*refs, experts, late_first):
    step = pl.program_id(0)
    if experts:
        me_ref, place_ref, code_ref = refs[:3]
        payloads = refs[3 : 3 + 2 * experts]
        cot_ref, gh_ref, wg_ref, wu_ref, x_ref, xt_ref, gate_ref, gc_ref = refs[3 + 2 * experts : 11 + 2 * experts]

        @pl.when(step == 0)
        def _():
            expert_first(me_ref, place_ref, code_ref, payloads, cot_ref, x_ref, xt_ref, gate_ref, gc_ref)

    else:
        x_ref, xt_ref, gate_ref, gh_ref, wg_ref, wu_ref = refs[:6]
    keep_ref, send_ref, sc_ref, hid_ref, hidt_ref, gg_ref, gu_ref = refs[-7:]

    @pl.when(step == 0)
    def _():
        sc_ref[...] = jnp.zeros_like(sc_ref)

    wg, wu = wg_ref[0], wu_ref[0]
    width = wg.shape[1]
    for start in range(0, x_ref.shape[0], ROW_BLOCK):
        part = slice(start, start + ROW_BLOCK)
        x = x_ref[part, :]
        gate_pre = dot(x, wg)
        up_pre = dot(x, wu)
        grad = gh_ref[part, :].astype(F32)
        act, slope = gelu_parts(gate_pre)
        hidden = act * up_pre
        hid_ref[part, :] = hidden.astype(BF)
        product = hidden * grad
        folded = product[:, 0:LANES]
        for i in range(1, width // LANES):
            folded = folded + product[:, i * LANES : (i + 1) * LANES]
        sc_ref[part, :] += folded
        grad = grad * gate_ref[part, 0:1]
        gg_ref[part, :] = (slope * up_pre * grad).astype(BF)
        gu_ref[part, :] = (act * grad).astype(BF)
    hidt_ref[...] = hid_ref[...].T
    xt = xt_ref[...]
    half = xt.shape[0] // 2
    for i, grad_ref in enumerate((gg_ref, gu_ref)):
        term = dot(xt, grad_ref[...]).astype(BF)
        if not late_first:
            keep_ref[i] = term[:half]
            send_ref[i] = term[half:]
            continue
        rows = term.shape[0] // late_first
        for place in range(late_first):
            block = (place & 1) * (late_first // 2) + (place >> 1)
            out_ref, at = (keep_ref, place) if place < late_first // 2 else (send_ref, place - late_first // 2)
            out_ref[i, at * rows : (at + 1) * rows] = term[block * rows : (block + 1) * rows]


def expert_a(source, gh, gh_first, w_gate, w_up, first, count, late_first, filled=()):
    opening = 0 if filled else len(source[3]) // 2
    rows = gh.shape[0]
    width, ff = w_gate.shape[1:]
    span = count * FF_BLOCK
    col_weight = pl.BlockSpec((1, width, FF_BLOCK), lambda f: (0, 0, first + f))
    out_block = pl.BlockSpec((rows, FF_BLOCK), lambda f: (0, first + f))
    wide = jax.ShapeDtypeStruct((rows, ff), BF)
    tall = jax.ShapeDtypeStruct((ff, rows), BF)
    term = jax.ShapeDtypeStruct((2, width // 2, span), BF)
    term_block = pl.BlockSpec((2, width // 2, FF_BLOCK), lambda f: (0, 0, f))
    if opening:
        me, place, code, payloads, cot_rows = source
        args = (me, place, code, *payloads, cot_rows)
        specs = [pl.BlockSpec(memory_space=pltpu.SMEM)] * 2 + whole_specs((code, *payloads, cot_rows))
        shared = [
            jax.ShapeDtypeStruct((rows, width), BF),
            jax.ShapeDtypeStruct((width, rows), BF),
            jax.ShapeDtypeStruct((rows, LANES), F32),
            jax.ShapeDtypeStruct((rows, width), BF),
        ]
    else:
        args = tuple(source)
        specs = whole_specs(source)
        shared = []
    args = (*args, gh, w_gate, w_up)
    used = len(args)
    first_filled = len(shared) + 3

    def run(*refs):
        expert_a_kernel(*refs[:used], *refs[used + len(filled) :], experts=opening, late_first=late_first)

    return call(
        run,
        (*args, *filled),
        specs
        + [pl.BlockSpec((rows, FF_BLOCK), lambda f: (0, first - gh_first + f)), col_weight, col_weight]
        + [pl.BlockSpec(memory_space=pl.ANY)] * len(filled),
        grid=(count,),
        out_specs=whole_specs(shared)
        + [term_block, term_block, const_spec((rows, LANES)), out_block]
        + [pl.BlockSpec((FF_BLOCK, rows), lambda f: (first + f, 0)), out_block, out_block],
        out_shape=shared + [term, term, jax.ShapeDtypeStruct((rows, LANES), F32), wide, tall, wide, wide],
        input_output_aliases={used + i: first_filled + i for i in range(len(filled))},
        cost_estimate=estimate("expert_grads"),
        name="expert_grads",
    )


def expert_b_kernel(gg_ref, gu_ref, *refs, cap, experts):
    outs, acc = refs[-1 - experts : -1], refs[-1]
    sc_refs, (wg_ref, wu_ref) = refs[: -3 - experts], refs[-3 - experts : -1 - experts]
    part_sum = dot_nt(gg_ref[...], wg_ref[0]) + dot_nt(gu_ref[...], wu_ref[0])
    step, block = pl.program_id(0), pl.program_id(1)

    @pl.when(step == 0)
    def _():
        acc[block] = part_sum

    def finish(out_ref):
        total = acc[block] + part_sum
        row = lax.broadcasted_iota(jnp.int32, (cap, cap), 0)
        lane = lax.broadcasted_iota(jnp.int32, (cap, cap), 1)
        place = lax.broadcasted_iota(jnp.int32, (TAIL, cap), 0)
        out_ref[0:cap, :] = total.astype(BF)
        folded = sc_refs[0][...]
        for other in sc_refs[1:]:
            folded = folded + other[...]
        column = jnp.sum(folded, axis=1, keepdims=True)
        flat = jnp.sum(jnp.where(row == lane, column, 0.0), axis=0, keepdims=True)
        hi, mid, low = split3(flat)
        packed = jnp.where(
            place == 0, hi.astype(F32), jnp.where(place == 1, mid.astype(F32), jnp.where(place == 2, low.astype(F32), 0.0))
        )
        out_ref[cap : cap + TAIL, :] = jnp.zeros((TAIL, total.shape[1]), BF)
        out_ref[cap : cap + TAIL, 0:cap] = packed.astype(BF)

    for m, out_ref in enumerate(outs):

        @pl.when(jnp.logical_and(step == pl.num_programs(0) - 1, block == m))
        def _(out_ref=out_ref):
            finish(out_ref)


def expert_b(gg, gu, scs, w_gate, w_up, experts):
    rows, ff = gg.shape
    width = w_gate.shape[1]
    cap = rows // experts
    cut = ff // 2
    grads = pl.BlockSpec((cap, cut), lambda k, m: (m, k))
    sums = pl.BlockSpec((cap, LANES), lambda k, m: (m, 0))
    weight = pl.BlockSpec((1, width, cut), lambda k, m: (0, 0, k))
    return call(
        functools.partial(expert_b_kernel, cap=cap, experts=experts),
        (gg, gu, *scs, w_gate, w_up),
        [grads, grads] + [sums] * len(scs) + [weight, weight],
        grid=(2, experts),
        out_specs=[const_spec((cap + TAIL, width))] * experts,
        out_shape=[jax.ShapeDtypeStruct((cap + TAIL, width), BF)] * experts,
        scratch_shapes=[pltpu.VMEM((experts, cap, width), F32)],
        cost_estimate=estimate("expert_input_grad"),
        name="expert_input_grad",
    )


def down_kernel(place_a_ref, place_b_ref, hidt_ref, gc_ref, *outs):
    owners = place_a_ref.shape[0]
    shard = 2 * outs[0].shape[0] // owners
    size = int(np.gcd(shard, 32))
    rows = hidt_ref.shape[0]
    step = pl.program_id(0)
    total = dot(hidt_ref[...], gc_ref[...]).astype(BF)
    half = total.shape[1] // 2
    for i in range(rows // size):
        row = step * rows + i * size
        owner = row // shard
        piece = total[i * size : (i + 1) * size]
        for keep_ref, send_ref, place_ref, cols in (
            (outs[0], outs[1], place_a_ref, piece[:, :half]),
            (outs[2], outs[3], place_b_ref, piece[:, half:]),
        ):
            place = place_ref[owner]
            at = pl.multiple_of((place % (owners // 2)) * shard + (row - owner * shard), size)

            @pl.when(place < owners // 2)
            def _(keep_ref=keep_ref, at=at, cols=cols):
                keep_ref[pl.ds(at, size), :] = cols

            @pl.when(place >= owners // 2)
            def _(send_ref=send_ref, at=at, cols=cols):
                send_ref[pl.ds(at, size), :] = cols


def down_grads(hid_t, grad_cots, place_a, place_b):
    rows, width = grad_cots.shape
    ff = hid_t.shape[0]
    table = pl.BlockSpec(memory_space=pltpu.SMEM)
    part = jax.ShapeDtypeStruct((ff // 2, width // 2), BF)
    return call(
        down_kernel,
        (place_a, place_b, hid_t, grad_cots),
        [table, table, pl.BlockSpec((ff // 4, rows), lambda f: (f, 0)), const_spec((rows, width))],
        grid=(4,),
        out_specs=[const_spec(part.shape)] * 4,
        out_shape=[part] * 4,
        cost_estimate=estimate("down_grads"),
        name="down_grads",
    )


def produced_kernel(hid_ref, wd_ref, low_ref, high_ref):
    rows = dot(hid_ref[...], wd_ref[0]).astype(BF)
    lower = pl.program_id(0) < pl.num_programs(0) // 2

    @pl.when(lower)
    def _():
        low_ref[0] = rows

    @pl.when(jnp.logical_not(lower))
    def _():
        high_ref[0] = rows


def produced_rows(hid, w_down, experts):
    rows, ff = hid.shape
    width = w_down.shape[2]
    cap, half = rows // experts, experts // 2
    return call(
        produced_kernel,
        (hid, w_down),
        [pl.BlockSpec((cap, ff), lambda m: (m, 0)), const_spec(w_down.shape)],
        grid=(experts,),
        out_specs=[
            pl.BlockSpec((1, cap, width), lambda m: (jnp.minimum(m, half - 1), 0, 0)),
            pl.BlockSpec((1, cap, width), lambda m: (jnp.maximum(m - half, 0), 0, 0)),
        ],
        out_shape=[jax.ShapeDtypeStruct((half, cap, width), BF)] * 2,
        cost_estimate=estimate("produced_rows"),
        name="produced_rows",
    )


def distinct(slots):
    arrays, found = [], []
    for array, index in slots:
        which = next((i for i, other in enumerate(arrays) if other is array), None)
        if which is None:
            which = len(arrays)
            arrays.append(array)
        found.append((which, index))
    return arrays, found


def layer_out_kernel(mid_ref, ch_ref, code_ref, *refs, slots):
    parts, out_ref = refs[:-1], refs[-1]
    cap = parts[0].shape[1]
    total = mid_ref[...]
    chances = ch_ref[...].T
    for m, (which, index) in enumerate(slots):
        picked = dot(selector_t(code_ref[:, m : m + 1], cap), parts[which][index])
        total = total + chances[:, m : m + 1] * picked
    out_ref[...] = total.astype(BF)


def layer_output(middle, chances, code_t, slots):
    rows, width = middle.shape
    arrays, found = distinct(slots)
    args = (middle, chances, code_t, *arrays)
    return call(
        functools.partial(layer_out_kernel, slots=found),
        args,
        [pl.BlockSpec(memory_space=pltpu.VMEM)] * len(args),
        out_shape=jax.ShapeDtypeStruct((rows, width), BF),
        cost_estimate=estimate("layer_output"),
        name="layer_output",
    )


def moe_bwd_kernel(
    cot_ref, mid_ref, gain_ref, nm_ref, ch_ref, wr_ref, code_ref, codet_ref, wo_ref, att_ref, *refs
):
    backs, (gmid_ref, branch_ref, ga_ref, keep_ref, send_ref, gain_o_ref, router_o_ref) = refs[:-7], refs[-7:]
    experts, cap = len(backs), backs[0].shape[0] - TAIL
    rows = cot_ref.shape[0]
    grad = jnp.zeros(mid_ref.shape, F32)
    gate_rows = []
    for m, back in enumerate(backs):
        grad = grad + dot(selector_t(codet_ref[:, m : m + 1], cap), back[0:cap, :])
        picked = dot(back[cap : cap + TAIL, 0:cap], selector(code_ref[m : m + 1, :], cap))
        gate_rows.append(jnp.sum(picked, axis=0, keepdims=True))
    gate_rows.append(jnp.zeros((TAIL - experts, rows), F32))
    grad_chances = jnp.concatenate(gate_rows, axis=0)
    chances = ch_ref[...]
    grad_logits = chances * (grad_chances - jnp.sum(chances * grad_chances, axis=0, keepdims=True))
    pieces = jnp.concatenate(split3(grad_logits), axis=0)
    wr = wr_ref[...]
    grad = grad + dot_tn(pieces, jnp.concatenate([wr, wr, wr], axis=0))
    router = dot(pieces, nm_ref[...])
    router_o_ref[...] = router[0:TAIL] + router[TAIL : 2 * TAIL] + router[2 * TAIL : 3 * TAIL]
    mid = mid_ref[...]
    scale = rms_scale(mid)
    unit = mid * scale
    gain_o_ref[...] = jnp.sum(grad * unit, axis=0, keepdims=True)
    scaled = grad * gain_ref[...]
    grad_mid = cot_ref[...].astype(F32) + scale * (scaled - unit * jnp.mean(scaled * unit, axis=-1, keepdims=True))
    gmid_ref[...] = grad_mid
    branch = grad_mid.astype(BF)
    branch_ref[...] = branch
    ga_ref[...] = dot_nt(branch, wo_ref[...]).astype(BF)
    term = dot(att_ref[...], branch).astype(BF)
    half = term.shape[0] // 2
    keep_ref[0] = term[:half]
    send_ref[0] = term[half:]


def sort_rows(place_ref, value, out_ref):
    owners = place_ref.shape[0]
    rows = value.shape[0] // owners
    for b in range(owners):
        out_ref[pl.ds(pl.multiple_of(place_ref[b] * rows, rows), rows), :] = value[b * rows : (b + 1) * rows]


def moe_bwd(cot, middle, gain_moe, normed_moe, chances, wr_t, code, code_t, w_out, att_t, backs):
    rows, width = cot.shape
    args = (cot, middle, gain_moe[None], normed_moe, chances, wr_t, code, code_t, w_out, att_t, *backs)
    wide = jax.ShapeDtypeStruct((rows, width), BF)
    half = jax.ShapeDtypeStruct((1, width // 2, width), BF)
    return call(
        moe_bwd_kernel,
        args,
        [pl.BlockSpec(memory_space=pltpu.VMEM)] * len(args),
        out_shape=[
            jax.ShapeDtypeStruct((rows, width), F32),
            wide,
            wide,
            half,
            half,
            jax.ShapeDtypeStruct((1, width), F32),
            jax.ShapeDtypeStruct((TAIL, width), F32),
        ],
        cost_estimate=estimate("moe_bwd"),
        name="moe_bwd",
    )


def attn_bwd_kernel(
    qs_ref, k_ref, v_ref, ga_ref, lse_ref, woff_ref, seg_ref,
    dq_ref, dk_ref, dv_ref, dwoff_ref, mask_scr, p_scr, ds_scr,
    *, head_dim,
):
    rows = qs_ref.shape[0]
    blocks = rows // LANES

    @pl.when(pl.program_id(0) == 0)
    def _():
        mask_scr[...] = segment_mask(seg_ref, 0, rows)

    scaled, keys, values, grads = qs_ref[...], k_ref[...], v_ref[...], ga_ref[...]
    q_t, g_t, k_t = scaled.T, grads.T, keys.T
    low_half = lax.broadcasted_iota(jnp.int32, (rows, LANES), 1) < head_dim
    dq_t, dk_parts, dv_parts = [], [], []
    lane = lax.broadcasted_iota(jnp.int32, (1, BAND), 1)
    for h in range(HEAD_GROUP):
        row = woff_ref[0, h : h + 1, :]
        band = band_of(row)
        pair = slice(LANES * (h // 2), LANES * (h // 2 + 1))
        k_pair, v_pair = keys[:, pair], values[:, pair]
        q_only, g_only = only_rows(q_t, h, head_dim), only_rows(g_t, h, head_dim)
        tiles = {}
        for b in range(0, blocks, 2):
            lanes = slice(b * LANES, (b + 2) * LANES)
            s = dot(k_pair, q_only[:, lanes]) + bias_block(band, row, b, 2, blocks) + mask_scr[:, lanes]
            p = jnp.exp(s - lse_ref[0, h : h + 1, lanes])
            dp = dot(v_pair, g_only[:, lanes])
            ds = p * (dp - jnp.sum(p * dp, axis=0, keepdims=True))
            p_scr[:, lanes] = p.astype(BF)
            ds_scr[:, lanes] = ds.astype(BF)
            for q_block in range(2):
                for k_block in range(blocks):
                    d = max(-2, min(2, k_block - b - q_block))
                    tile = ds[k_block * LANES : (k_block + 1) * LANES, q_block * LANES : (q_block + 1) * LANES]
                    tiles[d] = tiles[d] + tile if d in tiles else tile
        skewed = jnp.concatenate([tiles[1], tiles[0], tiles[-1], jnp.zeros_like(tiles[0])], axis=1)
        offsets = diagonal_sums(skewed)
        offsets = offsets + jnp.where(lane == FAR_AFTER, jnp.sum(tiles[2]), 0.0)
        offsets = offsets + jnp.where(lane == FAR_BEFORE, jnp.sum(tiles[-2]), 0.0)
        dwoff_ref[0, h : h + 1, :] = offsets
        p_all, ds_all = p_scr[...], ds_scr[...]
        dv_parts.append(dot(p_all, grads[:, pair]))
        dk_parts.append(dot(ds_all, scaled[:, pair]))
        dq_t.append(dot(k_t[h * head_dim : (h + 1) * head_dim], ds_all))
    dq = jnp.concatenate(dq_t, axis=0).T * head_dim ** (-0.5)
    dq_ref[...] = dq.astype(BF)
    for i in range(HEAD_GROUP // 2):
        pair = slice(LANES * i, LANES * (i + 1))
        dk_ref[:, pair] = jnp.where(low_half, dk_parts[2 * i], dk_parts[2 * i + 1]).astype(BF)
        dv_ref[:, pair] = jnp.where(low_half, dv_parts[2 * i], dv_parts[2 * i + 1]).astype(BF)


def attn_bwd(scaled, keys, values, grad_att, lse, woff, seg):
    rows, width = scaled.shape
    groups = woff.shape[0]
    cols = width // groups
    col_block = pl.BlockSpec((rows, cols), lambda g: (0, g))
    wide = jax.ShapeDtypeStruct((rows, width), BF)
    return call(
        functools.partial(attn_bwd_kernel, head_dim=cols // HEAD_GROUP),
        (scaled, keys, values, grad_att, lse, woff, seg),
        [
            col_block,
            col_block,
            col_block,
            col_block,
            pl.BlockSpec((1, HEAD_GROUP, rows), lambda g: (g, 0, 0)),
            pl.BlockSpec((1, HEAD_GROUP, BAND), lambda g: (g, 0, 0)),
            const_spec(seg.shape),
        ],
        grid=(groups,),
        out_specs=[col_block, col_block, col_block, pl.BlockSpec((1, HEAD_GROUP, BAND), lambda g: (g, 0, 0))],
        out_shape=[wide, wide, wide, jax.ShapeDtypeStruct((groups, HEAD_GROUP, BAND), F32)],
        scratch_shapes=[
            pltpu.VMEM((rows, rows), F32),
            pltpu.VMEM((rows, rows), BF),
            pltpu.VMEM((rows, rows), BF),
        ],
        cost_estimate=estimate("attn_bwd"),
        name="attn_bwd",
    )


def sorted_rows_kernel(pq_ref, pk_ref, tok_ref, gain_ref, att_ref, att_o_ref, out_ref, sort_scr):
    start = tok_ref[...].astype(F32)
    normed_t = (start * rms_scale(start) * gain_ref[...]).T
    attended_t = att_ref[...].astype(F32).T
    sort_rows(pq_ref, attended_t, sort_scr)
    att_o_ref[...] = sort_scr[...].astype(BF)
    for i, place_ref in enumerate((pq_ref, pk_ref)):
        sort_rows(place_ref, normed_t, sort_scr)
        out_ref[i] = sort_scr[...].astype(BF)


def sorted_rows(place_q, place_k, tokens, gain_attn, attended):
    rows, width = tokens.shape
    return call(
        sorted_rows_kernel,
        (place_q, place_k, tokens, gain_attn[None], attended),
        [pl.BlockSpec(memory_space=pltpu.SMEM)] * 2 + [pl.BlockSpec(memory_space=pltpu.VMEM)] * 3,
        out_shape=[jax.ShapeDtypeStruct((width, rows), BF), jax.ShapeDtypeStruct((2, width, rows), BF)],
        scratch_shapes=[pltpu.VMEM((width, rows), F32)],
        cost_estimate=estimate("sorted_rows"),
        name="sorted_rows",
    )


def dense_terms_kernel(rows_ref, dq_ref, dk_ref, dv_ref, keep_ref, send_ref):
    half = keep_ref.shape[1]
    for i, d_ref in enumerate((dq_ref, dk_ref, dv_ref)):
        term = dot(rows_ref[min(i, 1)], d_ref[...]).astype(BF)
        keep_ref[i] = term[:half]
        send_ref[i] = term[half:]


def dense_terms(lhs, dq, dk, dv):
    _, width, rows = lhs.shape
    cols = 256
    col_block = pl.BlockSpec((rows, cols), lambda g: (0, g))
    return call(
        dense_terms_kernel,
        (lhs, dq, dk, dv),
        [const_spec(lhs.shape)] + [col_block] * 3,
        grid=(width // cols,),
        out_specs=[pl.BlockSpec((3, width // 2, cols), lambda g: (0, 0, g))] * 2,
        out_shape=[jax.ShapeDtypeStruct((3, width // 2, width), BF)] * 2,
        cost_estimate=estimate("dense_terms"),
        name="dense_terms",
    )


def norm_bwd_kernel(
    tok_ref, gain_ref, gmid_ref, dq_ref, dk_ref, dv_ref, wq_ref, wk_ref, wv_ref, tg_ref, gain_o_ref, acc
):
    step = pl.program_id(0)
    total = dot_nt(dq_ref[...], wq_ref[...]) + dot_nt(dk_ref[...], wk_ref[...]) + dot_nt(dv_ref[...], wv_ref[...])

    @pl.when(step == 0)
    def _():
        acc[...] = total

    @pl.when(step > 0)
    def _():
        acc[...] += total

    @pl.when(step == pl.num_programs(0) - 1)
    def _():
        grad = acc[...]
        start = tok_ref[...].astype(F32)
        scale = rms_scale(start)
        unit = start * scale
        gain_o_ref[...] = jnp.sum(grad * unit, axis=0, keepdims=True)
        scaled = grad * gain_ref[...]
        tg_ref[...] = gmid_ref[...] + scale * (scaled - unit * jnp.mean(scaled * unit, axis=-1, keepdims=True))


def norm_bwd(tokens, gain_attn, grad_mid, dq, dk, dv, w_query, w_key, w_value):
    rows, width = tokens.shape
    cols = 256
    col_block = pl.BlockSpec((rows, cols), lambda g: (0, g))
    weight_block = pl.BlockSpec((width, cols), lambda g: (0, g))
    return call(
        norm_bwd_kernel,
        (tokens, gain_attn[None], grad_mid, dq, dk, dv, w_query, w_key, w_value),
        [const_spec((rows, width)), const_spec((1, width)), const_spec((rows, width))] + [col_block] * 3 + [weight_block] * 3,
        grid=(width // cols,),
        out_specs=[const_spec((rows, width)), const_spec((1, width))],
        out_shape=[jax.ShapeDtypeStruct((rows, width), F32), jax.ShapeDtypeStruct((1, width), F32)],
        scratch_shapes=[pltpu.VMEM((rows, width), F32)],
        cost_estimate=estimate("norm_bwd"),
        name="norm_bwd",
    )


def bits_of(size):
    return size.bit_length() - 1


def swap(value, axis, size, mask):
    return lax.ppermute(value, axis, [(i, i ^ mask) for i in range(size)])


def pick(value, index, axis):
    return lax.dynamic_index_in_dim(value, index, axis, keepdims=False)


class Order:
    def __init__(self, token):
        self.token = token

    def enter(self, tree):
        tree, self.token = lax.optimization_barrier((tree, self.token))
        return tree

    leave = enter


def places(me, bits, order):
    key = jnp.arange(1 << bits, dtype=jnp.int32) ^ me
    place = jnp.zeros_like(key)
    for bit in order:
        place = place * 2 + ((key >> bit) & 1)
    return place


class Halving:
    def __init__(self, order, keep, send, dim, route, name):
        self.order, self.keep, self.to_send, self.dim, self.route, self.name = order, keep, send, dim, list(route), name
        self.got = None

    def start(self):
        axis, size, bit = self.route[0]
        with jax.named_scope(f"{self.name}_{axis}{1 << bit}"):
            value = self.order.enter(self.keep if self.to_send is None else self.to_send)
            self.got = swap(value, axis, size, 1 << bit)


def fold_kernel(*refs, cuts):
    pairs, outs = refs[: 2 * len(cuts)], list(refs[2 * len(cuts) :])
    for i, (dim, last) in enumerate(cuts):
        keep, got = pairs[2 * i][...].astype(F32), pairs[2 * i + 1][...].astype(F32)
        total = keep + got
        if last:
            outs.pop(0)[...] = total
            continue
        rows = total.shape[dim] // 2
        for start in (0, rows):
            outs.pop(0)[...] = lax.slice_in_dim(total, start, start + rows, axis=dim).astype(BF)


def fold(*units, hold=()):
    order = units[0].order
    args, cuts, shapes = [], [], []
    for unit in units:
        unit.route.pop(0)
        got = order.leave(unit.got)
        args += [unit.keep, got]
        whole = unit.to_send is None
        last = whole or not unit.route
        cuts.append((unit.dim, last))
        if last:
            shapes.append(jax.ShapeDtypeStruct(got.shape, F32))
        else:
            shape = list(got.shape)
            shape[unit.dim] //= 2
            shapes += [jax.ShapeDtypeStruct(tuple(shape), BF)] * 2
    args = order.enter(args)
    outs = list(
        call(
            functools.partial(fold_kernel, cuts=cuts),
            args,
            [pl.BlockSpec(memory_space=pltpu.VMEM)] * len(args),
            out_shape=shapes,
            cost_estimate=estimate("fold"),
            name="fold",
        )
    )
    outs = order.leave(outs)
    for unit, (_, last) in zip(units, cuts):
        unit.keep = outs.pop(0)
        if not last:
            unit.to_send = outs.pop(0)
        if unit.route and unit not in hold:
            unit.start()


def fold_first_kernel(*refs, groups):
    pairs, outs = refs[: -2 * len(groups)], refs[-2 * len(groups) :]
    for i, members in enumerate(groups):
        for at, (array, index) in enumerate(members):
            total = pairs[2 * array][index].astype(F32) + pairs[2 * array + 1][index].astype(F32)
            rows = total.shape[0] // 2
            outs[2 * i][at] = total[:rows].astype(BF)
            outs[2 * i + 1][at] = total[rows:].astype(BF)


def fold_first(pairs, groups):
    args = [v for pair in pairs for v in pair]
    _, rows, width = args[0].shape
    shapes = [jax.ShapeDtypeStruct((len(members), rows // 2, width), BF) for members in groups for _ in range(2)]
    return call(
        functools.partial(fold_first_kernel, groups=groups),
        args,
        [pl.BlockSpec(memory_space=pltpu.VMEM)] * len(args),
        out_shape=shapes,
        cost_estimate=estimate("fold_first"),
        name="fold_first",
    )


class Return:
    def __init__(self, order, low, high, axis, size, name):
        self.order, self.axis, self.size, self.name = order, axis, size, name
        half = low.shape[0]
        self.slots = [(low, i) for i in range(half)] + [(high, i) for i in range(half)]
        self.bit = bits_of(size) - 1
        self.start(high)

    def moving(self):
        return [m for m in range(self.size) if (m >> self.bit) & 1]

    def start(self, value):
        with jax.named_scope(f"{self.name}{1 << self.bit}"):
            self.got = swap(self.order.enter(value), self.axis, self.size, 1 << self.bit)

    def fold(self):
        got = self.order.leave(self.got)
        for i, m in enumerate(self.moving()):
            self.slots[m] = (got[i], 0) if isinstance(got, list) else (got, i)
        self.bit -= 1
        if self.bit >= 0:
            self.pieces = [self.slots[m][0][self.slots[m][1]][None] for m in self.moving()]
            self.got = []
            for i, piece in enumerate(self.pieces):
                with jax.named_scope(f"{self.name}{1 << self.bit}_{i}"):
                    self.got.append(swap(self.order.enter(piece), self.axis, self.size, 1 << self.bit))

    def finish(self):
        while self.bit >= 0:
            self.fold()


class Gather:
    def __init__(self, order, value, axis, size, name):
        self.order, self.axis, self.size, self.name = order, axis, size, name
        self.blocks = {0: value}
        self.send(0, size // 2)
        if size > 2:
            self.send(0, 1)

    def send(self, m, bit):
        with jax.named_scope(f"{self.name}{m}_{bit}"):
            self.blocks[m ^ bit] = swap(self.blocks[m], self.axis, self.size, bit)

    def relay(self):
        self.blocks[self.size // 2] = self.order.leave(self.blocks[self.size // 2])
        bit = self.size // 2
        while bit:
            for m in range(0, self.size, 2 * bit):
                if m ^ bit not in self.blocks:
                    self.send(m, bit)
            bit //= 2

    def finish(self):
        self.blocks = self.order.leave(self.blocks)
        return [self.blocks[m] for m in range(self.size)]


def body(
    tokens,
    cotangent,
    gain_attn,
    w_query,
    w_key,
    w_value,
    w_out,
    rel_bias,
    gain_moe,
    w_router,
    w_gate,
    w_up,
    w_down,
    segments,
    routes,
    *,
    dp_size,
    ep_size,
):
    TURNS.clear()
    rows, width = tokens.shape
    buckets, heads = rel_bias.shape
    experts = w_router.shape[1]
    cap = 10 * rows // (4 * experts)
    ff = w_gate.shape[2]
    me = lax.axis_index("expert")

    cots = Gather(None, cotangent, "expert", ep_size, "cot")
    scaled, keys, values, woff, token, *filled, payload = attn_first(
        tokens, gain_attn, w_query, w_key, w_value, w_out, rel_bias, segments, gain_moe, w_router
    )
    order = Order(token)
    cots.order = order
    numbers = jnp.arange(experts, dtype=jnp.int32)
    named = jnp.any(order.enter(routes)[None, :, :] == numbers[:, None, None], axis=-1)
    before = jnp.asarray(np.triu(np.ones((rows, rows), np.float32), 1)).astype(BF)
    slots = jnp.dot(named.astype(BF), before, preferred_element_type=F32).astype(jnp.int32)
    code = jnp.where(named, slots, -1)

    dp_bits, ep_bits = bits_of(dp_size), bits_of(ep_size)
    dp_me = lax.axis_index("dp")
    dp_order = list(range(dp_bits))
    late_x = dp_order[1:] + [0]
    place_x = places(dp_me, dp_bits, dp_order)
    place_late = places(dp_me, dp_bits, late_x)

    def dp_route(bits):
        return [("dp", dp_size, b) for b in bits]

    dp_part = [ep_bits + b for b in dp_order]
    ep_part = list(range(1, ep_bits))
    q_bits = [0] + ep_part + dp_part
    k_bits = [0] + dp_part + ep_part
    whole_me = dp_me * ep_size + me

    def route(bits):
        return [("expert", ep_size, b) if b < ep_bits else ("dp", dp_size, b - ep_bits) for b in bits]

    place_q, place_k = [places(whole_me, dp_bits + ep_bits, bits) for bits in (q_bits, k_bits)]

    codes = Gather(order, order.enter(code), "expert", ep_size, "code")
    cots.relay()
    codes.relay()
    first_half = Gather(order, order.enter(payload), "expert", ep_size, "rows_a")
    attended, lse, middle, normed_moe, chances, payload = order.leave(
        attn_second(tokens, order.enter(scaled), keys, values, w_out, woff, segments, gain_moe, w_router, filled)
    )
    second_half = Gather(order, order.enter(payload), "expert", ep_size, "rows_b")
    first_half.relay()
    cots, codes = cots.finish(), codes.finish()
    code_here = jnp.stack([pick(v, me, 0) for v in codes])
    blocks = ff // FF_BLOCK
    counts = [blocks // 2, blocks - blocks // 2]
    starts = [sum(counts[:i]) for i in range(len(counts))]
    gh_first, cot_rows = order.leave(cot_hidden(order.enter(code_here), cots, w_down, cap, starts[1]))
    second_half.relay()
    payloads = [v for pair in zip(first_half.finish(), second_half.finish()) for v in pair]
    me_ref = me.reshape(1).astype(jnp.int32)
    scs, units = [], []

    def expert_part(i, source, filled=()):
        *shared, keep, send, sc, hid, hid_t, gg, gu = order.leave(
            expert_a(
                order.enter(source), gh_second if i else gh_first, starts[i], w_gate, w_up,
                starts[i], counts[i], 0 if i else dp_size, filled,
            )
        )
        scs.append(sc)
        units.append(Halving(order, keep, send, 1, dp_route(dp_order if i else late_x), f"gate_up{i}"))
        return shared, (hid, hid_t, gg, gu)

    def by_xor(value):
        return jnp.stack([pick(value, me ^ m, 0) for m in range(experts)])

    def padded(value):
        return jnp.pad(value, ((0, TAIL - experts), (0, 0)))

    (x_all, x_t, gate_all, grad_cots), filled = expert_part(0, (me_ref, place_x, code_here, payloads, cot_rows))
    units[0].start()
    gh_second = order.leave(cot_hidden_more(order.enter(cot_rows), w_down, starts[1]))
    _, (hid, hid_t, gg, gu) = expert_part(1, (x_all, x_t, gate_all), filled)
    units[1].start()
    backs = list(order.leave(expert_b(order.enter(gg), gu, scs, w_gate, w_up, experts)))
    for m in reversed(range(1, experts)):
        with jax.named_scope(f"grad_rows{m}"):
            backs[m] = swap(order.enter(backs[m]), "expert", ep_size, m)
    fold(units[0])
    down_parts = order.leave(down_grads(order.enter(hid_t), grad_cots, place_x, place_late))
    down_units = [
        Halving(order, down_parts[2 * i], down_parts[2 * i + 1], 0, dp_route(bits), f"down{i}")
        for i, bits in enumerate((dp_order, late_x))
    ]
    code_xor, chances_xor, wr_xor = order.enter((by_xor(code), padded(by_xor(chances)), padded(by_xor(w_router.T))))
    att_t, normed_t = order.leave(sorted_rows(place_q, place_k, order.enter(tokens), gain_attn, attended))
    backs = order.leave(backs)
    down_units[0].start()
    down_units[1].start()
    grad_mid, branch, grad_att, out_keep, out_send, gain_moe_term, router_term = order.leave(
        moe_bwd(
            cotangent, order.enter(middle), gain_moe, normed_moe, chances_xor, wr_xor, code_xor, code_xor.T, w_out, att_t,
            backs,
        )
    )
    out_unit = Halving(order, out_keep, out_send, 1, route(q_bits)[:1], "out")
    out_unit.start()
    fold(units[1])
    dq, dk, dv, dwoff = order.leave(attn_bwd(scaled, keys, values, order.enter(grad_att), lse, woff, segments))
    out_got = order.leave(out_unit.got)
    fold(units[0])
    qkv_keep, qkv_send = order.leave(dense_terms(normed_t, order.enter(dq), dk, dv))
    fold(*down_units)
    core = Halving(order, qkv_keep, qkv_send, 1, route(q_bits)[:1], "qkv")
    core.start()
    token_grad, gain_attn_term = order.leave(
        norm_bwd(tokens, gain_attn, grad_mid, order.enter(dq), dk, dv, w_query, w_key, w_value)
    )
    onehot = jnp.asarray(band_onehot(rows, buckets))
    bias_term = jnp.dot(onehot, dwoff.reshape(heads, BAND).T, precision=HIGHEST)
    devices = dp_size * ep_size
    share = width // devices
    small = jnp.concatenate(
        [
            by_xor(router_term).T.reshape(devices, -1),
            gain_attn_term.reshape(devices, -1),
            gain_moe_term.reshape(devices, -1),
            bias_term.reshape(devices, -1),
        ],
        axis=1,
    )
    small = Halving(order, small, None, 0, route(q_bits), "small")
    small.start()
    core_got = order.leave(core.got)
    halves = order.leave(
        fold_first([order.enter((out_keep, out_got)), (qkv_keep, core_got)], [[(0, 0), (1, 0)], [(1, 1), (1, 2)]])
    )
    dense = [
        Halving(order, halves[2 * i], halves[2 * i + 1], 1, route(bits)[1:], name)
        for i, (bits, name) in enumerate(((q_bits, "out_q"), (k_bits, "k_v")))
    ]
    out_q, k_v = dense
    k_v.start()
    out_q.start()
    fold(small, *units)
    prod_low, prod_high = order.leave(produced_rows(order.enter(hid), w_down, experts))
    fold(small, down_units[1], k_v)
    returned = Return(order, prod_low, prod_high, "expert", ep_size, "produced_rows")
    fold(small, down_units[0], out_q)
    fold(small, units[1], k_v)
    fold(small, down_units[1], out_q)
    fold(k_v)
    returned.fold()
    fold(down_units[0], out_q)
    returned.finish()
    layer_out = order.leave(layer_output(middle, chances_xor, code_xor.T, returned.slots))
    rest = units + down_units + dense + [small]
    while any(unit.route for unit in rest):
        fold(*[unit for unit in rest if unit.route])
    small_sum = pick(small.keep, whole_me, 0) + order.token[0, :1]

    terms = [unit.keep for unit in units]
    gate_grad = jnp.concatenate([term[0] for term in terms], axis=1)[None]
    up_grad = jnp.concatenate([term[1] for term in terms], axis=1)[None]
    down_grad = jnp.concatenate([unit.keep for unit in down_units], axis=1)[None]
    n_router = width * experts // devices
    n_gain = width // devices
    router_grad = small_sum[:n_router].reshape(share, experts)
    gain_attn_grad = small_sum[n_router : n_router + n_gain]
    gain_moe_grad = small_sum[n_router + n_gain : n_router + 2 * n_gain]
    bias_grad = small_sum[n_router + 2 * n_gain :]
    return (
        layer_out,
        token_grad,
        dense[0].keep[1],
        dense[1].keep[0],
        dense[1].keep[1],
        dense[0].keep[0],
        gain_attn_grad,
        gain_moe_grad,
        bias_grad,
        router_grad,
        gate_grad,
        up_grad,
        down_grad,
    )


def solution(mesh):
    in_specs = (
        P(("dp", "expert"), None),
        P(("dp", "expert"), None),
        P(),
        P(),
        P(),
        P(),
        P(),
        P(),
        P(),
        P(),
        P("expert", None, None),
        P("expert", None, None),
        P("expert", None, None),
        P(("dp", "expert"), None),
        P(("dp", "expert"), None),
    )
    out_specs = (
        P(("dp", "expert"), None),
        P(("dp", "expert"), None),
        P(("dp", "expert"), None),
        P(("dp", "expert"), None),
        P(("dp", "expert"), None),
        P(("dp", "expert"), None),
        P(("dp", "expert")),
        P(("dp", "expert")),
        P(("dp", "expert")),
        P(("dp", "expert"), None),
        P("expert", "dp", None),
        P("expert", "dp", None),
        P("expert", "dp", None),
    )
    run = functools.partial(body, dp_size=mesh.shape["dp"], ep_size=mesh.shape["expert"])
    return jax.shard_map(run, mesh=mesh, in_specs=in_specs, out_specs=out_specs, check_vma=False)
```

time: 469 us -> 439 us (0.936)
  waiting for transfers between devices: 118 us -> 92 us
    pallas_call x19 -> x28, Pallas kernels: 151 us -> 262 us  [call(): pl.pallas_call(kernel, in_specs=list(in_specs), compiler_params=params(),...]
    pallas_call x6 -> x0, Pallas kernels: 110 us -> none  [the longest x3 62.8 us: expert_a(): pl.pallas_call(run, grid=(count,), in_specs=specs + [out_block, col_weigh...]
    ppermute x33 -> x45, waiting for transfers between devices: 118 us -> 92 us  [swap(): return lax.ppermute(value, axis, [(i, i ^ mask) for i in range(size)])]
    all_to_all x2 -> x0, starting transfers between devices: 7.64 us -> none  [the longest x1 4.04 us: body(): returned = lax.all_to_all(order.enter(produced), 'expert', 0, 0, tiled=True)]
    unnamed x92 -> x99, local copies, waits for them, and re-layouts: 11.9 us -> 18.7 us
    ppermute x33 -> x45, starting transfers between devices: 27.7 us -> 34.1 us  [swap(): return lax.ppermute(value, axis, [(i, i ^ mask) for i in range(size)])]
    slice x6 -> x2, local copies, waits for them, and re-layouts: 6.56 us -> 0.09 us  [fold(): self.slots[m][0][self.slots[m][1]][None]]
  transfers between devices with their start and end apart: 35 -> 45, of which waited for: 12 -> 13; matrix products, arithmetic and copies ran while one was open for 5% -> 5% of each run, Pallas kernels for 51% -> 53%
where the time goes in v2:
time: 439 us; the launch traced here: 432 us
  Pallas kernels  262 us (60%)
  waiting for transfers between devices  92 us (21%)
  starting transfers between devices  34.1 us (8%)
  local copies, waits for them, and re-layouts  30.7 us (7%)
  other arithmetic  10.6 us (2%)
    pallas_call x28, Pallas kernels, call(): pl.pallas_call(kernel, in_specs=list(in_specs), compiler_params=params(),...  262 us
    ppermute x45, waiting for transfers between devices, swap(): return lax.ppermute(value, axis, [(i, i ^ mask) for i in range(size)])  92 us
    ppermute x45, starting transfers between devices, swap(): return lax.ppermute(value, axis, [(i, i ^ mask) for i in range(size)])  34.1 us
    unnamed x99, local copies, waits for them, and re-layouts  18.7 us
  transfers between devices with their start and end apart: 45, of which 13 were waited for; matrix products, arithmetic and copies ran while one was open for 5% of the time, Pallas kernels for 53%

profile of v2, /device:TPU:0, one launch (start us, length us, event | category | flops | bytes accessed | tf_op | source)
XLA Modules:
  0.0 431.8 jit_solution(7722008714910523920)
XLA Ops:
  0.6 3.0 collective-permute-start.1
  6.6 15.7 %attn_first.1 = (bf16[512,1024]{1,0:T(8,128)(2,1)}, bf16[512,1024]{1,0:T(8,128)(2,1)}, bf16[512,1024]{1,0:T(8,128)(2,1)}, f32[4,4,512]{2,1,0:T(4,128)}, f32[1,12...) custom-call(bf16[512,1024]{1,0:T(8,128)(2,1)} %tok_ref.6, ...), custom_call_target="tpu_custom_call" | custom-call | flops 1150000000 | bytes 100000 | tf_op jit(solution)/shard_map/attn_first/pallas_call | solution.py:101
  22.6 4.5 %collective-permute-done.1.refs_3_ = bf16[512,1024]{1,0:T(8,128)(2,1)S(1)} collective-permute-done((bf16[512,1024]{1,0:T(8,128)(2,1)}, bf16[512,1024]{1,0:T(8,128)(2,1)S(1)}, u32[]{:S(2)}, u32[]{:S(2)}) %collective-permute-start.1) | collective-permute-done | bytes 1048608 | tf_op jit(solution)/shard_map/cot0_2/ppermute | solution.py:967
  29.0 12.4 %attn_second.1 = (bf16[512,1024]{1,0:T(8,128)(2,1)}, f32[4,4,512]{2,1,0:T(4,128)}, f32[512,1024]{1,0:T(8,128)}, bf16[512,1024]{1,0:T(8,128)(2,1)}, f32[16,512]{1,0:T(8,128)}, /*index=5*/bf16[272,1024]{1,0:T(8,128)(2,1)}) custom-call(bf16[512,1024]{1,0:T(8,128)(2,1)} %tok_ref.6, ...), custom_call_target="tpu_custom_call", output_to_operand_aliasing={{0}: (9, {}), {1}: (10, {}), {2}: (11, {}), {3}: (12, {}), ... | custom-call | flops 28750000128 | bytes 100000 | tf_op jit(solution)/shard_map/attn_second/pallas_call | solution.py:101
  43.8 10.0 %cot_hidden.1 = (bf16[1280,1280]{1,0:T(8,128)(2,1)}, bf16[1280,1024]{1,0:T(8,128)(2,1)}) custom-call(s32[4,512]{1,0:T(4,128)} %pad_add_fusion.1.refs_0_.refs_2_, bf16[512,1024]{1,0:T(8,128)(2,1)} %cot_ref.1, bf16[512,1024]{1,0:T(8,128)(2,1)} %copy-done.10, bf16[512,1024]{1,0:T(8,128)(2,1)} %copy-done.9, bf16[512,1024]{1,0:T(8,128)(2,1)} %collective-permute-done.5.refs_4_, ...), custom_call_target="tpu_custom_call" | custom-call | flops 1150000000 | bytes 100000 | tf_op jit(solution)/shard_map/cot_hidden/pallas_call | solution.py:101
  59.8 28.5 %expert_grads.2 = (bf16[1280,1024]{1,0:T(8,128)(2,1)}, bf16[1024,1280]{1,0:T(8,128)(2,1)}, f32[1280,128]{1,0:T(8,128)}, bf16[1280,1024]{1,0:T(8,128)(2,1)}, bf16...) custom-call(s32[1]{0:T(128)} %bitcast.6.refs_0_, ...), custom_call_target="tpu_custom_call" | custom-call | flops 1150000000 | bytes 100000 | tf_op jit(solution)/shard_map/expert_grads/pallas_call | solution.py:101
  90.0 9.0 %cot_hidden_more.1.refs_3_ = bf16[1280,1536]{1,0:T(8,128)(2,1)} custom-call(bf16[1280,1024]{1,0:T(8,128)(2,1)} %get-tuple-element.613.refs_11_.rows_ref, bf16[1,2816,1024]{2,1,0:T(8,128)(2,1)} %wd_ref.3), custom_call_target="tpu_custom_call" | custom-call | flops 1150000000 | bytes 100000 | tf_op jit(solution)/shard_map/cot_hidden_more/pallas_call | solution.py:101
  99.0 29.2 %expert_grads.3 = (bf16[2,512,1536]{2,1,0:T(8,128)(2,1)}, bf16[2,512,1536]{2,1,0:T(8,128)(2,1)}, f32[1280,128]{1,0:T(8,128)}, bf16[1280,2816]{1,0:T(8,128)(2,1)}...) custom-call(bf16[1280,1024]{1,0:T(8,128)(2,1)} %get-tuple-element.61, ...), custom_call_target="tpu_custom_call", output_to_operand_aliasing={{3}: (6, {}), {4}: (7, {}), {5}: (8, {}), {6}: (9, {})} | custom-call | flops 1150000000 | bytes 100000 | tf_op jit(solution)/shard_map/expert_grads/pallas_call | solution.py:101
  129.9 25.5 %expert_input_grad.1 = (bf16[336,1024]{1,0:T(8,128)(2,1)}, bf16[336,1024]{1,0:T(8,128)(2,1)}, bf16[336,1024]{1,0:T(8,128)(2,1)}, bf16[336,1024]{1,0:T(8,128)(2,1)}) custom-call(bf16[1280,2816]{1,0:T(8,128)(2,1)} %get-tuple-element.639.gg_ref, bf16[1280,2816]{1,0:T(8,128)(2,1)} %get-tuple-element.640.gu_ref, f32[1280,128]{1,0:T(8,128)} %get-tuple-element.641.refs_0_, ...), custom_call_target="tpu_custom_call" | custom-call | flops 1150000000 | bytes 100000 | tf_op jit(solution)/shard_map/expert_input_grad/pallas_call | solution.py:101
  160.1 4.4 %fold.12 = (bf16[2,256,1280]{2,1,0:T(8,128)(2,1)}, bf16[2,256,1280]{2,1,0:T(8,128)(2,1)}) custom-call(bf16[2,512,1280]{2,1,0:T(8,128)(2,1)} %get-tuple-element.657.refs_0_, bf16[2,512,1280]{2,1,0:T(8,128)(2,1)} %collective-permute-done.12.refs_1_), custom_call_target="tpu_custom_call" | custom-call | flops 1150000000 | bytes 100000 | tf_op jit(solution)/shard_map/fold/pallas_call | solution.py:101
  167.0 16.8 %down_grads.1 = (bf16[1408,512]{1,0:T(8,128)(2,1)}, bf16[1408,512]{1,0:T(8,128)(2,1)}, bf16[1408,512]{1,0:T(8,128)(2,1)}, bf16[1408,512]{1,0:T(8,128)(2,1)}) custom-call(s32[8]{0:T(128)} %get-tuple-element.583.refs_1_.place_a_ref, s32[8]{0:T(128)} %get-tuple-element.1101.place_b_ref, bf16[2816,1280]{1,0:T(8,128)(2,1)} %get-tuple-element.665.hidt_ref, ...), custom_call_target="tpu_custom_call" | custom-call | flops 1150000000 | bytes 100000 | tf_op jit(solution)/shard_map/down_grads/pallas_call | solution.py:101
  183.8 4.7 %sorted_rows.1 = (bf16[1024,512]{1,0:T(8,128)(2,1)}, bf16[2,1024,512]{2,1,0:T(8,128)(2,1)}) custom-call(s32[32]{0:T(128)} %get-tuple-element.1100.pq_ref, s32[32]{0:T(128)} %get-tuple-element.1099.pk_ref, bf16[512,1024]{1,0:T(8,128)(2,1)} %tok_ref.6, f32[1,1024]{1,0:T(1,128)} %bitcast.54, bf16[512,1024]{1,0:T(8,128)(2,1)} %get-tuple-element.684.att_ref), custom_call_target="tpu_custom_call" | custom-call | flops 1150000000 | bytes 100000 | tf_op jit(solution)/shard_map/sorted_rows/pallas_call | solution.py:101
  190.3 11.8 %moe_bwd.1 = (f32[512,1024]{1,0:T(8,128)}, bf16[512,1024]{1,0:T(8,128)(2,1)}, bf16[512,1024]{1,0:T(8,128)(2,1)}, bf16[1,512,1024]{2,1,0:T(8,128)(2,1)}, bf16[1,5...) custom-call(bf16[512,1024]{1,0:T(8,128)(2,1)} %cot_ref.1, f32[512,1024]{1,0:T(8,128)} %get-tuple-element.692.mid_ref, ...), custom_call_target="tpu_custom_call" | custom-call | flops 1150000000 | bytes 100000 | tf_op jit(solution)/shard_map/moe_bwd/pallas_call | solution.py:101
  203.7 4.8 %fold.13 = (bf16[2,256,1536]{2,1,0:T(8,128)(2,1)}, bf16[2,256,1536]{2,1,0:T(8,128)(2,1)}) custom-call(bf16[2,512,1536]{2,1,0:T(8,128)(2,1)} %get-tuple-element.717.refs_0_, bf16[2,512,1536]{2,1,0:T(8,128)(2,1)} %copy-done.1), custom_call_target="tpu_custom_call" | custom-call | flops 1150000000 | bytes 100000 | tf_op jit(solution)/shard_map/fold/pallas_call | solution.py:101
  208.6 16.2 %attn_bwd.1 = (bf16[512,1024]{1,0:T(8,128)(2,1)}, bf16[512,1024]{1,0:T(8,128)(2,1)}, bf16[512,1024]{1,0:T(8,128)(2,1)}, f32[4,4,512]{2,1,0:T(4,128)}) custom-call(bf16[512,1024]{1,0:T(8,128)(2,1)} %get-tuple-element.527.qs_ref, bf16[512,1024]{1,0:T(8,128)(2,1)} %get-tuple-element.528.k_ref, bf16[512,1024]{1,0:T(8,128)(2,1)} %get-tuple-element.529.v_ref, ...), custom_call_target="tpu_custom_call" | custom-call | flops 1150000000 | bytes 100000 | tf_op jit(solution)/shard_map/attn_bwd/pallas_call | solution.py:101
  224.9 3.4 fold.14
  228.2 7.6 %dense_terms.1 = (bf16[3,512,1024]{2,1,0:T(8,128)(2,1)}, bf16[3,512,1024]{2,1,0:T(8,128)(2,1)}) custom-call(bf16[2,1024,512]{2,1,0:T(8,128)(2,1)} %get-tuple-element.733.rows_ref, bf16[512,1024]{1,0:T(8,128)(2,1)} %get-tuple-element.780.dq_ref, bf16[512,1024]{1,0:T(8,128)(2,1)} %get-tuple-element.750.dk_ref, bf16[512,1024]{1,0:T(8,128)(2,1)} %get-tuple-element.751.dv_ref), custom_call_target="tpu_custom_call" | custom-call | flops 1150000000 | bytes 100000 | tf_op jit(solution)/shard_map/dense_terms/pallas_call | solution.py:101
  235.9 15.5 %collective-permute-done.20.refs_3_ = bf16[1408,512]{1,0:T(8,128)(2,1)S(1)} collective-permute-done((bf16[1408,512]{1,0:T(8,128)(2,1)}, bf16[1408,512]{1,0:T(8,128)(2,1)S(1)}, u32[]{:S(2)}, u32[]{:S(2)}) %collective-permute-start.20) | collective-permute-done | bytes 1441824 | tf_op jit(solution)/shard_map/down1_dp2/ppermute | solution.py:967
  252.5 4.4 %fold.15 = (bf16[704,512]{1,0:T(8,128)(2,1)}, bf16[704,512]{1,0:T(8,128)(2,1)}, bf16[704,512]{1,0:T(8,128)(2,1)}, bf16[704,512]{1,0:T(8,128)(2,1)}) custom-call(bf16[1408,512]{1,0:T(8,128)(2,1)} %get-tuple-element.765.refs_0_, bf16[1408,512]{1,0:T(8,128)(2,1)} %copy-done.5, bf16[1408,512]{1,0:T(8,128)(2,1)} %get-tuple-element.767.refs_2_, ...), custom_call_target="tpu_custom_call" | custom-call | flops 1150000000 | bytes 100000 | tf_op jit(solution)/shard_map/fold/pallas_call | solution.py:101
  263.3 10.7 %norm_bwd.1 = (f32[512,1024]{1,0:T(8,128)}, f32[1,1024]{1,0:T(1,128)}) custom-call(bf16[512,1024]{1,0:T(8,128)(2,1)} %tok_ref.6, f32[1,1024]{1,0:T(1,128)} %bitcast.55, f32[512,1024]{1,0:T(8,128)} %get-tuple-element.708.gmid_ref, bf16[512,1024]{1,0:T(8,128)(2,1)} %get-tuple-element.780.dq_ref, bf16[512,1024]{1,0:T(8,128)(2,1)} %get-tuple-element.750.dk_ref, ...), custom_call_target="tpu_custom_call" | custom-call | flops 8049999872 | bytes 100000 | tf_op jit(solution)/shard_map/norm_bwd/pallas_call | solution.py:101
  277.1 5.7 %fold_first.1 = (bf16[2,256,1024]{2,1,0:T(8,128)(2,1)}, bf16[2,256,1024]{2,1,0:T(8,128)(2,1)}, bf16[2,256,1024]{2,1,0:T(8,128)(2,1)}, bf16[2,256,1024]{2,1,0:T(8,128)(2,1)}) custom-call(bf16[1,512,1024]{2,1,0:T(8,128)(2,1)} %get-tuple-element.794.refs_0_, bf16[1,512,1024]{2,1,0:T(8,128)(2,1)} %copy-done.8, bf16[3,512,1024]{2,1,0:T(8,128)(2,1)} %get-tuple-element.796.refs_2_, ...), custom_call_target="tpu_custom_call" | custom-call | flops 1150000000 | bytes 100000 | tf_op jit(solution)/shard_map/fold_first/pallas_call | solution.py:101
  287.2 21.3 %collective-permute-done.24.refs_5_ = bf16[2,256,1536]{2,1,0:T(8,128)(2,1)} collective-permute-done((bf16[2,256,1536]{2,1,0:T(8,128)(2,1)}, bf16[2,256,1536]{2,1,0:T(8,128)(2,1)}, u32[]{:S(2)}, u32[]{:S(2)}) %collective-permute-start.24) | collective-permute-done | bytes 1572896 | tf_op jit(solution)/shard_map/gate_up1_dp2/ppermute | solution.py:967
  308.5 4.0 fold.16
  312.5 13.0 %produced_rows.1 = (bf16[2,320,1024]{2,1,0:T(8,128)(2,1)}, bf16[2,320,1024]{2,1,0:T(8,128)(2,1)}) custom-call(bf16[1280,2816]{1,0:T(8,128)(2,1)} %get-tuple-element.834.hid_ref, bf16[1,2816,1024]{2,1,0:T(8,128)(2,1)} %wd_ref.3), custom_call_target="tpu_custom_call" | custom-call | flops 1150000000 | bytes 100000 | tf_op jit(solution)/shard_map/produced_rows/pallas_call | solution.py:101
  327.4 3.3 fold.17
  337.9 3.3 fold.18
  344.0 16.6 %collective-permute-done.32.refs_1_ = f32[32,208]{1,0:T(8,128)S(1)} collective-permute-done((f32[32,208]{1,0:T(8,128)}, f32[32,208]{1,0:T(8,128)S(1)}, u32[]{:S(2)}, u32[]{:S(2)}) %collective-permute-start.32) | collective-permute-done | bytes 26656 | tf_op jit(solution)/shard_map/small_dp2/ppermute | solution.py:967
  361.1 6.9 %collective-permute-done.33.refs_3_ = bf16[2,128,1536]{2,1,0:T(8,128)(2,1)} collective-permute-done((bf16[2,128,1536]{2,1,0:T(8,128)(2,1)S(1)}, bf16[2,128,1536]{2,1,0:T(8,128)(2,1)}, u32[]{:S(2)}, u32[]{:S(2)}) %collective-permute-start.33) | collective-permute-done | bytes 786464 | tf_op jit(solution)/shard_map/gate_up1_dp4/ppermute | solution.py:967
  368.0 3.2 fold.19
  375.6 14.3 %collective-permute-done.36.refs_1_ = f32[32,208]{1,0:T(8,128)S(1)} collective-permute-done((f32[32,208]{1,0:T(8,128)}, f32[32,208]{1,0:T(8,128)S(1)}, u32[]{:S(2)}, u32[]{:S(2)}) %collective-permute-start.36) | collective-permute-done | bytes 26656 | tf_op jit(solution)/shard_map/small_dp4/ppermute | solution.py:967
  402.8 5.4 %collective-permute-done.42.refs_3_ = bf16[2,64,1024]{2,1,0:T(8,128)(2,1)S(1)} collective-permute-done((bf16[2,64,1024]{2,1,0:T(8,128)(2,1)S(1)}, bf16[2,64,1024]{2,1,0:T(8,128)(2,1)S(1)}, u32[]{:S(2)}, u32[]{:S(2)}) %collective-permute-start.42) | collective-permute-done | bytes 262176 | tf_op jit(solution)/shard_map/out_q_dp2/ppermute | solution.py:967
  415.7 6.3 %layer_output.1 = bf16[512,1024]{1,0:T(8,128)(2,1)} custom-call(f32[512,1024]{1,0:T(8,128)} %get-tuple-element.692.mid_ref, f32[16,512]{1,0:T(8,128)} %select_maximum_fusion.ch_ref, s32[512,4]{1,0:T(8,128)} %bitcast.49, bf16[2,320,1024]{2,1,0:T(8,128)(2,1)} %get-tuple-element.838.refs_0_, bf16[1,320,1024]{2,1,0:T(8,128)(2,1)} %copy-done.13, ...), custom_call_target="tpu_custom_call" | custom-call | flops 1150000000 | bytes 100000 | tf_op jit(solution)/shard_map/layer_output/pallas_call | solution.py:101
  (225 shorter events, 88.9 us)
Async XLA Ops:
  0.6 26.5 %collective-permute-start.1 = (bf16[512,1024]{1,0:T(8,128)(2,1)}, bf16[512,1024]{1,0:T(8,128)(2,1)S(1)}, u32[]{:S(2)}, u32[]{:S(2)}) collective-permute-start(bf16[512,1024]{1,0:T(8,128)(2,1)} %cot_ref.1), channel_id=1, source_target_pairs={{0,2},{1,3},{2,0},{3,1},{4,6},{5,7},{6,4},{7,5},{8,10},{9,11},{10,... | collective-permute-start | bytes 3145736 | tf_op jit(solution)/shard_map/cot0_2/ppermute | solution.py:967
  22.6 19.6 %collective-permute-start.4 = (bf16[512,1024]{1,0:T(8,128)(2,1)S(1)}, bf16[512,1024]{1,0:T(8,128)(2,1)S(1)}, u32[]{:S(2)}, u32[]{:S(2)}) collective-permute-start(bf16[512,1024]{1,0:T(8,128)(2,1)S(1)} %copy-done), channel_id=1, source_target_pairs={{0,1},{1,0},{2,3},{3,2},{4,5},{5,4},{6,7},{7,6},{8,9},{9,8},{10,11... | collective-permute-start | bytes 3145736 | tf_op jit(solution)/shard_map/cot0_1/ppermute | solution.py:967
  41.3 15.4 %collective-permute-start.9 = (bf16[272,1024]{1,0:T(8,128)(2,1)}, bf16[272,1024]{1,0:T(8,128)(2,1)}, u32[]{:S(2)}, u32[]{:S(2)}) collective-permute-start(bf16[272,1024]{1,0:T(8,128)(2,1)} %get-tuple-element.586.refs_4_), channel_id=1, source_target_pairs={{0,2},{1,3},{2,0},{3,1},{4,6},{5,7},{6,4},{7,5},{8,10},{9,11},{10,... | collective-permute-start | bytes 1671176 | tf_op jit(solution)/shard_map/rows_b0_2/ppermute | solution.py:967
  42.2 15.1 %collective-permute-start.7 = (bf16[272,1024]{1,0:T(8,128)(2,1)}, bf16[272,1024]{1,0:T(8,128)(2,1)S(1)}, u32[]{:S(2)}, u32[]{:S(2)}) collective-permute-start(bf16[272,1024]{1,0:T(8,128)(2,1)} %get-tuple-element.585.refs_3_), channel_id=1, source_target_pairs={{0,1},{1,0},{2,3},{3,2},{4,5},{5,4},{6,7},{7,6},{8,9},{9,8},{10,11... | collective-permute-start | bytes 1671176 | tf_op jit(solution)/shard_map/rows_a0_1/ppermute | solution.py:967
  42.5 14.8 %collective-permute-start.10 = (bf16[272,1024]{1,0:T(8,128)(2,1)}, bf16[272,1024]{1,0:T(8,128)(2,1)S(1)}, u32[]{:S(2)}, u32[]{:S(2)}) collective-permute-start(bf16[272,1024]{1,0:T(8,128)(2,1)} %get-tuple-element.586.refs_4_), channel_id=1, source_target_pairs={{0,1},{1,0},{2,3},{3,2},{4,5},{5,4},{6,7},{7,6},{8,9},{9,8},{10,11... | collective-permute-start | bytes 1671176 | tf_op jit(solution)/shard_map/rows_b0_1/ppermute | solution.py:967
  88.3 71.7 %collective-permute-start.12 = (bf16[2,512,1280]{2,1,0:T(8,128)(2,1)}, bf16[2,512,1280]{2,1,0:T(8,128)(2,1)}, u32[]{:S(2)}, u32[]{:S(2)}) collective-permute-start(bf16[2,512,1280]{2,1,0:T(8,128)(2,1)} %get-tuple-element.634), channel_id=1, source_target_pairs={{0,8},{4,12},{8,0},{12,4},{16,24},{20,28},{24,16},{28,20},{1,9},{5... | collective-permute-start | bytes 7864328 | tf_op jit(solution)/shard_map/gate_up0_dp2/ppermute | solution.py:967
  128.2 73.9 %collective-permute-start.16 = (bf16[2,512,1536]{2,1,0:T(8,128)(2,1)}, bf16[2,512,1536]{2,1,0:T(8,128)(2,1)S(1)}, u32[]{:S(2)}, u32[]{:S(2)}) collective-permute-start(bf16[2,512,1536]{2,1,0:T(8,128)(2,1)} %get-tuple-element.711), channel_id=1, source_target_pairs={{0,4},{4,0},{8,12},{12,8},{16,20},{20,16},{24,28},{28,24},{1,5},{5... | collective-permute-start | bytes 9437192 | tf_op jit(solution)/shard_map/gate_up1_dp1/ppermute | solution.py:967
  155.4 33.1 %collective-permute-start.13 = (bf16[336,1024]{1,0:T(8,128)(2,1)}, bf16[336,1024]{1,0:T(8,128)(2,1)}, u32[]{:S(2)}, u32[]{:S(2)}) collective-permute-start(bf16[336,1024]{1,0:T(8,128)(2,1)} %get-tuple-element.679), channel_id=1, source_target_pairs={{0,1},{1,0},{2,3},{3,2},{4,5},{5,4},{6,7},{7,6},{8,9},{9,8},{10,11... | collective-permute-start | bytes 2064392 | tf_op jit(solution)/shard_map/grad_rows1/ppermute | solution.py:967
  155.5 33.0 %collective-permute-start.14 = (bf16[336,1024]{1,0:T(8,128)(2,1)}, bf16[336,1024]{1,0:T(8,128)(2,1)}, u32[]{:S(2)}, u32[]{:S(2)}) collective-permute-start(bf16[336,1024]{1,0:T(8,128)(2,1)} %get-tuple-element.680), channel_id=1, source_target_pairs={{0,2},{1,3},{2,0},{3,1},{4,6},{5,7},{6,4},{7,5},{8,10},{9,11},{10,... | collective-permute-start | bytes 2064392 | tf_op jit(solution)/shard_map/grad_rows2/ppermute | solution.py:967
  156.0 32.4 %collective-permute-start.15 = (bf16[336,1024]{1,0:T(8,128)(2,1)}, bf16[336,1024]{1,0:T(8,128)(2,1)}, u32[]{:S(2)}, u32[]{:S(2)}) collective-permute-start(bf16[336,1024]{1,0:T(8,128)(2,1)} %get-tuple-element.681), channel_id=1, source_target_pairs={{0,3},{1,2},{2,1},{3,0},{4,7},{5,6},{6,5},{7,4},{8,11},{9,10},{10,... | collective-permute-start | bytes 2064392 | tf_op jit(solution)/shard_map/grad_rows3/ppermute | solution.py:967
  164.4 60.4 %collective-permute-start.17 = (bf16[2,256,1280]{2,1,0:T(8,128)(2,1)}, bf16[2,256,1280]{2,1,0:T(8,128)(2,1)}, u32[]{:S(2)}, u32[]{:S(2)}) collective-permute-start(bf16[2,256,1280]{2,1,0:T(8,128)(2,1)} %get-tuple-element.735), channel_id=1, source_target_pairs={{0,16},{4,20},{8,24},{12,28},{16,0},{20,4},{24,8},{28,12},{1,17},{... | collective-permute-start | bytes 3932168 | tf_op jit(solution)/shard_map/gate_up0_dp4/ppermute | solution.py:967
  189.4 46.5 %collective-permute-start.19 = (bf16[1408,512]{1,0:T(8,128)(2,1)}, bf16[1408,512]{1,0:T(8,128)(2,1)S(1)}, u32[]{:S(2)}, u32[]{:S(2)}) collective-permute-start(bf16[1408,512]{1,0:T(8,128)(2,1)} %get-tuple-element.757), channel_id=1, source_target_pairs={{0,4},{4,0},{8,12},{12,8},{16,20},{20,16},{24,28},{28,24},{1,5},{5... | collective-permute-start | bytes 4325384 | tf_op jit(solution)/shard_map/down0_dp1/ppermute | solution.py:967
  189.9 61.5 %collective-permute-start.20 = (bf16[1408,512]{1,0:T(8,128)(2,1)}, bf16[1408,512]{1,0:T(8,128)(2,1)S(1)}, u32[]{:S(2)}, u32[]{:S(2)}) collective-permute-start(bf16[1408,512]{1,0:T(8,128)(2,1)} %get-tuple-element.761), channel_id=1, source_target_pairs={{0,8},{4,12},{8,0},{12,4},{16,24},{20,28},{24,16},{28,20},{1,9},{5... | collective-permute-start | bytes 4325384 | tf_op jit(solution)/shard_map/down1_dp2/ppermute | solution.py:967
  202.1 22.7 %collective-permute-start.18 = (bf16[1,512,1024]{2,1,0:T(8,128)(2,1)}, bf16[1,512,1024]{2,1,0:T(8,128)(2,1)S(1)}, u32[]{:S(2)}, u32[]{:S(2)}) collective-permute-start(bf16[1,512,1024]{2,1,0:T(8,128)(2,1)} %get-tuple-element.736), channel_id=1, source_target_pairs={{0,1},{1,0},{2,3},{3,2},{4,5},{5,4},{6,7},{7,6},{8,9},{9,8},{10,11... | collective-permute-start | bytes 3145736 | tf_op jit(solution)/shard_map/out_expert1/ppermute | solution.py:967
  256.9 18.6 %collective-permute-start.22 = (bf16[3,512,1024]{2,1,0:T(8,128)(2,1)}, bf16[3,512,1024]{2,1,0:T(8,128)(2,1)S(1)}, u32[]{:S(2)}, u32[]{:S(2)}) collective-permute-start(bf16[3,512,1024]{2,1,0:T(8,128)(2,1)} %get-tuple-element.791), channel_id=1, source_target_pairs={{0,1},{1,0},{2,3},{3,2},{4,5},{5,4},{6,7},{7,6},{8,9},{9,8},{10,11... | collective-permute-start | bytes 9437192 | tf_op jit(solution)/shard_map/qkv_expert1/ppermute | solution.py:967
  261.4 47.0 %collective-permute-start.24 = (bf16[2,256,1536]{2,1,0:T(8,128)(2,1)}, bf16[2,256,1536]{2,1,0:T(8,128)(2,1)}, u32[]{:S(2)}, u32[]{:S(2)}) collective-permute-start(bf16[2,256,1536]{2,1,0:T(8,128)(2,1)} %get-tuple-element.814), channel_id=1, source_target_pairs={{0,8},{4,12},{8,0},{12,4},{16,24},{20,28},{24,16},{28,20},{1,9},{5... | collective-permute-start | bytes 4718600 | tf_op jit(solution)/shard_map/gate_up1_dp2/ppermute | solution.py:967
  261.7 25.3 %collective-permute-start.23 = (bf16[2,128,1280]{2,1,0:T(8,128)(2,1)}, bf16[2,128,1280]{2,1,0:T(8,128)(2,1)}, u32[]{:S(2)}, u32[]{:S(2)}) collective-permute-start(bf16[2,128,1280]{2,1,0:T(8,128)(2,1)} %get-tuple-element.810), channel_id=1, source_target_pairs={{0,4},{4,0},{8,12},{12,8},{16,20},{20,16},{24,28},{28,24},{1,5},{5... | collective-permute-start | bytes 1966088 | tf_op jit(solution)/shard_map/gate_up0_dp1/ppermute | solution.py:967
  282.9 42.7 %collective-permute-start.27 = (bf16[2,256,1024]{2,1,0:T(8,128)(2,1)}, bf16[2,256,1024]{2,1,0:T(8,128)(2,1)S(1)}, u32[]{:S(2)}, u32[]{:S(2)}) collective-permute-start(bf16[2,256,1024]{2,1,0:T(8,128)(2,1)} %get-tuple-element.848), channel_id=1, source_target_pairs={{0,4},{4,0},{8,12},{12,8},{16,20},{20,16},{24,28},{28,24},{1,5},{5... | collective-permute-start | bytes 3145736 | tf_op jit(solution)/shard_map/k_v_dp1/ppermute | solution.py:967
  283.4 53.5 %collective-permute-start.31 = (bf16[2,256,1024]{2,1,0:T(8,128)(2,1)}, bf16[2,256,1024]{2,1,0:T(8,128)(2,1)S(1)}, u32[]{:S(2)}, u32[]{:S(2)}) collective-permute-start(bf16[2,256,1024]{2,1,0:T(8,128)(2,1)} %get-tuple-element.880), channel_id=1, source_target_pairs={{0,2},{1,3},{2,0},{3,1},{4,6},{5,7},{6,4},{7,5},{8,10},{9,11},{10,... | collective-permute-start | bytes 3145736 | tf_op jit(solution)/shard_map/out_q_expert2/ppermute | solution.py:967
  285.1 40.4 %collective-permute-start.26 = (bf16[704,512]{1,0:T(8,128)(2,1)S(1)}, bf16[704,512]{1,0:T(8,128)(2,1)S(1)}, u32[]{:S(2)}, u32[]{:S(2)}) collective-permute-start(bf16[704,512]{1,0:T(8,128)(2,1)S(1)} %copy-done.32), channel_id=1, source_target_pairs={{0,16},{4,20},{8,24},{12,28},{16,0},{20,4},{24,8},{28,12},{1,17},{... | collective-permute-start | bytes 2162696 | tf_op jit(solution)/shard_map/down1_dp4/ppermute | solution.py:967
  287.1 49.8 %collective-permute-start.30 = (bf16[704,512]{1,0:T(8,128)(2,1)}, bf16[704,512]{1,0:T(8,128)(2,1)}, u32[]{:S(2)}, u32[]{:S(2)}) collective-permute-start(bf16[704,512]{1,0:T(8,128)(2,1)} %get-tuple-element.876), channel_id=1, source_target_pairs={{0,8},{4,12},{8,0},{12,4},{16,24},{20,28},{24,16},{28,20},{1,9},{5... | collective-permute-start | bytes 2162696 | tf_op jit(solution)/shard_map/down0_dp2/ppermute | solution.py:967
  332.2 35.8 %collective-permute-start.33 = (bf16[2,128,1536]{2,1,0:T(8,128)(2,1)S(1)}, bf16[2,128,1536]{2,1,0:T(8,128)(2,1)}, u32[]{:S(2)}, u32[]{:S(2)}) collective-permute-start(bf16[2,128,1536]{2,1,0:T(8,128)(2,1)S(1)} %copy-done.31), channel_id=1, source_target_pairs={{0,16},{4,20},{8,24},{12,28},{16,0},{20,4},{24,8},{28,12},{1,17},{... | collective-permute-start | bytes 2359304 | tf_op jit(solution)/shard_map/gate_up1_dp4/ppermute | solution.py:967
  332.4 35.6 %collective-permute-start.34 = (bf16[2,128,1024]{2,1,0:T(8,128)(2,1)}, bf16[2,128,1024]{2,1,0:T(8,128)(2,1)}, u32[]{:S(2)}, u32[]{:S(2)}) collective-permute-start(bf16[2,128,1024]{2,1,0:T(8,128)(2,1)} %get-tuple-element.910), channel_id=1, source_target_pairs={{0,8},{4,12},{8,0},{12,4},{16,24},{20,28},{24,16},{28,20},{1,9},{5... | collective-permute-start | bytes 1572872 | tf_op jit(solution)/shard_map/k_v_dp2/ppermute | solution.py:967
  334.8 63.1 %collective-permute-start.28 = (bf16[2,320,1024]{2,1,0:T(8,128)(2,1)S(1)}, bf16[2,320,1024]{2,1,0:T(8,128)(2,1)S(1)}, u32[]{:S(2)}, u32[]{:S(2)}) collective-permute-start(bf16[2,320,1024]{2,1,0:T(8,128)(2,1)S(1)} %copy-done.28), channel_id=1, source_target_pairs={{0,2},{1,3},{2,0},{3,1},{4,6},{5,7},{6,4},{7,5},{8,10},{9,11},{10,... | collective-permute-start | bytes 3932168 | tf_op jit(solution)/shard_map/produced_rows2/ppermute | solution.py:967
  341.2 19.4 %collective-permute-start.32 = (f32[32,208]{1,0:T(8,128)}, f32[32,208]{1,0:T(8,128)S(1)}, u32[]{:S(2)}, u32[]{:S(2)}) collective-permute-start(f32[32,208]{1,0:T(8,128)} %get-tuple-element.914.refs_0_), channel_id=1, source_target_pairs={{0,8},{4,12},{8,0},{12,4},{16,24},{20,28},{24,16},{28,20},{1,9},{5... | collective-permute-start | bytes 79880 | tf_op jit(solution)/shard_map/small_dp2/ppermute | solution.py:967
  342.6 47.4 %collective-permute-start.37 = (bf16[352,512]{1,0:T(8,128)(2,1)}, bf16[352,512]{1,0:T(8,128)(2,1)}, u32[]{:S(2)}, u32[]{:S(2)}) collective-permute-start(bf16[352,512]{1,0:T(8,128)(2,1)} %get-tuple-element.935), channel_id=1, source_target_pairs={{0,4},{4,0},{8,12},{12,8},{16,20},{20,16},{24,28},{28,24},{1,5},{5... | collective-permute-start | bytes 1081352 | tf_op jit(solution)/shard_map/down1_dp1/ppermute | solution.py:967
  360.6 29.4 %collective-permute-start.38 = (bf16[2,128,1024]{2,1,0:T(8,128)(2,1)S(1)}, bf16[2,128,1024]{2,1,0:T(8,128)(2,1)S(1)}, u32[]{:S(2)}, u32[]{:S(2)}) collective-permute-start(bf16[2,128,1024]{2,1,0:T(8,128)(2,1)S(1)} %copy-done.34), channel_id=1, source_target_pairs={{0,4},{4,0},{8,12},{12,8},{16,20},{20,16},{24,28},{28,24},{1,5},{5... | collective-permute-start | bytes 1572872 | tf_op jit(solution)/shard_map/out_q_dp1/ppermute | solution.py:967
  371.2 18.7 %collective-permute-start.36 = (f32[32,208]{1,0:T(8,128)}, f32[32,208]{1,0:T(8,128)S(1)}, u32[]{:S(2)}, u32[]{:S(2)}) collective-permute-start(f32[32,208]{1,0:T(8,128)} %get-tuple-element.943.refs_0_), channel_id=1, source_target_pairs={{0,16},{4,20},{8,24},{12,28},{16,0},{20,4},{24,8},{28,12},{1,17},{... | collective-permute-start | bytes 79880 | tf_op jit(solution)/shard_map/small_dp4/ppermute | solution.py:967
  371.2 24.3 %collective-permute-start.35 = (bf16[2,64,1024]{2,1,0:T(8,128)(2,1)}, bf16[2,64,1024]{2,1,0:T(8,128)(2,1)S(1)}, u32[]{:S(2)}, u32[]{:S(2)}) collective-permute-start(bf16[2,64,1024]{2,1,0:T(8,128)(2,1)} %get-tuple-element.930), channel_id=1, source_target_pairs={{0,16},{4,20},{8,24},{12,28},{16,0},{20,4},{24,8},{28,12},{1,17},{... | collective-permute-start | bytes 786440 | tf_op jit(solution)/shard_map/k_v_dp4/ppermute | solution.py:967
  398.0 16.0 %collective-permute-start.40 = (bf16[1,320,1024]{2,1,0:T(8,128)(2,1)S(1)}, bf16[1,320,1024]{2,1,0:T(8,128)(2,1)S(1)}, u32[]{:S(2)}, u32[]{:S(2)}) collective-permute-start(bf16[1,320,1024]{2,1,0:T(8,128)(2,1)S(1)} %slice.59), channel_id=1, source_target_pairs={{0,1},{1,0},{2,3},{3,2},{4,5},{5,4},{6,7},{7,6},{8,9},{9,8},{10,11... | collective-permute-start | bytes 1966088 | tf_op jit(solution)/shard_map/produced_rows1_1/ppermute | solution.py:967
  398.1 16.0 %collective-permute-start.39 = (bf16[1,320,1024]{2,1,0:T(8,128)(2,1)S(1)}, bf16[1,320,1024]{2,1,0:T(8,128)(2,1)S(1)}, u32[]{:S(2)}, u32[]{:S(2)}) collective-permute-start(bf16[1,320,1024]{2,1,0:T(8,128)(2,1)S(1)} %slice.58), channel_id=1, source_target_pairs={{0,1},{1,0},{2,3},{3,2},{4,5},{5,4},{6,7},{7,6},{8,9},{9,8},{10,11... | collective-permute-start | bytes 1966088 | tf_op jit(solution)/shard_map/produced_rows1_0/ppermute | solution.py:967
  401.0 21.0 %collective-permute-start.44 = (bf16[2,32,1024]{2,1,0:T(8,128)(2,1)S(1)}, bf16[2,32,1024]{2,1,0:T(8,128)(2,1)S(1)}, u32[]{:S(2)}, u32[]{:S(2)}) collective-permute-start(bf16[2,32,1024]{2,1,0:T(8,128)(2,1)S(1)} %copy-done.41), channel_id=1, source_target_pairs={{0,2},{1,3},{2,0},{3,1},{4,6},{5,7},{6,4},{7,5},{8,10},{9,11},{10,... | collective-permute-start | bytes 393224 | tf_op jit(solution)/shard_map/k_v_expert2/ppermute | solution.py:967
  (61 other events, 533.8 us)

commit v3 on v2

--- a/solution.py
+++ b/solution.py
@@ -80,10 +80,9 @@
 
 
 TIMES = {
-    ("attn_second", 0): 25.0,
+    ("down_grads", 0): 10.0,
+    ("dense_terms", 0): 13.1,
     ("fold", 2): 2.0,
-    ("norm_bwd", 0): 7.0,
-    ("fold", 6): 40.0,
 }
 
 
@@ -93,7 +92,7 @@
 def estimate(name):
     turn = TURNS.get(name, 0)
     TURNS[name] = turn + 1
-    time = TIMES.get((name, turn), 1.0)
+    time = TIMES.get((name, turn), 0.1)
     return pl.CostEstimate(flops=int(time * 1.15e9), bytes_accessed=100000, transcendentals=0)
 
 
@@ -168,7 +167,29 @@
     return jnp.concatenate(heads_t, axis=0).T.astype(BF), jnp.concatenate(totals, axis=0)
 
 
-def route_rows(mid, gain_ref, wr_ref, experts, nm_ref, ch_ref, payload_ref):
+def slot_codes(routes):
+    chosen = routes.astype(F32).T
+    tokens = chosen.shape[1]
+    numbers = lax.broadcasted_iota(jnp.int32, (TAIL // 2, tokens), 0).astype(F32)
+    named = jnp.logical_or(numbers == chosen[0:1], numbers == chosen[1:2])
+    row = lax.broadcasted_iota(jnp.int32, (tokens, tokens), 0)
+    lane = lax.broadcasted_iota(jnp.int32, (tokens, tokens), 1)
+    before = jnp.where(row < lane, 1.0, 0.0).astype(BF)
+    return jnp.where(named, dot(jnp.where(named, 1.0, 0.0).astype(BF), before), -1.0)
+
+
+def packed_codes(codes):
+    upper = jnp.floor((codes + 1.0) * (1.0 / 16.0))
+    return jnp.concatenate([upper, codes + 1.0 - 16.0 * upper], axis=0)
+
+
+def own_code(me, packed):
+    row = lax.broadcasted_iota(jnp.int32, packed.shape, 0)
+    weight = jnp.where(row == me, 16.0, jnp.where(row == me + TAIL // 2, 1.0, 0.0))
+    return (jnp.sum(packed.astype(F32) * weight, axis=0, keepdims=True) - 1.0).astype(jnp.int32)
+
+
+def route_rows(mid, gain_ref, wr_ref, experts, nm_ref, ch_ref, payload_ref, codes=None):
     rows = mid.shape[0]
     nm = (mid * rms_scale(mid) * gain_ref[...]).astype(BF)
     nm_ref[...] = nm
@@ -182,7 +203,10 @@
     hi = chances.astype(BF).astype(F32)
     both = jnp.concatenate([hi[: TAIL // 2], (chances - hi)[: TAIL // 2]], axis=0)
     payload_ref[0:rows, :] = nm
-    payload_ref[rows:, :] = jnp.concatenate([both, jnp.zeros((TAIL, nm.shape[1] - rows), F32)], axis=1).astype(BF)
+    tail = [both] if codes is None else [both, packed_codes(codes)]
+    used = sum(v.shape[1] for v in tail)
+    tail.append(jnp.zeros((TAIL, nm.shape[1] - used), F32))
+    payload_ref[rows:, :] = jnp.concatenate(tail, axis=1).astype(BF)
 
 
 def segment_mask(seg_ref, first, count):
@@ -192,9 +216,9 @@
 
 
 def attn_first_kernel(
-    tok_ref, gain_a_ref, wq_ref, wk_ref, wv_ref, wo_ref, bias_ref, onehot_ref, seg_ref, gain_m_ref, wr_ref,
-    qs_ref, k_ref, v_ref, woff_ref, token_ref, att_ref, lse_ref, mid_ref, nm_ref, ch_ref, payload_ref,
-    n_scr, mask_scr, woff_scr,
+    tok_ref, gain_a_ref, wq_ref, wk_ref, wv_ref, wo_ref, bias_ref, onehot_ref, seg_ref, gain_m_ref, wr_ref, routes_ref,
+    qs_ref, k_ref, v_ref, woff_ref, token_ref, code_ref, att_ref, lse_ref, mid_ref, nm_ref, ch_ref, payload_ref,
+    n_scr, mask_scr, woff_scr, code_scr,
     *, experts, head_dim,
 ):
     step = pl.program_id(0)
@@ -207,6 +231,9 @@
         mid_ref[...] = start[:rows]
         mask_scr[...] = segment_mask(seg_ref, 0, rows)
         token_ref[...] = jnp.where(seg_ref[:, 0:LANES] < 0, 1.0, 0.0)
+        codes = slot_codes(routes_ref[...])
+        code_scr[...] = codes
+        code_ref[...] = codes[:experts].astype(jnp.int32)
         table = onehot_ref[...]
         offsets = sum(dot_tn(part, table) for part in split3(bias_ref[...]))
         for g in range(woff_scr.shape[0]):
@@ -228,7 +255,7 @@
 
     @pl.when(step == pl.num_programs(0) - 1)
     def _():
-        route_rows(mid_ref[...], gain_m_ref, wr_ref, experts, nm_ref, ch_ref, payload_ref)
+        route_rows(mid_ref[...], gain_m_ref, wr_ref, experts, nm_ref, ch_ref, payload_ref, code_scr[...])
 
 
 def attn_second_kernel(
@@ -275,7 +302,7 @@
     return shapes, specs
 
 
-def attn_first(tokens, gain_attn, w_query, w_key, w_value, w_out, rel_bias, seg, gain_moe, w_router):
+def attn_first(tokens, gain_attn, w_query, w_key, w_value, w_out, rel_bias, seg, gain_moe, w_router, routes):
     rows, width = tokens.shape
     buckets, heads = rel_bias.shape
     experts = w_router.shape[1]
@@ -287,7 +314,7 @@
     return call(
         functools.partial(attn_first_kernel, experts=experts, head_dim=cols // HEAD_GROUP),
         (tokens, gain_attn[None], w_query, w_key, w_value, w_out, rel_bias, jnp.asarray(band_onehot(rows, buckets)).astype(BF),
-         seg, gain_moe[None], w_router),
+         seg, gain_moe[None], w_router, routes),
         [
             const_spec((rows, width)),
             const_spec((1, width)),
@@ -300,18 +327,21 @@
             const_spec(seg.shape),
             const_spec((1, width)),
             const_spec(w_router.shape),
+            const_spec(routes.shape),
         ],
         grid=(groups,),
         out_specs=[pl.BlockSpec((rows, cols), lambda g: (0, g))] * 3
-        + [pl.BlockSpec((1, HEAD_GROUP, BAND), lambda g: (g, 0, 0)), const_spec((1, LANES))]
+        + [pl.BlockSpec((1, HEAD_GROUP, BAND), lambda g: (g, 0, 0)), const_spec((1, LANES)), const_spec((experts, rows))]
         + specs,
         out_shape=[wide] * 3
         + [jax.ShapeDtypeStruct((groups, HEAD_GROUP, BAND), F32), jax.ShapeDtypeStruct((1, LANES), F32)]
+        + [jax.ShapeDtypeStruct((experts, rows), jnp.int32)]
         + shapes,
         scratch_shapes=[
             pltpu.VMEM((rows, width), BF),
             pltpu.VMEM((rows, part), F32),
             pltpu.VMEM((groups, HEAD_GROUP, BAND), F32),
+            pltpu.VMEM((TAIL // 2, rows), F32),
         ],
         cost_estimate=estimate("attn_first"),
         name="attn_first",
@@ -365,27 +395,33 @@
 FF_BLOCK = 256
 
 
-def cot_hidden_kernel(*refs, experts):
-    code_ref, cot_refs, wd_ref = refs[0], refs[1 : 1 + experts], refs[1 + experts]
-    out_ref, rows_ref = refs[2 + experts :]
+def cot_hidden_kernel(me_ref, *refs, experts):
+    tail_refs, cot_refs, wd_ref = refs[:experts], refs[experts : 2 * experts], refs[2 * experts]
+    out_ref, rows_ref = refs[2 * experts + 1 :]
 
     @pl.when(pl.program_id(0) == 0)
     def _():
         cap = rows_ref.shape[0] // experts
-        for m, cot_ref in enumerate(cot_refs):
-            rows_ref[m * cap : (m + 1) * cap, :] = dot(selector(code_ref[m : m + 1, :], cap), cot_ref[...]).astype(BF)
+        tokens = cot_refs[0].shape[0]
+        for m, (tail_ref, cot_ref) in enumerate(zip(tail_refs, cot_refs)):
+            code = own_code(me_ref[0], tail_ref[:, tokens // 2 : tokens // 2 + tokens])
+            rows_ref[m * cap : (m + 1) * cap, :] = dot(selector(code, cap), cot_ref[...]).astype(BF)
 
     out_ref[...] = dot_nt(rows_ref[...], wd_ref[0]).astype(BF)
 
 
-def cot_hidden(code, cots, w_down, cap, count):
+def cot_hidden(me, payloads, cots, w_down, cap, count):
     experts = len(cots)
     width = cots[0].shape[1]
     rows = experts * cap
+    last = payloads[0].shape[0] // TAIL - 1
     return call(
         functools.partial(cot_hidden_kernel, experts=experts),
-        (code, *cots, w_down),
-        whole_specs((code, *cots)) + [pl.BlockSpec((1, FF_BLOCK, width), lambda f: (0, f, 0))],
+        (me, *payloads, *cots, w_down),
+        [pl.BlockSpec(memory_space=pltpu.SMEM)]
+        + [pl.BlockSpec((TAIL, width), lambda f: (last, 0))] * experts
+        + whole_specs(cots)
+        + [pl.BlockSpec((1, FF_BLOCK, width), lambda f: (0, f, 0))],
         grid=(count,),
         out_specs=[pl.BlockSpec((rows, FF_BLOCK), lambda f: (0, f)), const_spec((rows, width))],
         out_shape=[jax.ShapeDtypeStruct((rows, count * FF_BLOCK), BF), jax.ShapeDtypeStruct((rows, width), BF)],
@@ -416,14 +452,15 @@
 ROW_BLOCK = 320
 
 
-def expert_first(me_ref, place_ref, code_ref, payloads, cot_ref, x_ref, xt_ref, gate_ref, gc_ref):
+def expert_first(me_ref, place_ref, payloads, cot_ref, x_ref, xt_ref, gate_ref, gc_ref):
     experts = len(payloads) // 2
     cap = x_ref.shape[0] // experts
     part = payloads[0].shape[0] - TAIL
     row = lax.broadcasted_iota(jnp.int32, (TAIL, part), 0)
     mine = jnp.logical_or(row == me_ref[0], row == me_ref[0] + TAIL // 2)
     for m in range(experts):
-        chosen = selector(code_ref[m : m + 1, :], cap)
+        code = own_code(me_ref[0], payloads[2 * m][part:, part : 3 * part])
+        chosen = selector(code, cap)
         place = slice(m * cap, (m + 1) * cap)
         total = jnp.zeros((cap, x_ref.shape[1]), F32)
         gate = jnp.zeros((cap, 1), F32)
@@ -444,20 +481,20 @@
         xt_ref[pl.ds(at, rows), :] = flipped[b * rows : (b + 1) * rows]
 
 
-def expert_a_kernel(*refs, experts, late_first):
+def expert_a_kernel(*refs, experts):
     step = pl.program_id(0)
     if experts:
-        me_ref, place_ref, code_ref = refs[:3]
-        payloads = refs[3 : 3 + 2 * experts]
-        cot_ref, gh_ref, wg_ref, wu_ref, x_ref, xt_ref, gate_ref, gc_ref = refs[3 + 2 * experts : 11 + 2 * experts]
+        me_ref, place_ref = refs[:2]
+        payloads = refs[2 : 2 + 2 * experts]
+        cot_ref, gh_ref, wg_ref, wu_ref, x_ref, xt_ref, gate_ref, gc_ref = refs[2 + 2 * experts : 10 + 2 * experts]
 
         @pl.when(step == 0)
         def _():
-            expert_first(me_ref, place_ref, code_ref, payloads, cot_ref, x_ref, xt_ref, gate_ref, gc_ref)
+            expert_first(me_ref, place_ref, payloads, cot_ref, x_ref, xt_ref, gate_ref, gc_ref)
 
     else:
         x_ref, xt_ref, gate_ref, gh_ref, wg_ref, wu_ref = refs[:6]
-    keep_ref, send_ref, sc_ref, hid_ref, hidt_ref, gg_ref, gu_ref = refs[-7:]
+    gate_keep_ref, gate_send_ref, up_keep_ref, up_send_ref, sc_ref, hid_ref, hidt_ref, gg_ref, gu_ref = refs[-9:]
 
     @pl.when(step == 0)
     def _():
@@ -484,22 +521,16 @@
         gu_ref[part, :] = (act * grad).astype(BF)
     hidt_ref[...] = hid_ref[...].T
     xt = xt_ref[...]
-    half = xt.shape[0] // 2
-    for i, grad_ref in enumerate((gg_ref, gu_ref)):
+    cut = xt.shape[0] // 4
+    for grad_ref, keep_ref, send_ref, second in ((gg_ref, gate_keep_ref, gate_send_ref, 1), (gu_ref, up_keep_ref, up_send_ref, 0)):
         term = dot(xt, grad_ref[...]).astype(BF)
-        if not late_first:
-            keep_ref[i] = term[:half]
-            send_ref[i] = term[half:]
-            continue
-        rows = term.shape[0] // late_first
-        for place in range(late_first):
-            block = (place & 1) * (late_first // 2) + (place >> 1)
-            out_ref, at = (keep_ref, place) if place < late_first // 2 else (send_ref, place - late_first // 2)
-            out_ref[i, at * rows : (at + 1) * rows] = term[block * rows : (block + 1) * rows]
-
-
-def expert_a(source, gh, gh_first, w_gate, w_up, first, count, late_first, filled=()):
-    opening = 0 if filled else len(source[3]) // 2
+        for q in range(4):
+            upper, lower = (q % 2, q // 2) if second else (q // 2, q % 2)
+            (send_ref if upper else keep_ref)[lower * cut : (lower + 1) * cut] = term[q * cut : (q + 1) * cut]
+
+
+def expert_a(source, gh, gh_first, w_gate, w_up, first, count, filled=()):
+    opening = 0 if filled else len(source[2]) // 2
     rows = gh.shape[0]
     width, ff = w_gate.shape[1:]
     span = count * FF_BLOCK
@@ -507,12 +538,12 @@
     out_block = pl.BlockSpec((rows, FF_BLOCK), lambda f: (0, first + f))
     wide = jax.ShapeDtypeStruct((rows, ff), BF)
     tall = jax.ShapeDtypeStruct((ff, rows), BF)
-    term = jax.ShapeDtypeStruct((2, width // 2, span), BF)
-    term_block = pl.BlockSpec((2, width // 2, FF_BLOCK), lambda f: (0, 0, f))
+    term = jax.ShapeDtypeStruct((width // 2, span), BF)
+    term_block = pl.BlockSpec((width // 2, FF_BLOCK), lambda f: (0, f))
     if opening:
-        me, place, code, payloads, cot_rows = source
-        args = (me, place, code, *payloads, cot_rows)
-        specs = [pl.BlockSpec(memory_space=pltpu.SMEM)] * 2 + whole_specs((code, *payloads, cot_rows))
+        me, place, payloads, cot_rows = source
+        args = (me, place, *payloads, cot_rows)
+        specs = [pl.BlockSpec(memory_space=pltpu.SMEM)] * 2 + whole_specs((*payloads, cot_rows))
         shared = [
             jax.ShapeDtypeStruct((rows, width), BF),
             jax.ShapeDtypeStruct((width, rows), BF),
@@ -525,10 +556,10 @@
         shared = []
     args = (*args, gh, w_gate, w_up)
     used = len(args)
-    first_filled = len(shared) + 3
+    first_filled = len(shared) + 5
 
     def run(*refs):
-        expert_a_kernel(*refs[:used], *refs[used + len(filled) :], experts=opening, late_first=late_first)
+        expert_a_kernel(*refs[:used], *refs[used + len(filled) :], experts=opening)
 
     return call(
         run,
@@ -538,9 +569,10 @@
         + [pl.BlockSpec(memory_space=pl.ANY)] * len(filled),
         grid=(count,),
         out_specs=whole_specs(shared)
-        + [term_block, term_block, const_spec((rows, LANES)), out_block]
+        + [term_block] * 4
+        + [const_spec((rows, LANES)), out_block]
         + [pl.BlockSpec((FF_BLOCK, rows), lambda f: (first + f, 0)), out_block, out_block],
-        out_shape=shared + [term, term, jax.ShapeDtypeStruct((rows, LANES), F32), wide, tall, wide, wide],
+        out_shape=shared + [term] * 4 + [jax.ShapeDtypeStruct((rows, LANES), F32), wide, tall, wide, wide],
         input_output_aliases={used + i: first_filled + i for i in range(len(filled))},
         cost_estimate=estimate("expert_grads"),
         name="expert_grads",
@@ -548,8 +580,7 @@
 
 
 def expert_b_kernel(gg_ref, gu_ref, *refs, cap, experts):
-    outs, acc = refs[-1 - experts : -1], refs[-1]
-    sc_refs, (wg_ref, wu_ref) = refs[: -3 - experts], refs[-3 - experts : -1 - experts]
+    sc_refs, (wg_ref, wu_ref, *outs, acc) = refs[:-5], refs[-5:]
     part_sum = dot_nt(gg_ref[...], wg_ref[0]) + dot_nt(gu_ref[...], wu_ref[0])
     step, block = pl.program_id(0), pl.program_id(1)
 
@@ -575,11 +606,12 @@
         out_ref[cap : cap + TAIL, :] = jnp.zeros((TAIL, total.shape[1]), BF)
         out_ref[cap : cap + TAIL, 0:cap] = packed.astype(BF)
 
-    for m, out_ref in enumerate(outs):
-
-        @pl.when(jnp.logical_and(step == pl.num_programs(0) - 1, block == m))
-        def _(out_ref=out_ref):
-            finish(out_ref)
+    last = step == pl.num_programs(0) - 1
+    for m in range(experts):
+
+        @pl.when(jnp.logical_and(last, block == m))
+        def _(m=m):
+            finish(outs[m // (experts // 2)].at[m % (experts // 2)])
 
 
 def expert_b(gg, gu, scs, w_gate, w_up, experts):
@@ -595,8 +627,8 @@
         (gg, gu, *scs, w_gate, w_up),
         [grads, grads] + [sums] * len(scs) + [weight, weight],
         grid=(2, experts),
-        out_specs=[const_spec((cap + TAIL, width))] * experts,
-        out_shape=[jax.ShapeDtypeStruct((cap + TAIL, width), BF)] * experts,
+        out_specs=[const_spec((experts // 2, cap + TAIL, width))] * 2,
+        out_shape=[jax.ShapeDtypeStruct((experts // 2, cap + TAIL, width), BF)] * 2,
         scratch_shapes=[pltpu.VMEM((experts, cap, width), F32)],
         cost_estimate=estimate("expert_input_grad"),
         name="expert_input_grad",
@@ -717,16 +749,16 @@
 
 
 def moe_bwd_kernel(
-    cot_ref, mid_ref, gain_ref, nm_ref, ch_ref, wr_ref, code_ref, codet_ref, wo_ref, att_ref, *refs
+    cot_ref, mid_ref, gain_ref, nm_ref, ch_ref, wr_ref, code_ref, codet_ref, wo_ref, *refs, slots
 ):
-    backs, (gmid_ref, branch_ref, ga_ref, keep_ref, send_ref, gain_o_ref, router_o_ref) = refs[:-7], refs[-7:]
-    experts, cap = len(backs), backs[0].shape[0] - TAIL
+    backs, (gmid_ref, branch_ref, ga_ref, gain_o_ref, router_o_ref) = refs[:-5], refs[-5:]
+    experts, cap = len(slots), backs[0].shape[1] - TAIL
     rows = cot_ref.shape[0]
     grad = jnp.zeros(mid_ref.shape, F32)
     gate_rows = []
-    for m, back in enumerate(backs):
-        grad = grad + dot(selector_t(codet_ref[:, m : m + 1], cap), back[0:cap, :])
-        picked = dot(back[cap : cap + TAIL, 0:cap], selector(code_ref[m : m + 1, :], cap))
+    for m, (which, index) in enumerate(slots):
+        grad = grad + dot(selector_t(codet_ref[:, m : m + 1], cap), backs[which][index, 0:cap, :])
+        picked = dot(backs[which][index, cap : cap + TAIL, 0:cap], selector(code_ref[m : m + 1, :], cap))
         gate_rows.append(jnp.sum(picked, axis=0, keepdims=True))
     gate_rows.append(jnp.zeros((TAIL - experts, rows), F32))
     grad_chances = jnp.concatenate(gate_rows, axis=0)
@@ -747,10 +779,6 @@
     branch = grad_mid.astype(BF)
     branch_ref[...] = branch
     ga_ref[...] = dot_nt(branch, wo_ref[...]).astype(BF)
-    term = dot(att_ref[...], branch).astype(BF)
-    half = term.shape[0] // 2
-    keep_ref[0] = term[:half]
-    send_ref[0] = term[half:]
 
 
 def sort_rows(place_ref, value, out_ref):
@@ -760,21 +788,19 @@
         out_ref[pl.ds(pl.multiple_of(place_ref[b] * rows, rows), rows), :] = value[b * rows : (b + 1) * rows]
 
 
-def moe_bwd(cot, middle, gain_moe, normed_moe, chances, wr_t, code, code_t, w_out, att_t, backs):
+def moe_bwd(cot, middle, gain_moe, normed_moe, chances, wr_t, code, code_t, w_out, slots):
     rows, width = cot.shape
-    args = (cot, middle, gain_moe[None], normed_moe, chances, wr_t, code, code_t, w_out, att_t, *backs)
+    arrays, found = distinct(slots)
+    args = (cot, middle, gain_moe[None], normed_moe, chances, wr_t, code, code_t, w_out, *arrays)
     wide = jax.ShapeDtypeStruct((rows, width), BF)
-    half = jax.ShapeDtypeStruct((1, width // 2, width), BF)
     return call(
-        moe_bwd_kernel,
+        functools.partial(moe_bwd_kernel, slots=found),
         args,
         [pl.BlockSpec(memory_space=pltpu.VMEM)] * len(args),
         out_shape=[
             jax.ShapeDtypeStruct((rows, width), F32),
             wide,
             wide,
-            half,
-            half,
             jax.ShapeDtypeStruct((1, width), F32),
             jax.ShapeDtypeStruct((TAIL, width), F32),
         ],
@@ -892,25 +918,26 @@
     )
 
 
-def dense_terms_kernel(rows_ref, dq_ref, dk_ref, dv_ref, keep_ref, send_ref):
+def dense_terms_kernel(att_ref, rows_ref, branch_ref, dq_ref, dk_ref, dv_ref, keep_ref, send_ref):
     half = keep_ref.shape[1]
-    for i, d_ref in enumerate((dq_ref, dk_ref, dv_ref)):
-        term = dot(rows_ref[min(i, 1)], d_ref[...]).astype(BF)
+    for i, d_ref in enumerate((branch_ref, dq_ref, dk_ref, dv_ref)):
+        lhs = att_ref[...] if i == 0 else rows_ref[min(i - 1, 1)]
+        term = dot(lhs, d_ref[...]).astype(BF)
         keep_ref[i] = term[:half]
         send_ref[i] = term[half:]
 
 
-def dense_terms(lhs, dq, dk, dv):
+def dense_terms(att_t, lhs, branch, dq, dk, dv):
     _, width, rows = lhs.shape
     cols = 256
     col_block = pl.BlockSpec((rows, cols), lambda g: (0, g))
     return call(
         dense_terms_kernel,
-        (lhs, dq, dk, dv),
-        [const_spec(lhs.shape)] + [col_block] * 3,
+        (att_t, lhs, branch, dq, dk, dv),
+        [const_spec(att_t.shape), const_spec(lhs.shape)] + [col_block] * 4,
         grid=(width // cols,),
-        out_specs=[pl.BlockSpec((3, width // 2, cols), lambda g: (0, 0, g))] * 2,
-        out_shape=[jax.ShapeDtypeStruct((3, width // 2, width), BF)] * 2,
+        out_specs=[pl.BlockSpec((4, width // 2, cols), lambda g: (0, 0, g))] * 2,
+        out_shape=[jax.ShapeDtypeStruct((4, width // 2, width), BF)] * 2,
         cost_estimate=estimate("dense_terms"),
         name="dense_terms",
     )
@@ -1002,39 +1029,57 @@
             self.got = swap(value, axis, size, 1 << bit)
 
 
-def fold_kernel(*refs, cuts):
-    pairs, outs = refs[: 2 * len(cuts)], list(refs[2 * len(cuts) :])
-    for i, (dim, last) in enumerate(cuts):
-        keep, got = pairs[2 * i][...].astype(F32), pairs[2 * i + 1][...].astype(F32)
-        total = keep + got
+def arrive(*units):
+    for unit in units:
+        unit.got = unit.order.leave(unit.got)
+
+
+def fold_kernel(*refs, cuts, inputs):
+    pairs, outs = refs[:inputs], list(refs[inputs:])
+    at = 0
+    for dim, last, width in cuts:
+        total = []
+        for _ in range(width):
+            total.append(pairs[at][...].astype(F32) + pairs[at + 1][...].astype(F32))
+            at += 2
         if last:
-            outs.pop(0)[...] = total
+            outs.pop(0)[...] = total[0]
             continue
-        rows = total.shape[dim] // 2
+        rows = total[0].shape[dim] // 2
         for start in (0, rows):
-            outs.pop(0)[...] = lax.slice_in_dim(total, start, start + rows, axis=dim).astype(BF)
+            out = outs.pop(0)
+            cut = [lax.slice_in_dim(v, start, start + rows, axis=dim).astype(BF) for v in total]
+            if width == 1:
+                out[...] = cut[0]
+            else:
+                for i in range(width):
+                    out[i] = cut[i]
 
 
 def fold(*units, hold=()):
-    order = units[0].order
+    groups = [unit if isinstance(unit, tuple) else (unit,) for unit in units]
+    order = groups[0][0].order
     args, cuts, shapes = [], [], []
-    for unit in units:
-        unit.route.pop(0)
-        got = order.leave(unit.got)
-        args += [unit.keep, got]
-        whole = unit.to_send is None
-        last = whole or not unit.route
-        cuts.append((unit.dim, last))
+    for group in groups:
+        for unit in group:
+            unit.route.pop(0)
+            got = order.leave(unit.got)
+            args += [unit.keep, got]
+        unit = group[0]
+        last = unit.to_send is None or not unit.route
+        cuts.append((unit.dim, last, len(group)))
         if last:
             shapes.append(jax.ShapeDtypeStruct(got.shape, F32))
         else:
             shape = list(got.shape)
             shape[unit.dim] //= 2
+            if len(group) > 1:
+                shape = [len(group)] + shape
             shapes += [jax.ShapeDtypeStruct(tuple(shape), BF)] * 2
     args = order.enter(args)
     outs = list(
         call(
-            functools.partial(fold_kernel, cuts=cuts),
+            functools.partial(fold_kernel, cuts=cuts, inputs=len(args)),
             args,
             [pl.BlockSpec(memory_space=pltpu.VMEM)] * len(args),
             out_shape=shapes,
@@ -1043,32 +1088,38 @@
         )
     )
     outs = order.leave(outs)
-    for unit, (_, last) in zip(units, cuts):
+    for group, (_, last, width) in zip(groups, cuts):
+        unit = group[0]
         unit.keep = outs.pop(0)
         if not last:
             unit.to_send = outs.pop(0)
+        if width > 1:
+            unit.dim += 1
         if unit.route and unit not in hold:
             unit.start()
 
 
-def fold_first_kernel(*refs, groups):
-    pairs, outs = refs[: -2 * len(groups)], refs[-2 * len(groups) :]
-    for i, members in enumerate(groups):
-        for at, (array, index) in enumerate(members):
-            total = pairs[2 * array][index].astype(F32) + pairs[2 * array + 1][index].astype(F32)
-            rows = total.shape[0] // 2
-            outs[2 * i][at] = total[:rows].astype(BF)
-            outs[2 * i + 1][at] = total[rows:].astype(BF)
-
-
-def fold_first(pairs, groups):
-    args = [v for pair in pairs for v in pair]
-    _, rows, width = args[0].shape
-    shapes = [jax.ShapeDtypeStruct((len(members), rows // 2, width), BF) for members in groups for _ in range(2)]
+def fold_first_kernel(keep_ref, got_ref, small_keep_ref, small_got_ref, *outs):
+    width = keep_ref.shape[2]
+    small = (small_keep_ref[...] + small_got_ref[...]).astype(F32)
+    for i in range(keep_ref.shape[0]):
+        total = keep_ref[i].astype(F32) + got_ref[i].astype(F32)
+        rows = total.shape[0] // 2
+        for j in range(2):
+            out = outs[i // 2 * 2 + j]
+            out[i % 2, :, 0:width] = total[j * rows : (j + 1) * rows].astype(BF)
+            if i < 2:
+                extra = small[j * rows : (j + 1) * rows] if i == 0 else jnp.zeros((rows, LANES), F32)
+                out[i, :, width:] = extra.astype(BF)
+
+
+def fold_first(keep, got, small_keep, small_got):
+    _, rows, width = keep.shape
+    shapes = [jax.ShapeDtypeStruct((2, rows // 2, width + extra), BF) for extra in (LANES, LANES, 0, 0)]
     return call(
-        functools.partial(fold_first_kernel, groups=groups),
-        args,
-        [pl.BlockSpec(memory_space=pltpu.VMEM)] * len(args),
+        fold_first_kernel,
+        (keep, got, small_keep, small_got),
+        [pl.BlockSpec(memory_space=pltpu.VMEM)] * 4,
         out_shape=shapes,
         cost_estimate=estimate("fold_first"),
         name="fold_first",
@@ -1076,19 +1127,26 @@
 
 
 class Return:
-    def __init__(self, order, low, high, axis, size, name):
+    def __init__(self, order, low, high, axis, size, name, pieces=False):
         self.order, self.axis, self.size, self.name = order, axis, size, name
         half = low.shape[0]
         self.slots = [(low, i) for i in range(half)] + [(high, i) for i in range(half)]
         self.bit = bits_of(size) - 1
-        self.start(high)
+        if pieces:
+            self.start_pieces()
+        else:
+            with jax.named_scope(f"{self.name}{1 << self.bit}"):
+                self.got = swap(self.order.enter(high), self.axis, self.size, 1 << self.bit)
 
     def moving(self):
         return [m for m in range(self.size) if (m >> self.bit) & 1]
 
-    def start(self, value):
-        with jax.named_scope(f"{self.name}{1 << self.bit}"):
-            self.got = swap(self.order.enter(value), self.axis, self.size, 1 << self.bit)
+    def start_pieces(self):
+        self.got = []
+        for m in self.moving():
+            array, index = self.slots[m]
+            with jax.named_scope(f"{self.name}{1 << self.bit}_{m}"):
+                self.got.append(swap(self.order.enter(array[index][None]), self.axis, self.size, 1 << self.bit))
 
     def fold(self):
         got = self.order.leave(self.got)
@@ -1096,11 +1154,7 @@
             self.slots[m] = (got[i], 0) if isinstance(got, list) else (got, i)
         self.bit -= 1
         if self.bit >= 0:
-            self.pieces = [self.slots[m][0][self.slots[m][1]][None] for m in self.moving()]
-            self.got = []
-            for i, piece in enumerate(self.pieces):
-                with jax.named_scope(f"{self.name}{1 << self.bit}_{i}"):
-                    self.got.append(swap(self.order.enter(piece), self.axis, self.size, 1 << self.bit))
+            self.start_pieces()
 
     def finish(self):
         while self.bit >= 0:
@@ -1162,23 +1216,19 @@
     me = lax.axis_index("expert")
 
     cots = Gather(None, cotangent, "expert", ep_size, "cot")
-    scaled, keys, values, woff, token, *filled, payload = attn_first(
-        tokens, gain_attn, w_query, w_key, w_value, w_out, rel_bias, segments, gain_moe, w_router
+    scaled, keys, values, woff, token, code, *filled, payload = attn_first(
+        tokens, gain_attn, w_query, w_key, w_value, w_out, rel_bias, segments, gain_moe, w_router, routes
     )
     order = Order(token)
     cots.order = order
-    numbers = jnp.arange(experts, dtype=jnp.int32)
-    named = jnp.any(order.enter(routes)[None, :, :] == numbers[:, None, None], axis=-1)
-    before = jnp.asarray(np.triu(np.ones((rows, rows), np.float32), 1)).astype(BF)
-    slots = jnp.dot(named.astype(BF), before, preferred_element_type=F32).astype(jnp.int32)
-    code = jnp.where(named, slots, -1)
+    me_ref = me.reshape(1).astype(jnp.int32)
 
     dp_bits, ep_bits = bits_of(dp_size), bits_of(ep_size)
     dp_me = lax.axis_index("dp")
     dp_order = list(range(dp_bits))
-    late_x = dp_order[1:] + [0]
+    z_order = [1, 0] + dp_order[2:]
     place_x = places(dp_me, dp_bits, dp_order)
-    place_late = places(dp_me, dp_bits, late_x)
+    place_z = places(dp_me, dp_bits, z_order)
 
     def dp_route(bits):
         return [("dp", dp_size, b) for b in bits]
@@ -1186,7 +1236,7 @@
     dp_part = [ep_bits + b for b in dp_order]
     ep_part = list(range(1, ep_bits))
     q_bits = [0] + ep_part + dp_part
-    k_bits = [0] + dp_part + ep_part
+    k_bits = [0] + dp_part[:2] + ep_part + dp_part[2:]
     whole_me = dp_me * ep_size + me
 
     def route(bits):
@@ -1194,35 +1244,31 @@
 
     place_q, place_k = [places(whole_me, dp_bits + ep_bits, bits) for bits in (q_bits, k_bits)]
 
-    codes = Gather(order, order.enter(code), "expert", ep_size, "code")
     cots.relay()
-    codes.relay()
     first_half = Gather(order, order.enter(payload), "expert", ep_size, "rows_a")
     attended, lse, middle, normed_moe, chances, payload = order.leave(
         attn_second(tokens, order.enter(scaled), keys, values, w_out, woff, segments, gain_moe, w_router, filled)
     )
     second_half = Gather(order, order.enter(payload), "expert", ep_size, "rows_b")
     first_half.relay()
-    cots, codes = cots.finish(), codes.finish()
-    code_here = jnp.stack([pick(v, me, 0) for v in codes])
+    cots, heads_rows = cots.finish(), first_half.finish()
     blocks = ff // FF_BLOCK
-    counts = [blocks // 2, blocks - blocks // 2]
+    counts = [blocks - blocks // 2, blocks // 2]
     starts = [sum(counts[:i]) for i in range(len(counts))]
-    gh_first, cot_rows = order.leave(cot_hidden(order.enter(code_here), cots, w_down, cap, starts[1]))
+    gh_first, cot_rows = order.leave(cot_hidden(order.enter(me_ref), heads_rows, cots, w_down, cap, starts[1]))
     second_half.relay()
-    payloads = [v for pair in zip(first_half.finish(), second_half.finish()) for v in pair]
-    me_ref = me.reshape(1).astype(jnp.int32)
+    payloads = [v for pair in zip(heads_rows, second_half.finish()) for v in pair]
     scs, units = [], []
 
     def expert_part(i, source, filled=()):
-        *shared, keep, send, sc, hid, hid_t, gg, gu = order.leave(
+        *shared, gate_keep, gate_send, up_keep, up_send, sc, hid, hid_t, gg, gu = order.leave(
             expert_a(
-                order.enter(source), gh_second if i else gh_first, starts[i], w_gate, w_up,
-                starts[i], counts[i], 0 if i else dp_size, filled,
+                order.enter(source), gh_second if i else gh_first, starts[i], w_gate, w_up, starts[i], counts[i], filled
             )
         )
         scs.append(sc)
-        units.append(Halving(order, keep, send, 1, dp_route(dp_order if i else late_x), f"gate_up{i}"))
+        gate = Halving(order, gate_keep, gate_send, 0, dp_route(z_order), f"gate{i}")
+        units.append((gate, Halving(order, up_keep, up_send, 0, dp_route(dp_order), f"up{i}")))
         return shared, (hid, hid_t, gg, gu)
 
     def by_xor(value):
@@ -1231,42 +1277,44 @@
     def padded(value):
         return jnp.pad(value, ((0, TAIL - experts), (0, 0)))
 
-    (x_all, x_t, gate_all, grad_cots), filled = expert_part(0, (me_ref, place_x, code_here, payloads, cot_rows))
-    units[0].start()
+    (x_all, x_t, gate_all, grad_cots), filled = expert_part(0, (me_ref, place_x, payloads, cot_rows))
+    for unit in units[0]:
+        unit.start()
     gh_second = order.leave(cot_hidden_more(order.enter(cot_rows), w_down, starts[1]))
     _, (hid, hid_t, gg, gu) = expert_part(1, (x_all, x_t, gate_all), filled)
-    units[1].start()
-    backs = list(order.leave(expert_b(order.enter(gg), gu, scs, w_gate, w_up, experts)))
-    for m in reversed(range(1, experts)):
-        with jax.named_scope(f"grad_rows{m}"):
-            backs[m] = swap(order.enter(backs[m]), "expert", ep_size, m)
+    fold(*units[0])
+    for unit in units[1]:
+        unit.start()
+    back_low, back_high = order.leave(expert_b(order.enter(gg), gu, scs, w_gate, w_up, experts))
+    backs = Return(order, back_low, back_high, "expert", ep_size, "grad_rows")
+    first, second = units[0][0], units[1][0]
     fold(units[0])
-    down_parts = order.leave(down_grads(order.enter(hid_t), grad_cots, place_x, place_late))
-    down_units = [
+    down_parts = order.leave(down_grads(order.enter(hid_t), grad_cots, place_z, place_x))
+    down_units = tuple(
         Halving(order, down_parts[2 * i], down_parts[2 * i + 1], 0, dp_route(bits), f"down{i}")
-        for i, bits in enumerate((dp_order, late_x))
-    ]
+        for i, bits in enumerate((z_order, dp_order))
+    )
+    down = down_units[0]
+    fold(*units[1])
     code_xor, chances_xor, wr_xor = order.enter((by_xor(code), padded(by_xor(chances)), padded(by_xor(w_router.T))))
+    backs.fold()
     att_t, normed_t = order.leave(sorted_rows(place_q, place_k, order.enter(tokens), gain_attn, attended))
-    backs = order.leave(backs)
-    down_units[0].start()
-    down_units[1].start()
-    grad_mid, branch, grad_att, out_keep, out_send, gain_moe_term, router_term = order.leave(
+    backs.finish()
+    for unit in down_units:
+        unit.start()
+    grad_mid, branch, grad_att, gain_moe_term, router_term = order.leave(
         moe_bwd(
-            cotangent, order.enter(middle), gain_moe, normed_moe, chances_xor, wr_xor, code_xor, code_xor.T, w_out, att_t,
-            backs,
+            cotangent, order.enter(middle), gain_moe, normed_moe, chances_xor, wr_xor, code_xor, code_xor.T, w_out,
+            backs.slots,
         )
     )
-    out_unit = Halving(order, out_keep, out_send, 1, route(q_bits)[:1], "out")
-    out_unit.start()
-    fold(units[1])
     dq, dk, dv, dwoff = order.leave(attn_bwd(scaled, keys, values, order.enter(grad_att), lse, woff, segments))
-    out_got = order.leave(out_unit.got)
-    fold(units[0])
-    qkv_keep, qkv_send = order.leave(dense_terms(normed_t, order.enter(dq), dk, dv))
-    fold(*down_units)
-    core = Halving(order, qkv_keep, qkv_send, 1, route(q_bits)[:1], "qkv")
+    arrive(first, *units[1])
+    dense_keep, dense_send = order.leave(dense_terms(att_t, normed_t, branch, order.enter(dq), dk, dv))
+    arrive(*units[1], *down_units)
+    core = Halving(order, dense_keep, dense_send, 1, route(q_bits)[:1], "dense")
     core.start()
+    fold(*down_units, first, units[1], hold=units[1])
     token_grad, gain_attn_term = order.leave(
         norm_bwd(tokens, gain_attn, grad_mid, order.enter(dq), dk, dv, w_query, w_key, w_value)
     )
@@ -1283,40 +1331,43 @@
         ],
         axis=1,
     )
-    small = Halving(order, small, None, 0, route(q_bits), "small")
-    small.start()
+    count = small.shape[1]
+    lines = -(-count // LANES)
+    at_place = (place_q[None, :] == jnp.arange(devices, dtype=jnp.int32)[:, None]).astype(F32)
+    small = jnp.dot(at_place, jnp.pad(small, ((0, 0), (0, lines * LANES - count))), precision=HIGHEST)
+    small = small.reshape(devices, lines, LANES).astype(BF)
+    small = jnp.pad(small, ((0, 0), (0, share - lines), (0, 0))).reshape(2, width // 2, LANES)
+    small_keep, small_send = order.enter((small[0], small[1]))
+    with jax.named_scope("small_expert1"):
+        small_got = swap(small_send, "expert", ep_size, 1)
     core_got = order.leave(core.got)
-    halves = order.leave(
-        fold_first([order.enter((out_keep, out_got)), (qkv_keep, core_got)], [[(0, 0), (1, 0)], [(1, 1), (1, 2)]])
-    )
+    halves = order.leave(fold_first(order.enter(dense_keep), core_got, small_keep, order.leave(small_got)))
     dense = [
         Halving(order, halves[2 * i], halves[2 * i + 1], 1, route(bits)[1:], name)
         for i, (bits, name) in enumerate(((q_bits, "out_q"), (k_bits, "k_v")))
     ]
     out_q, k_v = dense
+    arrive(*down_units)
     k_v.start()
     out_q.start()
-    fold(small, *units)
+    second.start()
     prod_low, prod_high = order.leave(produced_rows(order.enter(hid), w_down, experts))
-    fold(small, down_units[1], k_v)
     returned = Return(order, prod_low, prod_high, "expert", ep_size, "produced_rows")
-    fold(small, down_units[0], out_q)
-    fold(small, units[1], k_v)
-    fold(small, down_units[1], out_q)
-    fold(k_v)
+    fold(k_v, out_q, down_units)
+    fold(k_v, out_q, second)
     returned.fold()
-    fold(down_units[0], out_q)
     returned.finish()
     layer_out = order.leave(layer_output(middle, chances_xor, code_xor.T, returned.slots))
-    rest = units + down_units + dense + [small]
+    fold(k_v, out_q, down)
+    rest = [first, second, down, *dense]
     while any(unit.route for unit in rest):
         fold(*[unit for unit in rest if unit.route])
-    small_sum = pick(small.keep, whole_me, 0) + order.token[0, :1]
-
-    terms = [unit.keep for unit in units]
+    small_sum = out_q.keep[0, 0:lines, width:].reshape(-1)[:count] + order.token[0, :1]
+
+    terms = [first.keep, second.keep]
     gate_grad = jnp.concatenate([term[0] for term in terms], axis=1)[None]
     up_grad = jnp.concatenate([term[1] for term in terms], axis=1)[None]
-    down_grad = jnp.concatenate([unit.keep for unit in down_units], axis=1)[None]
+    down_grad = jnp.concatenate([down.keep[0], down.keep[1]], axis=1)[None]
     n_router = width * experts // devices
     n_gain = width // devices
     router_grad = small_sum[:n_router].reshape(share, experts)
@@ -1326,10 +1377,10 @@
     return (
         layer_out,
         token_grad,
-        dense[0].keep[1],
-        dense[1].keep[0],
-        dense[1].keep[1],
-        dense[0].keep[0],
+        out_q.keep[1, :, :width],
+        k_v.keep[0],
+        k_v.keep[1],
+        out_q.keep[0, :, :width],
         gain_attn_grad,
         gain_moe_grad,
         bias_grad,

time: 439 us -> 420 us (0.957)
  waiting for transfers between devices: 92 us -> 75 us
  Pallas kernels: 262 us -> 256 us
    ppermute x45 -> x40, waiting for transfers between devices: 92 us -> 75 us  [swap(): return lax.ppermute(value, axis, [(i, i ^ mask) for i in range(size)])]
    pallas_call x28 -> x24, Pallas kernels: 262 us -> 256 us  [call(): pl.pallas_call(kernel, in_specs=list(in_specs), compiler_params=params(),...]
    ppermute x45 -> x40, starting transfers between devices: 34.1 us -> 37.7 us  [swap(): return lax.ppermute(value, axis, [(i, i ^ mask) for i in range(size)])]
    unnamed x99 -> x98, local copies, waits for them, and re-layouts: 18.7 us -> 21.1 us
  transfers between devices with their start and end apart: 45 -> 40, of which waited for: 13 -> 14; matrix products, arithmetic and copies ran while one was open for 5% -> 5% of each run, Pallas kernels for 53% -> 52%
where the time goes in v3:
time: 420 us; the launch traced here: 414 us
  Pallas kernels  256 us (61%)
  waiting for transfers between devices  75 us (18%)
  starting transfers between devices  37.7 us (9%)
  local copies, waits for them, and re-layouts  34.9 us (8%)
  other arithmetic  8.09 us (2%)
    pallas_call x24, Pallas kernels, call(): pl.pallas_call(kernel, in_specs=list(in_specs), compiler_params=params(),...  256 us
    ppermute x40, waiting for transfers between devices, swap(): return lax.ppermute(value, axis, [(i, i ^ mask) for i in range(size)])  75 us
    ppermute x40, starting transfers between devices, swap(): return lax.ppermute(value, axis, [(i, i ^ mask) for i in range(size)])  37.7 us
    unnamed x98, local copies, waits for them, and re-layouts  21.1 us
  transfers between devices with their start and end apart: 40, of which 14 were waited for; matrix products, arithmetic and copies ran while one was open for 5% of the time, Pallas kernels for 52%

profile of v3, /device:TPU:0, one launch (start us, length us, event | category | flops | bytes accessed | tf_op | source)
XLA Modules:
  0.0 413.5 jit_solution(8348368262115822509)
XLA Ops:
  0.6 3.0 collective-permute-start
  8.2 15.8 %attn_first.1 = (bf16[512,1024]{1,0:T(8,128)(2,1)}, bf16[512,1024]{1,0:T(8,128)(2,1)}, bf16[512,1024]{1,0:T(8,128)(2,1)}, f32[4,4,512]{2,1,0:T(4,128)}, f32[1,12...) custom-call(bf16[512,1024]{1,0:T(8,128)(2,1)} %tok_ref.6, ...), custom_call_target="tpu_custom_call" | custom-call | flops 115000000 | bytes 100000 | tf_op jit(solution)/shard_map/attn_first/pallas_call | solution.py:100
  24.0 3.2 collective-permute-done.refs_6_
  29.4 12.4 %attn_second.1 = (bf16[512,1024]{1,0:T(8,128)(2,1)}, f32[4,4,512]{2,1,0:T(4,128)}, f32[512,1024]{1,0:T(8,128)}, bf16[512,1024]{1,0:T(8,128)(2,1)}, f32[16,512]{1,0:T(8,128)}, /*index=5*/bf16[272,1024]{1,0:T(8,128)(2,1)}) custom-call(bf16[512,1024]{1,0:T(8,128)(2,1)} %tok_ref.6, ...), custom_call_target="tpu_custom_call", output_to_operand_aliasing={{0}: (9, {}), {1}: (10, {}), {2}: (11, {}), {3}: (12, {}), ... | custom-call | flops 115000000 | bytes 100000 | tf_op jit(solution)/shard_map/attn_second/pallas_call | solution.py:100
  44.7 11.2 %cot_hidden.1 = (bf16[1280,1536]{1,0:T(8,128)(2,1)}, bf16[1280,1024]{1,0:T(8,128)(2,1)}) custom-call(s32[1]{0:T(128)} %bitcast.6.me_ref.refs_0_, bf16[272,1024]{1,0:T(8,128)(2,1)} %get-tuple-element.555.refs_0_.refs_2_, bf16[272,1024]{1,0:T(8,128)(2,1)} %copy-done.5, bf16[272,1024]{1,0:T(8,128)(2,1)} %copy-done.4, bf16[272,1024]{1,0:T(8,128)(2,1)} %copy-done.6, ...), custom_call_target="tpu_custom_call" | custom-call | flops 115000000 | bytes 100000 | tf_op jit(solution)/shard_map/cot_hidden/pallas_call | solution.py:100
  60.0 32.8 %expert_grads.2 = (bf16[1280,1024]{1,0:T(8,128)(2,1)}, bf16[1024,1280]{1,0:T(8,128)(2,1)}, f32[1280,128]{1,0:T(8,128)}, bf16[1280,1024]{1,0:T(8,128)(2,1)}, bf16...) custom-call(s32[1]{0:T(128)} %bitcast.6.me_ref.refs_0_, ...), custom_call_target="tpu_custom_call" | custom-call | flops 115000000 | bytes 100000 | tf_op jit(solution)/shard_map/expert_grads/pallas_call | solution.py:100
  95.9 8.0 %cot_hidden_more.1.refs_3_ = bf16[1280,1280]{1,0:T(8,128)(2,1)} custom-call(bf16[1280,1024]{1,0:T(8,128)(2,1)} %get-tuple-element.587.refs_10_.rows_ref, bf16[1,2816,1024]{2,1,0:T(8,128)(2,1)} %wd_ref.3), custom_call_target="tpu_custom_call" | custom-call | flops 115000000 | bytes 100000 | tf_op jit(solution)/shard_map/cot_hidden_more/pallas_call | solution.py:100
  104.0 25.3 %expert_grads.3 = (bf16[512,1280]{1,0:T(8,128)(2,1)}, bf16[512,1280]{1,0:T(8,128)(2,1)}, bf16[512,1280]{1,0:T(8,128)(2,1)}, bf16[512,1280]{1,0:T(8,128)(2,1)}, f...) custom-call(bf16[1280,1024]{1,0:T(8,128)(2,1)} %get-tuple-element.59, ...), custom_call_target="tpu_custom_call", output_to_operand_aliasing={{5}: (6, {}), {6}: (7, {}), {7}: (8, {}), {8}: (9, {})} | custom-call | flops 115000000 | bytes 100000 | tf_op jit(solution)/shard_map/expert_grads/pallas_call | solution.py:100
  132.0 4.7 %fold.8 = (bf16[256,1536]{1,0:T(8,128)(2,1)}, bf16[256,1536]{1,0:T(8,128)(2,1)}, bf16[256,1536]{1,0:T(8,128)(2,1)}, bf16[256,1536]{1,0:T(8,128)(2,1)}) custom-call(bf16[512,1536]{1,0:T(8,128)(2,1)} %get-tuple-element.619.refs_0_, bf16[512,1536]{1,0:T(8,128)(2,1)} %copy-done.8, bf16[512,1536]{1,0:T(8,128)(2,1)} %get-tuple-element.621.refs_2_, ...), custom_call_target="tpu_custom_call" | custom-call | flops 115000000 | bytes 100000 | tf_op jit(solution)/shard_map/fold/pallas_call | solution.py:100
  142.3 25.5 %expert_input_grad.1 = (bf16[2,336,1024]{2,1,0:T(8,128)(2,1)}, bf16[2,336,1024]{2,1,0:T(8,128)(2,1)}) custom-call(bf16[1280,2816]{1,0:T(8,128)(2,1)} %get-tuple-element.641.gg_ref, bf16[1280,2816]{1,0:T(8,128)(2,1)} %get-tuple-element.642.gu_ref, f32[1280,128]{1,0:T(8,128)} %get-tuple-element.643.refs_0_, f32[1280,128]{1,0:T(8,128)} %get-tuple-element.644.refs_1_, ...), custom_call_target="tpu_custom_call" | custom-call | flops 115000000 | bytes 100000 | tf_op jit(solution)/shard_map/expert_input_grad/pallas_call | solution.py:100
  172.9 3.2 fold.9
  176.0 16.8 %down_grads.1 = (bf16[1408,512]{1,0:T(8,128)(2,1)}, bf16[1408,512]{1,0:T(8,128)(2,1)}, bf16[1408,512]{1,0:T(8,128)(2,1)}, bf16[1408,512]{1,0:T(8,128)(2,1)}) custom-call(s32[8]{0:T(128)} %get-tuple-element.1043.place_a_ref, s32[8]{0:T(128)} %get-tuple-element.554.refs_1_.place_b_ref, bf16[2816,1280]{1,0:T(8,128)(2,1)} %get-tuple-element.667.hidt_ref, ...), custom_call_target="tpu_custom_call" | custom-call | flops 11500000256 | bytes 100000 | tf_op jit(solution)/shard_map/down_grads/pallas_call | solution.py:100
  197.5 4.2 %fold.10 = (bf16[256,1280]{1,0:T(8,128)(2,1)}, bf16[256,1280]{1,0:T(8,128)(2,1)}, bf16[256,1280]{1,0:T(8,128)(2,1)}, bf16[256,1280]{1,0:T(8,128)(2,1)}) custom-call(bf16[512,1280]{1,0:T(8,128)(2,1)} %get-tuple-element.681.refs_0_, bf16[512,1280]{1,0:T(8,128)(2,1)} %copy-done.43, bf16[512,1280]{1,0:T(8,128)(2,1)} %get-tuple-element.683.refs_2_, ...), custom_call_target="tpu_custom_call" | custom-call | flops 2300000000 | bytes 100000 | tf_op jit(solution)/shard_map/fold/pallas_call | solution.py:100
  205.8 4.7 %sorted_rows.1 = (bf16[1024,512]{1,0:T(8,128)(2,1)}, bf16[2,1024,512]{2,1,0:T(8,128)(2,1)}) custom-call(s32[32]{0:T(128)} %get-tuple-element.1042.pq_ref, s32[32]{0:T(128)} %get-tuple-element.1041.pk_ref, bf16[512,1024]{1,0:T(8,128)(2,1)} %tok_ref.6, f32[1,1024]{1,0:T(1,128)} %bitcast.56, bf16[512,1024]{1,0:T(8,128)(2,1)} %get-tuple-element.710.att_ref), custom_call_target="tpu_custom_call" | custom-call | flops 115000000 | bytes 100000 | tf_op jit(solution)/shard_map/sorted_rows/pallas_call | solution.py:100
  214.2 10.2 %moe_bwd.1 = (f32[512,1024]{1,0:T(8,128)}, bf16[512,1024]{1,0:T(8,128)(2,1)}, bf16[512,1024]{1,0:T(8,128)(2,1)}, f32[1,1024]{1,0:T(1,128)}, f32[16,1024]{1,0:T(8,128)}) custom-call(bf16[512,1024]{1,0:T(8,128)(2,1)} %cot_ref.1, f32[512,1024]{1,0:T(8,128)} %get-tuple-element.723.mid_ref, f32[1,1024]{1,0:T(1,128)} %bitcast.54, ...), custom_call_target="tpu_custom_call" | custom-call | flops 115000000 | bytes 100000 | tf_op jit(solution)/shard_map/moe_bwd/pallas_call | solution.py:100
  224.5 16.3 %attn_bwd.1 = (bf16[512,1024]{1,0:T(8,128)(2,1)}, bf16[512,1024]{1,0:T(8,128)(2,1)}, bf16[512,1024]{1,0:T(8,128)(2,1)}, f32[4,4,512]{2,1,0:T(4,128)}) custom-call(bf16[512,1024]{1,0:T(8,128)(2,1)} %get-tuple-element.503.qs_ref, bf16[512,1024]{1,0:T(8,128)(2,1)} %get-tuple-element.504.k_ref, bf16[512,1024]{1,0:T(8,128)(2,1)} %get-tuple-element.505.v_ref, ...), custom_call_target="tpu_custom_call" | custom-call | flops 115000000 | bytes 100000 | tf_op jit(solution)/shard_map/attn_bwd/pallas_call | solution.py:100
  240.8 9.3 %dense_terms.1 = (bf16[4,512,1024]{2,1,0:T(8,128)(2,1)}, bf16[4,512,1024]{2,1,0:T(8,128)(2,1)}) custom-call(bf16[1024,512]{1,0:T(8,128)(2,1)} %get-tuple-element.748.att_ref, bf16[2,1024,512]{2,1,0:T(8,128)(2,1)} %get-tuple-element.749.rows_ref, bf16[512,1024]{1,0:T(8,128)(2,1)} %get-tuple-element.750.branch_ref, ...), custom_call_target="tpu_custom_call" | custom-call | flops 15064999936 | bytes 100000 | tf_op jit(solution)/shard_map/dense_terms/pallas_call | solution.py:100
  250.1 17.2 %collective-permute-done.18.refs_1_ = bf16[1408,512]{1,0:T(8,128)(2,1)S(1)} collective-permute-done((bf16[1408,512]{1,0:T(8,128)(2,1)}, bf16[1408,512]{1,0:T(8,128)(2,1)S(1)}, u32[]{:S(2)}, u32[]{:S(2)}) %collective-permute-start.18) | collective-permute-done | bytes 1441824 | tf_op jit(solution)/shard_map/down0_dp2/ppermute | solution.py:994
  270.1 6.5 %fold.11 = (bf16[704,512]{1,0:T(8,128)(2,1)}, bf16[704,512]{1,0:T(8,128)(2,1)}, bf16[704,512]{1,0:T(8,128)(2,1)}, bf16[704,512]{1,0:T(8,128)(2,1)}, f32[2,128,15...) custom-call(bf16[1408,512]{1,0:T(8,128)(2,1)} %get-tuple-element.786.refs_0_, ...), custom_call_target="tpu_custom_call" | custom-call | flops 115000000 | bytes 100000 | tf_op jit(solution)/shard_map/fold/pallas_call | solution.py:100
  277.3 10.7 %norm_bwd.1 = (f32[512,1024]{1,0:T(8,128)}, f32[1,1024]{1,0:T(1,128)}) custom-call(bf16[512,1024]{1,0:T(8,128)(2,1)} %tok_ref.6, f32[1,1024]{1,0:T(1,128)} %bitcast.57, f32[512,1024]{1,0:T(8,128)} %get-tuple-element.808.gmid_ref, bf16[512,1024]{1,0:T(8,128)(2,1)} %get-tuple-element.814.dq_ref, bf16[512,1024]{1,0:T(8,128)(2,1)} %get-tuple-element.754.dk_ref, ...), custom_call_target="tpu_custom_call" | custom-call | flops 115000000 | bytes 100000 | tf_op jit(solution)/shard_map/norm_bwd/pallas_call | solution.py:100
  292.4 5.8 %fold_first.1 = (bf16[2,256,1152]{2,1,0:T(8,128)(2,1)}, bf16[2,256,1152]{2,1,0:T(8,128)(2,1)}, bf16[2,256,1024]{2,1,0:T(8,128)(2,1)}, bf16[2,256,1024]{2,1,0:T(8,128)(2,1)}) custom-call(bf16[4,512,1024]{2,1,0:T(8,128)(2,1)} %get-tuple-element.824.keep_ref, bf16[4,512,1024]{2,1,0:T(8,128)(2,1)} %collective-permute-done.23.got_ref, bf16[512,128]{1,0:T(8,128)(2,1)} %bitcast.50, ...), custom_call_target="tpu_custom_call" | custom-call | flops 115000000 | bytes 100000 | tf_op jit(solution)/shard_map/fold_first/pallas_call | solution.py:100
  301.2 12.9 %produced_rows.1 = (bf16[2,320,1024]{2,1,0:T(8,128)(2,1)}, bf16[2,320,1024]{2,1,0:T(8,128)(2,1)}) custom-call(bf16[1280,2816]{1,0:T(8,128)(2,1)} %get-tuple-element.845.hid_ref, bf16[1,2816,1024]{2,1,0:T(8,128)(2,1)} %wd_ref.3), custom_call_target="tpu_custom_call" | custom-call | flops 115000000 | bytes 100000 | tf_op jit(solution)/shard_map/produced_rows/pallas_call | solution.py:100
  314.9 2.7 collective-permute-start.32
  317.6 7.2 %collective-permute-done.28.refs_1_ = bf16[2,256,1024]{2,1,0:T(8,128)(2,1)S(1)} collective-permute-done((bf16[2,256,1024]{2,1,0:T(8,128)(2,1)}, bf16[2,256,1024]{2,1,0:T(8,128)(2,1)S(1)}, u32[]{:S(2)}, u32[]{:S(2)}) %collective-permute-start.28) | collective-permute-done | bytes 1048608 | tf_op jit(solution)/shard_map/k_v_dp1/ppermute | solution.py:994
  328.4 5.0 %fold.12 = (bf16[2,128,1024]{2,1,0:T(8,128)(2,1)}, bf16[2,128,1024]{2,1,0:T(8,128)(2,1)}, bf16[2,128,1152]{2,1,0:T(8,128)(2,1)}, bf16[2,128,1152]{2,1,0:T(8,128)...) custom-call(bf16[2,256,1024]{2,1,0:T(8,128)(2,1)} %get-tuple-element.870.refs_0_, ...), custom_call_target="tpu_custom_call" | custom-call | flops 115000000 | bytes 100000 | tf_op jit(solution)/shard_map/fold/pallas_call | solution.py:100
  337.9 22.8 %collective-permute-done.30.refs_1_ = bf16[2,128,1024]{2,1,0:T(8,128)(2,1)S(1)} collective-permute-done((bf16[2,128,1024]{2,1,0:T(8,128)(2,1)}, bf16[2,128,1024]{2,1,0:T(8,128)(2,1)S(1)}, u32[]{:S(2)}, u32[]{:S(2)}) %collective-permute-start.30) | collective-permute-done | bytes 524320 | tf_op jit(solution)/shard_map/k_v_dp2/ppermute | solution.py:994
  362.6 3.4 fold.13
  372.2 6.3 %layer_output.1 = bf16[512,1024]{1,0:T(8,128)(2,1)} custom-call(f32[512,1024]{1,0:T(8,128)} %get-tuple-element.723.mid_ref, f32[16,512]{1,0:T(8,128)} %select_maximum_fusion.6.ch_ref, s32[512,4]{1,0:T(8,128)} %bitcast.49, bf16[2,320,1024]{2,1,0:T(8,128)(2,1)} %get-tuple-element.849.refs_0_, bf16[1,320,1024]{2,1,0:T(8,128)(2,1)} %copy-done.24, ...), custom_call_target="tpu_custom_call" | custom-call | flops 115000000 | bytes 100000 | tf_op jit(solution)/shard_map/layer_output/pallas_call | solution.py:100
  378.5 4.9 %collective-permute-done.36.refs_3_ = bf16[2,64,1152]{2,1,0:T(8,128)(2,1)S(1)} collective-permute-done((bf16[2,64,1152]{2,1,0:T(8,128)(2,1)}, bf16[2,64,1152]{2,1,0:T(8,128)(2,1)S(1)}, u32[]{:S(2)}, u32[]{:S(2)}) %collective-permute-start.36) | collective-permute-done | bytes 294944 | tf_op jit(solution)/shard_map/out_q_dp2/ppermute | solution.py:994
  384.9 3.0 fold.14
  393.7 8.0 %collective-permute-done.38.refs_1_ = bf16[2,32,1152]{2,1,0:T(8,128)(2,1)S(1)} collective-permute-done((bf16[2,32,1152]{2,1,0:T(8,128)(2,1)S(1)}, bf16[2,32,1152]{2,1,0:T(8,128)(2,1)S(1)}, u32[]{:S(2)}, u32[]{:S(2)}) %collective-permute-start.38) | collective-permute-done | bytes 147488 | tf_op jit(solution)/shard_map/out_q_dp4/ppermute | solution.py:994
  401.7 2.7 collective-permute-done.39.refs_3_
  (212 shorter events, 86.4 us)
Async XLA Ops:
  0.6 26.5 %collective-permute-start = (bf16[512,1024]{1,0:T(8,128)(2,1)}, bf16[512,1024]{1,0:T(8,128)(2,1)}, u32[]{:S(2)}, u32[]{:S(2)}) collective-permute-start(bf16[512,1024]{1,0:T(8,128)(2,1)} %cot_ref.1), channel_id=1, source_target_pairs={{0,2},{1,3},{2,0},{3,1},{4,6},{5,7},{6,4},{7,5},{8,10},{9,11},{10,... | collective-permute-start | bytes 3145736 | tf_op jit(solution)/shard_map/cot0_2/ppermute | solution.py:994
  27.2 14.6 %collective-permute-start.2 = (bf16[272,1024]{1,0:T(8,128)(2,1)}, bf16[272,1024]{1,0:T(8,128)(2,1)S(1)}, u32[]{:S(2)}, u32[]{:S(2)}) collective-permute-start(bf16[272,1024]{1,0:T(8,128)(2,1)} %get-tuple-element.555.refs_0_.refs_2_), channel_id=1, source_target_pairs={{0,2},{1,3},{2,0},{3,1},{4,6},{5,7},{6,4},{7,5},{8,10},{9,11},{10,... | collective-permute-start | bytes 1671176 | tf_op jit(solution)/shard_map/rows_a0_2/ppermute | solution.py:994
  28.9 13.8 %collective-permute-start.4 = (bf16[512,1024]{1,0:T(8,128)(2,1)S(1)}, bf16[512,1024]{1,0:T(8,128)(2,1)}, u32[]{:S(2)}, u32[]{:S(2)}) collective-permute-start(bf16[512,1024]{1,0:T(8,128)(2,1)S(1)} %copy-done), channel_id=1, source_target_pairs={{0,1},{1,0},{2,3},{3,2},{4,5},{5,4},{6,7},{7,6},{8,9},{9,8},{10,11... | collective-permute-start | bytes 3145736 | tf_op jit(solution)/shard_map/cot0_1/ppermute | solution.py:994
  28.9 13.9 %collective-permute-start.5 = (bf16[512,1024]{1,0:T(8,128)(2,1)}, bf16[512,1024]{1,0:T(8,128)(2,1)}, u32[]{:S(2)}, u32[]{:S(2)}) collective-permute-start(bf16[512,1024]{1,0:T(8,128)(2,1)} %collective-permute-done.refs_6_), channel_id=1, source_target_pairs={{0,1},{1,0},{2,3},{3,2},{4,5},{5,4},{6,7},{7,6},{8,9},{9,8},{10,11... | collective-permute-start | bytes 3145736 | tf_op jit(solution)/shard_map/cot2_1/ppermute | solution.py:994
  29.4 13.4 %collective-permute-start.1 = (bf16[272,1024]{1,0:T(8,128)(2,1)}, bf16[272,1024]{1,0:T(8,128)(2,1)S(1)}, u32[]{:S(2)}, u32[]{:S(2)}) collective-permute-start(bf16[272,1024]{1,0:T(8,128)(2,1)} %get-tuple-element.555.refs_0_.refs_2_), channel_id=1, source_target_pairs={{0,1},{1,0},{2,3},{3,2},{4,5},{5,4},{6,7},{7,6},{8,9},{9,8},{10,11... | collective-permute-start | bytes 1671176 | tf_op jit(solution)/shard_map/rows_a0_1/ppermute | solution.py:994
  42.4 14.8 %collective-permute-start.7 = (bf16[272,1024]{1,0:T(8,128)(2,1)}, bf16[272,1024]{1,0:T(8,128)(2,1)S(1)}, u32[]{:S(2)}, u32[]{:S(2)}) collective-permute-start(bf16[272,1024]{1,0:T(8,128)(2,1)} %get-tuple-element.556.refs_3_), channel_id=1, source_target_pairs={{0,2},{1,3},{2,0},{3,1},{4,6},{5,7},{6,4},{7,5},{8,10},{9,11},{10,... | collective-permute-start | bytes 1671176 | tf_op jit(solution)/shard_map/rows_b0_2/ppermute | solution.py:994
  42.7 15.1 %collective-permute-start.6 = (bf16[272,1024]{1,0:T(8,128)(2,1)}, bf16[272,1024]{1,0:T(8,128)(2,1)S(1)}, u32[]{:S(2)}, u32[]{:S(2)}) collective-permute-start(bf16[272,1024]{1,0:T(8,128)(2,1)} %get-tuple-element.556.refs_3_), channel_id=1, source_target_pairs={{0,1},{1,0},{2,3},{3,2},{4,5},{5,4},{6,7},{7,6},{8,9},{9,8},{10,11... | collective-permute-start | bytes 1671176 | tf_op jit(solution)/shard_map/rows_b0_1/ppermute | solution.py:994
  92.8 36.7 %collective-permute-start.9 = (bf16[512,1536]{1,0:T(8,128)(2,1)}, bf16[512,1536]{1,0:T(8,128)(2,1)S(1)}, u32[]{:S(2)}, u32[]{:S(2)}) collective-permute-start(bf16[512,1536]{1,0:T(8,128)(2,1)} %get-tuple-element.611), channel_id=1, source_target_pairs={{0,8},{4,12},{8,0},{12,4},{16,24},{20,28},{24,16},{28,20},{1,9},{5... | collective-permute-start | bytes 4718600 | tf_op jit(solution)/shard_map/gate0_dp2/ppermute | solution.py:994
  94.4 36.4 %collective-permute-start.10 = (bf16[512,1536]{1,0:T(8,128)(2,1)}, bf16[512,1536]{1,0:T(8,128)(2,1)S(1)}, u32[]{:S(2)}, u32[]{:S(2)}) collective-permute-start(bf16[512,1536]{1,0:T(8,128)(2,1)} %get-tuple-element.615), channel_id=1, source_target_pairs={{0,4},{4,0},{8,12},{12,8},{16,20},{20,16},{24,28},{28,24},{1,5},{5... | collective-permute-start | bytes 4718600 | tf_op jit(solution)/shard_map/up0_dp1/ppermute | solution.py:994
  136.6 34.5 %collective-permute-start.12 = (bf16[256,1536]{1,0:T(8,128)(2,1)}, bf16[256,1536]{1,0:T(8,128)(2,1)S(1)}, u32[]{:S(2)}, u32[]{:S(2)}) collective-permute-start(bf16[256,1536]{1,0:T(8,128)(2,1)} %get-tuple-element.636), channel_id=1, source_target_pairs={{0,4},{4,0},{8,12},{12,8},{16,20},{20,16},{24,28},{28,24},{1,5},{5... | collective-permute-start | bytes 2359304 | tf_op jit(solution)/shard_map/gate0_dp1/ppermute | solution.py:994
  138.1 33.0 %collective-permute-start.13 = (bf16[256,1536]{1,0:T(8,128)(2,1)}, bf16[256,1536]{1,0:T(8,128)(2,1)S(1)}, u32[]{:S(2)}, u32[]{:S(2)}) collective-permute-start(bf16[256,1536]{1,0:T(8,128)(2,1)} %get-tuple-element.653), channel_id=1, source_target_pairs={{0,8},{4,12},{8,0},{12,4},{16,24},{20,28},{24,16},{28,20},{1,9},{5... | collective-permute-start | bytes 2359304 | tf_op jit(solution)/shard_map/up0_dp2/ppermute | solution.py:994
  140.3 55.1 %collective-permute-start.11 = (bf16[512,1280]{1,0:T(8,128)(2,1)}, bf16[512,1280]{1,0:T(8,128)(2,1)S(1)}, u32[]{:S(2)}, u32[]{:S(2)}) collective-permute-start(bf16[512,1280]{1,0:T(8,128)(2,1)} %get-tuple-element.633), channel_id=1, source_target_pairs={{0,8},{4,12},{8,0},{12,4},{16,24},{20,28},{24,16},{28,20},{1,9},{5... | collective-permute-start | bytes 3932168 | tf_op jit(solution)/shard_map/gate1_dp2/ppermute | solution.py:994
  140.9 54.5 %collective-permute-start.14 = (bf16[512,1280]{1,0:T(8,128)(2,1)}, bf16[512,1280]{1,0:T(8,128)(2,1)S(1)}, u32[]{:S(2)}, u32[]{:S(2)}) collective-permute-start(bf16[512,1280]{1,0:T(8,128)(2,1)} %get-tuple-element.677), channel_id=1, source_target_pairs={{0,4},{4,0},{8,12},{12,8},{16,20},{20,16},{24,28},{28,24},{1,5},{5... | collective-permute-start | bytes 3932168 | tf_op jit(solution)/shard_map/up1_dp1/ppermute | solution.py:994
  167.8 33.9 %collective-permute-start.15 = (bf16[2,336,1024]{2,1,0:T(8,128)(2,1)}, bf16[2,336,1024]{2,1,0:T(8,128)(2,1)S(1)}, u32[]{:S(2)}, u32[]{:S(2)}) collective-permute-start(bf16[2,336,1024]{2,1,0:T(8,128)(2,1)} %get-tuple-element.701), channel_id=1, source_target_pairs={{0,2},{1,3},{2,0},{3,1},{4,6},{5,7},{6,4},{7,5},{8,10},{9,11},{10,... | collective-permute-start | bytes 4128776 | tf_op jit(solution)/shard_map/grad_rows2/ppermute | solution.py:994
  192.8 47.9 %collective-permute-start.21 = (bf16[2,128,1536]{2,1,0:T(8,128)(2,1)}, bf16[2,128,1536]{2,1,0:T(8,128)(2,1)}, u32[]{:S(2)}, u32[]{:S(2)}) collective-permute-start(bf16[2,128,1536]{2,1,0:T(8,128)(2,1)} %get-tuple-element.719), channel_id=1, source_target_pairs={{0,16},{4,20},{8,24},{12,28},{16,0},{20,4},{24,8},{28,12},{1,17},{... | collective-permute-start | bytes 2359304 | tf_op jit(solution)/shard_map/gate0_dp4/ppermute | solution.py:994
  202.4 38.4 %collective-permute-start.20 = (bf16[256,1280]{1,0:T(8,128)(2,1)}, bf16[256,1280]{1,0:T(8,128)(2,1)}, u32[]{:S(2)}, u32[]{:S(2)}) collective-permute-start(bf16[256,1280]{1,0:T(8,128)(2,1)} %get-tuple-element.718), channel_id=1, source_target_pairs={{0,4},{4,0},{8,12},{12,8},{16,20},{20,16},{24,28},{28,24},{1,5},{5... | collective-permute-start | bytes 1966088 | tf_op jit(solution)/shard_map/gate1_dp1/ppermute | solution.py:994
  203.9 36.9 %collective-permute-start.19 = (bf16[256,1280]{1,0:T(8,128)(2,1)}, bf16[256,1280]{1,0:T(8,128)(2,1)}, u32[]{:S(2)}, u32[]{:S(2)}) collective-permute-start(bf16[256,1280]{1,0:T(8,128)(2,1)} %get-tuple-element.717), channel_id=1, source_target_pairs={{0,8},{4,12},{8,0},{12,4},{16,24},{20,28},{24,16},{28,20},{1,9},{5... | collective-permute-start | bytes 1966088 | tf_op jit(solution)/shard_map/up1_dp2/ppermute | solution.py:994
  212.2 55.0 %collective-permute-start.18 = (bf16[1408,512]{1,0:T(8,128)(2,1)}, bf16[1408,512]{1,0:T(8,128)(2,1)S(1)}, u32[]{:S(2)}, u32[]{:S(2)}) collective-permute-start(bf16[1408,512]{1,0:T(8,128)(2,1)} %get-tuple-element.716), channel_id=1, source_target_pairs={{0,8},{4,12},{8,0},{12,4},{16,24},{20,28},{24,16},{28,20},{1,9},{5... | collective-permute-start | bytes 4325384 | tf_op jit(solution)/shard_map/down0_dp2/ppermute | solution.py:994
  212.8 54.4 %collective-permute-start.22 = (bf16[1408,512]{1,0:T(8,128)(2,1)}, bf16[1408,512]{1,0:T(8,128)(2,1)S(1)}, u32[]{:S(2)}, u32[]{:S(2)}) collective-permute-start(bf16[1408,512]{1,0:T(8,128)(2,1)} %get-tuple-element.764), channel_id=1, source_target_pairs={{0,4},{4,0},{8,12},{12,8},{16,20},{20,16},{24,28},{28,24},{1,5},{5... | collective-permute-start | bytes 4325384 | tf_op jit(solution)/shard_map/down1_dp1/ppermute | solution.py:994
  267.2 23.3 %collective-permute-start.23 = (bf16[4,512,1024]{2,1,0:T(8,128)(2,1)}, bf16[4,512,1024]{2,1,0:T(8,128)(2,1)}, u32[]{:S(2)}, u32[]{:S(2)}) collective-permute-start(bf16[4,512,1024]{2,1,0:T(8,128)(2,1)} %get-tuple-element.806), channel_id=1, source_target_pairs={{0,1},{1,0},{2,3},{3,2},{4,5},{5,4},{6,7},{7,6},{8,9},{9,8},{10,11... | collective-permute-start | bytes 12582920 | tf_op jit(solution)/shard_map/dense_expert1/ppermute | solution.py:994
  276.7 21.6 %collective-permute-start.26 = (bf16[704,512]{1,0:T(8,128)(2,1)}, bf16[704,512]{1,0:T(8,128)(2,1)S(1)}, u32[]{:S(2)}, u32[]{:S(2)}) collective-permute-start(bf16[704,512]{1,0:T(8,128)(2,1)} %get-tuple-element.838), channel_id=1, source_target_pairs={{0,4},{4,0},{8,12},{12,8},{16,20},{20,16},{24,28},{28,24},{1,5},{5... | collective-permute-start | bytes 2162696 | tf_op jit(solution)/shard_map/down0_dp1/ppermute | solution.py:994
  277.1 21.1 %collective-permute-start.25 = (bf16[704,512]{1,0:T(8,128)(2,1)}, bf16[704,512]{1,0:T(8,128)(2,1)S(1)}, u32[]{:S(2)}, u32[]{:S(2)}) collective-permute-start(bf16[704,512]{1,0:T(8,128)(2,1)} %get-tuple-element.837), channel_id=1, source_target_pairs={{0,8},{4,12},{8,0},{12,4},{16,24},{20,28},{24,16},{28,20},{1,9},{5... | collective-permute-start | bytes 2162696 | tf_op jit(solution)/shard_map/down1_dp2/ppermute | solution.py:994
  298.2 29.1 %collective-permute-start.29 = (bf16[2,256,1152]{2,1,0:T(8,128)(2,1)}, bf16[2,256,1152]{2,1,0:T(8,128)(2,1)S(1)}, u32[]{:S(2)}, u32[]{:S(2)}) collective-permute-start(bf16[2,256,1152]{2,1,0:T(8,128)(2,1)} %get-tuple-element.858), channel_id=1, source_target_pairs={{0,2},{1,3},{2,0},{3,1},{4,6},{5,7},{6,4},{7,5},{8,10},{9,11},{10,... | collective-permute-start | bytes 3538952 | tf_op jit(solution)/shard_map/out_q_expert2/ppermute | solution.py:994
  299.7 25.2 %collective-permute-start.28 = (bf16[2,256,1024]{2,1,0:T(8,128)(2,1)}, bf16[2,256,1024]{2,1,0:T(8,128)(2,1)S(1)}, u32[]{:S(2)}, u32[]{:S(2)}) collective-permute-start(bf16[2,256,1024]{2,1,0:T(8,128)(2,1)} %get-tuple-element.854), channel_id=1, source_target_pairs={{0,4},{4,0},{8,12},{12,8},{16,20},{20,16},{24,28},{28,24},{1,5},{5... | collective-permute-start | bytes 3145736 | tf_op jit(solution)/shard_map/k_v_dp1/ppermute | solution.py:994
  314.2 51.8 %collective-permute-start.27 = (bf16[2,320,1024]{2,1,0:T(8,128)(2,1)}, bf16[2,320,1024]{2,1,0:T(8,128)(2,1)S(1)}, u32[]{:S(2)}, u32[]{:S(2)}) collective-permute-start(bf16[2,320,1024]{2,1,0:T(8,128)(2,1)} %get-tuple-element.852), channel_id=1, source_target_pairs={{0,2},{1,3},{2,0},{3,1},{4,6},{5,7},{6,4},{7,5},{8,10},{9,11},{10,... | collective-permute-start | bytes 3932168 | tf_op jit(solution)/shard_map/produced_rows2/ppermute | solution.py:994
  314.9 45.8 %collective-permute-start.32 = (bf16[2,128,1280]{2,1,0:T(8,128)(2,1)}, bf16[2,128,1280]{2,1,0:T(8,128)(2,1)S(1)}, u32[]{:S(2)}, u32[]{:S(2)}) collective-permute-start(bf16[2,128,1280]{2,1,0:T(8,128)(2,1)} %get-tuple-element.900), channel_id=1, source_target_pairs={{0,16},{4,20},{8,24},{12,28},{16,0},{20,4},{24,8},{28,12},{1,17},{... | collective-permute-start | bytes 1966088 | tf_op jit(solution)/shard_map/gate1_dp4/ppermute | solution.py:994
  333.5 27.3 %collective-permute-start.31 = (bf16[2,128,1152]{2,1,0:T(8,128)(2,1)}, bf16[2,128,1152]{2,1,0:T(8,128)(2,1)S(1)}, u32[]{:S(2)}, u32[]{:S(2)}) collective-permute-start(bf16[2,128,1152]{2,1,0:T(8,128)(2,1)} %get-tuple-element.896), channel_id=1, source_target_pairs={{0,4},{4,0},{8,12},{12,8},{16,20},{20,16},{24,28},{28,24},{1,5},{5... | collective-permute-start | bytes 1769480 | tf_op jit(solution)/shard_map/out_q_dp1/ppermute | solution.py:994
  335.0 25.7 %collective-permute-start.30 = (bf16[2,128,1024]{2,1,0:T(8,128)(2,1)}, bf16[2,128,1024]{2,1,0:T(8,128)(2,1)S(1)}, u32[]{:S(2)}, u32[]{:S(2)}) collective-permute-start(bf16[2,128,1024]{2,1,0:T(8,128)(2,1)} %get-tuple-element.888), channel_id=1, source_target_pairs={{0,8},{4,12},{8,0},{12,4},{16,24},{20,28},{24,16},{28,20},{1,9},{5... | collective-permute-start | bytes 1572872 | tf_op jit(solution)/shard_map/k_v_dp2/ppermute | solution.py:994
  337.2 46.1 %collective-permute-start.37 = (bf16[2,352,512]{2,1,0:T(8,128)(2,1)}, bf16[2,352,512]{2,1,0:T(8,128)(2,1)S(1)}, u32[]{:S(2)}, u32[]{:S(2)}) collective-permute-start(bf16[2,352,512]{2,1,0:T(8,128)(2,1)} %get-tuple-element.941), channel_id=1, source_target_pairs={{0,16},{4,20},{8,24},{12,28},{16,0},{20,4},{24,8},{28,12},{1,17},{... | collective-permute-start | bytes 2162696 | tf_op jit(solution)/shard_map/down0_dp4/ppermute | solution.py:994
  368.0 15.3 %collective-permute-start.36 = (bf16[2,64,1152]{2,1,0:T(8,128)(2,1)}, bf16[2,64,1152]{2,1,0:T(8,128)(2,1)S(1)}, u32[]{:S(2)}, u32[]{:S(2)}) collective-permute-start(bf16[2,64,1152]{2,1,0:T(8,128)(2,1)} %get-tuple-element.937), channel_id=1, source_target_pairs={{0,8},{4,12},{8,0},{12,4},{16,24},{20,28},{24,16},{28,20},{1,9},{5... | collective-permute-start | bytes 884744 | tf_op jit(solution)/shard_map/out_q_dp2/ppermute | solution.py:994
  389.4 12.2 %collective-permute-start.38 = (bf16[2,32,1152]{2,1,0:T(8,128)(2,1)S(1)}, bf16[2,32,1152]{2,1,0:T(8,128)(2,1)S(1)}, u32[]{:S(2)}, u32[]{:S(2)}) collective-permute-start(bf16[2,32,1152]{2,1,0:T(8,128)(2,1)S(1)} %copy-done.45), channel_id=1, source_target_pairs={{0,16},{4,20},{8,24},{12,28},{16,0},{20,4},{24,8},{28,12},{1,17},{... | collective-permute-start | bytes 442376 | tf_op jit(solution)/shard_map/out_q_dp4/ppermute | solution.py:994
  389.8 14.6 %collective-permute-start.39 = (bf16[2,32,1024]{2,1,0:T(8,128)(2,1)S(1)}, bf16[2,32,1024]{2,1,0:T(8,128)(2,1)S(1)}, u32[]{:S(2)}, u32[]{:S(2)}) collective-permute-start(bf16[2,32,1024]{2,1,0:T(8,128)(2,1)S(1)} %copy-done.46), channel_id=1, source_target_pairs={{0,16},{4,20},{8,24},{12,28},{16,0},{20,4},{24,8},{28,12},{1,17},{... | collective-permute-start | bytes 393224 | tf_op jit(solution)/shard_map/k_v_dp4/ppermute | solution.py:994
  (55 other events, 364.9 us)

commit v4 on v3

--- a/solution.py
+++ b/solution.py
@@ -168,7 +168,7 @@
 
 
 def slot_codes(routes):
-    chosen = routes.astype(F32).T
+    chosen = routes.astype(F32)
     tokens = chosen.shape[1]
     numbers = lax.broadcasted_iota(jnp.int32, (TAIL // 2, tokens), 0).astype(F32)
     named = jnp.logical_or(numbers == chosen[0:1], numbers == chosen[1:2])
@@ -193,8 +193,8 @@
     rows = mid.shape[0]
     nm = (mid * rms_scale(mid) * gain_ref[...]).astype(BF)
     nm_ref[...] = nm
-    router = jnp.concatenate([wr_ref[...].astype(F32).T, jnp.zeros((TAIL - experts, nm.shape[1]), F32)], axis=0)
-    logits = dot_nt(router.astype(BF), nm)
+    router = jnp.concatenate([wr_ref[...], jnp.zeros((TAIL - experts, nm.shape[1]), BF)], axis=0)
+    logits = dot_nt(router, nm)
     live = lax.broadcasted_iota(jnp.int32, logits.shape, 0) < experts
     logits = jnp.where(live, logits, FAR)
     raised = jnp.exp(logits - jnp.max(logits, axis=0, keepdims=True))
@@ -235,7 +235,7 @@
         code_scr[...] = codes
         code_ref[...] = codes[:experts].astype(jnp.int32)
         table = onehot_ref[...]
-        offsets = sum(dot_tn(part, table) for part in split3(bias_ref[...]))
+        offsets = sum(dot(part, table) for part in split3(bias_ref[...]))
         for g in range(woff_scr.shape[0]):
             woff_scr[g] = offsets[g * HEAD_GROUP : (g + 1) * HEAD_GROUP]
 
@@ -304,8 +304,8 @@
 
 def attn_first(tokens, gain_attn, w_query, w_key, w_value, w_out, rel_bias, seg, gain_moe, w_router, routes):
     rows, width = tokens.shape
-    buckets, heads = rel_bias.shape
-    experts = w_router.shape[1]
+    heads, buckets = rel_bias.shape
+    experts = w_router.shape[0]
     groups = heads // HEAD_GROUP
     cols, part = width // groups, rows // 2
     weight_block = pl.BlockSpec((width, cols), lambda g: (0, g))
@@ -350,7 +350,7 @@
 
 def attn_second(tokens, scaled, keys, values, w_out, woff, seg, gain_moe, w_router, filled):
     rows, width = tokens.shape
-    experts = w_router.shape[1]
+    experts = w_router.shape[0]
     groups = woff.shape[0]
     cols, part = width // groups, rows // 2
     col_block = pl.BlockSpec((rows, cols), lambda g: (0, g))
@@ -944,7 +944,8 @@
 
 
 def norm_bwd_kernel(
-    tok_ref, gain_ref, gmid_ref, dq_ref, dk_ref, dv_ref, wq_ref, wk_ref, wv_ref, tg_ref, gain_o_ref, acc
+    place_ref, tok_ref, gain_ref, gmid_ref, small_ref, dq_ref, dk_ref, dv_ref, wq_ref, wk_ref, wv_ref,
+    tg_ref, keep_ref, send_ref, acc, sort_scr, *, gain_row,
 ):
     step = pl.program_id(0)
     total = dot_nt(dq_ref[...], wq_ref[...]) + dot_nt(dk_ref[...], wk_ref[...]) + dot_nt(dv_ref[...], wv_ref[...])
@@ -963,26 +964,69 @@
         start = tok_ref[...].astype(F32)
         scale = rms_scale(start)
         unit = start * scale
-        gain_o_ref[...] = jnp.sum(grad * unit, axis=0, keepdims=True)
+        gain_grad = jnp.sum(grad * unit, axis=0, keepdims=True)
         scaled = grad * gain_ref[...]
         tg_ref[...] = gmid_ref[...] + scale * (scaled - unit * jnp.mean(scaled * unit, axis=-1, keepdims=True))
-
-
-def norm_bwd(tokens, gain_attn, grad_mid, dq, dk, dv, w_query, w_key, w_value):
+        small = small_ref[...]
+        row = lax.broadcasted_iota(jnp.int32, small.shape, 0)
+        small = jnp.where(row == gain_row, gain_grad, small)
+        small = jnp.concatenate([small, jnp.zeros((LANES - small.shape[0], small.shape[1]), F32)], axis=0)
+        sort_rows(place_ref, small.T, sort_scr)
+        half = sort_scr.shape[0] // 2
+        keep_ref[...] = sort_scr[0:half].astype(BF)
+        send_ref[...] = sort_scr[half:].astype(BF)
+
+
+def norm_bwd(place, tokens, gain_attn, grad_mid, small, gain_row, dq, dk, dv, w_query, w_key, w_value):
     rows, width = tokens.shape
     cols = 256
     col_block = pl.BlockSpec((rows, cols), lambda g: (0, g))
     weight_block = pl.BlockSpec((width, cols), lambda g: (0, g))
-    return call(
-        norm_bwd_kernel,
-        (tokens, gain_attn[None], grad_mid, dq, dk, dv, w_query, w_key, w_value),
-        [const_spec((rows, width)), const_spec((1, width)), const_spec((rows, width))] + [col_block] * 3 + [weight_block] * 3,
+    half = jax.ShapeDtypeStruct((width // 2, LANES), BF)
+    return call(
+        functools.partial(norm_bwd_kernel, gain_row=gain_row),
+        (place, tokens, gain_attn[None], grad_mid, small, dq, dk, dv, w_query, w_key, w_value),
+        [pl.BlockSpec(memory_space=pltpu.SMEM)]
+        + [const_spec((rows, width)), const_spec((1, width)), const_spec((rows, width)), const_spec(small.shape)]
+        + [col_block] * 3
+        + [weight_block] * 3,
         grid=(width // cols,),
-        out_specs=[const_spec((rows, width)), const_spec((1, width))],
-        out_shape=[jax.ShapeDtypeStruct((rows, width), F32), jax.ShapeDtypeStruct((1, width), F32)],
-        scratch_shapes=[pltpu.VMEM((rows, width), F32)],
+        out_specs=[const_spec((rows, width)), const_spec(half.shape), const_spec(half.shape)],
+        out_shape=[jax.ShapeDtypeStruct((rows, width), F32), half, half],
+        scratch_shapes=[pltpu.VMEM((rows, width), F32), pltpu.VMEM((width, LANES), F32)],
         cost_estimate=estimate("norm_bwd"),
         name="norm_bwd",
+    )
+
+
+def last_sums_kernel(token_ref, *refs, experts, counts):
+    pairs, outs = refs[:4], refs[4:]
+    first = pairs[0][...].astype(F32) + pairs[1][...].astype(F32)
+    second = pairs[2][...].astype(F32) + pairs[3][...].astype(F32)
+    width = second.shape[2]
+    outs[0][...] = first[0, :, 0:width]
+    outs[1][...] = first[1, :, 0:width]
+    outs[2][...] = second[0]
+    outs[3][...] = second[1]
+    small = first[0, :, width:] + token_ref[...]
+    outs[4][...] = small[:, 0:experts]
+    flat = small.T
+    for i, count in enumerate(counts):
+        outs[5 + i][...] = flat[TAIL // 2 + i : TAIL // 2 + i + 1, 0:count]
+
+
+def last_sums(token, pairs, experts, counts):
+    rows, width = pairs[2].shape[1:]
+    args = (token, *pairs)
+    return call(
+        functools.partial(last_sums_kernel, experts=experts, counts=counts),
+        args,
+        [pl.BlockSpec(memory_space=pltpu.VMEM)] * len(args),
+        out_shape=[jax.ShapeDtypeStruct((rows, width), F32)] * 4
+        + [jax.ShapeDtypeStruct((rows, experts), F32)]
+        + [jax.ShapeDtypeStruct((1, count), F32) for count in counts],
+        cost_estimate=estimate("last_sums"),
+        name="last_sums",
     )
 
 
@@ -1217,7 +1261,7 @@
 
     cots = Gather(None, cotangent, "expert", ep_size, "cot")
     scaled, keys, values, woff, token, code, *filled, payload = attn_first(
-        tokens, gain_attn, w_query, w_key, w_value, w_out, rel_bias, segments, gain_moe, w_router, routes
+        tokens, gain_attn, w_query, w_key, w_value, w_out, rel_bias.T, segments, gain_moe, w_router.T, routes.T
     )
     order = Order(token)
     cots.order = order
@@ -1247,7 +1291,7 @@
     cots.relay()
     first_half = Gather(order, order.enter(payload), "expert", ep_size, "rows_a")
     attended, lse, middle, normed_moe, chances, payload = order.leave(
-        attn_second(tokens, order.enter(scaled), keys, values, w_out, woff, segments, gain_moe, w_router, filled)
+        attn_second(tokens, order.enter(scaled), keys, values, w_out, woff, segments, gain_moe, w_router.T, filled)
     )
     second_half = Gather(order, order.enter(payload), "expert", ep_size, "rows_b")
     first_half.relay()
@@ -1288,7 +1332,7 @@
     back_low, back_high = order.leave(expert_b(order.enter(gg), gu, scs, w_gate, w_up, experts))
     backs = Return(order, back_low, back_high, "expert", ep_size, "grad_rows")
     first, second = units[0][0], units[1][0]
-    fold(units[0])
+    fold(units[0], hold=units[0])
     down_parts = order.leave(down_grads(order.enter(hid_t), grad_cots, place_z, place_x))
     down_units = tuple(
         Halving(order, down_parts[2 * i], down_parts[2 * i + 1], 0, dp_route(bits), f"down{i}")
@@ -1309,37 +1353,36 @@
         )
     )
     dq, dk, dv, dwoff = order.leave(attn_bwd(scaled, keys, values, order.enter(grad_att), lse, woff, segments))
-    arrive(first, *units[1])
+    arrive(*units[1])
     dense_keep, dense_send = order.leave(dense_terms(att_t, normed_t, branch, order.enter(dq), dk, dv))
-    arrive(*units[1], *down_units)
+    arrive(*down_units)
     core = Halving(order, dense_keep, dense_send, 1, route(q_bits)[:1], "dense")
     core.start()
-    fold(*down_units, first, units[1], hold=units[1])
-    token_grad, gain_attn_term = order.leave(
-        norm_bwd(tokens, gain_attn, grad_mid, order.enter(dq), dk, dv, w_query, w_key, w_value)
-    )
-    onehot = jnp.asarray(band_onehot(rows, buckets))
-    bias_term = jnp.dot(onehot, dwoff.reshape(heads, BAND).T, precision=HIGHEST)
+    first.start()
+    fold(*down_units, units[1], hold=units[1])
     devices = dp_size * ep_size
     share = width // devices
+    onehot = jnp.asarray(band_onehot(rows, buckets))
+    bias_term = jnp.dot(onehot, dwoff.reshape(heads, BAND).T, precision=HIGHEST).reshape(devices, -1)
+    bias_share = bias_term.shape[1]
+    bias_row = jnp.pad(bias_term, ((0, 0), (0, share - bias_share))).reshape(1, width)
     small = jnp.concatenate(
         [
-            by_xor(router_term).T.reshape(devices, -1),
-            gain_attn_term.reshape(devices, -1),
-            gain_moe_term.reshape(devices, -1),
-            bias_term.reshape(devices, -1),
+            jnp.pad(by_xor(router_term), ((0, TAIL // 2 - experts), (0, 0))),
+            jnp.zeros((1, width), F32),
+            gain_moe_term,
+            bias_row,
+            jnp.zeros((TAIL // 2 - 3, width), F32),
         ],
-        axis=1,
-    )
-    count = small.shape[1]
-    lines = -(-count // LANES)
-    at_place = (place_q[None, :] == jnp.arange(devices, dtype=jnp.int32)[:, None]).astype(F32)
-    small = jnp.dot(at_place, jnp.pad(small, ((0, 0), (0, lines * LANES - count))), precision=HIGHEST)
-    small = small.reshape(devices, lines, LANES).astype(BF)
-    small = jnp.pad(small, ((0, 0), (0, share - lines), (0, 0))).reshape(2, width // 2, LANES)
-    small_keep, small_send = order.enter((small[0], small[1]))
+        axis=0,
+    )
+    token_grad, small_keep, small_send = order.leave(
+        norm_bwd(
+            place_q, tokens, gain_attn, grad_mid, order.enter(small), TAIL // 2, dq, dk, dv, w_query, w_key, w_value
+        )
+    )
     with jax.named_scope("small_expert1"):
-        small_got = swap(small_send, "expert", ep_size, 1)
+        small_got = swap(order.enter(small_send), "expert", ep_size, 1)
     core_got = order.leave(core.got)
     halves = order.leave(fold_first(order.enter(dense_keep), core_got, small_keep, order.leave(small_got)))
     dense = [
@@ -1347,40 +1390,39 @@
         for i, (bits, name) in enumerate(((q_bits, "out_q"), (k_bits, "k_v")))
     ]
     out_q, k_v = dense
-    arrive(*down_units)
+    arrive(*down_units, first)
     k_v.start()
     out_q.start()
     second.start()
     prod_low, prod_high = order.leave(produced_rows(order.enter(hid), w_down, experts))
     returned = Return(order, prod_low, prod_high, "expert", ep_size, "produced_rows")
-    fold(k_v, out_q, down_units)
-    fold(k_v, out_q, second)
+    fold(k_v, out_q, down_units, first, second)
+    fold(k_v, out_q)
+    while first.route or second.route:
+        fold(*[unit for unit in (first, second) if unit.route])
+    terms = [first.keep, second.keep]
+    gate_grad = order.leave(jnp.concatenate([term[0] for term in terms], axis=1)[None])
+    up_grad = order.leave(jnp.concatenate([term[1] for term in terms], axis=1)[None])
     returned.fold()
     returned.finish()
     layer_out = order.leave(layer_output(middle, chances_xor, code_xor.T, returned.slots))
     fold(k_v, out_q, down)
     rest = [first, second, down, *dense]
-    while any(unit.route for unit in rest):
+    while any(unit.route[1:] for unit in rest) or down.route:
         fold(*[unit for unit in rest if unit.route])
-    small_sum = out_q.keep[0, 0:lines, width:].reshape(-1)[:count] + order.token[0, :1]
-
-    terms = [first.keep, second.keep]
-    gate_grad = jnp.concatenate([term[0] for term in terms], axis=1)[None]
-    up_grad = jnp.concatenate([term[1] for term in terms], axis=1)[None]
-    down_grad = jnp.concatenate([down.keep[0], down.keep[1]], axis=1)[None]
-    n_router = width * experts // devices
-    n_gain = width // devices
-    router_grad = small_sum[:n_router].reshape(share, experts)
-    gain_attn_grad = small_sum[n_router : n_router + n_gain]
-    gain_moe_grad = small_sum[n_router + n_gain : n_router + 2 * n_gain]
-    bias_grad = small_sum[n_router + 2 * n_gain :]
+    down_grad = order.leave(jnp.concatenate([down.keep[0], down.keep[1]], axis=1)[None])
+    pairs = order.leave([out_q.keep, out_q.got, k_v.keep, k_v.got])
+    out_grad, query_grad, key_grad, value_grad, router_grad, *gains = last_sums(
+        order.token, pairs, experts, (share, share, bias_share)
+    )
+    gain_attn_grad, gain_moe_grad, bias_grad = [value.reshape(-1) for value in gains]
     return (
         layer_out,
         token_grad,
-        out_q.keep[1, :, :width],
-        k_v.keep[0],
-        k_v.keep[1],
-        out_q.keep[0, :, :width],
+        query_grad,
+        key_grad,
+        value_grad,
+        out_grad,
         gain_attn_grad,
         gain_moe_grad,
         bias_grad,

time: 420 us -> 407 us (0.969)
  local copies, waits for them, and re-layouts: 34.9 us -> 27.1 us
    unnamed x98 -> x91, local copies, waits for them, and re-layouts: 21.1 us -> 16.7 us
  transfers between devices with their start and end apart: 40 -> 40, of which waited for: 14 -> 17; matrix products, arithmetic and copies ran while one was open for 5% -> 4% of each run, Pallas kernels for 52% -> 53%
where the time goes in v4:
time: 407 us; the launch traced here: 400 us
  Pallas kernels  256 us (63%)
  waiting for transfers between devices  74.7 us (18%)
  starting transfers between devices  34.6 us (9%)
  local copies, waits for them, and re-layouts  27.1 us (7%)
  other arithmetic  6.01 us (1%)
    pallas_call x24, Pallas kernels, call(): pl.pallas_call(kernel, in_specs=list(in_specs), compiler_params=params(),...  256 us
    ppermute x40, waiting for transfers between devices, swap(): return lax.ppermute(value, axis, [(i, i ^ mask) for i in range(size)])  74.7 us
    ppermute x40, starting transfers between devices, swap(): return lax.ppermute(value, axis, [(i, i ^ mask) for i in range(size)])  34.6 us
    unnamed x91, local copies, waits for them, and re-layouts  16.7 us
  transfers between devices with their start and end apart: 40, of which 17 were waited for; matrix products, arithmetic and copies ran while one was open for 4% of the time, Pallas kernels for 53%

profile of v4, /device:TPU:0, one launch (start us, length us, event | category | flops | bytes accessed | tf_op | source)
XLA Modules:
  0.0 399.5 jit_solution(18097327947629627579)
XLA Ops:
  0.6 3.0 collective-permute-start
  3.7 15.6 %attn_first.1 = (bf16[512,1024]{1,0:T(8,128)(2,1)}, bf16[512,1024]{1,0:T(8,128)(2,1)}, bf16[512,1024]{1,0:T(8,128)(2,1)}, f32[4,4,512]{2,1,0:T(4,128)}, f32[1,12...) custom-call(bf16[512,1024]{1,0:T(8,128)(2,1)} %tok_ref.6, ...), custom_call_target="tpu_custom_call" | custom-call | flops 115000000 | bytes 100000 | tf_op jit(solution)/shard_map/attn_first/pallas_call | solution.py:100
  19.3 7.8 %collective-permute-done.refs_6_ = bf16[512,1024]{1,0:T(8,128)(2,1)} collective-permute-done((bf16[512,1024]{1,0:T(8,128)(2,1)}, bf16[512,1024]{1,0:T(8,128)(2,1)}, u32[]{:S(2)}, u32[]{:S(2)}) %collective-permute-start) | collective-permute-done | bytes 1048608 | tf_op jit(solution)/shard_map/cot0_2/ppermute | solution.py:1038
  29.4 12.3 %attn_second.1 = (bf16[512,1024]{1,0:T(8,128)(2,1)}, f32[4,4,512]{2,1,0:T(4,128)}, f32[512,1024]{1,0:T(8,128)}, bf16[512,1024]{1,0:T(8,128)(2,1)}, f32[16,512]{1,0:T(8,128)}, /*index=5*/bf16[272,1024]{1,0:T(8,128)(2,1)}) custom-call(bf16[512,1024]{1,0:T(8,128)(2,1)} %tok_ref.6, ...), custom_call_target="tpu_custom_call", output_to_operand_aliasing={{0}: (9, {}), {1}: (10, {}), {2}: (11, {}), {3}: (12, {}), ... | custom-call | flops 115000000 | bytes 100000 | tf_op jit(solution)/shard_map/attn_second/pallas_call | solution.py:100
  44.7 11.1 %cot_hidden.1 = (bf16[1280,1536]{1,0:T(8,128)(2,1)}, bf16[1280,1024]{1,0:T(8,128)(2,1)}) custom-call(s32[1]{0:T(128)} %bitcast.9.me_ref.refs_0_, bf16[272,1024]{1,0:T(8,128)(2,1)} %get-tuple-element.557.refs_0_.refs_2_, bf16[272,1024]{1,0:T(8,128)(2,1)} %copy-done.4, bf16[272,1024]{1,0:T(8,128)(2,1)} %copy-done.3, bf16[272,1024]{1,0:T(8,128)(2,1)} %copy-done.5, ...), custom_call_target="tpu_custom_call" | custom-call | flops 115000000 | bytes 100000 | tf_op jit(solution)/shard_map/cot_hidden/pallas_call | solution.py:100
  59.9 32.5 %expert_grads.2 = (bf16[1280,1024]{1,0:T(8,128)(2,1)}, bf16[1024,1280]{1,0:T(8,128)(2,1)}, f32[1280,128]{1,0:T(8,128)}, bf16[1280,1024]{1,0:T(8,128)(2,1)}, bf16...) custom-call(s32[1]{0:T(128)} %bitcast.9.me_ref.refs_0_, ...), custom_call_target="tpu_custom_call" | custom-call | flops 115000000 | bytes 100000 | tf_op jit(solution)/shard_map/expert_grads/pallas_call | solution.py:100
  95.6 8.0 %cot_hidden_more.1.refs_3_ = bf16[1280,1280]{1,0:T(8,128)(2,1)} custom-call(bf16[1280,1024]{1,0:T(8,128)(2,1)} %get-tuple-element.589.refs_10_.rows_ref, bf16[1,2816,1024]{2,1,0:T(8,128)(2,1)} %wd_ref.3), custom_call_target="tpu_custom_call" | custom-call | flops 115000000 | bytes 100000 | tf_op jit(solution)/shard_map/cot_hidden_more/pallas_call | solution.py:100
  103.7 25.2 %expert_grads.3 = (bf16[512,1280]{1,0:T(8,128)(2,1)}, bf16[512,1280]{1,0:T(8,128)(2,1)}, bf16[512,1280]{1,0:T(8,128)(2,1)}, bf16[512,1280]{1,0:T(8,128)(2,1)}, f...) custom-call(bf16[1280,1024]{1,0:T(8,128)(2,1)} %get-tuple-element.59, ...), custom_call_target="tpu_custom_call", output_to_operand_aliasing={{5}: (6, {}), {6}: (7, {}), {7}: (8, {}), {8}: (9, {})} | custom-call | flops 115000000 | bytes 100000 | tf_op jit(solution)/shard_map/expert_grads/pallas_call | solution.py:100
  131.6 4.7 %fold.7 = (bf16[256,1536]{1,0:T(8,128)(2,1)}, bf16[256,1536]{1,0:T(8,128)(2,1)}, bf16[256,1536]{1,0:T(8,128)(2,1)}, bf16[256,1536]{1,0:T(8,128)(2,1)}) custom-call(bf16[512,1536]{1,0:T(8,128)(2,1)} %get-tuple-element.621.refs_0_, bf16[512,1536]{1,0:T(8,128)(2,1)} %copy-done.6, bf16[512,1536]{1,0:T(8,128)(2,1)} %get-tuple-element.623.refs_2_, ...), custom_call_target="tpu_custom_call" | custom-call | flops 115000000 | bytes 100000 | tf_op jit(solution)/shard_map/fold/pallas_call | solution.py:100
  142.0 25.7 %expert_input_grad.1 = (bf16[2,336,1024]{2,1,0:T(8,128)(2,1)}, bf16[2,336,1024]{2,1,0:T(8,128)(2,1)}) custom-call(bf16[1280,2816]{1,0:T(8,128)(2,1)} %get-tuple-element.643.gg_ref, bf16[1280,2816]{1,0:T(8,128)(2,1)} %get-tuple-element.644.gu_ref, f32[1280,128]{1,0:T(8,128)} %get-tuple-element.645.refs_0_, f32[1280,128]{1,0:T(8,128)} %get-tuple-element.646.refs_1_, ...), custom_call_target="tpu_custom_call" | custom-call | flops 115000000 | bytes 100000 | tf_op jit(solution)/shard_map/expert_input_grad/pallas_call | solution.py:100
  172.8 3.2 fold.8
  175.9 16.8 %down_grads.1 = (bf16[1408,512]{1,0:T(8,128)(2,1)}, bf16[1408,512]{1,0:T(8,128)(2,1)}, bf16[1408,512]{1,0:T(8,128)(2,1)}, bf16[1408,512]{1,0:T(8,128)(2,1)}) custom-call(s32[8]{0:T(128)} %get-tuple-element.1037.place_a_ref, s32[8]{0:T(128)} %get-tuple-element.556.refs_1_.place_b_ref, bf16[2816,1280]{1,0:T(8,128)(2,1)} %get-tuple-element.667.hidt_ref, ...), custom_call_target="tpu_custom_call" | custom-call | flops 11500000256 | bytes 100000 | tf_op jit(solution)/shard_map/down_grads/pallas_call | solution.py:100
  194.9 4.1 %fold.9 = (bf16[256,1280]{1,0:T(8,128)(2,1)}, bf16[256,1280]{1,0:T(8,128)(2,1)}, bf16[256,1280]{1,0:T(8,128)(2,1)}, bf16[256,1280]{1,0:T(8,128)(2,1)}) custom-call(bf16[512,1280]{1,0:T(8,128)(2,1)} %get-tuple-element.681.refs_0_, bf16[512,1280]{1,0:T(8,128)(2,1)} %copy-done.39, bf16[512,1280]{1,0:T(8,128)(2,1)} %get-tuple-element.683.refs_2_, ...), custom_call_target="tpu_custom_call" | custom-call | flops 2300000000 | bytes 100000 | tf_op jit(solution)/shard_map/fold/pallas_call | solution.py:100
  203.1 4.7 %sorted_rows.1 = (bf16[1024,512]{1,0:T(8,128)(2,1)}, bf16[2,1024,512]{2,1,0:T(8,128)(2,1)}) custom-call(s32[32]{0:T(128)} %get-tuple-element.1036.pq_ref.place_ref, s32[32]{0:T(128)} %get-tuple-element.1035.pk_ref, bf16[512,1024]{1,0:T(8,128)(2,1)} %tok_ref.6, f32[1,1024]{1,0:T(1,128)} %bitcast.46, bf16[512,1024]{1,0:T(8,128)(2,1)} %get-tuple-element.710.att_ref), custom_call_target="tpu_custom_call" | custom-call | flops 115000000 | bytes 100000 | tf_op jit(solution)/shard_map/sorted_rows/pallas_call | solution.py:100
  211.5 10.2 %moe_bwd.1 = (f32[512,1024]{1,0:T(8,128)}, bf16[512,1024]{1,0:T(8,128)(2,1)}, bf16[512,1024]{1,0:T(8,128)(2,1)}, f32[1,1024]{1,0:T(1,128)}, f32[16,1024]{1,0:T(8,128)}) custom-call(bf16[512,1024]{1,0:T(8,128)(2,1)} %cot_ref.1, f32[512,1024]{1,0:T(8,128)} %get-tuple-element.722.mid_ref, f32[1,1024]{1,0:T(1,128)} %bitcast.44, ...), custom_call_target="tpu_custom_call" | custom-call | flops 115000000 | bytes 100000 | tf_op jit(solution)/shard_map/moe_bwd/pallas_call | solution.py:100
  221.7 16.2 %attn_bwd.1 = (bf16[512,1024]{1,0:T(8,128)(2,1)}, bf16[512,1024]{1,0:T(8,128)(2,1)}, bf16[512,1024]{1,0:T(8,128)(2,1)}, f32[4,4,512]{2,1,0:T(4,128)}) custom-call(bf16[512,1024]{1,0:T(8,128)(2,1)} %get-tuple-element.505.qs_ref, bf16[512,1024]{1,0:T(8,128)(2,1)} %get-tuple-element.506.k_ref, bf16[512,1024]{1,0:T(8,128)(2,1)} %get-tuple-element.507.v_ref, ...), custom_call_target="tpu_custom_call" | custom-call | flops 115000000 | bytes 100000 | tf_op jit(solution)/shard_map/attn_bwd/pallas_call | solution.py:100
  238.0 9.3 %dense_terms.1 = (bf16[4,512,1024]{2,1,0:T(8,128)(2,1)}, bf16[4,512,1024]{2,1,0:T(8,128)(2,1)}) custom-call(bf16[1024,512]{1,0:T(8,128)(2,1)} %get-tuple-element.717.att_ref, bf16[2,1024,512]{2,1,0:T(8,128)(2,1)} %get-tuple-element.718.rows_ref, bf16[512,1024]{1,0:T(8,128)(2,1)} %get-tuple-element.733.branch_ref, ...), custom_call_target="tpu_custom_call" | custom-call | flops 15064999936 | bytes 100000 | tf_op jit(solution)/shard_map/dense_terms/pallas_call | solution.py:100
  251.4 5.6 %fold.10 = (bf16[704,512]{1,0:T(8,128)(2,1)}, bf16[704,512]{1,0:T(8,128)(2,1)}, bf16[704,512]{1,0:T(8,128)(2,1)}, bf16[704,512]{1,0:T(8,128)(2,1)}, bf16[2,128,1...) custom-call(bf16[1408,512]{1,0:T(8,128)(2,1)} %get-tuple-element.778.refs_0_, bf16[1408,512]{1,0:T(8,128)(2,1)} %copy-done.8, ...), custom_call_target="tpu_custom_call" | custom-call | flops 115000000 | bytes 100000 | tf_op jit(solution)/shard_map/fold/pallas_call | solution.py:100
  261.5 10.9 %norm_bwd.1 = (f32[512,1024]{1,0:T(8,128)}, bf16[512,128]{1,0:T(8,128)(2,1)}, bf16[512,128]{1,0:T(8,128)(2,1)}) custom-call(s32[32]{0:T(128)} %get-tuple-element.1036.pq_ref.place_ref, bf16[512,1024]{1,0:T(8,128)(2,1)} %tok_ref.6, f32[1,1024]{1,0:T(1,128)} %bitcast.47, f32[512,1024]{1,0:T(8,128)} %get-tuple-element.796.gmid_ref, ...), custom_call_target="tpu_custom_call" | custom-call | flops 115000000 | bytes 100000 | tf_op jit(solution)/shard_map/norm_bwd/pallas_call | solution.py:100
  274.7 5.8 %fold_first.1 = (bf16[2,256,1152]{2,1,0:T(8,128)(2,1)}, bf16[2,256,1152]{2,1,0:T(8,128)(2,1)}, bf16[2,256,1024]{2,1,0:T(8,128)(2,1)}, bf16[2,256,1024]{2,1,0:T(8,128)(2,1)}) custom-call(bf16[4,512,1024]{2,1,0:T(8,128)(2,1)} %get-tuple-element.814.keep_ref, bf16[4,512,1024]{2,1,0:T(8,128)(2,1)} %collective-permute-done.22.got_ref, ...), custom_call_target="tpu_custom_call" | custom-call | flops 115000000 | bytes 100000 | tf_op jit(solution)/shard_map/fold_first/pallas_call | solution.py:100
  280.5 11.0 %collective-permute-done.25.refs_7_ = bf16[704,512]{1,0:T(8,128)(2,1)S(1)} collective-permute-done((bf16[704,512]{1,0:T(8,128)(2,1)}, bf16[704,512]{1,0:T(8,128)(2,1)S(1)}, u32[]{:S(2)}, u32[]{:S(2)}) %collective-permute-start.25) | collective-permute-done | bytes 720928 | tf_op jit(solution)/shard_map/down1_dp2/ppermute | solution.py:1038
  294.6 12.9 %produced_rows.1 = (bf16[2,320,1024]{2,1,0:T(8,128)(2,1)}, bf16[2,320,1024]{2,1,0:T(8,128)(2,1)}) custom-call(bf16[1280,2816]{1,0:T(8,128)(2,1)} %get-tuple-element.837.hid_ref, bf16[1,2816,1024]{2,1,0:T(8,128)(2,1)} %wd_ref.3), custom_call_target="tpu_custom_call" | custom-call | flops 115000000 | bytes 100000 | tf_op jit(solution)/shard_map/produced_rows/pallas_call | solution.py:100
  309.4 7.5 %collective-permute-done.28.refs_1_ = bf16[2,256,1024]{2,1,0:T(8,128)(2,1)S(1)} collective-permute-done((bf16[2,256,1024]{2,1,0:T(8,128)(2,1)}, bf16[2,256,1024]{2,1,0:T(8,128)(2,1)S(1)}, u32[]{:S(2)}, u32[]{:S(2)}) %collective-permute-start.28) | collective-permute-done | bytes 1048608 | tf_op jit(solution)/shard_map/k_v_dp1/ppermute | solution.py:1038
  316.9 3.8 collective-permute-done.29.refs_3_
  320.7 2.8 collective-permute-done.30.refs_11_
  324.3 6.8 %fold.11 = (bf16[2,128,1024]{2,1,0:T(8,128)(2,1)}, bf16[2,128,1024]{2,1,0:T(8,128)(2,1)}, bf16[2,128,1152]{2,1,0:T(8,128)(2,1)}, bf16[2,128,1152]{2,1,0:T(8,128)...) custom-call(bf16[2,256,1024]{2,1,0:T(8,128)(2,1)} %get-tuple-element, ...), custom_call_target="tpu_custom_call" | custom-call | flops 115000000 | bytes 100000 | tf_op jit(solution)/shard_map/fold/pallas_call | solution.py:100
  338.1 15.9 %collective-permute-done.31.refs_1_ = bf16[2,128,1024]{2,1,0:T(8,128)(2,1)S(1)} collective-permute-done((bf16[2,128,1024]{2,1,0:T(8,128)(2,1)}, bf16[2,128,1024]{2,1,0:T(8,128)(2,1)S(1)}, u32[]{:S(2)}, u32[]{:S(2)}) %collective-permute-start.31) | collective-permute-done | bytes 524320 | tf_op jit(solution)/shard_map/k_v_dp2/ppermute | solution.py:1038
  362.4 6.3 %layer_output.1 = bf16[512,1024]{1,0:T(8,128)(2,1)} custom-call(f32[512,1024]{1,0:T(8,128)} %get-tuple-element.722.mid_ref, f32[16,512]{1,0:T(8,128)} %select_maximum_fusion.3.ch_ref, s32[512,4]{1,0:T(8,128)} %bitcast.39, bf16[2,320,1024]{2,1,0:T(8,128)(2,1)} %get-tuple-element.841.refs_0_, bf16[1,320,1024]{2,1,0:T(8,128)(2,1)} %copy-done.22, ...), custom_call_target="tpu_custom_call" | custom-call | flops 115000000 | bytes 100000 | tf_op jit(solution)/shard_map/layer_output/pallas_call | solution.py:100
  368.6 5.3 %collective-permute-done.36.refs_3_ = bf16[2,64,1152]{2,1,0:T(8,128)(2,1)S(1)} collective-permute-done((bf16[2,64,1152]{2,1,0:T(8,128)(2,1)}, bf16[2,64,1152]{2,1,0:T(8,128)(2,1)S(1)}, u32[]{:S(2)}, u32[]{:S(2)}) %collective-permute-start.36) | collective-permute-done | bytes 294944 | tf_op jit(solution)/shard_map/out_q_dp2/ppermute | solution.py:1038
  375.5 3.0 fold.13
  380.2 2.9 collective-permute-start.39
  384.3 10.4 %collective-permute-done.39.refs_3_ = bf16[2,32,1024]{2,1,0:T(8,128)(2,1)S(1)} collective-permute-done((bf16[2,32,1024]{2,1,0:T(8,128)(2,1)S(1)}, bf16[2,32,1024]{2,1,0:T(8,128)(2,1)S(1)}, u32[]{:S(2)}, u32[]{:S(2)}) %collective-permute-start.39) | collective-permute-done | bytes 131104 | tf_op jit(solution)/shard_map/k_v_dp4/ppermute | solution.py:1038
  (191 shorter events, 76.6 us)
Async XLA Ops:
  0.6 26.5 %collective-permute-start = (bf16[512,1024]{1,0:T(8,128)(2,1)}, bf16[512,1024]{1,0:T(8,128)(2,1)}, u32[]{:S(2)}, u32[]{:S(2)}) collective-permute-start(bf16[512,1024]{1,0:T(8,128)(2,1)} %cot_ref.1), channel_id=1, source_target_pairs={{0,2},{1,3},{2,0},{3,1},{4,6},{5,7},{6,4},{7,5},{8,10},{9,11},{10,... | collective-permute-start | bytes 3145736 | tf_op jit(solution)/shard_map/cot0_2/ppermute | solution.py:1038
  27.2 14.6 %collective-permute-start.2 = (bf16[272,1024]{1,0:T(8,128)(2,1)}, bf16[272,1024]{1,0:T(8,128)(2,1)S(1)}, u32[]{:S(2)}, u32[]{:S(2)}) collective-permute-start(bf16[272,1024]{1,0:T(8,128)(2,1)} %get-tuple-element.557.refs_0_.refs_2_), channel_id=1, source_target_pairs={{0,2},{1,3},{2,0},{3,1},{4,6},{5,7},{6,4},{7,5},{8,10},{9,11},{10,... | collective-permute-start | bytes 1671176 | tf_op jit(solution)/shard_map/rows_a0_2/ppermute | solution.py:1038
  28.9 13.7 %collective-permute-start.4 = (bf16[512,1024]{1,0:T(8,128)(2,1)S(1)}, bf16[512,1024]{1,0:T(8,128)(2,1)}, u32[]{:S(2)}, u32[]{:S(2)}) collective-permute-start(bf16[512,1024]{1,0:T(8,128)(2,1)S(1)} %copy-done), channel_id=1, source_target_pairs={{0,1},{1,0},{2,3},{3,2},{4,5},{5,4},{6,7},{7,6},{8,9},{9,8},{10,11... | collective-permute-start | bytes 3145736 | tf_op jit(solution)/shard_map/cot0_1/ppermute | solution.py:1038
  28.9 13.9 %collective-permute-start.5 = (bf16[512,1024]{1,0:T(8,128)(2,1)}, bf16[512,1024]{1,0:T(8,128)(2,1)}, u32[]{:S(2)}, u32[]{:S(2)}) collective-permute-start(bf16[512,1024]{1,0:T(8,128)(2,1)} %collective-permute-done.refs_6_), channel_id=1, source_target_pairs={{0,1},{1,0},{2,3},{3,2},{4,5},{5,4},{6,7},{7,6},{8,9},{9,8},{10,11... | collective-permute-start | bytes 3145736 | tf_op jit(solution)/shard_map/cot2_1/ppermute | solution.py:1038
  29.4 13.4 %collective-permute-start.1 = (bf16[272,1024]{1,0:T(8,128)(2,1)}, bf16[272,1024]{1,0:T(8,128)(2,1)S(1)}, u32[]{:S(2)}, u32[]{:S(2)}) collective-permute-start(bf16[272,1024]{1,0:T(8,128)(2,1)} %get-tuple-element.557.refs_0_.refs_2_), channel_id=1, source_target_pairs={{0,1},{1,0},{2,3},{3,2},{4,5},{5,4},{6,7},{7,6},{8,9},{9,8},{10,11... | collective-permute-start | bytes 1671176 | tf_op jit(solution)/shard_map/rows_a0_1/ppermute | solution.py:1038
  42.3 14.8 %collective-permute-start.7 = (bf16[272,1024]{1,0:T(8,128)(2,1)}, bf16[272,1024]{1,0:T(8,128)(2,1)S(1)}, u32[]{:S(2)}, u32[]{:S(2)}) collective-permute-start(bf16[272,1024]{1,0:T(8,128)(2,1)} %get-tuple-element.558.refs_3_), channel_id=1, source_target_pairs={{0,2},{1,3},{2,0},{3,1},{4,6},{5,7},{6,4},{7,5},{8,10},{9,11},{10,... | collective-permute-start | bytes 1671176 | tf_op jit(solution)/shard_map/rows_b0_2/ppermute | solution.py:1038
  42.6 15.1 %collective-permute-start.6 = (bf16[272,1024]{1,0:T(8,128)(2,1)}, bf16[272,1024]{1,0:T(8,128)(2,1)S(1)}, u32[]{:S(2)}, u32[]{:S(2)}) collective-permute-start(bf16[272,1024]{1,0:T(8,128)(2,1)} %get-tuple-element.558.refs_3_), channel_id=1, source_target_pairs={{0,1},{1,0},{2,3},{3,2},{4,5},{5,4},{6,7},{7,6},{8,9},{9,8},{10,11... | collective-permute-start | bytes 1671176 | tf_op jit(solution)/shard_map/rows_b0_1/ppermute | solution.py:1038
  92.5 36.7 %collective-permute-start.9 = (bf16[512,1536]{1,0:T(8,128)(2,1)}, bf16[512,1536]{1,0:T(8,128)(2,1)S(1)}, u32[]{:S(2)}, u32[]{:S(2)}) collective-permute-start(bf16[512,1536]{1,0:T(8,128)(2,1)} %get-tuple-element.613), channel_id=1, source_target_pairs={{0,8},{4,12},{8,0},{12,4},{16,24},{20,28},{24,16},{28,20},{1,9},{5... | collective-permute-start | bytes 4718600 | tf_op jit(solution)/shard_map/gate0_dp2/ppermute | solution.py:1038
  94.1 36.4 %collective-permute-start.10 = (bf16[512,1536]{1,0:T(8,128)(2,1)}, bf16[512,1536]{1,0:T(8,128)(2,1)S(1)}, u32[]{:S(2)}, u32[]{:S(2)}) collective-permute-start(bf16[512,1536]{1,0:T(8,128)(2,1)} %get-tuple-element.617), channel_id=1, source_target_pairs={{0,4},{4,0},{8,12},{12,8},{16,20},{20,16},{24,28},{28,24},{1,5},{5... | collective-permute-start | bytes 4718600 | tf_op jit(solution)/shard_map/up0_dp1/ppermute | solution.py:1038
  136.3 34.7 %collective-permute-start.12 = (bf16[256,1536]{1,0:T(8,128)(2,1)}, bf16[256,1536]{1,0:T(8,128)(2,1)S(1)}, u32[]{:S(2)}, u32[]{:S(2)}) collective-permute-start(bf16[256,1536]{1,0:T(8,128)(2,1)} %get-tuple-element.638), channel_id=1, source_target_pairs={{0,4},{4,0},{8,12},{12,8},{16,20},{20,16},{24,28},{28,24},{1,5},{5... | collective-permute-start | bytes 2359304 | tf_op jit(solution)/shard_map/gate0_dp1/ppermute | solution.py:1038
  137.8 33.2 %collective-permute-start.13 = (bf16[256,1536]{1,0:T(8,128)(2,1)}, bf16[256,1536]{1,0:T(8,128)(2,1)S(1)}, u32[]{:S(2)}, u32[]{:S(2)}) collective-permute-start(bf16[256,1536]{1,0:T(8,128)(2,1)} %get-tuple-element.655), channel_id=1, source_target_pairs={{0,8},{4,12},{8,0},{12,4},{16,24},{20,28},{24,16},{28,20},{1,9},{5... | collective-permute-start | bytes 2359304 | tf_op jit(solution)/shard_map/up0_dp2/ppermute | solution.py:1038
  139.9 52.8 %collective-permute-start.11 = (bf16[512,1280]{1,0:T(8,128)(2,1)}, bf16[512,1280]{1,0:T(8,128)(2,1)S(1)}, u32[]{:S(2)}, u32[]{:S(2)}) collective-permute-start(bf16[512,1280]{1,0:T(8,128)(2,1)} %get-tuple-element.635), channel_id=1, source_target_pairs={{0,8},{4,12},{8,0},{12,4},{16,24},{20,28},{24,16},{28,20},{1,9},{5... | collective-permute-start | bytes 3932168 | tf_op jit(solution)/shard_map/gate1_dp2/ppermute | solution.py:1038
  140.6 52.2 %collective-permute-start.14 = (bf16[512,1280]{1,0:T(8,128)(2,1)}, bf16[512,1280]{1,0:T(8,128)(2,1)S(1)}, u32[]{:S(2)}, u32[]{:S(2)}) collective-permute-start(bf16[512,1280]{1,0:T(8,128)(2,1)} %get-tuple-element.677), channel_id=1, source_target_pairs={{0,4},{4,0},{8,12},{12,8},{16,20},{20,16},{24,28},{28,24},{1,5},{5... | collective-permute-start | bytes 3932168 | tf_op jit(solution)/shard_map/up1_dp1/ppermute | solution.py:1038
  167.7 31.3 %collective-permute-start.15 = (bf16[2,336,1024]{2,1,0:T(8,128)(2,1)}, bf16[2,336,1024]{2,1,0:T(8,128)(2,1)S(1)}, u32[]{:S(2)}, u32[]{:S(2)}) collective-permute-start(bf16[2,336,1024]{2,1,0:T(8,128)(2,1)} %get-tuple-element.701), channel_id=1, source_target_pairs={{0,2},{1,3},{2,0},{3,1},{4,6},{5,7},{6,4},{7,5},{8,10},{9,11},{10,... | collective-permute-start | bytes 4128776 | tf_op jit(solution)/shard_map/grad_rows2/ppermute | solution.py:1038
  199.6 38.3 %collective-permute-start.20 = (bf16[256,1280]{1,0:T(8,128)(2,1)}, bf16[256,1280]{1,0:T(8,128)(2,1)}, u32[]{:S(2)}, u32[]{:S(2)}) collective-permute-start(bf16[256,1280]{1,0:T(8,128)(2,1)} %get-tuple-element.745), channel_id=1, source_target_pairs={{0,4},{4,0},{8,12},{12,8},{16,20},{20,16},{24,28},{28,24},{1,5},{5... | collective-permute-start | bytes 1966088 | tf_op jit(solution)/shard_map/gate1_dp1/ppermute | solution.py:1038
  201.1 36.9 %collective-permute-start.19 = (bf16[256,1280]{1,0:T(8,128)(2,1)}, bf16[256,1280]{1,0:T(8,128)(2,1)}, u32[]{:S(2)}, u32[]{:S(2)}) collective-permute-start(bf16[256,1280]{1,0:T(8,128)(2,1)} %get-tuple-element.744), channel_id=1, source_target_pairs={{0,8},{4,12},{8,0},{12,4},{16,24},{20,28},{24,16},{28,20},{1,9},{5... | collective-permute-start | bytes 1966088 | tf_op jit(solution)/shard_map/up1_dp2/ppermute | solution.py:1038
  209.5 39.1 %collective-permute-start.18 = (bf16[1408,512]{1,0:T(8,128)(2,1)}, bf16[1408,512]{1,0:T(8,128)(2,1)S(1)}, u32[]{:S(2)}, u32[]{:S(2)}) collective-permute-start(bf16[1408,512]{1,0:T(8,128)(2,1)} %get-tuple-element.716), channel_id=1, source_target_pairs={{0,8},{4,12},{8,0},{12,4},{16,24},{20,28},{24,16},{28,20},{1,9},{5... | collective-permute-start | bytes 4325384 | tf_op jit(solution)/shard_map/down0_dp2/ppermute | solution.py:1038
  210.1 38.5 %collective-permute-start.21 = (bf16[1408,512]{1,0:T(8,128)(2,1)}, bf16[1408,512]{1,0:T(8,128)(2,1)S(1)}, u32[]{:S(2)}, u32[]{:S(2)}) collective-permute-start(bf16[1408,512]{1,0:T(8,128)(2,1)} %get-tuple-element.759), channel_id=1, source_target_pairs={{0,4},{4,0},{8,12},{12,8},{16,20},{20,16},{24,28},{28,24},{1,5},{5... | collective-permute-start | bytes 4325384 | tf_op jit(solution)/shard_map/down1_dp1/ppermute | solution.py:1038
  248.7 23.9 %collective-permute-start.22 = (bf16[4,512,1024]{2,1,0:T(8,128)(2,1)}, bf16[4,512,1024]{2,1,0:T(8,128)(2,1)}, u32[]{:S(2)}, u32[]{:S(2)}) collective-permute-start(bf16[4,512,1024]{2,1,0:T(8,128)(2,1)} %get-tuple-element.795), channel_id=1, source_target_pairs={{0,1},{1,0},{2,3},{3,2},{4,5},{5,4},{6,7},{7,6},{8,9},{9,8},{10,11... | collective-permute-start | bytes 12582920 | tf_op jit(solution)/shard_map/dense_expert1/ppermute | solution.py:1038
  248.7 42.8 %collective-permute-start.24 = (bf16[2,128,1536]{2,1,0:T(8,128)(2,1)}, bf16[2,128,1536]{2,1,0:T(8,128)(2,1)}, u32[]{:S(2)}, u32[]{:S(2)}) collective-permute-start(bf16[2,128,1536]{2,1,0:T(8,128)(2,1)} %get-tuple-element.827), channel_id=1, source_target_pairs={{0,16},{4,20},{8,24},{12,28},{16,0},{20,4},{24,8},{28,12},{1,17},{... | collective-permute-start | bytes 2359304 | tf_op jit(solution)/shard_map/gate0_dp4/ppermute | solution.py:1038
  257.0 23.6 %collective-permute-start.26 = (bf16[704,512]{1,0:T(8,128)(2,1)}, bf16[704,512]{1,0:T(8,128)(2,1)S(1)}, u32[]{:S(2)}, u32[]{:S(2)}) collective-permute-start(bf16[704,512]{1,0:T(8,128)(2,1)} %get-tuple-element.829), channel_id=1, source_target_pairs={{0,4},{4,0},{8,12},{12,8},{16,20},{20,16},{24,28},{28,24},{1,5},{5... | collective-permute-start | bytes 2162696 | tf_op jit(solution)/shard_map/down0_dp1/ppermute | solution.py:1038
  257.5 34.0 %collective-permute-start.25 = (bf16[704,512]{1,0:T(8,128)(2,1)}, bf16[704,512]{1,0:T(8,128)(2,1)S(1)}, u32[]{:S(2)}, u32[]{:S(2)}) collective-permute-start(bf16[704,512]{1,0:T(8,128)(2,1)} %get-tuple-element.828), channel_id=1, source_target_pairs={{0,8},{4,12},{8,0},{12,4},{16,24},{20,28},{24,16},{28,20},{1,9},{5... | collective-permute-start | bytes 2162696 | tf_op jit(solution)/shard_map/down1_dp2/ppermute | solution.py:1038
  291.6 29.1 %collective-permute-start.29 = (bf16[2,256,1152]{2,1,0:T(8,128)(2,1)}, bf16[2,256,1152]{2,1,0:T(8,128)(2,1)S(1)}, u32[]{:S(2)}, u32[]{:S(2)}) collective-permute-start(bf16[2,256,1152]{2,1,0:T(8,128)(2,1)} %get-tuple-element.850), channel_id=1, source_target_pairs={{0,2},{1,3},{2,0},{3,1},{4,6},{5,7},{6,4},{7,5},{8,10},{9,11},{10,... | collective-permute-start | bytes 3538952 | tf_op jit(solution)/shard_map/out_q_expert2/ppermute | solution.py:1038
  292.9 24.0 %collective-permute-start.28 = (bf16[2,256,1024]{2,1,0:T(8,128)(2,1)}, bf16[2,256,1024]{2,1,0:T(8,128)(2,1)S(1)}, u32[]{:S(2)}, u32[]{:S(2)}) collective-permute-start(bf16[2,256,1024]{2,1,0:T(8,128)(2,1)} %get-tuple-element.846), channel_id=1, source_target_pairs={{0,4},{4,0},{8,12},{12,8},{16,20},{20,16},{24,28},{28,24},{1,5},{5... | collective-permute-start | bytes 3145736 | tf_op jit(solution)/shard_map/k_v_dp1/ppermute | solution.py:1038
  294.4 29.1 %collective-permute-start.30 = (bf16[2,128,1280]{2,1,0:T(8,128)(2,1)S(1)}, bf16[2,128,1280]{2,1,0:T(8,128)(2,1)S(1)}, u32[]{:S(2)}, u32[]{:S(2)}) collective-permute-start(bf16[2,128,1280]{2,1,0:T(8,128)(2,1)S(1)} %copy-done.42), channel_id=1, source_target_pairs={{0,16},{4,20},{8,24},{12,28},{16,0},{20,4},{24,8},{28,12},{1,17},{... | collective-permute-start | bytes 1966088 | tf_op jit(solution)/shard_map/gate1_dp4/ppermute | solution.py:1038
  307.5 50.9 %collective-permute-start.27 = (bf16[2,320,1024]{2,1,0:T(8,128)(2,1)}, bf16[2,320,1024]{2,1,0:T(8,128)(2,1)S(1)}, u32[]{:S(2)}, u32[]{:S(2)}) collective-permute-start(bf16[2,320,1024]{2,1,0:T(8,128)(2,1)} %get-tuple-element.844), channel_id=1, source_target_pairs={{0,2},{1,3},{2,0},{3,1},{4,6},{5,7},{6,4},{7,5},{8,10},{9,11},{10,... | collective-permute-start | bytes 3932168 | tf_op jit(solution)/shard_map/produced_rows2/ppermute | solution.py:1038
  331.1 22.9 %collective-permute-start.32 = (bf16[2,128,1152]{2,1,0:T(8,128)(2,1)}, bf16[2,128,1152]{2,1,0:T(8,128)(2,1)S(1)}, u32[]{:S(2)}, u32[]{:S(2)}) collective-permute-start(bf16[2,128,1152]{2,1,0:T(8,128)(2,1)} %get-tuple-element.904), channel_id=1, source_target_pairs={{0,4},{4,0},{8,12},{12,8},{16,20},{20,16},{24,28},{28,24},{1,5},{5... | collective-permute-start | bytes 1769480 | tf_op jit(solution)/shard_map/out_q_dp1/ppermute | solution.py:1038
  331.7 22.3 %collective-permute-start.31 = (bf16[2,128,1024]{2,1,0:T(8,128)(2,1)}, bf16[2,128,1024]{2,1,0:T(8,128)(2,1)S(1)}, u32[]{:S(2)}, u32[]{:S(2)}) collective-permute-start(bf16[2,128,1024]{2,1,0:T(8,128)(2,1)} %get-tuple-element.896), channel_id=1, source_target_pairs={{0,8},{4,12},{8,0},{12,4},{16,24},{20,28},{24,16},{28,20},{1,9},{5... | collective-permute-start | bytes 1572872 | tf_op jit(solution)/shard_map/k_v_dp2/ppermute | solution.py:1038
  333.3 40.7 %collective-permute-start.37 = (bf16[2,352,512]{2,1,0:T(8,128)(2,1)S(1)}, bf16[2,352,512]{2,1,0:T(8,128)(2,1)S(1)}, u32[]{:S(2)}, u32[]{:S(2)}) collective-permute-start(bf16[2,352,512]{2,1,0:T(8,128)(2,1)S(1)} %copy-done.41), channel_id=1, source_target_pairs={{0,16},{4,20},{8,24},{12,28},{16,0},{20,4},{24,8},{28,12},{1,17},{... | collective-permute-start | bytes 2162696 | tf_op jit(solution)/shard_map/down0_dp4/ppermute | solution.py:1038
  359.0 15.0 %collective-permute-start.36 = (bf16[2,64,1152]{2,1,0:T(8,128)(2,1)}, bf16[2,64,1152]{2,1,0:T(8,128)(2,1)S(1)}, u32[]{:S(2)}, u32[]{:S(2)}) collective-permute-start(bf16[2,64,1152]{2,1,0:T(8,128)(2,1)} %get-tuple-element.940), channel_id=1, source_target_pairs={{0,8},{4,12},{8,0},{12,4},{16,24},{20,28},{24,16},{28,20},{1,9},{5... | collective-permute-start | bytes 884744 | tf_op jit(solution)/shard_map/out_q_dp2/ppermute | solution.py:1038
  380.1 14.6 %collective-permute-start.38 = (bf16[2,32,1152]{2,1,0:T(8,128)(2,1)S(1)}, bf16[2,32,1152]{2,1,0:T(8,128)(2,1)S(1)}, u32[]{:S(2)}, u32[]{:S(2)}) collective-permute-start(bf16[2,32,1152]{2,1,0:T(8,128)(2,1)S(1)} %copy-done.43), channel_id=1, source_target_pairs={{0,16},{4,20},{8,24},{12,28},{16,0},{20,4},{24,8},{28,12},{1,17},{... | collective-permute-start | bytes 442376 | tf_op jit(solution)/shard_map/out_q_dp4/ppermute | solution.py:1038
  380.2 14.5 %collective-permute-start.39 = (bf16[2,32,1024]{2,1,0:T(8,128)(2,1)S(1)}, bf16[2,32,1024]{2,1,0:T(8,128)(2,1)S(1)}, u32[]{:S(2)}, u32[]{:S(2)}) collective-permute-start(bf16[2,32,1024]{2,1,0:T(8,128)(2,1)S(1)} %copy-done.44), channel_id=1, source_target_pairs={{0,16},{4,20},{8,24},{12,28},{16,0},{20,4},{24,8},{28,12},{1,17},{... | collective-permute-start | bytes 393224 | tf_op jit(solution)/shard_map/k_v_dp4/ppermute | solution.py:1038
  (53 other events, 322.3 us)

commit v5 on v4

--- a/solution.py
+++ b/solution.py
@@ -82,7 +82,7 @@
 TIMES = {
     ("down_grads", 0): 10.0,
     ("dense_terms", 0): 13.1,
-    ("fold", 2): 2.0,
+    ("fold", 1): 2.0,
 }
 
 
@@ -999,29 +999,25 @@
     )
 
 
-def last_sums_kernel(token_ref, *refs, experts, counts):
-    pairs, outs = refs[:4], refs[4:]
-    first = pairs[0][...].astype(F32) + pairs[1][...].astype(F32)
-    second = pairs[2][...].astype(F32) + pairs[3][...].astype(F32)
-    width = second.shape[2]
-    outs[0][...] = first[0, :, 0:width]
-    outs[1][...] = first[1, :, 0:width]
-    outs[2][...] = second[0]
-    outs[3][...] = second[1]
-    small = first[0, :, width:] + token_ref[...]
+def last_sums_kernel(token_ref, keep_ref, got_ref, *outs, experts, counts):
+    total = keep_ref[...].astype(F32) + got_ref[...].astype(F32)
+    width = outs[0].shape[1]
+    for i in range(2):
+        outs[i][...] = total[i, :, 0:width]
+        outs[2 + i][...] = total[i, :, width + LANES :]
+    small = total[0, :, width : width + LANES] + token_ref[...]
     outs[4][...] = small[:, 0:experts]
     flat = small.T
     for i, count in enumerate(counts):
         outs[5 + i][...] = flat[TAIL // 2 + i : TAIL // 2 + i + 1, 0:count]
 
 
-def last_sums(token, pairs, experts, counts):
-    rows, width = pairs[2].shape[1:]
-    args = (token, *pairs)
+def last_sums(token, keep, got, width, experts, counts):
+    rows = keep.shape[1]
     return call(
         functools.partial(last_sums_kernel, experts=experts, counts=counts),
-        args,
-        [pl.BlockSpec(memory_space=pltpu.VMEM)] * len(args),
+        (token, keep, got),
+        [pl.BlockSpec(memory_space=pltpu.VMEM)] * 3,
         out_shape=[jax.ShapeDtypeStruct((rows, width), F32)] * 4
         + [jax.ShapeDtypeStruct((rows, experts), F32)]
         + [jax.ShapeDtypeStruct((1, count), F32) for count in counts],
@@ -1093,8 +1089,11 @@
         for start in (0, rows):
             out = outs.pop(0)
             cut = [lax.slice_in_dim(v, start, start + rows, axis=dim).astype(BF) for v in total]
-            if width == 1:
-                out[...] = cut[0]
+            if len(out.shape) == len(cut[0].shape):
+                at_lane = 0
+                for part in cut:
+                    out[..., at_lane : at_lane + part.shape[-1]] = part
+                    at_lane += part.shape[-1]
             else:
                 for i in range(width):
                     out[i] = cut[i]
@@ -1117,8 +1116,11 @@
         else:
             shape = list(got.shape)
             shape[unit.dim] //= 2
-            if len(group) > 1:
+            stacked = len(group) > 1 and len(shape) == 2
+            if stacked:
                 shape = [len(group)] + shape
+            else:
+                shape[-1] = sum(member.keep.shape[-1] for member in group)
             shapes += [jax.ShapeDtypeStruct(tuple(shape), BF)] * 2
     args = order.enter(args)
     outs = list(
@@ -1137,7 +1139,7 @@
         unit.keep = outs.pop(0)
         if not last:
             unit.to_send = outs.pop(0)
-        if width > 1:
+        if width > 1 and unit.keep.ndim > group[1].keep.ndim:
             unit.dim += 1
         if unit.route and unit not in hold:
             unit.start()
@@ -1326,29 +1328,28 @@
         unit.start()
     gh_second = order.leave(cot_hidden_more(order.enter(cot_rows), w_down, starts[1]))
     _, (hid, hid_t, gg, gu) = expert_part(1, (x_all, x_t, gate_all), filled)
-    fold(*units[0])
     for unit in units[1]:
         unit.start()
     back_low, back_high = order.leave(expert_b(order.enter(gg), gu, scs, w_gate, w_up, experts))
     backs = Return(order, back_low, back_high, "expert", ep_size, "grad_rows")
     first, second = units[0][0], units[1][0]
-    fold(units[0], hold=units[0])
+    fold(*units[0])
     down_parts = order.leave(down_grads(order.enter(hid_t), grad_cots, place_z, place_x))
     down_units = tuple(
         Halving(order, down_parts[2 * i], down_parts[2 * i + 1], 0, dp_route(bits), f"down{i}")
         for i, bits in enumerate((z_order, dp_order))
     )
     down = down_units[0]
-    fold(*units[1])
+    fold(*units[1], units[0], hold=units[0])
     code_xor, chances_xor, wr_xor = order.enter((by_xor(code), padded(by_xor(chances)), padded(by_xor(w_router.T))))
     backs.fold()
-    att_t, normed_t = order.leave(sorted_rows(place_q, place_k, order.enter(tokens), gain_attn, attended))
+    att_t, normed_t = order.leave(sorted_rows(place_q, place_k, tokens, gain_attn, order.enter(attended)))
     backs.finish()
     for unit in down_units:
         unit.start()
     grad_mid, branch, grad_att, gain_moe_term, router_term = order.leave(
         moe_bwd(
-            cotangent, order.enter(middle), gain_moe, normed_moe, chances_xor, wr_xor, code_xor, code_xor.T, w_out,
+            cotangent, middle, gain_moe, normed_moe, chances_xor, wr_xor, code_xor, code_xor.T, w_out,
             backs.slots,
         )
     )
@@ -1390,7 +1391,7 @@
         for i, (bits, name) in enumerate(((q_bits, "out_q"), (k_bits, "k_v")))
     ]
     out_q, k_v = dense
-    arrive(*down_units, first)
+    arrive(down, first)
     k_v.start()
     out_q.start()
     second.start()
@@ -1406,14 +1407,13 @@
     returned.fold()
     returned.finish()
     layer_out = order.leave(layer_output(middle, chances_xor, code_xor.T, returned.slots))
-    fold(k_v, out_q, down)
-    rest = [first, second, down, *dense]
-    while any(unit.route[1:] for unit in rest) or down.route:
-        fold(*[unit for unit in rest if unit.route])
+    while len(out_q.route) > 2:
+        fold(*[unit for unit in (out_q, k_v, down) if unit.route])
+    fold(*[(out_q, k_v)] + ([down] if down.route else []))
     down_grad = order.leave(jnp.concatenate([down.keep[0], down.keep[1]], axis=1)[None])
-    pairs = order.leave([out_q.keep, out_q.got, k_v.keep, k_v.got])
+    pairs = order.leave([out_q.keep, out_q.got])
     out_grad, query_grad, key_grad, value_grad, router_grad, *gains = last_sums(
-        order.token, pairs, experts, (share, share, bias_share)
+        order.token, *pairs, width, experts, (share, share, bias_share)
     )
     gain_attn_grad, gain_moe_grad, bias_grad = [value.reshape(-1) for value in gains]
     return (

time: 407 us -> 397 us (0.975)
  waiting for transfers between devices: 74.7 us -> 67.5 us
    ppermute x40 -> x39, waiting for transfers between devices: 74.7 us -> 67.5 us  [swap(): return lax.ppermute(value, axis, [(i, i ^ mask) for i in range(size)])]
    pallas_call x24 -> x23, Pallas kernels: 256 us -> 254 us  [call(): pl.pallas_call(kernel, in_specs=list(in_specs), compiler_params=params(),...]
    unnamed x91 -> x85, local copies, waits for them, and re-layouts: 16.7 us -> 15.9 us
    ppermute x40 -> x39, starting transfers between devices: 34.6 us -> 35 us  [swap(): return lax.ppermute(value, axis, [(i, i ^ mask) for i in range(size)])]
  transfers between devices with their start and end apart: 40 -> 39, of which waited for: 17 -> 15; matrix products, arithmetic and copies ran while one was open for 4% -> 4% of each run, Pallas kernels for 53% -> 55%
where the time goes in v5:
time: 397 us; the launch traced here: 390 us
  Pallas kernels  254 us (64%)
  waiting for transfers between devices  67.5 us (17%)
  starting transfers between devices  35 us (9%)
  local copies, waits for them, and re-layouts  26.2 us (7%)
  other arithmetic  6.01 us (2%)
    pallas_call x23, Pallas kernels, call(): pl.pallas_call(kernel, in_specs=list(in_specs), compiler_params=params(),...  254 us
    ppermute x39, waiting for transfers between devices, swap(): return lax.ppermute(value, axis, [(i, i ^ mask) for i in range(size)])  67.5 us
    ppermute x39, starting transfers between devices, swap(): return lax.ppermute(value, axis, [(i, i ^ mask) for i in range(size)])  35 us
    unnamed x85, local copies, waits for them, and re-layouts  15.9 us
  transfers between devices with their start and end apart: 39, of which 15 were waited for; matrix products, arithmetic and copies ran while one was open for 4% of the time, Pallas kernels for 55%

profile of v5, /device:TPU:0, one launch (start us, length us, event | category | flops | bytes accessed | tf_op | source)
XLA Modules:
  0.0 390.2 jit_solution(18151722988248126482)
XLA Ops:
  0.6 3.0 collective-permute-start
  3.7 15.6 %attn_first.1 = (bf16[512,1024]{1,0:T(8,128)(2,1)}, bf16[512,1024]{1,0:T(8,128)(2,1)}, bf16[512,1024]{1,0:T(8,128)(2,1)}, f32[4,4,512]{2,1,0:T(4,128)}, f32[1,12...) custom-call(bf16[512,1024]{1,0:T(8,128)(2,1)} %tok_ref.7, ...), custom_call_target="tpu_custom_call" | custom-call | flops 115000000 | bytes 100000 | tf_op jit(solution)/shard_map/attn_first/pallas_call | solution.py:100
  19.3 7.8 %collective-permute-done.refs_6_ = bf16[512,1024]{1,0:T(8,128)(2,1)} collective-permute-done((bf16[512,1024]{1,0:T(8,128)(2,1)}, bf16[512,1024]{1,0:T(8,128)(2,1)}, u32[]{:S(2)}, u32[]{:S(2)}) %collective-permute-start) | collective-permute-done | bytes 1048608 | tf_op jit(solution)/shard_map/cot0_2/ppermute | solution.py:1034
  29.4 12.3 %attn_second.1 = (bf16[512,1024]{1,0:T(8,128)(2,1)}, f32[4,4,512]{2,1,0:T(4,128)}, f32[512,1024]{1,0:T(8,128)}, bf16[512,1024]{1,0:T(8,128)(2,1)}, f32[16,512]{1,0:T(8,128)}, /*index=5*/bf16[272,1024]{1,0:T(8,128)(2,1)}) custom-call(bf16[512,1024]{1,0:T(8,128)(2,1)} %tok_ref.7, ...), custom_call_target="tpu_custom_call", output_to_operand_aliasing={{0}: (9, {}), {1}: (10, {}), {2}: (11, {}), {3}: (12, {}), ... | custom-call | flops 115000000 | bytes 100000 | tf_op jit(solution)/shard_map/attn_second/pallas_call | solution.py:100
  44.8 11.2 %cot_hidden.1 = (bf16[1280,1536]{1,0:T(8,128)(2,1)}, bf16[1280,1024]{1,0:T(8,128)(2,1)}) custom-call(s32[1]{0:T(128)} %bitcast.9.me_ref.refs_0_, bf16[272,1024]{1,0:T(8,128)(2,1)} %get-tuple-element.543.refs_0_.refs_2_, bf16[272,1024]{1,0:T(8,128)(2,1)} %copy-done.4, bf16[272,1024]{1,0:T(8,128)(2,1)} %copy-done.3, bf16[272,1024]{1,0:T(8,128)(2,1)} %copy-done.5, ...), custom_call_target="tpu_custom_call" | custom-call | flops 115000000 | bytes 100000 | tf_op jit(solution)/shard_map/cot_hidden/pallas_call | solution.py:100
  60.0 32.8 %expert_grads.2 = (bf16[1280,1024]{1,0:T(8,128)(2,1)}, bf16[1024,1280]{1,0:T(8,128)(2,1)}, f32[1280,128]{1,0:T(8,128)}, bf16[1280,1024]{1,0:T(8,128)(2,1)}, bf16...) custom-call(s32[1]{0:T(128)} %bitcast.9.me_ref.refs_0_, ...), custom_call_target="tpu_custom_call" | custom-call | flops 115000000 | bytes 100000 | tf_op jit(solution)/shard_map/expert_grads/pallas_call | solution.py:100
  96.6 8.1 %cot_hidden_more.1.refs_3_ = bf16[1280,1280]{1,0:T(8,128)(2,1)} custom-call(bf16[1280,1024]{1,0:T(8,128)(2,1)} %get-tuple-element.575.refs_10_.rows_ref, bf16[1,2816,1024]{2,1,0:T(8,128)(2,1)} %wd_ref.3), custom_call_target="tpu_custom_call" | custom-call | flops 115000000 | bytes 100000 | tf_op jit(solution)/shard_map/cot_hidden_more/pallas_call | solution.py:100
  104.7 25.2 %expert_grads.3 = (bf16[512,1280]{1,0:T(8,128)(2,1)}, bf16[512,1280]{1,0:T(8,128)(2,1)}, bf16[512,1280]{1,0:T(8,128)(2,1)}, bf16[512,1280]{1,0:T(8,128)(2,1)}, f...) custom-call(bf16[1280,1024]{1,0:T(8,128)(2,1)} %get-tuple-element.57, ...), custom_call_target="tpu_custom_call", output_to_operand_aliasing={{5}: (6, {}), {6}: (7, {}), {7}: (8, {}), {8}: (9, {})} | custom-call | flops 115000000 | bytes 100000 | tf_op jit(solution)/shard_map/expert_grads/pallas_call | solution.py:100
  131.8 25.4 %expert_input_grad.1 = (bf16[2,336,1024]{2,1,0:T(8,128)(2,1)}, bf16[2,336,1024]{2,1,0:T(8,128)(2,1)}) custom-call(bf16[1280,2816]{1,0:T(8,128)(2,1)} %get-tuple-element.607.gg_ref, bf16[1280,2816]{1,0:T(8,128)(2,1)} %get-tuple-element.608.gu_ref, f32[1280,128]{1,0:T(8,128)} %get-tuple-element.609.refs_0_, f32[1280,128]{1,0:T(8,128)} %get-tuple-element.610.refs_1_, ...), custom_call_target="tpu_custom_call" | custom-call | flops 115000000 | bytes 100000 | tf_op jit(solution)/shard_map/expert_input_grad/pallas_call | solution.py:100
  161.8 4.8 %fold.6 = (bf16[256,1536]{1,0:T(8,128)(2,1)}, bf16[256,1536]{1,0:T(8,128)(2,1)}, bf16[256,1536]{1,0:T(8,128)(2,1)}, bf16[256,1536]{1,0:T(8,128)(2,1)}) custom-call(bf16[512,1536]{1,0:T(8,128)(2,1)} %get-tuple-element.623.refs_0_, bf16[512,1536]{1,0:T(8,128)(2,1)} %copy-done.6, bf16[512,1536]{1,0:T(8,128)(2,1)} %get-tuple-element.625.refs_2_, ...), custom_call_target="tpu_custom_call" | custom-call | flops 115000000 | bytes 100000 | tf_op jit(solution)/shard_map/fold/pallas_call | solution.py:100
  169.6 16.8 %down_grads.1 = (bf16[1408,512]{1,0:T(8,128)(2,1)}, bf16[1408,512]{1,0:T(8,128)(2,1)}, bf16[1408,512]{1,0:T(8,128)(2,1)}, bf16[1408,512]{1,0:T(8,128)(2,1)}) custom-call(s32[8]{0:T(128)} %get-tuple-element.1009.place_a_ref, s32[8]{0:T(128)} %get-tuple-element.542.refs_1_.place_b_ref, bf16[2816,1280]{1,0:T(8,128)(2,1)} %get-tuple-element.637.hidt_ref, ...), custom_call_target="tpu_custom_call" | custom-call | flops 11500000256 | bytes 100000 | tf_op jit(solution)/shard_map/down_grads/pallas_call | solution.py:100
  189.1 5.5 %fold.7 = (bf16[256,1280]{1,0:T(8,128)(2,1)}, bf16[256,1280]{1,0:T(8,128)(2,1)}, bf16[256,1280]{1,0:T(8,128)(2,1)}, bf16[256,1280]{1,0:T(8,128)(2,1)}, bf16[2,12...) custom-call(bf16[512,1280]{1,0:T(8,128)(2,1)} %get-tuple-element.659.refs_0_, bf16[512,1280]{1,0:T(8,128)(2,1)} %copy-done.35, ...), custom_call_target="tpu_custom_call" | custom-call | flops 2300000000 | bytes 100000 | tf_op jit(solution)/shard_map/fold/pallas_call | solution.py:100
  196.8 4.7 %sorted_rows.1 = (bf16[1024,512]{1,0:T(8,128)(2,1)}, bf16[2,1024,512]{2,1,0:T(8,128)(2,1)}) custom-call(s32[32]{0:T(128)} %get-tuple-element.1008.pq_ref.place_ref, s32[32]{0:T(128)} %get-tuple-element.1007.pk_ref, bf16[512,1024]{1,0:T(8,128)(2,1)} %tok_ref.7, f32[1,1024]{1,0:T(1,128)} %bitcast.46, bf16[512,1024]{1,0:T(8,128)(2,1)} %get-tuple-element.694.att_ref), custom_call_target="tpu_custom_call" | custom-call | flops 115000000 | bytes 100000 | tf_op jit(solution)/shard_map/sorted_rows/pallas_call | solution.py:100
  207.2 10.2 %moe_bwd.1 = (f32[512,1024]{1,0:T(8,128)}, bf16[512,1024]{1,0:T(8,128)(2,1)}, bf16[512,1024]{1,0:T(8,128)(2,1)}, f32[1,1024]{1,0:T(1,128)}, f32[16,1024]{1,0:T(8,128)}) custom-call(bf16[512,1024]{1,0:T(8,128)(2,1)} %cot_ref.1, f32[512,1024]{1,0:T(8,128)} %get-tuple-element.507.mid_ref, f32[1,1024]{1,0:T(1,128)} %bitcast.44, ...), custom_call_target="tpu_custom_call" | custom-call | flops 115000000 | bytes 100000 | tf_op jit(solution)/shard_map/moe_bwd/pallas_call | solution.py:100
  217.3 16.2 %attn_bwd.1 = (bf16[512,1024]{1,0:T(8,128)(2,1)}, bf16[512,1024]{1,0:T(8,128)(2,1)}, bf16[512,1024]{1,0:T(8,128)(2,1)}, f32[4,4,512]{2,1,0:T(4,128)}) custom-call(bf16[512,1024]{1,0:T(8,128)(2,1)} %get-tuple-element.491.qs_ref, bf16[512,1024]{1,0:T(8,128)(2,1)} %get-tuple-element.492.k_ref, bf16[512,1024]{1,0:T(8,128)(2,1)} %get-tuple-element.493.v_ref, ...), custom_call_target="tpu_custom_call" | custom-call | flops 115000000 | bytes 100000 | tf_op jit(solution)/shard_map/attn_bwd/pallas_call | solution.py:100
  233.6 9.3 %dense_terms.1 = (bf16[4,512,1024]{2,1,0:T(8,128)(2,1)}, bf16[4,512,1024]{2,1,0:T(8,128)(2,1)}) custom-call(bf16[1024,512]{1,0:T(8,128)(2,1)} %get-tuple-element.701.att_ref, bf16[2,1024,512]{2,1,0:T(8,128)(2,1)} %get-tuple-element.702.rows_ref, bf16[512,1024]{1,0:T(8,128)(2,1)} %get-tuple-element.715.branch_ref, ...), custom_call_target="tpu_custom_call" | custom-call | flops 15064999936 | bytes 100000 | tf_op jit(solution)/shard_map/dense_terms/pallas_call | solution.py:100
  243.4 2.7 collective-permute-start.24
  246.1 5.6 %fold.8 = (bf16[704,512]{1,0:T(8,128)(2,1)}, bf16[704,512]{1,0:T(8,128)(2,1)}, bf16[704,512]{1,0:T(8,128)(2,1)}, bf16[704,512]{1,0:T(8,128)(2,1)}, bf16[2,128,12...) custom-call(bf16[1408,512]{1,0:T(8,128)(2,1)} %get-tuple-element.760.refs_0_, bf16[1408,512]{1,0:T(8,128)(2,1)} %copy-done.7, ...), custom_call_target="tpu_custom_call" | custom-call | flops 115000000 | bytes 100000 | tf_op jit(solution)/shard_map/fold/pallas_call | solution.py:100
  255.7 10.9 %norm_bwd.1 = (f32[512,1024]{1,0:T(8,128)}, bf16[512,128]{1,0:T(8,128)(2,1)}, bf16[512,128]{1,0:T(8,128)(2,1)}) custom-call(s32[32]{0:T(128)} %get-tuple-element.1008.pq_ref.place_ref, bf16[512,1024]{1,0:T(8,128)(2,1)} %tok_ref.7, f32[1,1024]{1,0:T(1,128)} %bitcast.47, f32[512,1024]{1,0:T(8,128)} %get-tuple-element.778.gmid_ref, ...), custom_call_target="tpu_custom_call" | custom-call | flops 115000000 | bytes 100000 | tf_op jit(solution)/shard_map/norm_bwd/pallas_call | solution.py:100
  269.0 5.8 %fold_first.1 = (bf16[2,256,1152]{2,1,0:T(8,128)(2,1)}, bf16[2,256,1152]{2,1,0:T(8,128)(2,1)}, bf16[2,256,1024]{2,1,0:T(8,128)(2,1)}, bf16[2,256,1024]{2,1,0:T(8,128)(2,1)}) custom-call(bf16[4,512,1024]{2,1,0:T(8,128)(2,1)} %get-tuple-element.796.keep_ref, bf16[4,512,1024]{2,1,0:T(8,128)(2,1)} %collective-permute-done.22.got_ref, ...), custom_call_target="tpu_custom_call" | custom-call | flops 115000000 | bytes 100000 | tf_op jit(solution)/shard_map/fold_first/pallas_call | solution.py:100
  274.8 6.5 %collective-permute-done.24.refs_9_ = bf16[2,128,1536]{2,1,0:T(8,128)(2,1)} collective-permute-done((bf16[2,128,1536]{2,1,0:T(8,128)(2,1)}, bf16[2,128,1536]{2,1,0:T(8,128)(2,1)}, u32[]{:S(2)}, u32[]{:S(2)}) %collective-permute-start.24) | collective-permute-done | bytes 786464 | tf_op jit(solution)/shard_map/gate0_dp4/ppermute | solution.py:1034
  284.2 3.1 collective-permute-start.30
  287.3 12.9 %produced_rows.1 = (bf16[2,320,1024]{2,1,0:T(8,128)(2,1)}, bf16[2,320,1024]{2,1,0:T(8,128)(2,1)}) custom-call(bf16[1280,2816]{1,0:T(8,128)(2,1)} %get-tuple-element.817.hid_ref, bf16[1,2816,1024]{2,1,0:T(8,128)(2,1)} %wd_ref.3), custom_call_target="tpu_custom_call" | custom-call | flops 115000000 | bytes 100000 | tf_op jit(solution)/shard_map/produced_rows/pallas_call | solution.py:100
  302.1 5.6 %collective-permute-done.27.refs_1_ = bf16[2,256,1024]{2,1,0:T(8,128)(2,1)S(1)} collective-permute-done((bf16[2,256,1024]{2,1,0:T(8,128)(2,1)}, bf16[2,256,1024]{2,1,0:T(8,128)(2,1)S(1)}, u32[]{:S(2)}, u32[]{:S(2)}) %collective-permute-start.27) | collective-permute-done | bytes 1048608 | tf_op jit(solution)/shard_map/k_v_dp1/ppermute | solution.py:1034
  310.3 5.4 %collective-permute-done.29.refs_7_ = bf16[704,512]{1,0:T(8,128)(2,1)S(1)} collective-permute-done((bf16[704,512]{1,0:T(8,128)(2,1)S(1)}, bf16[704,512]{1,0:T(8,128)(2,1)S(1)}, u32[]{:S(2)}, u32[]{:S(2)}) %collective-permute-start.29) | collective-permute-done | bytes 720928 | tf_op jit(solution)/shard_map/down1_dp2/ppermute | solution.py:1034
  317.5 6.8 %fold.9 = (bf16[2,128,1024]{2,1,0:T(8,128)(2,1)}, bf16[2,128,1024]{2,1,0:T(8,128)(2,1)}, bf16[2,128,1152]{2,1,0:T(8,128)(2,1)}, bf16[2,128,1152]{2,1,0:T(8,128)(...) custom-call(bf16[2,256,1024]{2,1,0:T(8,128)(2,1)} %get-tuple-element, ...), custom_call_target="tpu_custom_call" | custom-call | flops 115000000 | bytes 100000 | tf_op jit(solution)/shard_map/fold/pallas_call | solution.py:100
  326.5 2.7 collective-permute-start.37
  331.7 15.3 %collective-permute-done.31.refs_1_ = bf16[2,128,1024]{2,1,0:T(8,128)(2,1)S(1)} collective-permute-done((bf16[2,128,1024]{2,1,0:T(8,128)(2,1)}, bf16[2,128,1024]{2,1,0:T(8,128)(2,1)S(1)}, u32[]{:S(2)}, u32[]{:S(2)}) %collective-permute-start.31) | collective-permute-done | bytes 524320 | tf_op jit(solution)/shard_map/k_v_dp2/ppermute | solution.py:1034
  355.3 6.3 %layer_output.1 = bf16[512,1024]{1,0:T(8,128)(2,1)} custom-call(f32[512,1024]{1,0:T(8,128)} %get-tuple-element.507.mid_ref, f32[16,512]{1,0:T(8,128)} %select_maximum_fusion.3.ch_ref, s32[512,4]{1,0:T(8,128)} %bitcast.39, bf16[2,320,1024]{2,1,0:T(8,128)(2,1)} %get-tuple-element.821.refs_0_, bf16[1,320,1024]{2,1,0:T(8,128)(2,1)} %copy-done.19, ...), custom_call_target="tpu_custom_call" | custom-call | flops 115000000 | bytes 100000 | tf_op jit(solution)/shard_map/layer_output/pallas_call | solution.py:100
  361.5 4.5 %collective-permute-done.35.refs_1_ = bf16[2,64,1152]{2,1,0:T(8,128)(2,1)S(1)} collective-permute-done((bf16[2,64,1152]{2,1,0:T(8,128)(2,1)}, bf16[2,64,1152]{2,1,0:T(8,128)(2,1)S(1)}, u32[]{:S(2)}, u32[]{:S(2)}) %collective-permute-start.35) | collective-permute-done | bytes 294944 | tf_op jit(solution)/shard_map/out_q_dp2/ppermute | solution.py:1034
  367.8 3.0 fold.11
  373.8 12.2 %collective-permute-done.38.got_ref = bf16[2,32,2176]{2,1,0:T(8,128)(2,1)S(1)} collective-permute-done((bf16[2,32,2176]{2,1,0:T(8,128)(2,1)}, bf16[2,32,2176]{2,1,0:T(8,128)(2,1)S(1)}, u32[]{:S(2)}, u32[]{:S(2)}) %collective-permute-start.38) | collective-permute-done | bytes 278560 | tf_op jit(solution)/shard_map/out_q_dp4/ppermute | solution.py:1034
  (182 shorter events, 70.6 us)
Async XLA Ops:
  0.6 26.5 %collective-permute-start = (bf16[512,1024]{1,0:T(8,128)(2,1)}, bf16[512,1024]{1,0:T(8,128)(2,1)}, u32[]{:S(2)}, u32[]{:S(2)}) collective-permute-start(bf16[512,1024]{1,0:T(8,128)(2,1)} %cot_ref.1), channel_id=1, source_target_pairs={{0,2},{1,3},{2,0},{3,1},{4,6},{5,7},{6,4},{7,5},{8,10},{9,11},{10,... | collective-permute-start | bytes 3145736 | tf_op jit(solution)/shard_map/cot0_2/ppermute | solution.py:1034
  27.2 14.6 %collective-permute-start.2 = (bf16[272,1024]{1,0:T(8,128)(2,1)}, bf16[272,1024]{1,0:T(8,128)(2,1)S(1)}, u32[]{:S(2)}, u32[]{:S(2)}) collective-permute-start(bf16[272,1024]{1,0:T(8,128)(2,1)} %get-tuple-element.543.refs_0_.refs_2_), channel_id=1, source_target_pairs={{0,2},{1,3},{2,0},{3,1},{4,6},{5,7},{6,4},{7,5},{8,10},{9,11},{10,... | collective-permute-start | bytes 1671176 | tf_op jit(solution)/shard_map/rows_a0_2/ppermute | solution.py:1034
  28.9 13.8 %collective-permute-start.4 = (bf16[512,1024]{1,0:T(8,128)(2,1)S(1)}, bf16[512,1024]{1,0:T(8,128)(2,1)}, u32[]{:S(2)}, u32[]{:S(2)}) collective-permute-start(bf16[512,1024]{1,0:T(8,128)(2,1)S(1)} %copy-done), channel_id=1, source_target_pairs={{0,1},{1,0},{2,3},{3,2},{4,5},{5,4},{6,7},{7,6},{8,9},{9,8},{10,11... | collective-permute-start | bytes 3145736 | tf_op jit(solution)/shard_map/cot0_1/ppermute | solution.py:1034
  28.9 13.9 %collective-permute-start.5 = (bf16[512,1024]{1,0:T(8,128)(2,1)}, bf16[512,1024]{1,0:T(8,128)(2,1)}, u32[]{:S(2)}, u32[]{:S(2)}) collective-permute-start(bf16[512,1024]{1,0:T(8,128)(2,1)} %collective-permute-done.refs_6_), channel_id=1, source_target_pairs={{0,1},{1,0},{2,3},{3,2},{4,5},{5,4},{6,7},{7,6},{8,9},{9,8},{10,11... | collective-permute-start | bytes 3145736 | tf_op jit(solution)/shard_map/cot2_1/ppermute | solution.py:1034
  29.4 13.4 %collective-permute-start.1 = (bf16[272,1024]{1,0:T(8,128)(2,1)}, bf16[272,1024]{1,0:T(8,128)(2,1)S(1)}, u32[]{:S(2)}, u32[]{:S(2)}) collective-permute-start(bf16[272,1024]{1,0:T(8,128)(2,1)} %get-tuple-element.543.refs_0_.refs_2_), channel_id=1, source_target_pairs={{0,1},{1,0},{2,3},{3,2},{4,5},{5,4},{6,7},{7,6},{8,9},{9,8},{10,11... | collective-permute-start | bytes 1671176 | tf_op jit(solution)/shard_map/rows_a0_1/ppermute | solution.py:1034
  42.4 14.8 %collective-permute-start.7 = (bf16[272,1024]{1,0:T(8,128)(2,1)}, bf16[272,1024]{1,0:T(8,128)(2,1)S(1)}, u32[]{:S(2)}, u32[]{:S(2)}) collective-permute-start(bf16[272,1024]{1,0:T(8,128)(2,1)} %get-tuple-element.544.refs_3_), channel_id=1, source_target_pairs={{0,2},{1,3},{2,0},{3,1},{4,6},{5,7},{6,4},{7,5},{8,10},{9,11},{10,... | collective-permute-start | bytes 1671176 | tf_op jit(solution)/shard_map/rows_b0_2/ppermute | solution.py:1034
  42.7 15.1 %collective-permute-start.6 = (bf16[272,1024]{1,0:T(8,128)(2,1)}, bf16[272,1024]{1,0:T(8,128)(2,1)S(1)}, u32[]{:S(2)}, u32[]{:S(2)}) collective-permute-start(bf16[272,1024]{1,0:T(8,128)(2,1)} %get-tuple-element.544.refs_3_), channel_id=1, source_target_pairs={{0,1},{1,0},{2,3},{3,2},{4,5},{5,4},{6,7},{7,6},{8,9},{9,8},{10,11... | collective-permute-start | bytes 1671176 | tf_op jit(solution)/shard_map/rows_b0_1/ppermute | solution.py:1034
  92.8 67.9 %collective-permute-start.10 = (bf16[512,1536]{1,0:T(8,128)(2,1)}, bf16[512,1536]{1,0:T(8,128)(2,1)S(1)}, u32[]{:S(2)}, u32[]{:S(2)}) collective-permute-start(bf16[512,1536]{1,0:T(8,128)(2,1)} %get-tuple-element.602), channel_id=1, source_target_pairs={{0,8},{4,12},{8,0},{12,4},{16,24},{20,28},{24,16},{28,20},{1,9},{5... | collective-permute-start | bytes 4718600 | tf_op jit(solution)/shard_map/gate0_dp2/ppermute | solution.py:1034
  94.4 66.3 %collective-permute-start.11 = (bf16[512,1536]{1,0:T(8,128)(2,1)}, bf16[512,1536]{1,0:T(8,128)(2,1)}, u32[]{:S(2)}, u32[]{:S(2)}) collective-permute-start(bf16[512,1536]{1,0:T(8,128)(2,1)} %get-tuple-element.619), channel_id=1, source_target_pairs={{0,4},{4,0},{8,12},{12,8},{16,20},{20,16},{24,28},{28,24},{1,5},{5... | collective-permute-start | bytes 4718600 | tf_op jit(solution)/shard_map/up0_dp1/ppermute | solution.py:1034
  129.9 56.6 %collective-permute-start.9 = (bf16[512,1280]{1,0:T(8,128)(2,1)}, bf16[512,1280]{1,0:T(8,128)(2,1)S(1)}, u32[]{:S(2)}, u32[]{:S(2)}) collective-permute-start(bf16[512,1280]{1,0:T(8,128)(2,1)} %get-tuple-element.599), channel_id=1, source_target_pairs={{0,8},{4,12},{8,0},{12,4},{16,24},{20,28},{24,16},{28,20},{1,9},{5... | collective-permute-start | bytes 3932168 | tf_op jit(solution)/shard_map/gate1_dp2/ppermute | solution.py:1034
  130.4 56.0 %collective-permute-start.12 = (bf16[512,1280]{1,0:T(8,128)(2,1)}, bf16[512,1280]{1,0:T(8,128)(2,1)S(1)}, u32[]{:S(2)}, u32[]{:S(2)}) collective-permute-start(bf16[512,1280]{1,0:T(8,128)(2,1)} %get-tuple-element.647), channel_id=1, source_target_pairs={{0,4},{4,0},{8,12},{12,8},{16,20},{20,16},{24,28},{28,24},{1,5},{5... | collective-permute-start | bytes 3932168 | tf_op jit(solution)/shard_map/up1_dp1/ppermute | solution.py:1034
  157.2 37.4 %collective-permute-start.15 = (bf16[2,336,1024]{2,1,0:T(8,128)(2,1)}, bf16[2,336,1024]{2,1,0:T(8,128)(2,1)S(1)}, u32[]{:S(2)}, u32[]{:S(2)}) collective-permute-start(bf16[2,336,1024]{2,1,0:T(8,128)(2,1)} %get-tuple-element.685), channel_id=1, source_target_pairs={{0,2},{1,3},{2,0},{3,1},{4,6},{5,7},{6,4},{7,5},{8,10},{9,11},{10,... | collective-permute-start | bytes 4128776 | tf_op jit(solution)/shard_map/grad_rows2/ppermute | solution.py:1034
  166.6 19.9 %collective-permute-start.13 = (bf16[256,1536]{1,0:T(8,128)(2,1)}, bf16[256,1536]{1,0:T(8,128)(2,1)S(1)}, u32[]{:S(2)}, u32[]{:S(2)}) collective-permute-start(bf16[256,1536]{1,0:T(8,128)(2,1)} %get-tuple-element.651), channel_id=1, source_target_pairs={{0,4},{4,0},{8,12},{12,8},{16,20},{20,16},{24,28},{28,24},{1,5},{5... | collective-permute-start | bytes 2359304 | tf_op jit(solution)/shard_map/gate0_dp1/ppermute | solution.py:1034
  168.0 18.4 %collective-permute-start.14 = (bf16[256,1536]{1,0:T(8,128)(2,1)}, bf16[256,1536]{1,0:T(8,128)(2,1)S(1)}, u32[]{:S(2)}, u32[]{:S(2)}) collective-permute-start(bf16[256,1536]{1,0:T(8,128)(2,1)} %get-tuple-element.655), channel_id=1, source_target_pairs={{0,8},{4,12},{8,0},{12,4},{16,24},{20,28},{24,16},{28,20},{1,9},{5... | collective-permute-start | bytes 2359304 | tf_op jit(solution)/shard_map/up0_dp2/ppermute | solution.py:1034
  195.3 38.3 %collective-permute-start.20 = (bf16[256,1280]{1,0:T(8,128)(2,1)}, bf16[256,1280]{1,0:T(8,128)(2,1)}, u32[]{:S(2)}, u32[]{:S(2)}) collective-permute-start(bf16[256,1280]{1,0:T(8,128)(2,1)} %get-tuple-element.727), channel_id=1, source_target_pairs={{0,4},{4,0},{8,12},{12,8},{16,20},{20,16},{24,28},{28,24},{1,5},{5... | collective-permute-start | bytes 1966088 | tf_op jit(solution)/shard_map/gate1_dp1/ppermute | solution.py:1034
  195.8 37.8 %collective-permute-start.19 = (bf16[256,1280]{1,0:T(8,128)(2,1)}, bf16[256,1280]{1,0:T(8,128)(2,1)}, u32[]{:S(2)}, u32[]{:S(2)}) collective-permute-start(bf16[256,1280]{1,0:T(8,128)(2,1)} %get-tuple-element.726), channel_id=1, source_target_pairs={{0,8},{4,12},{8,0},{12,4},{16,24},{20,28},{24,16},{28,20},{1,9},{5... | collective-permute-start | bytes 1966088 | tf_op jit(solution)/shard_map/up1_dp2/ppermute | solution.py:1034
  203.2 40.1 %collective-permute-start.18 = (bf16[1408,512]{1,0:T(8,128)(2,1)}, bf16[1408,512]{1,0:T(8,128)(2,1)S(1)}, u32[]{:S(2)}, u32[]{:S(2)}) collective-permute-start(bf16[1408,512]{1,0:T(8,128)(2,1)} %get-tuple-element.700), channel_id=1, source_target_pairs={{0,8},{4,12},{8,0},{12,4},{16,24},{20,28},{24,16},{28,20},{1,9},{5... | collective-permute-start | bytes 4325384 | tf_op jit(solution)/shard_map/down0_dp2/ppermute | solution.py:1034
  204.8 38.5 %collective-permute-start.21 = (bf16[1408,512]{1,0:T(8,128)(2,1)}, bf16[1408,512]{1,0:T(8,128)(2,1)S(1)}, u32[]{:S(2)}, u32[]{:S(2)}) collective-permute-start(bf16[1408,512]{1,0:T(8,128)(2,1)} %get-tuple-element.741), channel_id=1, source_target_pairs={{0,4},{4,0},{8,12},{12,8},{16,20},{20,16},{24,28},{28,24},{1,5},{5... | collective-permute-start | bytes 4325384 | tf_op jit(solution)/shard_map/down1_dp1/ppermute | solution.py:1034
  243.3 23.4 %collective-permute-start.22 = (bf16[4,512,1024]{2,1,0:T(8,128)(2,1)}, bf16[4,512,1024]{2,1,0:T(8,128)(2,1)}, u32[]{:S(2)}, u32[]{:S(2)}) collective-permute-start(bf16[4,512,1024]{2,1,0:T(8,128)(2,1)} %get-tuple-element.777), channel_id=1, source_target_pairs={{0,1},{1,0},{2,3},{3,2},{4,5},{5,4},{6,7},{7,6},{8,9},{9,8},{10,11... | collective-permute-start | bytes 12582920 | tf_op jit(solution)/shard_map/dense_expert1/ppermute | solution.py:1034
  243.4 37.9 %collective-permute-start.24 = (bf16[2,128,1536]{2,1,0:T(8,128)(2,1)}, bf16[2,128,1536]{2,1,0:T(8,128)(2,1)}, u32[]{:S(2)}, u32[]{:S(2)}) collective-permute-start(bf16[2,128,1536]{2,1,0:T(8,128)(2,1)} %get-tuple-element.809), channel_id=1, source_target_pairs={{0,16},{4,20},{8,24},{12,28},{16,0},{20,4},{24,8},{28,12},{1,17},{... | collective-permute-start | bytes 2359304 | tf_op jit(solution)/shard_map/gate0_dp4/ppermute | solution.py:1034
  251.7 23.1 %collective-permute-start.25 = (bf16[704,512]{1,0:T(8,128)(2,1)}, bf16[704,512]{1,0:T(8,128)(2,1)S(1)}, u32[]{:S(2)}, u32[]{:S(2)}) collective-permute-start(bf16[704,512]{1,0:T(8,128)(2,1)} %get-tuple-element.810), channel_id=1, source_target_pairs={{0,4},{4,0},{8,12},{12,8},{16,20},{20,16},{24,28},{28,24},{1,5},{5... | collective-permute-start | bytes 2162696 | tf_op jit(solution)/shard_map/down0_dp1/ppermute | solution.py:1034
  281.3 29.0 %collective-permute-start.28 = (bf16[2,256,1152]{2,1,0:T(8,128)(2,1)}, bf16[2,256,1152]{2,1,0:T(8,128)(2,1)S(1)}, u32[]{:S(2)}, u32[]{:S(2)}) collective-permute-start(bf16[2,256,1152]{2,1,0:T(8,128)(2,1)} %get-tuple-element.830), channel_id=1, source_target_pairs={{0,2},{1,3},{2,0},{3,1},{4,6},{5,7},{6,4},{7,5},{8,10},{9,11},{10,... | collective-permute-start | bytes 3538952 | tf_op jit(solution)/shard_map/out_q_expert2/ppermute | solution.py:1034
  282.7 25.1 %collective-permute-start.27 = (bf16[2,256,1024]{2,1,0:T(8,128)(2,1)}, bf16[2,256,1024]{2,1,0:T(8,128)(2,1)S(1)}, u32[]{:S(2)}, u32[]{:S(2)}) collective-permute-start(bf16[2,256,1024]{2,1,0:T(8,128)(2,1)} %get-tuple-element.826), channel_id=1, source_target_pairs={{0,4},{4,0},{8,12},{12,8},{16,20},{20,16},{24,28},{28,24},{1,5},{5... | collective-permute-start | bytes 3145736 | tf_op jit(solution)/shard_map/k_v_dp1/ppermute | solution.py:1034
  284.2 31.6 %collective-permute-start.29 = (bf16[704,512]{1,0:T(8,128)(2,1)S(1)}, bf16[704,512]{1,0:T(8,128)(2,1)S(1)}, u32[]{:S(2)}, u32[]{:S(2)}) collective-permute-start(bf16[704,512]{1,0:T(8,128)(2,1)S(1)} %copy-done.39), channel_id=1, source_target_pairs={{0,8},{4,12},{8,0},{12,4},{16,24},{20,28},{24,16},{28,20},{1,9},{5... | collective-permute-start | bytes 2162696 | tf_op jit(solution)/shard_map/down1_dp2/ppermute | solution.py:1034
  284.2 31.6 %collective-permute-start.30 = (bf16[2,128,1280]{2,1,0:T(8,128)(2,1)S(1)}, bf16[2,128,1280]{2,1,0:T(8,128)(2,1)S(1)}, u32[]{:S(2)}, u32[]{:S(2)}) collective-permute-start(bf16[2,128,1280]{2,1,0:T(8,128)(2,1)S(1)} %copy-done.41), channel_id=1, source_target_pairs={{0,16},{4,20},{8,24},{12,28},{16,0},{20,4},{24,8},{28,12},{1,17},{... | collective-permute-start | bytes 1966088 | tf_op jit(solution)/shard_map/gate1_dp4/ppermute | solution.py:1034
  300.3 51.0 %collective-permute-start.26 = (bf16[2,320,1024]{2,1,0:T(8,128)(2,1)}, bf16[2,320,1024]{2,1,0:T(8,128)(2,1)S(1)}, u32[]{:S(2)}, u32[]{:S(2)}) collective-permute-start(bf16[2,320,1024]{2,1,0:T(8,128)(2,1)} %get-tuple-element.824), channel_id=1, source_target_pairs={{0,2},{1,3},{2,0},{3,1},{4,6},{5,7},{6,4},{7,5},{8,10},{9,11},{10,... | collective-permute-start | bytes 3932168 | tf_op jit(solution)/shard_map/produced_rows2/ppermute | solution.py:1034
  324.3 22.7 %collective-permute-start.32 = (bf16[2,128,1152]{2,1,0:T(8,128)(2,1)}, bf16[2,128,1152]{2,1,0:T(8,128)(2,1)S(1)}, u32[]{:S(2)}, u32[]{:S(2)}) collective-permute-start(bf16[2,128,1152]{2,1,0:T(8,128)(2,1)} %get-tuple-element.884), channel_id=1, source_target_pairs={{0,4},{4,0},{8,12},{12,8},{16,20},{20,16},{24,28},{28,24},{1,5},{5... | collective-permute-start | bytes 1769480 | tf_op jit(solution)/shard_map/out_q_dp1/ppermute | solution.py:1034
  324.9 22.1 %collective-permute-start.31 = (bf16[2,128,1024]{2,1,0:T(8,128)(2,1)}, bf16[2,128,1024]{2,1,0:T(8,128)(2,1)S(1)}, u32[]{:S(2)}, u32[]{:S(2)}) collective-permute-start(bf16[2,128,1024]{2,1,0:T(8,128)(2,1)} %get-tuple-element.876), channel_id=1, source_target_pairs={{0,8},{4,12},{8,0},{12,4},{16,24},{20,28},{24,16},{28,20},{1,9},{5... | collective-permute-start | bytes 1572872 | tf_op jit(solution)/shard_map/k_v_dp2/ppermute | solution.py:1034
  326.5 39.6 %collective-permute-start.37 = (bf16[2,352,512]{2,1,0:T(8,128)(2,1)S(1)}, bf16[2,352,512]{2,1,0:T(8,128)(2,1)S(1)}, u32[]{:S(2)}, u32[]{:S(2)}) collective-permute-start(bf16[2,352,512]{2,1,0:T(8,128)(2,1)S(1)} %copy-done.40), channel_id=1, source_target_pairs={{0,16},{4,20},{8,24},{12,28},{16,0},{20,4},{24,8},{28,12},{1,17},{... | collective-permute-start | bytes 2162696 | tf_op jit(solution)/shard_map/down0_dp4/ppermute | solution.py:1034
  351.9 14.2 %collective-permute-start.35 = (bf16[2,64,1152]{2,1,0:T(8,128)(2,1)}, bf16[2,64,1152]{2,1,0:T(8,128)(2,1)S(1)}, u32[]{:S(2)}, u32[]{:S(2)}) collective-permute-start(bf16[2,64,1152]{2,1,0:T(8,128)(2,1)} %get-tuple-element.916), channel_id=1, source_target_pairs={{0,8},{4,12},{8,0},{12,4},{16,24},{20,28},{24,16},{28,20},{1,9},{5... | collective-permute-start | bytes 884744 | tf_op jit(solution)/shard_map/out_q_dp2/ppermute | solution.py:1034
  351.9 14.2 %collective-permute-start.36 = (bf16[2,64,1024]{2,1,0:T(8,128)(2,1)}, bf16[2,64,1024]{2,1,0:T(8,128)(2,1)S(1)}, u32[]{:S(2)}, u32[]{:S(2)}) collective-permute-start(bf16[2,64,1024]{2,1,0:T(8,128)(2,1)} %get-tuple-element.920), channel_id=1, source_target_pairs={{0,2},{1,3},{2,0},{3,1},{4,6},{5,7},{6,4},{7,5},{8,10},{9,11},{10,... | collective-permute-start | bytes 786440 | tf_op jit(solution)/shard_map/k_v_expert2/ppermute | solution.py:1034
  370.8 15.2 %collective-permute-start.38 = (bf16[2,32,2176]{2,1,0:T(8,128)(2,1)}, bf16[2,32,2176]{2,1,0:T(8,128)(2,1)S(1)}, u32[]{:S(2)}, u32[]{:S(2)}) collective-permute-start(bf16[2,32,2176]{2,1,0:T(8,128)(2,1)} %get-tuple-element.941), channel_id=1, source_target_pairs={{0,16},{4,20},{8,24},{12,28},{16,0},{20,4},{24,8},{28,12},{1,17},{... | collective-permute-start | bytes 835592 | tf_op jit(solution)/shard_map/out_q_dp4/ppermute | solution.py:1034
  (49 other events, 385.8 us)

commit v6 on v5

--- a/solution.py
+++ b/solution.py
@@ -580,7 +580,8 @@
 
 
 def expert_b_kernel(gg_ref, gu_ref, *refs, cap, experts):
-    sc_refs, (wg_ref, wu_ref, *outs, acc) = refs[:-5], refs[-5:]
+    count = experts // 2 + 4
+    sc_refs, (wg_ref, wu_ref, *outs, acc) = refs[:-count], refs[-count:]
     part_sum = dot_nt(gg_ref[...], wg_ref[0]) + dot_nt(gu_ref[...], wu_ref[0])
     step, block = pl.program_id(0), pl.program_id(1)
 
@@ -588,12 +589,12 @@
     def _():
         acc[block] = part_sum
 
-    def finish(out_ref):
+    def finish(out_ref, at):
         total = acc[block] + part_sum
         row = lax.broadcasted_iota(jnp.int32, (cap, cap), 0)
         lane = lax.broadcasted_iota(jnp.int32, (cap, cap), 1)
         place = lax.broadcasted_iota(jnp.int32, (TAIL, cap), 0)
-        out_ref[0:cap, :] = total.astype(BF)
+        out_ref[at, 0:cap, :] = total.astype(BF)
         folded = sc_refs[0][...]
         for other in sc_refs[1:]:
             folded = folded + other[...]
@@ -603,15 +604,16 @@
         packed = jnp.where(
             place == 0, hi.astype(F32), jnp.where(place == 1, mid.astype(F32), jnp.where(place == 2, low.astype(F32), 0.0))
         )
-        out_ref[cap : cap + TAIL, :] = jnp.zeros((TAIL, total.shape[1]), BF)
-        out_ref[cap : cap + TAIL, 0:cap] = packed.astype(BF)
+        out_ref[at, cap : cap + TAIL, :] = jnp.zeros((TAIL, total.shape[1]), BF)
+        out_ref[at, cap : cap + TAIL, 0:cap] = packed.astype(BF)
 
     last = step == pl.num_programs(0) - 1
+    half = experts // 2
     for m in range(experts):
 
         @pl.when(jnp.logical_and(last, block == m))
         def _(m=m):
-            finish(outs[m // (experts // 2)].at[m % (experts // 2)])
+            finish(outs[m] if m < half else outs[half], 0 if m < half else m - half)
 
 
 def expert_b(gg, gu, scs, w_gate, w_up, experts):
@@ -627,8 +629,9 @@
         (gg, gu, *scs, w_gate, w_up),
         [grads, grads] + [sums] * len(scs) + [weight, weight],
         grid=(2, experts),
-        out_specs=[const_spec((experts // 2, cap + TAIL, width))] * 2,
-        out_shape=[jax.ShapeDtypeStruct((experts // 2, cap + TAIL, width), BF)] * 2,
+        out_specs=[const_spec((1, cap + TAIL, width))] * (experts // 2) + [const_spec((experts // 2, cap + TAIL, width))],
+        out_shape=[jax.ShapeDtypeStruct((1, cap + TAIL, width), BF)] * (experts // 2)
+        + [jax.ShapeDtypeStruct((experts // 2, cap + TAIL, width), BF)],
         scratch_shapes=[pltpu.VMEM((experts, cap, width), F32)],
         cost_estimate=estimate("expert_input_grad"),
         name="expert_input_grad",
@@ -1175,8 +1178,9 @@
 class Return:
     def __init__(self, order, low, high, axis, size, name, pieces=False):
         self.order, self.axis, self.size, self.name = order, axis, size, name
-        half = low.shape[0]
-        self.slots = [(low, i) for i in range(half)] + [(high, i) for i in range(half)]
+        half = high.shape[0]
+        low = [(value, 0) for value in low] if isinstance(low, list) else [(low, i) for i in range(half)]
+        self.slots = low + [(high, i) for i in range(half)]
         self.bit = bits_of(size) - 1
         if pieces:
             self.start_pieces()
@@ -1192,7 +1196,8 @@
         for m in self.moving():
             array, index = self.slots[m]
             with jax.named_scope(f"{self.name}{1 << self.bit}_{m}"):
-                self.got.append(swap(self.order.enter(array[index][None]), self.axis, self.size, 1 << self.bit))
+                piece = array if array.shape[0] == 1 else array[index][None]
+                self.got.append(swap(self.order.enter(piece), self.axis, self.size, 1 << self.bit))
 
     def fold(self):
         got = self.order.leave(self.got)
@@ -1218,6 +1223,9 @@
     def send(self, m, bit):
         with jax.named_scope(f"{self.name}{m}_{bit}"):
             self.blocks[m ^ bit] = swap(self.blocks[m], self.axis, self.size, bit)
+
+    def settle(self):
+        self.blocks[1] = self.order.leave(self.blocks[1])
 
     def relay(self):
         self.blocks[self.size // 2] = self.order.leave(self.blocks[self.size // 2])
@@ -1290,13 +1298,15 @@
 
     place_q, place_k = [places(whole_me, dp_bits + ep_bits, bits) for bits in (q_bits, k_bits)]
 
-    cots.relay()
     first_half = Gather(order, order.enter(payload), "expert", ep_size, "rows_a")
     attended, lse, middle, normed_moe, chances, payload = order.leave(
         attn_second(tokens, order.enter(scaled), keys, values, w_out, woff, segments, gain_moe, w_router.T, filled)
     )
+    cots.settle()
+    first_half.settle()
     second_half = Gather(order, order.enter(payload), "expert", ep_size, "rows_b")
     first_half.relay()
+    cots.relay()
     cots, heads_rows = cots.finish(), first_half.finish()
     blocks = ff // FF_BLOCK
     counts = [blocks - blocks // 2, blocks // 2]
@@ -1330,7 +1340,7 @@
     _, (hid, hid_t, gg, gu) = expert_part(1, (x_all, x_t, gate_all), filled)
     for unit in units[1]:
         unit.start()
-    back_low, back_high = order.leave(expert_b(order.enter(gg), gu, scs, w_gate, w_up, experts))
+    *back_low, back_high = order.leave(expert_b(order.enter(gg), gu, scs, w_gate, w_up, experts))
     backs = Return(order, back_low, back_high, "expert", ep_size, "grad_rows")
     first, second = units[0][0], units[1][0]
     fold(*units[0])

time: 397 us -> 394 us (level)
    unnamed x85 -> x83, local copies, waits for them, and re-layouts: 15.9 us -> 15.8 us
  transfers between devices with their start and end apart: 39 -> 39, of which waited for: 15 -> 13; matrix products, arithmetic and copies ran while one was open for 4% -> 4% of each run, Pallas kernels for 55% -> 56%
where the time goes in v6:
time: 394 us; the launch traced here: 387 us
  Pallas kernels  254 us (64%)
  waiting for transfers between devices  64.5 us (16%)
  starting transfers between devices  36.9 us (9%)
  local copies, waits for them, and re-layouts  24.1 us (6%)
  other arithmetic  5.96 us (2%)
    pallas_call x23, Pallas kernels, call(): pl.pallas_call(kernel, in_specs=list(in_specs), compiler_params=params(),...  254 us
    ppermute x39, waiting for transfers between devices, swap(): return lax.ppermute(value, axis, [(i, i ^ mask) for i in range(size)])  64.5 us
    ppermute x39, starting transfers between devices, swap(): return lax.ppermute(value, axis, [(i, i ^ mask) for i in range(size)])  36.9 us
    unnamed x83, local copies, waits for them, and re-layouts  15.8 us
  transfers between devices with their start and end apart: 39, of which 13 were waited for; matrix products, arithmetic and copies ran while one was open for 4% of the time, Pallas kernels for 56%

profile of v6, /device:TPU:0, one launch (start us, length us, event | category | flops | bytes accessed | tf_op | source)
XLA Modules:
  0.0 387.0 jit_solution(15820399571743244941)
XLA Ops:
  3.8 15.6 %attn_first.1 = (bf16[512,1024]{1,0:T(8,128)(2,1)}, bf16[512,1024]{1,0:T(8,128)(2,1)}, bf16[512,1024]{1,0:T(8,128)(2,1)}, f32[4,4,512]{2,1,0:T(4,128)}, f32[1,12...) custom-call(bf16[512,1024]{1,0:T(8,128)(2,1)} %tok_ref.7, ...), custom_call_target="tpu_custom_call" | custom-call | flops 115000000 | bytes 100000 | tf_op jit(solution)/shard_map/attn_first/pallas_call | solution.py:100
  19.8 12.3 %attn_second.1 = (bf16[512,1024]{1,0:T(8,128)(2,1)}, f32[4,4,512]{2,1,0:T(4,128)}, f32[512,1024]{1,0:T(8,128)}, bf16[512,1024]{1,0:T(8,128)(2,1)}, f32[16,512]{1,0:T(8,128)}, /*index=5*/bf16[272,1024]{1,0:T(8,128)(2,1)}) custom-call(bf16[512,1024]{1,0:T(8,128)(2,1)} %tok_ref.7, ...), custom_call_target="tpu_custom_call", output_to_operand_aliasing={{0}: (9, {}), {1}: (10, {}), {2}: (11, {}), {3}: (12, {}), ... | custom-call | flops 115000000 | bytes 100000 | tf_op jit(solution)/shard_map/attn_second/pallas_call | solution.py:100
  32.2 7.4 %collective-permute-done.2.refs_2_.refs_6_ = bf16[272,1024]{1,0:T(8,128)(2,1)S(1)} collective-permute-done((bf16[272,1024]{1,0:T(8,128)(2,1)}, bf16[272,1024]{1,0:T(8,128)(2,1)S(1)}, u32[]{:S(2)}, u32[]{:S(2)}) %collective-permute-start.2) | collective-permute-done | bytes 557088 | tf_op jit(solution)/shard_map/rows_a0_2/ppermute | solution.py:1037
  44.3 11.1 %cot_hidden.1 = (bf16[1280,1536]{1,0:T(8,128)(2,1)}, bf16[1280,1024]{1,0:T(8,128)(2,1)}) custom-call(s32[1]{0:T(128)} %bitcast.9.me_ref.refs_0_, bf16[272,1024]{1,0:T(8,128)(2,1)} %get-tuple-element.553.refs_0_.refs_2_, bf16[272,1024]{1,0:T(8,128)(2,1)} %copy-done.2, bf16[272,1024]{1,0:T(8,128)(2,1)} %copy-done.3, bf16[272,1024]{1,0:T(8,128)(2,1)} %copy-done.4, ...), custom_call_target="tpu_custom_call" | custom-call | flops 115000000 | bytes 100000 | tf_op jit(solution)/shard_map/cot_hidden/pallas_call | solution.py:100
  58.3 32.6 %expert_grads.2 = (bf16[1280,1024]{1,0:T(8,128)(2,1)}, bf16[1024,1280]{1,0:T(8,128)(2,1)}, f32[1280,128]{1,0:T(8,128)}, bf16[1280,1024]{1,0:T(8,128)(2,1)}, bf16...) custom-call(s32[1]{0:T(128)} %bitcast.9.me_ref.refs_0_, ...), custom_call_target="tpu_custom_call" | custom-call | flops 115000000 | bytes 100000 | tf_op jit(solution)/shard_map/expert_grads/pallas_call | solution.py:100
  96.4 8.1 %cot_hidden_more.1.refs_3_ = bf16[1280,1280]{1,0:T(8,128)(2,1)} custom-call(bf16[1280,1024]{1,0:T(8,128)(2,1)} %get-tuple-element.585.refs_10_.rows_ref, bf16[1,2816,1024]{2,1,0:T(8,128)(2,1)} %wd_ref.3), custom_call_target="tpu_custom_call" | custom-call | flops 115000000 | bytes 100000 | tf_op jit(solution)/shard_map/cot_hidden_more/pallas_call | solution.py:100
  104.6 25.3 %expert_grads.3 = (bf16[512,1280]{1,0:T(8,128)(2,1)}, bf16[512,1280]{1,0:T(8,128)(2,1)}, bf16[512,1280]{1,0:T(8,128)(2,1)}, bf16[512,1280]{1,0:T(8,128)(2,1)}, f...) custom-call(bf16[1280,1024]{1,0:T(8,128)(2,1)} %get-tuple-element.58, ...), custom_call_target="tpu_custom_call", output_to_operand_aliasing={{5}: (6, {}), {6}: (7, {}), {7}: (8, {}), {8}: (9, {})} | custom-call | flops 115000000 | bytes 100000 | tf_op jit(solution)/shard_map/expert_grads/pallas_call | solution.py:100
  130.7 25.9 %expert_input_grad.1 = (bf16[1,336,1024]{2,1,0:T(8,128)(2,1)}, bf16[1,336,1024]{2,1,0:T(8,128)(2,1)}, bf16[2,336,1024]{2,1,0:T(8,128)(2,1)}) custom-call(bf16[1280,2816]{1,0:T(8,128)(2,1)} %get-tuple-element.617.gg_ref, bf16[1280,2816]{1,0:T(8,128)(2,1)} %get-tuple-element.618.gu_ref, f32[1280,128]{1,0:T(8,128)} %get-tuple-element.619.refs_0_, ...), custom_call_target="tpu_custom_call" | custom-call | flops 115000000 | bytes 100000 | tf_op jit(solution)/shard_map/expert_input_grad/pallas_call | solution.py:100
  159.7 4.6 %fold.6 = (bf16[256,1536]{1,0:T(8,128)(2,1)}, bf16[256,1536]{1,0:T(8,128)(2,1)}, bf16[256,1536]{1,0:T(8,128)(2,1)}, bf16[256,1536]{1,0:T(8,128)(2,1)}) custom-call(bf16[512,1536]{1,0:T(8,128)(2,1)} %get-tuple-element.634.refs_0_, bf16[512,1536]{1,0:T(8,128)(2,1)} %copy-done.5, bf16[512,1536]{1,0:T(8,128)(2,1)} %get-tuple-element.636.refs_2_, ...), custom_call_target="tpu_custom_call" | custom-call | flops 115000000 | bytes 100000 | tf_op jit(solution)/shard_map/fold/pallas_call | solution.py:100
  167.4 16.8 %down_grads.1 = (bf16[1408,512]{1,0:T(8,128)(2,1)}, bf16[1408,512]{1,0:T(8,128)(2,1)}, bf16[1408,512]{1,0:T(8,128)(2,1)}, bf16[1408,512]{1,0:T(8,128)(2,1)}) custom-call(s32[8]{0:T(128)} %get-tuple-element.1021.place_a_ref, s32[8]{0:T(128)} %get-tuple-element.552.refs_1_.place_b_ref, bf16[2816,1280]{1,0:T(8,128)(2,1)} %get-tuple-element.648.hidt_ref, ...), custom_call_target="tpu_custom_call" | custom-call | flops 11500000256 | bytes 100000 | tf_op jit(solution)/shard_map/down_grads/pallas_call | solution.py:100
  186.9 5.5 %fold.7 = (bf16[256,1280]{1,0:T(8,128)(2,1)}, bf16[256,1280]{1,0:T(8,128)(2,1)}, bf16[256,1280]{1,0:T(8,128)(2,1)}, bf16[256,1280]{1,0:T(8,128)(2,1)}, bf16[2,12...) custom-call(bf16[512,1280]{1,0:T(8,128)(2,1)} %get-tuple-element.670.refs_0_, bf16[512,1280]{1,0:T(8,128)(2,1)} %copy-done.34, ...), custom_call_target="tpu_custom_call" | custom-call | flops 2300000000 | bytes 100000 | tf_op jit(solution)/shard_map/fold/pallas_call | solution.py:100
  194.5 4.7 %sorted_rows.1 = (bf16[1024,512]{1,0:T(8,128)(2,1)}, bf16[2,1024,512]{2,1,0:T(8,128)(2,1)}) custom-call(s32[32]{0:T(128)} %get-tuple-element.1020.pq_ref.place_ref, s32[32]{0:T(128)} %get-tuple-element.1019.pk_ref, bf16[512,1024]{1,0:T(8,128)(2,1)} %tok_ref.7, f32[1,1024]{1,0:T(1,128)} %bitcast.46, bf16[512,1024]{1,0:T(8,128)(2,1)} %get-tuple-element.705.att_ref), custom_call_target="tpu_custom_call" | custom-call | flops 115000000 | bytes 100000 | tf_op jit(solution)/shard_map/sorted_rows/pallas_call | solution.py:100
  204.9 10.0 %moe_bwd.1 = (f32[512,1024]{1,0:T(8,128)}, bf16[512,1024]{1,0:T(8,128)(2,1)}, bf16[512,1024]{1,0:T(8,128)(2,1)}, f32[1,1024]{1,0:T(1,128)}, f32[16,1024]{1,0:T(8,128)}) custom-call(bf16[512,1024]{1,0:T(8,128)(2,1)} %cot_ref.1, f32[512,1024]{1,0:T(8,128)} %get-tuple-element.512.mid_ref, f32[1,1024]{1,0:T(1,128)} %bitcast.44, ...), custom_call_target="tpu_custom_call" | custom-call | flops 115000000 | bytes 100000 | tf_op jit(solution)/shard_map/moe_bwd/pallas_call | solution.py:100
  215.0 16.2 %attn_bwd.1 = (bf16[512,1024]{1,0:T(8,128)(2,1)}, bf16[512,1024]{1,0:T(8,128)(2,1)}, bf16[512,1024]{1,0:T(8,128)(2,1)}, f32[4,4,512]{2,1,0:T(4,128)}) custom-call(bf16[512,1024]{1,0:T(8,128)(2,1)} %get-tuple-element.496.qs_ref, bf16[512,1024]{1,0:T(8,128)(2,1)} %get-tuple-element.497.k_ref, bf16[512,1024]{1,0:T(8,128)(2,1)} %get-tuple-element.498.v_ref, ...), custom_call_target="tpu_custom_call" | custom-call | flops 115000000 | bytes 100000 | tf_op jit(solution)/shard_map/attn_bwd/pallas_call | solution.py:100
  231.2 9.3 %dense_terms.1 = (bf16[4,512,1024]{2,1,0:T(8,128)(2,1)}, bf16[4,512,1024]{2,1,0:T(8,128)(2,1)}) custom-call(bf16[1024,512]{1,0:T(8,128)(2,1)} %get-tuple-element.712.att_ref, bf16[2,1024,512]{2,1,0:T(8,128)(2,1)} %get-tuple-element.713.rows_ref, bf16[512,1024]{1,0:T(8,128)(2,1)} %get-tuple-element.727.branch_ref, ...), custom_call_target="tpu_custom_call" | custom-call | flops 15064999936 | bytes 100000 | tf_op jit(solution)/shard_map/dense_terms/pallas_call | solution.py:100
  241.2 2.6 collective-permute-start.24
  243.8 5.6 %fold.8 = (bf16[704,512]{1,0:T(8,128)(2,1)}, bf16[704,512]{1,0:T(8,128)(2,1)}, bf16[704,512]{1,0:T(8,128)(2,1)}, bf16[704,512]{1,0:T(8,128)(2,1)}, bf16[2,128,12...) custom-call(bf16[1408,512]{1,0:T(8,128)(2,1)} %get-tuple-element.772.refs_0_, bf16[1408,512]{1,0:T(8,128)(2,1)} %copy-done.6, ...), custom_call_target="tpu_custom_call" | custom-call | flops 115000000 | bytes 100000 | tf_op jit(solution)/shard_map/fold/pallas_call | solution.py:100
  253.5 10.9 %norm_bwd.1 = (f32[512,1024]{1,0:T(8,128)}, bf16[512,128]{1,0:T(8,128)(2,1)}, bf16[512,128]{1,0:T(8,128)(2,1)}) custom-call(s32[32]{0:T(128)} %get-tuple-element.1020.pq_ref.place_ref, bf16[512,1024]{1,0:T(8,128)(2,1)} %tok_ref.7, f32[1,1024]{1,0:T(1,128)} %bitcast.47, f32[512,1024]{1,0:T(8,128)} %get-tuple-element.790.gmid_ref, ...), custom_call_target="tpu_custom_call" | custom-call | flops 115000000 | bytes 100000 | tf_op jit(solution)/shard_map/norm_bwd/pallas_call | solution.py:100
  266.8 5.8 %fold_first.1 = (bf16[2,256,1152]{2,1,0:T(8,128)(2,1)}, bf16[2,256,1152]{2,1,0:T(8,128)(2,1)}, bf16[2,256,1024]{2,1,0:T(8,128)(2,1)}, bf16[2,256,1024]{2,1,0:T(8,128)(2,1)}) custom-call(bf16[4,512,1024]{2,1,0:T(8,128)(2,1)} %get-tuple-element.808.keep_ref, bf16[4,512,1024]{2,1,0:T(8,128)(2,1)} %collective-permute-done.22.got_ref, ...), custom_call_target="tpu_custom_call" | custom-call | flops 115000000 | bytes 100000 | tf_op jit(solution)/shard_map/fold_first/pallas_call | solution.py:100
  272.6 6.5 %collective-permute-done.24.refs_9_ = bf16[2,128,1536]{2,1,0:T(8,128)(2,1)} collective-permute-done((bf16[2,128,1536]{2,1,0:T(8,128)(2,1)}, bf16[2,128,1536]{2,1,0:T(8,128)(2,1)}, u32[]{:S(2)}, u32[]{:S(2)}) %collective-permute-start.24) | collective-permute-done | bytes 786464 | tf_op jit(solution)/shard_map/gate0_dp4/ppermute | solution.py:1037
  281.0 3.1 collective-permute-start.30
  284.2 12.9 %produced_rows.1 = (bf16[2,320,1024]{2,1,0:T(8,128)(2,1)}, bf16[2,320,1024]{2,1,0:T(8,128)(2,1)}) custom-call(bf16[1280,2816]{1,0:T(8,128)(2,1)} %get-tuple-element.829.hid_ref, bf16[1,2816,1024]{2,1,0:T(8,128)(2,1)} %wd_ref.3), custom_call_target="tpu_custom_call" | custom-call | flops 115000000 | bytes 100000 | tf_op jit(solution)/shard_map/produced_rows/pallas_call | solution.py:100
  299.9 4.6 %collective-permute-done.27.refs_1_ = bf16[2,256,1024]{2,1,0:T(8,128)(2,1)S(1)} collective-permute-done((bf16[2,256,1024]{2,1,0:T(8,128)(2,1)}, bf16[2,256,1024]{2,1,0:T(8,128)(2,1)S(1)}, u32[]{:S(2)}, u32[]{:S(2)}) %collective-permute-start.27) | collective-permute-done | bytes 1048608 | tf_op jit(solution)/shard_map/k_v_dp1/ppermute | solution.py:1037
  304.5 3.6 collective-permute-done.28.refs_3_
  308.1 4.5 %collective-permute-done.29.refs_7_ = bf16[704,512]{1,0:T(8,128)(2,1)S(1)} collective-permute-done((bf16[704,512]{1,0:T(8,128)(2,1)S(1)}, bf16[704,512]{1,0:T(8,128)(2,1)S(1)}, u32[]{:S(2)}, u32[]{:S(2)}) %collective-permute-start.29) | collective-permute-done | bytes 720928 | tf_op jit(solution)/shard_map/down1_dp2/ppermute | solution.py:1037
  314.3 6.8 %fold.9 = (bf16[2,128,1024]{2,1,0:T(8,128)(2,1)}, bf16[2,128,1024]{2,1,0:T(8,128)(2,1)}, bf16[2,128,1152]{2,1,0:T(8,128)(2,1)}, bf16[2,128,1152]{2,1,0:T(8,128)(...) custom-call(bf16[2,256,1024]{2,1,0:T(8,128)(2,1)} %get-tuple-element, ...), custom_call_target="tpu_custom_call" | custom-call | flops 115000000 | bytes 100000 | tf_op jit(solution)/shard_map/fold/pallas_call | solution.py:100
  323.4 2.7 collective-permute-start.37
  328.5 15.3 %collective-permute-done.31.refs_1_ = bf16[2,128,1024]{2,1,0:T(8,128)(2,1)S(1)} collective-permute-done((bf16[2,128,1024]{2,1,0:T(8,128)(2,1)}, bf16[2,128,1024]{2,1,0:T(8,128)(2,1)S(1)}, u32[]{:S(2)}, u32[]{:S(2)}) %collective-permute-start.31) | collective-permute-done | bytes 524320 | tf_op jit(solution)/shard_map/k_v_dp2/ppermute | solution.py:1037
  352.1 6.3 %layer_output.1 = bf16[512,1024]{1,0:T(8,128)(2,1)} custom-call(f32[512,1024]{1,0:T(8,128)} %get-tuple-element.512.mid_ref, f32[16,512]{1,0:T(8,128)} %select_maximum_fusion.3.ch_ref, s32[512,4]{1,0:T(8,128)} %bitcast.39, bf16[2,320,1024]{2,1,0:T(8,128)(2,1)} %get-tuple-element.833.refs_0_, bf16[1,320,1024]{2,1,0:T(8,128)(2,1)} %copy-done.19, ...), custom_call_target="tpu_custom_call" | custom-call | flops 115000000 | bytes 100000 | tf_op jit(solution)/shard_map/layer_output/pallas_call | solution.py:100
  358.4 4.4 %collective-permute-done.35.refs_1_ = bf16[2,64,1152]{2,1,0:T(8,128)(2,1)S(1)} collective-permute-done((bf16[2,64,1152]{2,1,0:T(8,128)(2,1)}, bf16[2,64,1152]{2,1,0:T(8,128)(2,1)S(1)}, u32[]{:S(2)}, u32[]{:S(2)}) %collective-permute-start.35) | collective-permute-done | bytes 294944 | tf_op jit(solution)/shard_map/out_q_dp2/ppermute | solution.py:1037
  364.5 3.0 fold.11
  370.7 12.2 %collective-permute-done.38.got_ref = bf16[2,32,2176]{2,1,0:T(8,128)(2,1)S(1)} collective-permute-done((bf16[2,32,2176]{2,1,0:T(8,128)(2,1)}, bf16[2,32,2176]{2,1,0:T(8,128)(2,1)S(1)}, u32[]{:S(2)}, u32[]{:S(2)}) %collective-permute-start.38) | collective-permute-done | bytes 278560 | tf_op jit(solution)/shard_map/out_q_dp4/ppermute | solution.py:1037
  (179 shorter events, 69.2 us)
Async XLA Ops:
  0.6 31.5 %collective-permute-start.1 = (bf16[512,1024]{1,0:T(8,128)(2,1)}, bf16[512,1024]{1,0:T(8,128)(2,1)S(1)}, u32[]{:S(2)}, u32[]{:S(2)}) collective-permute-start(bf16[512,1024]{1,0:T(8,128)(2,1)} %cot_ref.1), channel_id=1, source_target_pairs={{0,1},{1,0},{2,3},{3,2},{4,5},{5,4},{6,7},{7,6},{8,9},{9,8},{10,11... | collective-permute-start | bytes 3145736 | tf_op jit(solution)/shard_map/cot0_1/ppermute | solution.py:1037
  1.2 38.5 %collective-permute-start.4 = (bf16[512,1024]{1,0:T(8,128)(2,1)}, bf16[512,1024]{1,0:T(8,128)(2,1)}, u32[]{:S(2)}, u32[]{:S(2)}) collective-permute-start(bf16[512,1024]{1,0:T(8,128)(2,1)} %cot_ref.1), channel_id=1, source_target_pairs={{0,2},{1,3},{2,0},{3,1},{4,6},{5,7},{6,4},{7,5},{8,10},{9,11},{10,... | collective-permute-start | bytes 3145736 | tf_op jit(solution)/shard_map/cot0_2/ppermute | solution.py:1037
  19.3 12.9 %collective-permute-start = (bf16[272,1024]{1,0:T(8,128)(2,1)}, bf16[272,1024]{1,0:T(8,128)(2,1)S(1)}, u32[]{:S(2)}, u32[]{:S(2)}) collective-permute-start(bf16[272,1024]{1,0:T(8,128)(2,1)} %get-tuple-element.553.refs_0_.refs_2_), channel_id=1, source_target_pairs={{0,1},{1,0},{2,3},{3,2},{4,5},{5,4},{6,7},{7,6},{8,9},{9,8},{10,11... | collective-permute-start | bytes 1671176 | tf_op jit(solution)/shard_map/rows_a0_1/ppermute | solution.py:1037
  19.6 20.1 %collective-permute-start.2 = (bf16[272,1024]{1,0:T(8,128)(2,1)}, bf16[272,1024]{1,0:T(8,128)(2,1)S(1)}, u32[]{:S(2)}, u32[]{:S(2)}) collective-permute-start(bf16[272,1024]{1,0:T(8,128)(2,1)} %get-tuple-element.553.refs_0_.refs_2_), channel_id=1, source_target_pairs={{0,2},{1,3},{2,0},{3,1},{4,6},{5,7},{6,4},{7,5},{8,10},{9,11},{10,... | collective-permute-start | bytes 1671176 | tf_op jit(solution)/shard_map/rows_a0_2/ppermute | solution.py:1037
  40.2 15.3 %collective-permute-start.7 = (bf16[272,1024]{1,0:T(8,128)(2,1)}, bf16[272,1024]{1,0:T(8,128)(2,1)S(1)}, u32[]{:S(2)}, u32[]{:S(2)}) collective-permute-start(bf16[272,1024]{1,0:T(8,128)(2,1)} %get-tuple-element.554.refs_3_), channel_id=1, source_target_pairs={{0,2},{1,3},{2,0},{3,1},{4,6},{5,7},{6,4},{7,5},{8,10},{9,11},{10,... | collective-permute-start | bytes 1671176 | tf_op jit(solution)/shard_map/rows_b0_2/ppermute | solution.py:1037
  41.9 14.2 %collective-permute-start.6 = (bf16[272,1024]{1,0:T(8,128)(2,1)}, bf16[272,1024]{1,0:T(8,128)(2,1)}, u32[]{:S(2)}, u32[]{:S(2)}) collective-permute-start(bf16[272,1024]{1,0:T(8,128)(2,1)} %get-tuple-element.554.refs_3_), channel_id=1, source_target_pairs={{0,1},{1,0},{2,3},{3,2},{4,5},{5,4},{6,7},{7,6},{8,9},{9,8},{10,11... | collective-permute-start | bytes 1671176 | tf_op jit(solution)/shard_map/rows_b0_1/ppermute | solution.py:1037
  90.9 67.6 %collective-permute-start.10 = (bf16[512,1536]{1,0:T(8,128)(2,1)}, bf16[512,1536]{1,0:T(8,128)(2,1)S(1)}, u32[]{:S(2)}, u32[]{:S(2)}) collective-permute-start(bf16[512,1536]{1,0:T(8,128)(2,1)} %get-tuple-element.612), channel_id=1, source_target_pairs={{0,8},{4,12},{8,0},{12,4},{16,24},{20,28},{24,16},{28,20},{1,9},{5... | collective-permute-start | bytes 4718600 | tf_op jit(solution)/shard_map/gate0_dp2/ppermute | solution.py:1037
  92.8 65.8 %collective-permute-start.11 = (bf16[512,1536]{1,0:T(8,128)(2,1)}, bf16[512,1536]{1,0:T(8,128)(2,1)}, u32[]{:S(2)}, u32[]{:S(2)}) collective-permute-start(bf16[512,1536]{1,0:T(8,128)(2,1)} %get-tuple-element.630), channel_id=1, source_target_pairs={{0,4},{4,0},{8,12},{12,8},{16,20},{20,16},{24,28},{28,24},{1,5},{5... | collective-permute-start | bytes 4718600 | tf_op jit(solution)/shard_map/up0_dp1/ppermute | solution.py:1037
  129.9 54.3 %collective-permute-start.9 = (bf16[512,1280]{1,0:T(8,128)(2,1)}, bf16[512,1280]{1,0:T(8,128)(2,1)S(1)}, u32[]{:S(2)}, u32[]{:S(2)}) collective-permute-start(bf16[512,1280]{1,0:T(8,128)(2,1)} %get-tuple-element.609), channel_id=1, source_target_pairs={{0,8},{4,12},{8,0},{12,4},{16,24},{20,28},{24,16},{28,20},{1,9},{5... | collective-permute-start | bytes 3932168 | tf_op jit(solution)/shard_map/gate1_dp2/ppermute | solution.py:1037
  130.4 53.8 %collective-permute-start.12 = (bf16[512,1280]{1,0:T(8,128)(2,1)}, bf16[512,1280]{1,0:T(8,128)(2,1)S(1)}, u32[]{:S(2)}, u32[]{:S(2)}) collective-permute-start(bf16[512,1280]{1,0:T(8,128)(2,1)} %get-tuple-element.658), channel_id=1, source_target_pairs={{0,4},{4,0},{8,12},{12,8},{16,20},{20,16},{24,28},{28,24},{1,5},{5... | collective-permute-start | bytes 3932168 | tf_op jit(solution)/shard_map/up1_dp1/ppermute | solution.py:1037
  156.6 35.8 %collective-permute-start.15 = (bf16[2,336,1024]{2,1,0:T(8,128)(2,1)}, bf16[2,336,1024]{2,1,0:T(8,128)(2,1)S(1)}, u32[]{:S(2)}, u32[]{:S(2)}) collective-permute-start(bf16[2,336,1024]{2,1,0:T(8,128)(2,1)} %get-tuple-element.696), channel_id=1, source_target_pairs={{0,2},{1,3},{2,0},{3,1},{4,6},{5,7},{6,4},{7,5},{8,10},{9,11},{10,... | collective-permute-start | bytes 4128776 | tf_op jit(solution)/shard_map/grad_rows2/ppermute | solution.py:1037
  164.3 19.9 %collective-permute-start.13 = (bf16[256,1536]{1,0:T(8,128)(2,1)}, bf16[256,1536]{1,0:T(8,128)(2,1)S(1)}, u32[]{:S(2)}, u32[]{:S(2)}) collective-permute-start(bf16[256,1536]{1,0:T(8,128)(2,1)} %get-tuple-element.662), channel_id=1, source_target_pairs={{0,4},{4,0},{8,12},{12,8},{16,20},{20,16},{24,28},{28,24},{1,5},{5... | collective-permute-start | bytes 2359304 | tf_op jit(solution)/shard_map/gate0_dp1/ppermute | solution.py:1037
  165.8 18.4 %collective-permute-start.14 = (bf16[256,1536]{1,0:T(8,128)(2,1)}, bf16[256,1536]{1,0:T(8,128)(2,1)S(1)}, u32[]{:S(2)}, u32[]{:S(2)}) collective-permute-start(bf16[256,1536]{1,0:T(8,128)(2,1)} %get-tuple-element.666), channel_id=1, source_target_pairs={{0,8},{4,12},{8,0},{12,4},{16,24},{20,28},{24,16},{28,20},{1,9},{5... | collective-permute-start | bytes 2359304 | tf_op jit(solution)/shard_map/up0_dp2/ppermute | solution.py:1037
  192.5 6.8 %collective-permute-start.17 = (bf16[1,336,1024]{2,1,0:T(8,128)(2,1)S(1)}, bf16[1,336,1024]{2,1,0:T(8,128)(2,1)S(1)}, u32[]{:S(2)}, u32[]{:S(2)}) collective-permute-start(bf16[1,336,1024]{2,1,0:T(8,128)(2,1)S(1)} %slice.27), channel_id=1, source_target_pairs={{0,1},{1,0},{2,3},{3,2},{4,5},{5,4},{6,7},{7,6},{8,9},{9,8},{10,11... | collective-permute-start | bytes 2064392 | tf_op jit(solution)/shard_map/grad_rows1_3/ppermute | solution.py:1037
  193.0 38.1 %collective-permute-start.20 = (bf16[256,1280]{1,0:T(8,128)(2,1)}, bf16[256,1280]{1,0:T(8,128)(2,1)}, u32[]{:S(2)}, u32[]{:S(2)}) collective-permute-start(bf16[256,1280]{1,0:T(8,128)(2,1)} %get-tuple-element.739), channel_id=1, source_target_pairs={{0,4},{4,0},{8,12},{12,8},{16,20},{20,16},{24,28},{28,24},{1,5},{5... | collective-permute-start | bytes 1966088 | tf_op jit(solution)/shard_map/gate1_dp1/ppermute | solution.py:1037
  193.6 37.6 %collective-permute-start.19 = (bf16[256,1280]{1,0:T(8,128)(2,1)}, bf16[256,1280]{1,0:T(8,128)(2,1)}, u32[]{:S(2)}, u32[]{:S(2)}) collective-permute-start(bf16[256,1280]{1,0:T(8,128)(2,1)} %get-tuple-element.738), channel_id=1, source_target_pairs={{0,8},{4,12},{8,0},{12,4},{16,24},{20,28},{24,16},{28,20},{1,9},{5... | collective-permute-start | bytes 1966088 | tf_op jit(solution)/shard_map/up1_dp2/ppermute | solution.py:1037
  201.0 40.1 %collective-permute-start.18 = (bf16[1408,512]{1,0:T(8,128)(2,1)}, bf16[1408,512]{1,0:T(8,128)(2,1)S(1)}, u32[]{:S(2)}, u32[]{:S(2)}) collective-permute-start(bf16[1408,512]{1,0:T(8,128)(2,1)} %get-tuple-element.711), channel_id=1, source_target_pairs={{0,8},{4,12},{8,0},{12,4},{16,24},{20,28},{24,16},{28,20},{1,9},{5... | collective-permute-start | bytes 4325384 | tf_op jit(solution)/shard_map/down0_dp2/ppermute | solution.py:1037
  202.6 38.5 %collective-permute-start.21 = (bf16[1408,512]{1,0:T(8,128)(2,1)}, bf16[1408,512]{1,0:T(8,128)(2,1)S(1)}, u32[]{:S(2)}, u32[]{:S(2)}) collective-permute-start(bf16[1408,512]{1,0:T(8,128)(2,1)} %get-tuple-element.753), channel_id=1, source_target_pairs={{0,4},{4,0},{8,12},{12,8},{16,20},{20,16},{24,28},{28,24},{1,5},{5... | collective-permute-start | bytes 4325384 | tf_op jit(solution)/shard_map/down1_dp1/ppermute | solution.py:1037
  241.1 23.4 %collective-permute-start.22 = (bf16[4,512,1024]{2,1,0:T(8,128)(2,1)}, bf16[4,512,1024]{2,1,0:T(8,128)(2,1)}, u32[]{:S(2)}, u32[]{:S(2)}) collective-permute-start(bf16[4,512,1024]{2,1,0:T(8,128)(2,1)} %get-tuple-element.789), channel_id=1, source_target_pairs={{0,1},{1,0},{2,3},{3,2},{4,5},{5,4},{6,7},{7,6},{8,9},{9,8},{10,11... | collective-permute-start | bytes 12582920 | tf_op jit(solution)/shard_map/dense_expert1/ppermute | solution.py:1037
  241.2 37.9 %collective-permute-start.24 = (bf16[2,128,1536]{2,1,0:T(8,128)(2,1)}, bf16[2,128,1536]{2,1,0:T(8,128)(2,1)}, u32[]{:S(2)}, u32[]{:S(2)}) collective-permute-start(bf16[2,128,1536]{2,1,0:T(8,128)(2,1)} %get-tuple-element.821), channel_id=1, source_target_pairs={{0,16},{4,20},{8,24},{12,28},{16,0},{20,4},{24,8},{28,12},{1,17},{... | collective-permute-start | bytes 2359304 | tf_op jit(solution)/shard_map/gate0_dp4/ppermute | solution.py:1037
  249.4 23.1 %collective-permute-start.25 = (bf16[704,512]{1,0:T(8,128)(2,1)}, bf16[704,512]{1,0:T(8,128)(2,1)S(1)}, u32[]{:S(2)}, u32[]{:S(2)}) collective-permute-start(bf16[704,512]{1,0:T(8,128)(2,1)} %get-tuple-element.822), channel_id=1, source_target_pairs={{0,4},{4,0},{8,12},{12,8},{16,20},{20,16},{24,28},{28,24},{1,5},{5... | collective-permute-start | bytes 2162696 | tf_op jit(solution)/shard_map/down0_dp1/ppermute | solution.py:1037
  279.1 29.0 %collective-permute-start.28 = (bf16[2,256,1152]{2,1,0:T(8,128)(2,1)}, bf16[2,256,1152]{2,1,0:T(8,128)(2,1)S(1)}, u32[]{:S(2)}, u32[]{:S(2)}) collective-permute-start(bf16[2,256,1152]{2,1,0:T(8,128)(2,1)} %get-tuple-element.842), channel_id=1, source_target_pairs={{0,2},{1,3},{2,0},{3,1},{4,6},{5,7},{6,4},{7,5},{8,10},{9,11},{10,... | collective-permute-start | bytes 3538952 | tf_op jit(solution)/shard_map/out_q_expert2/ppermute | solution.py:1037
  279.4 25.1 %collective-permute-start.27 = (bf16[2,256,1024]{2,1,0:T(8,128)(2,1)}, bf16[2,256,1024]{2,1,0:T(8,128)(2,1)S(1)}, u32[]{:S(2)}, u32[]{:S(2)}) collective-permute-start(bf16[2,256,1024]{2,1,0:T(8,128)(2,1)} %get-tuple-element.838), channel_id=1, source_target_pairs={{0,4},{4,0},{8,12},{12,8},{16,20},{20,16},{24,28},{28,24},{1,5},{5... | collective-permute-start | bytes 3145736 | tf_op jit(solution)/shard_map/k_v_dp1/ppermute | solution.py:1037
  281.0 31.6 %collective-permute-start.29 = (bf16[704,512]{1,0:T(8,128)(2,1)S(1)}, bf16[704,512]{1,0:T(8,128)(2,1)S(1)}, u32[]{:S(2)}, u32[]{:S(2)}) collective-permute-start(bf16[704,512]{1,0:T(8,128)(2,1)S(1)} %copy-done.38), channel_id=1, source_target_pairs={{0,8},{4,12},{8,0},{12,4},{16,24},{20,28},{24,16},{28,20},{1,9},{5... | collective-permute-start | bytes 2162696 | tf_op jit(solution)/shard_map/down1_dp2/ppermute | solution.py:1037
  281.0 31.6 %collective-permute-start.30 = (bf16[2,128,1280]{2,1,0:T(8,128)(2,1)S(1)}, bf16[2,128,1280]{2,1,0:T(8,128)(2,1)S(1)}, u32[]{:S(2)}, u32[]{:S(2)}) collective-permute-start(bf16[2,128,1280]{2,1,0:T(8,128)(2,1)S(1)} %copy-done.40), channel_id=1, source_target_pairs={{0,16},{4,20},{8,24},{12,28},{16,0},{20,4},{24,8},{28,12},{1,17},{... | collective-permute-start | bytes 1966088 | tf_op jit(solution)/shard_map/gate1_dp4/ppermute | solution.py:1037
  297.1 51.0 %collective-permute-start.26 = (bf16[2,320,1024]{2,1,0:T(8,128)(2,1)}, bf16[2,320,1024]{2,1,0:T(8,128)(2,1)S(1)}, u32[]{:S(2)}, u32[]{:S(2)}) collective-permute-start(bf16[2,320,1024]{2,1,0:T(8,128)(2,1)} %get-tuple-element.836), channel_id=1, source_target_pairs={{0,2},{1,3},{2,0},{3,1},{4,6},{5,7},{6,4},{7,5},{8,10},{9,11},{10,... | collective-permute-start | bytes 3932168 | tf_op jit(solution)/shard_map/produced_rows2/ppermute | solution.py:1037
  321.1 22.7 %collective-permute-start.32 = (bf16[2,128,1152]{2,1,0:T(8,128)(2,1)}, bf16[2,128,1152]{2,1,0:T(8,128)(2,1)S(1)}, u32[]{:S(2)}, u32[]{:S(2)}) collective-permute-start(bf16[2,128,1152]{2,1,0:T(8,128)(2,1)} %get-tuple-element.896), channel_id=1, source_target_pairs={{0,4},{4,0},{8,12},{12,8},{16,20},{20,16},{24,28},{28,24},{1,5},{5... | collective-permute-start | bytes 1769480 | tf_op jit(solution)/shard_map/out_q_dp1/ppermute | solution.py:1037
  321.7 22.2 %collective-permute-start.31 = (bf16[2,128,1024]{2,1,0:T(8,128)(2,1)}, bf16[2,128,1024]{2,1,0:T(8,128)(2,1)S(1)}, u32[]{:S(2)}, u32[]{:S(2)}) collective-permute-start(bf16[2,128,1024]{2,1,0:T(8,128)(2,1)} %get-tuple-element.888), channel_id=1, source_target_pairs={{0,8},{4,12},{8,0},{12,4},{16,24},{20,28},{24,16},{28,20},{1,9},{5... | collective-permute-start | bytes 1572872 | tf_op jit(solution)/shard_map/k_v_dp2/ppermute | solution.py:1037
  323.4 39.5 %collective-permute-start.37 = (bf16[2,352,512]{2,1,0:T(8,128)(2,1)S(1)}, bf16[2,352,512]{2,1,0:T(8,128)(2,1)S(1)}, u32[]{:S(2)}, u32[]{:S(2)}) collective-permute-start(bf16[2,352,512]{2,1,0:T(8,128)(2,1)S(1)} %copy-done.39), channel_id=1, source_target_pairs={{0,16},{4,20},{8,24},{12,28},{16,0},{20,4},{24,8},{28,12},{1,17},{... | collective-permute-start | bytes 2162696 | tf_op jit(solution)/shard_map/down0_dp4/ppermute | solution.py:1037
  348.7 14.1 %collective-permute-start.35 = (bf16[2,64,1152]{2,1,0:T(8,128)(2,1)}, bf16[2,64,1152]{2,1,0:T(8,128)(2,1)S(1)}, u32[]{:S(2)}, u32[]{:S(2)}) collective-permute-start(bf16[2,64,1152]{2,1,0:T(8,128)(2,1)} %get-tuple-element.928), channel_id=1, source_target_pairs={{0,8},{4,12},{8,0},{12,4},{16,24},{20,28},{24,16},{28,20},{1,9},{5... | collective-permute-start | bytes 884744 | tf_op jit(solution)/shard_map/out_q_dp2/ppermute | solution.py:1037
  348.7 14.1 %collective-permute-start.36 = (bf16[2,64,1024]{2,1,0:T(8,128)(2,1)}, bf16[2,64,1024]{2,1,0:T(8,128)(2,1)S(1)}, u32[]{:S(2)}, u32[]{:S(2)}) collective-permute-start(bf16[2,64,1024]{2,1,0:T(8,128)(2,1)} %get-tuple-element.932), channel_id=1, source_target_pairs={{0,2},{1,3},{2,0},{3,1},{4,6},{5,7},{6,4},{7,5},{8,10},{9,11},{10,... | collective-permute-start | bytes 786440 | tf_op jit(solution)/shard_map/k_v_expert2/ppermute | solution.py:1037
  367.5 15.3 %collective-permute-start.38 = (bf16[2,32,2176]{2,1,0:T(8,128)(2,1)}, bf16[2,32,2176]{2,1,0:T(8,128)(2,1)S(1)}, u32[]{:S(2)}, u32[]{:S(2)}) collective-permute-start(bf16[2,32,2176]{2,1,0:T(8,128)(2,1)} %get-tuple-element.953), channel_id=1, source_target_pairs={{0,16},{4,20},{8,24},{12,28},{16,0},{20,4},{24,8},{28,12},{1,17},{... | collective-permute-start | bytes 835592 | tf_op jit(solution)/shard_map/out_q_dp4/ppermute | solution.py:1037
  (48 other events, 304.3 us)

commit v7 on v6

--- a/solution.py
+++ b/solution.py
@@ -193,8 +193,8 @@
     rows = mid.shape[0]
     nm = (mid * rms_scale(mid) * gain_ref[...]).astype(BF)
     nm_ref[...] = nm
-    router = jnp.concatenate([wr_ref[...], jnp.zeros((TAIL - experts, nm.shape[1]), BF)], axis=0)
-    logits = dot_nt(router, nm)
+    router = jnp.concatenate([wr_ref[...].astype(F32), jnp.zeros((TAIL - experts, nm.shape[1]), F32)], axis=0)
+    logits = dot_nt(router.astype(BF), nm)
     live = lax.broadcasted_iota(jnp.int32, logits.shape, 0) < experts
     logits = jnp.where(live, logits, FAR)
     raised = jnp.exp(logits - jnp.max(logits, axis=0, keepdims=True))

time: 394 us -> 394 us (level)
  no operation moved by 1% of the time
where the time goes in v7:
time: 394 us; the launch traced here: 387 us
  Pallas kernels  254 us (64%)
  waiting for transfers between devices  64.5 us (16%)
  starting transfers between devices  36.9 us (9%)
  local copies, waits for them, and re-layouts  24.1 us (6%)
  other arithmetic  5.96 us (2%)
    pallas_call x23, Pallas kernels, call(): pl.pallas_call(kernel, in_specs=list(in_specs), compiler_params=params(),...  254 us
    ppermute x39, waiting for transfers between devices, swap(): return lax.ppermute(value, axis, [(i, i ^ mask) for i in range(size)])  64.5 us
    ppermute x39, starting transfers between devices, swap(): return lax.ppermute(value, axis, [(i, i ^ mask) for i in range(size)])  36.9 us
    unnamed x83, local copies, waits for them, and re-layouts  15.8 us
  transfers between devices with their start and end apart: 39, of which 13 were waited for; matrix products, arithmetic and copies ran while one was open for 4% of the time, Pallas kernels for 56%

profile of v7, /device:TPU:0, one launch (start us, length us, event | category | flops | bytes accessed | tf_op | source)
XLA Modules:
  0.0 387.0 jit_solution(16371647202524097531)
XLA Ops:
  3.8 15.6 %attn_first.1 = (bf16[512,1024]{1,0:T(8,128)(2,1)}, bf16[512,1024]{1,0:T(8,128)(2,1)}, bf16[512,1024]{1,0:T(8,128)(2,1)}, f32[4,4,512]{2,1,0:T(4,128)}, f32[1,12...) custom-call(bf16[512,1024]{1,0:T(8,128)(2,1)} %tok_ref.7, ...), custom_call_target="tpu_custom_call" | custom-call | flops 115000000 | bytes 100000 | tf_op jit(solution)/shard_map/attn_first/pallas_call | solution.py:100
  19.8 12.3 %attn_second.1 = (bf16[512,1024]{1,0:T(8,128)(2,1)}, f32[4,4,512]{2,1,0:T(4,128)}, f32[512,1024]{1,0:T(8,128)}, bf16[512,1024]{1,0:T(8,128)(2,1)}, f32[16,512]{1,0:T(8,128)}, /*index=5*/bf16[272,1024]{1,0:T(8,128)(2,1)}) custom-call(bf16[512,1024]{1,0:T(8,128)(2,1)} %tok_ref.7, ...), custom_call_target="tpu_custom_call", output_to_operand_aliasing={{0}: (9, {}), {1}: (10, {}), {2}: (11, {}), {3}: (12, {}), ... | custom-call | flops 115000000 | bytes 100000 | tf_op jit(solution)/shard_map/attn_second/pallas_call | solution.py:100
  32.2 7.4 %collective-permute-done.2.refs_2_.refs_6_ = bf16[272,1024]{1,0:T(8,128)(2,1)S(1)} collective-permute-done((bf16[272,1024]{1,0:T(8,128)(2,1)}, bf16[272,1024]{1,0:T(8,128)(2,1)S(1)}, u32[]{:S(2)}, u32[]{:S(2)}) %collective-permute-start.2) | collective-permute-done | bytes 557088 | tf_op jit(solution)/shard_map/rows_a0_2/ppermute | solution.py:1037
  44.3 11.1 %cot_hidden.1 = (bf16[1280,1536]{1,0:T(8,128)(2,1)}, bf16[1280,1024]{1,0:T(8,128)(2,1)}) custom-call(s32[1]{0:T(128)} %bitcast.9.me_ref.refs_0_, bf16[272,1024]{1,0:T(8,128)(2,1)} %get-tuple-element.553.refs_0_.refs_2_, bf16[272,1024]{1,0:T(8,128)(2,1)} %copy-done.2, bf16[272,1024]{1,0:T(8,128)(2,1)} %copy-done.3, bf16[272,1024]{1,0:T(8,128)(2,1)} %copy-done.4, ...), custom_call_target="tpu_custom_call" | custom-call | flops 115000000 | bytes 100000 | tf_op jit(solution)/shard_map/cot_hidden/pallas_call | solution.py:100
  58.3 32.6 %expert_grads.2 = (bf16[1280,1024]{1,0:T(8,128)(2,1)}, bf16[1024,1280]{1,0:T(8,128)(2,1)}, f32[1280,128]{1,0:T(8,128)}, bf16[1280,1024]{1,0:T(8,128)(2,1)}, bf16...) custom-call(s32[1]{0:T(128)} %bitcast.9.me_ref.refs_0_, ...), custom_call_target="tpu_custom_call" | custom-call | flops 115000000 | bytes 100000 | tf_op jit(solution)/shard_map/expert_grads/pallas_call | solution.py:100
  96.4 8.1 %cot_hidden_more.1.refs_3_ = bf16[1280,1280]{1,0:T(8,128)(2,1)} custom-call(bf16[1280,1024]{1,0:T(8,128)(2,1)} %get-tuple-element.585.refs_10_.rows_ref, bf16[1,2816,1024]{2,1,0:T(8,128)(2,1)} %wd_ref.3), custom_call_target="tpu_custom_call" | custom-call | flops 115000000 | bytes 100000 | tf_op jit(solution)/shard_map/cot_hidden_more/pallas_call | solution.py:100
  104.6 25.3 %expert_grads.3 = (bf16[512,1280]{1,0:T(8,128)(2,1)}, bf16[512,1280]{1,0:T(8,128)(2,1)}, bf16[512,1280]{1,0:T(8,128)(2,1)}, bf16[512,1280]{1,0:T(8,128)(2,1)}, f...) custom-call(bf16[1280,1024]{1,0:T(8,128)(2,1)} %get-tuple-element.58, ...), custom_call_target="tpu_custom_call", output_to_operand_aliasing={{5}: (6, {}), {6}: (7, {}), {7}: (8, {}), {8}: (9, {})} | custom-call | flops 115000000 | bytes 100000 | tf_op jit(solution)/shard_map/expert_grads/pallas_call | solution.py:100
  130.7 25.9 %expert_input_grad.1 = (bf16[1,336,1024]{2,1,0:T(8,128)(2,1)}, bf16[1,336,1024]{2,1,0:T(8,128)(2,1)}, bf16[2,336,1024]{2,1,0:T(8,128)(2,1)}) custom-call(bf16[1280,2816]{1,0:T(8,128)(2,1)} %get-tuple-element.617.gg_ref, bf16[1280,2816]{1,0:T(8,128)(2,1)} %get-tuple-element.618.gu_ref, f32[1280,128]{1,0:T(8,128)} %get-tuple-element.619.refs_0_, ...), custom_call_target="tpu_custom_call" | custom-call | flops 115000000 | bytes 100000 | tf_op jit(solution)/shard_map/expert_input_grad/pallas_call | solution.py:100
  159.7 4.6 %fold.6 = (bf16[256,1536]{1,0:T(8,128)(2,1)}, bf16[256,1536]{1,0:T(8,128)(2,1)}, bf16[256,1536]{1,0:T(8,128)(2,1)}, bf16[256,1536]{1,0:T(8,128)(2,1)}) custom-call(bf16[512,1536]{1,0:T(8,128)(2,1)} %get-tuple-element.634.refs_0_, bf16[512,1536]{1,0:T(8,128)(2,1)} %copy-done.5, bf16[512,1536]{1,0:T(8,128)(2,1)} %get-tuple-element.636.refs_2_, ...), custom_call_target="tpu_custom_call" | custom-call | flops 115000000 | bytes 100000 | tf_op jit(solution)/shard_map/fold/pallas_call | solution.py:100
  167.4 16.8 %down_grads.1 = (bf16[1408,512]{1,0:T(8,128)(2,1)}, bf16[1408,512]{1,0:T(8,128)(2,1)}, bf16[1408,512]{1,0:T(8,128)(2,1)}, bf16[1408,512]{1,0:T(8,128)(2,1)}) custom-call(s32[8]{0:T(128)} %get-tuple-element.1021.place_a_ref, s32[8]{0:T(128)} %get-tuple-element.552.refs_1_.place_b_ref, bf16[2816,1280]{1,0:T(8,128)(2,1)} %get-tuple-element.648.hidt_ref, ...), custom_call_target="tpu_custom_call" | custom-call | flops 11500000256 | bytes 100000 | tf_op jit(solution)/shard_map/down_grads/pallas_call | solution.py:100
  186.9 5.5 %fold.7 = (bf16[256,1280]{1,0:T(8,128)(2,1)}, bf16[256,1280]{1,0:T(8,128)(2,1)}, bf16[256,1280]{1,0:T(8,128)(2,1)}, bf16[256,1280]{1,0:T(8,128)(2,1)}, bf16[2,12...) custom-call(bf16[512,1280]{1,0:T(8,128)(2,1)} %get-tuple-element.670.refs_0_, bf16[512,1280]{1,0:T(8,128)(2,1)} %copy-done.34, ...), custom_call_target="tpu_custom_call" | custom-call | flops 2300000000 | bytes 100000 | tf_op jit(solution)/shard_map/fold/pallas_call | solution.py:100
  194.5 4.7 %sorted_rows.1 = (bf16[1024,512]{1,0:T(8,128)(2,1)}, bf16[2,1024,512]{2,1,0:T(8,128)(2,1)}) custom-call(s32[32]{0:T(128)} %get-tuple-element.1020.pq_ref.place_ref, s32[32]{0:T(128)} %get-tuple-element.1019.pk_ref, bf16[512,1024]{1,0:T(8,128)(2,1)} %tok_ref.7, f32[1,1024]{1,0:T(1,128)} %bitcast.46, bf16[512,1024]{1,0:T(8,128)(2,1)} %get-tuple-element.705.att_ref), custom_call_target="tpu_custom_call" | custom-call | flops 115000000 | bytes 100000 | tf_op jit(solution)/shard_map/sorted_rows/pallas_call | solution.py:100
  204.9 10.0 %moe_bwd.1 = (f32[512,1024]{1,0:T(8,128)}, bf16[512,1024]{1,0:T(8,128)(2,1)}, bf16[512,1024]{1,0:T(8,128)(2,1)}, f32[1,1024]{1,0:T(1,128)}, f32[16,1024]{1,0:T(8,128)}) custom-call(bf16[512,1024]{1,0:T(8,128)(2,1)} %cot_ref.1, f32[512,1024]{1,0:T(8,128)} %get-tuple-element.512.mid_ref, f32[1,1024]{1,0:T(1,128)} %bitcast.44, ...), custom_call_target="tpu_custom_call" | custom-call | flops 115000000 | bytes 100000 | tf_op jit(solution)/shard_map/moe_bwd/pallas_call | solution.py:100
  215.0 16.2 %attn_bwd.1 = (bf16[512,1024]{1,0:T(8,128)(2,1)}, bf16[512,1024]{1,0:T(8,128)(2,1)}, bf16[512,1024]{1,0:T(8,128)(2,1)}, f32[4,4,512]{2,1,0:T(4,128)}) custom-call(bf16[512,1024]{1,0:T(8,128)(2,1)} %get-tuple-element.496.qs_ref, bf16[512,1024]{1,0:T(8,128)(2,1)} %get-tuple-element.497.k_ref, bf16[512,1024]{1,0:T(8,128)(2,1)} %get-tuple-element.498.v_ref, ...), custom_call_target="tpu_custom_call" | custom-call | flops 115000000 | bytes 100000 | tf_op jit(solution)/shard_map/attn_bwd/pallas_call | solution.py:100
  231.2 9.3 %dense_terms.1 = (bf16[4,512,1024]{2,1,0:T(8,128)(2,1)}, bf16[4,512,1024]{2,1,0:T(8,128)(2,1)}) custom-call(bf16[1024,512]{1,0:T(8,128)(2,1)} %get-tuple-element.712.att_ref, bf16[2,1024,512]{2,1,0:T(8,128)(2,1)} %get-tuple-element.713.rows_ref, bf16[512,1024]{1,0:T(8,128)(2,1)} %get-tuple-element.727.branch_ref, ...), custom_call_target="tpu_custom_call" | custom-call | flops 15064999936 | bytes 100000 | tf_op jit(solution)/shard_map/dense_terms/pallas_call | solution.py:100
  241.2 2.6 collective-permute-start.24
  243.8 5.6 %fold.8 = (bf16[704,512]{1,0:T(8,128)(2,1)}, bf16[704,512]{1,0:T(8,128)(2,1)}, bf16[704,512]{1,0:T(8,128)(2,1)}, bf16[704,512]{1,0:T(8,128)(2,1)}, bf16[2,128,12...) custom-call(bf16[1408,512]{1,0:T(8,128)(2,1)} %get-tuple-element.772.refs_0_, bf16[1408,512]{1,0:T(8,128)(2,1)} %copy-done.6, ...), custom_call_target="tpu_custom_call" | custom-call | flops 115000000 | bytes 100000 | tf_op jit(solution)/shard_map/fold/pallas_call | solution.py:100
  253.5 10.9 %norm_bwd.1 = (f32[512,1024]{1,0:T(8,128)}, bf16[512,128]{1,0:T(8,128)(2,1)}, bf16[512,128]{1,0:T(8,128)(2,1)}) custom-call(s32[32]{0:T(128)} %get-tuple-element.1020.pq_ref.place_ref, bf16[512,1024]{1,0:T(8,128)(2,1)} %tok_ref.7, f32[1,1024]{1,0:T(1,128)} %bitcast.47, f32[512,1024]{1,0:T(8,128)} %get-tuple-element.790.gmid_ref, ...), custom_call_target="tpu_custom_call" | custom-call | flops 115000000 | bytes 100000 | tf_op jit(solution)/shard_map/norm_bwd/pallas_call | solution.py:100
  266.8 5.8 %fold_first.1 = (bf16[2,256,1152]{2,1,0:T(8,128)(2,1)}, bf16[2,256,1152]{2,1,0:T(8,128)(2,1)}, bf16[2,256,1024]{2,1,0:T(8,128)(2,1)}, bf16[2,256,1024]{2,1,0:T(8,128)(2,1)}) custom-call(bf16[4,512,1024]{2,1,0:T(8,128)(2,1)} %get-tuple-element.808.keep_ref, bf16[4,512,1024]{2,1,0:T(8,128)(2,1)} %collective-permute-done.22.got_ref, ...), custom_call_target="tpu_custom_call" | custom-call | flops 115000000 | bytes 100000 | tf_op jit(solution)/shard_map/fold_first/pallas_call | solution.py:100
  272.6 6.5 %collective-permute-done.24.refs_9_ = bf16[2,128,1536]{2,1,0:T(8,128)(2,1)} collective-permute-done((bf16[2,128,1536]{2,1,0:T(8,128)(2,1)}, bf16[2,128,1536]{2,1,0:T(8,128)(2,1)}, u32[]{:S(2)}, u32[]{:S(2)}) %collective-permute-start.24) | collective-permute-done | bytes 786464 | tf_op jit(solution)/shard_map/gate0_dp4/ppermute | solution.py:1037
  281.0 3.1 collective-permute-start.30
  284.2 12.9 %produced_rows.1 = (bf16[2,320,1024]{2,1,0:T(8,128)(2,1)}, bf16[2,320,1024]{2,1,0:T(8,128)(2,1)}) custom-call(bf16[1280,2816]{1,0:T(8,128)(2,1)} %get-tuple-element.829.hid_ref, bf16[1,2816,1024]{2,1,0:T(8,128)(2,1)} %wd_ref.3), custom_call_target="tpu_custom_call" | custom-call | flops 115000000 | bytes 100000 | tf_op jit(solution)/shard_map/produced_rows/pallas_call | solution.py:100
  299.9 4.6 %collective-permute-done.27.refs_1_ = bf16[2,256,1024]{2,1,0:T(8,128)(2,1)S(1)} collective-permute-done((bf16[2,256,1024]{2,1,0:T(8,128)(2,1)}, bf16[2,256,1024]{2,1,0:T(8,128)(2,1)S(1)}, u32[]{:S(2)}, u32[]{:S(2)}) %collective-permute-start.27) | collective-permute-done | bytes 1048608 | tf_op jit(solution)/shard_map/k_v_dp1/ppermute | solution.py:1037
  304.5 3.6 collective-permute-done.28.refs_3_
  308.1 4.5 %collective-permute-done.29.refs_7_ = bf16[704,512]{1,0:T(8,128)(2,1)S(1)} collective-permute-done((bf16[704,512]{1,0:T(8,128)(2,1)S(1)}, bf16[704,512]{1,0:T(8,128)(2,1)S(1)}, u32[]{:S(2)}, u32[]{:S(2)}) %collective-permute-start.29) | collective-permute-done | bytes 720928 | tf_op jit(solution)/shard_map/down1_dp2/ppermute | solution.py:1037
  314.3 6.8 %fold.9 = (bf16[2,128,1024]{2,1,0:T(8,128)(2,1)}, bf16[2,128,1024]{2,1,0:T(8,128)(2,1)}, bf16[2,128,1152]{2,1,0:T(8,128)(2,1)}, bf16[2,128,1152]{2,1,0:T(8,128)(...) custom-call(bf16[2,256,1024]{2,1,0:T(8,128)(2,1)} %get-tuple-element, ...), custom_call_target="tpu_custom_call" | custom-call | flops 115000000 | bytes 100000 | tf_op jit(solution)/shard_map/fold/pallas_call | solution.py:100
  323.4 2.7 collective-permute-start.37
  328.5 15.3 %collective-permute-done.31.refs_1_ = bf16[2,128,1024]{2,1,0:T(8,128)(2,1)S(1)} collective-permute-done((bf16[2,128,1024]{2,1,0:T(8,128)(2,1)}, bf16[2,128,1024]{2,1,0:T(8,128)(2,1)S(1)}, u32[]{:S(2)}, u32[]{:S(2)}) %collective-permute-start.31) | collective-permute-done | bytes 524320 | tf_op jit(solution)/shard_map/k_v_dp2/ppermute | solution.py:1037
  352.1 6.3 %layer_output.1 = bf16[512,1024]{1,0:T(8,128)(2,1)} custom-call(f32[512,1024]{1,0:T(8,128)} %get-tuple-element.512.mid_ref, f32[16,512]{1,0:T(8,128)} %select_maximum_fusion.3.ch_ref, s32[512,4]{1,0:T(8,128)} %bitcast.39, bf16[2,320,1024]{2,1,0:T(8,128)(2,1)} %get-tuple-element.833.refs_0_, bf16[1,320,1024]{2,1,0:T(8,128)(2,1)} %copy-done.19, ...), custom_call_target="tpu_custom_call" | custom-call | flops 115000000 | bytes 100000 | tf_op jit(solution)/shard_map/layer_output/pallas_call | solution.py:100
  358.4 4.4 %collective-permute-done.35.refs_1_ = bf16[2,64,1152]{2,1,0:T(8,128)(2,1)S(1)} collective-permute-done((bf16[2,64,1152]{2,1,0:T(8,128)(2,1)}, bf16[2,64,1152]{2,1,0:T(8,128)(2,1)S(1)}, u32[]{:S(2)}, u32[]{:S(2)}) %collective-permute-start.35) | collective-permute-done | bytes 294944 | tf_op jit(solution)/shard_map/out_q_dp2/ppermute | solution.py:1037
  364.5 3.0 fold.11
  370.7 12.2 %collective-permute-done.38.got_ref = bf16[2,32,2176]{2,1,0:T(8,128)(2,1)S(1)} collective-permute-done((bf16[2,32,2176]{2,1,0:T(8,128)(2,1)}, bf16[2,32,2176]{2,1,0:T(8,128)(2,1)S(1)}, u32[]{:S(2)}, u32[]{:S(2)}) %collective-permute-start.38) | collective-permute-done | bytes 278560 | tf_op jit(solution)/shard_map/out_q_dp4/ppermute | solution.py:1037
  (179 shorter events, 69.2 us)
Async XLA Ops:
  0.6 31.5 %collective-permute-start.1 = (bf16[512,1024]{1,0:T(8,128)(2,1)}, bf16[512,1024]{1,0:T(8,128)(2,1)S(1)}, u32[]{:S(2)}, u32[]{:S(2)}) collective-permute-start(bf16[512,1024]{1,0:T(8,128)(2,1)} %cot_ref.1), channel_id=1, source_target_pairs={{0,1},{1,0},{2,3},{3,2},{4,5},{5,4},{6,7},{7,6},{8,9},{9,8},{10,11... | collective-permute-start | bytes 3145736 | tf_op jit(solution)/shard_map/cot0_1/ppermute | solution.py:1037
  1.2 38.5 %collective-permute-start.4 = (bf16[512,1024]{1,0:T(8,128)(2,1)}, bf16[512,1024]{1,0:T(8,128)(2,1)}, u32[]{:S(2)}, u32[]{:S(2)}) collective-permute-start(bf16[512,1024]{1,0:T(8,128)(2,1)} %cot_ref.1), channel_id=1, source_target_pairs={{0,2},{1,3},{2,0},{3,1},{4,6},{5,7},{6,4},{7,5},{8,10},{9,11},{10,... | collective-permute-start | bytes 3145736 | tf_op jit(solution)/shard_map/cot0_2/ppermute | solution.py:1037
  19.3 12.9 %collective-permute-start = (bf16[272,1024]{1,0:T(8,128)(2,1)}, bf16[272,1024]{1,0:T(8,128)(2,1)S(1)}, u32[]{:S(2)}, u32[]{:S(2)}) collective-permute-start(bf16[272,1024]{1,0:T(8,128)(2,1)} %get-tuple-element.553.refs_0_.refs_2_), channel_id=1, source_target_pairs={{0,1},{1,0},{2,3},{3,2},{4,5},{5,4},{6,7},{7,6},{8,9},{9,8},{10,11... | collective-permute-start | bytes 1671176 | tf_op jit(solution)/shard_map/rows_a0_1/ppermute | solution.py:1037
  19.6 20.1 %collective-permute-start.2 = (bf16[272,1024]{1,0:T(8,128)(2,1)}, bf16[272,1024]{1,0:T(8,128)(2,1)S(1)}, u32[]{:S(2)}, u32[]{:S(2)}) collective-permute-start(bf16[272,1024]{1,0:T(8,128)(2,1)} %get-tuple-element.553.refs_0_.refs_2_), channel_id=1, source_target_pairs={{0,2},{1,3},{2,0},{3,1},{4,6},{5,7},{6,4},{7,5},{8,10},{9,11},{10,... | collective-permute-start | bytes 1671176 | tf_op jit(solution)/shard_map/rows_a0_2/ppermute | solution.py:1037
  40.2 15.3 %collective-permute-start.7 = (bf16[272,1024]{1,0:T(8,128)(2,1)}, bf16[272,1024]{1,0:T(8,128)(2,1)S(1)}, u32[]{:S(2)}, u32[]{:S(2)}) collective-permute-start(bf16[272,1024]{1,0:T(8,128)(2,1)} %get-tuple-element.554.refs_3_), channel_id=1, source_target_pairs={{0,2},{1,3},{2,0},{3,1},{4,6},{5,7},{6,4},{7,5},{8,10},{9,11},{10,... | collective-permute-start | bytes 1671176 | tf_op jit(solution)/shard_map/rows_b0_2/ppermute | solution.py:1037
  41.9 14.2 %collective-permute-start.6 = (bf16[272,1024]{1,0:T(8,128)(2,1)}, bf16[272,1024]{1,0:T(8,128)(2,1)}, u32[]{:S(2)}, u32[]{:S(2)}) collective-permute-start(bf16[272,1024]{1,0:T(8,128)(2,1)} %get-tuple-element.554.refs_3_), channel_id=1, source_target_pairs={{0,1},{1,0},{2,3},{3,2},{4,5},{5,4},{6,7},{7,6},{8,9},{9,8},{10,11... | collective-permute-start | bytes 1671176 | tf_op jit(solution)/shard_map/rows_b0_1/ppermute | solution.py:1037
  90.9 67.6 %collective-permute-start.10 = (bf16[512,1536]{1,0:T(8,128)(2,1)}, bf16[512,1536]{1,0:T(8,128)(2,1)S(1)}, u32[]{:S(2)}, u32[]{:S(2)}) collective-permute-start(bf16[512,1536]{1,0:T(8,128)(2,1)} %get-tuple-element.612), channel_id=1, source_target_pairs={{0,8},{4,12},{8,0},{12,4},{16,24},{20,28},{24,16},{28,20},{1,9},{5... | collective-permute-start | bytes 4718600 | tf_op jit(solution)/shard_map/gate0_dp2/ppermute | solution.py:1037
  92.8 65.8 %collective-permute-start.11 = (bf16[512,1536]{1,0:T(8,128)(2,1)}, bf16[512,1536]{1,0:T(8,128)(2,1)}, u32[]{:S(2)}, u32[]{:S(2)}) collective-permute-start(bf16[512,1536]{1,0:T(8,128)(2,1)} %get-tuple-element.630), channel_id=1, source_target_pairs={{0,4},{4,0},{8,12},{12,8},{16,20},{20,16},{24,28},{28,24},{1,5},{5... | collective-permute-start | bytes 4718600 | tf_op jit(solution)/shard_map/up0_dp1/ppermute | solution.py:1037
  129.9 54.3 %collective-permute-start.9 = (bf16[512,1280]{1,0:T(8,128)(2,1)}, bf16[512,1280]{1,0:T(8,128)(2,1)S(1)}, u32[]{:S(2)}, u32[]{:S(2)}) collective-permute-start(bf16[512,1280]{1,0:T(8,128)(2,1)} %get-tuple-element.609), channel_id=1, source_target_pairs={{0,8},{4,12},{8,0},{12,4},{16,24},{20,28},{24,16},{28,20},{1,9},{5... | collective-permute-start | bytes 3932168 | tf_op jit(solution)/shard_map/gate1_dp2/ppermute | solution.py:1037
  130.4 53.8 %collective-permute-start.12 = (bf16[512,1280]{1,0:T(8,128)(2,1)}, bf16[512,1280]{1,0:T(8,128)(2,1)S(1)}, u32[]{:S(2)}, u32[]{:S(2)}) collective-permute-start(bf16[512,1280]{1,0:T(8,128)(2,1)} %get-tuple-element.658), channel_id=1, source_target_pairs={{0,4},{4,0},{8,12},{12,8},{16,20},{20,16},{24,28},{28,24},{1,5},{5... | collective-permute-start | bytes 3932168 | tf_op jit(solution)/shard_map/up1_dp1/ppermute | solution.py:1037
  156.6 35.8 %collective-permute-start.15 = (bf16[2,336,1024]{2,1,0:T(8,128)(2,1)}, bf16[2,336,1024]{2,1,0:T(8,128)(2,1)S(1)}, u32[]{:S(2)}, u32[]{:S(2)}) collective-permute-start(bf16[2,336,1024]{2,1,0:T(8,128)(2,1)} %get-tuple-element.696), channel_id=1, source_target_pairs={{0,2},{1,3},{2,0},{3,1},{4,6},{5,7},{6,4},{7,5},{8,10},{9,11},{10,... | collective-permute-start | bytes 4128776 | tf_op jit(solution)/shard_map/grad_rows2/ppermute | solution.py:1037
  164.3 19.9 %collective-permute-start.13 = (bf16[256,1536]{1,0:T(8,128)(2,1)}, bf16[256,1536]{1,0:T(8,128)(2,1)S(1)}, u32[]{:S(2)}, u32[]{:S(2)}) collective-permute-start(bf16[256,1536]{1,0:T(8,128)(2,1)} %get-tuple-element.662), channel_id=1, source_target_pairs={{0,4},{4,0},{8,12},{12,8},{16,20},{20,16},{24,28},{28,24},{1,5},{5... | collective-permute-start | bytes 2359304 | tf_op jit(solution)/shard_map/gate0_dp1/ppermute | solution.py:1037
  165.8 18.4 %collective-permute-start.14 = (bf16[256,1536]{1,0:T(8,128)(2,1)}, bf16[256,1536]{1,0:T(8,128)(2,1)S(1)}, u32[]{:S(2)}, u32[]{:S(2)}) collective-permute-start(bf16[256,1536]{1,0:T(8,128)(2,1)} %get-tuple-element.666), channel_id=1, source_target_pairs={{0,8},{4,12},{8,0},{12,4},{16,24},{20,28},{24,16},{28,20},{1,9},{5... | collective-permute-start | bytes 2359304 | tf_op jit(solution)/shard_map/up0_dp2/ppermute | solution.py:1037
  192.5 6.8 %collective-permute-start.17 = (bf16[1,336,1024]{2,1,0:T(8,128)(2,1)S(1)}, bf16[1,336,1024]{2,1,0:T(8,128)(2,1)S(1)}, u32[]{:S(2)}, u32[]{:S(2)}) collective-permute-start(bf16[1,336,1024]{2,1,0:T(8,128)(2,1)S(1)} %slice.27), channel_id=1, source_target_pairs={{0,1},{1,0},{2,3},{3,2},{4,5},{5,4},{6,7},{7,6},{8,9},{9,8},{10,11... | collective-permute-start | bytes 2064392 | tf_op jit(solution)/shard_map/grad_rows1_3/ppermute | solution.py:1037
  193.0 38.1 %collective-permute-start.20 = (bf16[256,1280]{1,0:T(8,128)(2,1)}, bf16[256,1280]{1,0:T(8,128)(2,1)}, u32[]{:S(2)}, u32[]{:S(2)}) collective-permute-start(bf16[256,1280]{1,0:T(8,128)(2,1)} %get-tuple-element.739), channel_id=1, source_target_pairs={{0,4},{4,0},{8,12},{12,8},{16,20},{20,16},{24,28},{28,24},{1,5},{5... | collective-permute-start | bytes 1966088 | tf_op jit(solution)/shard_map/gate1_dp1/ppermute | solution.py:1037
  193.6 37.6 %collective-permute-start.19 = (bf16[256,1280]{1,0:T(8,128)(2,1)}, bf16[256,1280]{1,0:T(8,128)(2,1)}, u32[]{:S(2)}, u32[]{:S(2)}) collective-permute-start(bf16[256,1280]{1,0:T(8,128)(2,1)} %get-tuple-element.738), channel_id=1, source_target_pairs={{0,8},{4,12},{8,0},{12,4},{16,24},{20,28},{24,16},{28,20},{1,9},{5... | collective-permute-start | bytes 1966088 | tf_op jit(solution)/shard_map/up1_dp2/ppermute | solution.py:1037
  201.0 40.1 %collective-permute-start.18 = (bf16[1408,512]{1,0:T(8,128)(2,1)}, bf16[1408,512]{1,0:T(8,128)(2,1)S(1)}, u32[]{:S(2)}, u32[]{:S(2)}) collective-permute-start(bf16[1408,512]{1,0:T(8,128)(2,1)} %get-tuple-element.711), channel_id=1, source_target_pairs={{0,8},{4,12},{8,0},{12,4},{16,24},{20,28},{24,16},{28,20},{1,9},{5... | collective-permute-start | bytes 4325384 | tf_op jit(solution)/shard_map/down0_dp2/ppermute | solution.py:1037
  202.6 38.5 %collective-permute-start.21 = (bf16[1408,512]{1,0:T(8,128)(2,1)}, bf16[1408,512]{1,0:T(8,128)(2,1)S(1)}, u32[]{:S(2)}, u32[]{:S(2)}) collective-permute-start(bf16[1408,512]{1,0:T(8,128)(2,1)} %get-tuple-element.753), channel_id=1, source_target_pairs={{0,4},{4,0},{8,12},{12,8},{16,20},{20,16},{24,28},{28,24},{1,5},{5... | collective-permute-start | bytes 4325384 | tf_op jit(solution)/shard_map/down1_dp1/ppermute | solution.py:1037
  241.1 23.4 %collective-permute-start.22 = (bf16[4,512,1024]{2,1,0:T(8,128)(2,1)}, bf16[4,512,1024]{2,1,0:T(8,128)(2,1)}, u32[]{:S(2)}, u32[]{:S(2)}) collective-permute-start(bf16[4,512,1024]{2,1,0:T(8,128)(2,1)} %get-tuple-element.789), channel_id=1, source_target_pairs={{0,1},{1,0},{2,3},{3,2},{4,5},{5,4},{6,7},{7,6},{8,9},{9,8},{10,11... | collective-permute-start | bytes 12582920 | tf_op jit(solution)/shard_map/dense_expert1/ppermute | solution.py:1037
  241.2 37.9 %collective-permute-start.24 = (bf16[2,128,1536]{2,1,0:T(8,128)(2,1)}, bf16[2,128,1536]{2,1,0:T(8,128)(2,1)}, u32[]{:S(2)}, u32[]{:S(2)}) collective-permute-start(bf16[2,128,1536]{2,1,0:T(8,128)(2,1)} %get-tuple-element.821), channel_id=1, source_target_pairs={{0,16},{4,20},{8,24},{12,28},{16,0},{20,4},{24,8},{28,12},{1,17},{... | collective-permute-start | bytes 2359304 | tf_op jit(solution)/shard_map/gate0_dp4/ppermute | solution.py:1037
  249.4 23.1 %collective-permute-start.25 = (bf16[704,512]{1,0:T(8,128)(2,1)}, bf16[704,512]{1,0:T(8,128)(2,1)S(1)}, u32[]{:S(2)}, u32[]{:S(2)}) collective-permute-start(bf16[704,512]{1,0:T(8,128)(2,1)} %get-tuple-element.822), channel_id=1, source_target_pairs={{0,4},{4,0},{8,12},{12,8},{16,20},{20,16},{24,28},{28,24},{1,5},{5... | collective-permute-start | bytes 2162696 | tf_op jit(solution)/shard_map/down0_dp1/ppermute | solution.py:1037
  279.1 29.0 %collective-permute-start.28 = (bf16[2,256,1152]{2,1,0:T(8,128)(2,1)}, bf16[2,256,1152]{2,1,0:T(8,128)(2,1)S(1)}, u32[]{:S(2)}, u32[]{:S(2)}) collective-permute-start(bf16[2,256,1152]{2,1,0:T(8,128)(2,1)} %get-tuple-element.842), channel_id=1, source_target_pairs={{0,2},{1,3},{2,0},{3,1},{4,6},{5,7},{6,4},{7,5},{8,10},{9,11},{10,... | collective-permute-start | bytes 3538952 | tf_op jit(solution)/shard_map/out_q_expert2/ppermute | solution.py:1037
  279.4 25.1 %collective-permute-start.27 = (bf16[2,256,1024]{2,1,0:T(8,128)(2,1)}, bf16[2,256,1024]{2,1,0:T(8,128)(2,1)S(1)}, u32[]{:S(2)}, u32[]{:S(2)}) collective-permute-start(bf16[2,256,1024]{2,1,0:T(8,128)(2,1)} %get-tuple-element.838), channel_id=1, source_target_pairs={{0,4},{4,0},{8,12},{12,8},{16,20},{20,16},{24,28},{28,24},{1,5},{5... | collective-permute-start | bytes 3145736 | tf_op jit(solution)/shard_map/k_v_dp1/ppermute | solution.py:1037
  281.0 31.6 %collective-permute-start.29 = (bf16[704,512]{1,0:T(8,128)(2,1)S(1)}, bf16[704,512]{1,0:T(8,128)(2,1)S(1)}, u32[]{:S(2)}, u32[]{:S(2)}) collective-permute-start(bf16[704,512]{1,0:T(8,128)(2,1)S(1)} %copy-done.38), channel_id=1, source_target_pairs={{0,8},{4,12},{8,0},{12,4},{16,24},{20,28},{24,16},{28,20},{1,9},{5... | collective-permute-start | bytes 2162696 | tf_op jit(solution)/shard_map/down1_dp2/ppermute | solution.py:1037
  281.0 31.6 %collective-permute-start.30 = (bf16[2,128,1280]{2,1,0:T(8,128)(2,1)S(1)}, bf16[2,128,1280]{2,1,0:T(8,128)(2,1)S(1)}, u32[]{:S(2)}, u32[]{:S(2)}) collective-permute-start(bf16[2,128,1280]{2,1,0:T(8,128)(2,1)S(1)} %copy-done.40), channel_id=1, source_target_pairs={{0,16},{4,20},{8,24},{12,28},{16,0},{20,4},{24,8},{28,12},{1,17},{... | collective-permute-start | bytes 1966088 | tf_op jit(solution)/shard_map/gate1_dp4/ppermute | solution.py:1037
  297.1 51.0 %collective-permute-start.26 = (bf16[2,320,1024]{2,1,0:T(8,128)(2,1)}, bf16[2,320,1024]{2,1,0:T(8,128)(2,1)S(1)}, u32[]{:S(2)}, u32[]{:S(2)}) collective-permute-start(bf16[2,320,1024]{2,1,0:T(8,128)(2,1)} %get-tuple-element.836), channel_id=1, source_target_pairs={{0,2},{1,3},{2,0},{3,1},{4,6},{5,7},{6,4},{7,5},{8,10},{9,11},{10,... | collective-permute-start | bytes 3932168 | tf_op jit(solution)/shard_map/produced_rows2/ppermute | solution.py:1037
  321.1 22.7 %collective-permute-start.32 = (bf16[2,128,1152]{2,1,0:T(8,128)(2,1)}, bf16[2,128,1152]{2,1,0:T(8,128)(2,1)S(1)}, u32[]{:S(2)}, u32[]{:S(2)}) collective-permute-start(bf16[2,128,1152]{2,1,0:T(8,128)(2,1)} %get-tuple-element.896), channel_id=1, source_target_pairs={{0,4},{4,0},{8,12},{12,8},{16,20},{20,16},{24,28},{28,24},{1,5},{5... | collective-permute-start | bytes 1769480 | tf_op jit(solution)/shard_map/out_q_dp1/ppermute | solution.py:1037
  321.7 22.2 %collective-permute-start.31 = (bf16[2,128,1024]{2,1,0:T(8,128)(2,1)}, bf16[2,128,1024]{2,1,0:T(8,128)(2,1)S(1)}, u32[]{:S(2)}, u32[]{:S(2)}) collective-permute-start(bf16[2,128,1024]{2,1,0:T(8,128)(2,1)} %get-tuple-element.888), channel_id=1, source_target_pairs={{0,8},{4,12},{8,0},{12,4},{16,24},{20,28},{24,16},{28,20},{1,9},{5... | collective-permute-start | bytes 1572872 | tf_op jit(solution)/shard_map/k_v_dp2/ppermute | solution.py:1037
  323.4 39.5 %collective-permute-start.37 = (bf16[2,352,512]{2,1,0:T(8,128)(2,1)S(1)}, bf16[2,352,512]{2,1,0:T(8,128)(2,1)S(1)}, u32[]{:S(2)}, u32[]{:S(2)}) collective-permute-start(bf16[2,352,512]{2,1,0:T(8,128)(2,1)S(1)} %copy-done.39), channel_id=1, source_target_pairs={{0,16},{4,20},{8,24},{12,28},{16,0},{20,4},{24,8},{28,12},{1,17},{... | collective-permute-start | bytes 2162696 | tf_op jit(solution)/shard_map/down0_dp4/ppermute | solution.py:1037
  348.7 14.1 %collective-permute-start.35 = (bf16[2,64,1152]{2,1,0:T(8,128)(2,1)}, bf16[2,64,1152]{2,1,0:T(8,128)(2,1)S(1)}, u32[]{:S(2)}, u32[]{:S(2)}) collective-permute-start(bf16[2,64,1152]{2,1,0:T(8,128)(2,1)} %get-tuple-element.928), channel_id=1, source_target_pairs={{0,8},{4,12},{8,0},{12,4},{16,24},{20,28},{24,16},{28,20},{1,9},{5... | collective-permute-start | bytes 884744 | tf_op jit(solution)/shard_map/out_q_dp2/ppermute | solution.py:1037
  348.7 14.1 %collective-permute-start.36 = (bf16[2,64,1024]{2,1,0:T(8,128)(2,1)}, bf16[2,64,1024]{2,1,0:T(8,128)(2,1)S(1)}, u32[]{:S(2)}, u32[]{:S(2)}) collective-permute-start(bf16[2,64,1024]{2,1,0:T(8,128)(2,1)} %get-tuple-element.932), channel_id=1, source_target_pairs={{0,2},{1,3},{2,0},{3,1},{4,6},{5,7},{6,4},{7,5},{8,10},{9,11},{10,... | collective-permute-start | bytes 786440 | tf_op jit(solution)/shard_map/k_v_expert2/ppermute | solution.py:1037
  367.5 15.3 %collective-permute-start.38 = (bf16[2,32,2176]{2,1,0:T(8,128)(2,1)}, bf16[2,32,2176]{2,1,0:T(8,128)(2,1)S(1)}, u32[]{:S(2)}, u32[]{:S(2)}) collective-permute-start(bf16[2,32,2176]{2,1,0:T(8,128)(2,1)} %get-tuple-element.953), channel_id=1, source_target_pairs={{0,16},{4,20},{8,24},{12,28},{16,0},{20,4},{24,8},{28,12},{1,17},{... | collective-permute-start | bytes 835592 | tf_op jit(solution)/shard_map/out_q_dp4/ppermute | solution.py:1037
  (48 other events, 304.3 us)

commit v8 on v7

--- a/solution.py
+++ b/solution.py
@@ -430,25 +430,6 @@
     )
 
 
-def cot_hidden_more_kernel(rows_ref, wd_ref, out_ref):
-    out_ref[...] = dot_nt(rows_ref[...], wd_ref[0]).astype(BF)
-
-
-def cot_hidden_more(cot_rows, w_down, first):
-    rows, width = cot_rows.shape
-    count = w_down.shape[1] // FF_BLOCK - first
-    return call(
-        cot_hidden_more_kernel,
-        (cot_rows, w_down),
-        [const_spec((rows, width)), pl.BlockSpec((1, FF_BLOCK, width), lambda f: (0, first + f, 0))],
-        grid=(count,),
-        out_specs=pl.BlockSpec((rows, FF_BLOCK), lambda f: (0, f)),
-        out_shape=jax.ShapeDtypeStruct((rows, count * FF_BLOCK), BF),
-        cost_estimate=estimate("cot_hidden_more"),
-        name="cot_hidden_more",
-    )
-
-
 ROW_BLOCK = 320
 
 
@@ -1311,7 +1292,7 @@
     blocks = ff // FF_BLOCK
     counts = [blocks - blocks // 2, blocks // 2]
     starts = [sum(counts[:i]) for i in range(len(counts))]
-    gh_first, cot_rows = order.leave(cot_hidden(order.enter(me_ref), heads_rows, cots, w_down, cap, starts[1]))
+    grad_hidden, cot_rows = order.leave(cot_hidden(order.enter(me_ref), heads_rows, cots, w_down, cap, blocks))
     second_half.relay()
     payloads = [v for pair in zip(heads_rows, second_half.finish()) for v in pair]
     scs, units = [], []
@@ -1319,7 +1300,7 @@
     def expert_part(i, source, filled=()):
         *shared, gate_keep, gate_send, up_keep, up_send, sc, hid, hid_t, gg, gu = order.leave(
             expert_a(
-                order.enter(source), gh_second if i else gh_first, starts[i], w_gate, w_up, starts[i], counts[i], filled
+                order.enter(source), grad_hidden, 0, w_gate, w_up, starts[i], counts[i], filled
             )
         )
         scs.append(sc)
@@ -1336,7 +1317,6 @@
     (x_all, x_t, gate_all, grad_cots), filled = expert_part(0, (me_ref, place_x, payloads, cot_rows))
     for unit in units[0]:
         unit.start()
-    gh_second = order.leave(cot_hidden_more(order.enter(cot_rows), w_down, starts[1]))
     _, (hid, hid_t, gg, gu) = expert_part(1, (x_all, x_t, gate_all), filled)
     for unit in units[1]:
         unit.start()

time: 394 us -> 391 us (level)
    pallas_call x23 -> x22, Pallas kernels: 254 us -> 252 us  [call(): pl.pallas_call(kernel, in_specs=list(in_specs), compiler_params=params(),...]
where the time goes in v8:
time: 391 us; the launch traced here: 385 us
  Pallas kernels  252 us (64%)
  waiting for transfers between devices  64.5 us (16%)
  starting transfers between devices  36.9 us (9%)
  local copies, waits for them, and re-layouts  24 us (6%)
  other arithmetic  5.96 us (2%)
    pallas_call x22, Pallas kernels, call(): pl.pallas_call(kernel, in_specs=list(in_specs), compiler_params=params(),...  252 us
    ppermute x39, waiting for transfers between devices, swap(): return lax.ppermute(value, axis, [(i, i ^ mask) for i in range(size)])  64.5 us
    ppermute x39, starting transfers between devices, swap(): return lax.ppermute(value, axis, [(i, i ^ mask) for i in range(size)])  36.9 us
    unnamed x83, local copies, waits for them, and re-layouts  15.8 us
  transfers between devices with their start and end apart: 39, of which 13 were waited for; matrix products, arithmetic and copies ran while one was open for 4% of the time, Pallas kernels for 56%

profile of v8, /device:TPU:0, one launch (start us, length us, event | category | flops | bytes accessed | tf_op | source)
XLA Modules:
  0.0 384.9 jit_solution(18231439802787440997)
XLA Ops:
  3.8 15.6 %attn_first.1 = (bf16[512,1024]{1,0:T(8,128)(2,1)}, bf16[512,1024]{1,0:T(8,128)(2,1)}, bf16[512,1024]{1,0:T(8,128)(2,1)}, f32[4,4,512]{2,1,0:T(4,128)}, f32[1,12...) custom-call(bf16[512,1024]{1,0:T(8,128)(2,1)} %tok_ref.7, ...), custom_call_target="tpu_custom_call" | custom-call | flops 115000000 | bytes 100000 | tf_op jit(solution)/shard_map/attn_first/pallas_call | solution.py:100
  19.8 12.3 %attn_second.1 = (bf16[512,1024]{1,0:T(8,128)(2,1)}, f32[4,4,512]{2,1,0:T(4,128)}, f32[512,1024]{1,0:T(8,128)}, bf16[512,1024]{1,0:T(8,128)(2,1)}, f32[16,512]{1,0:T(8,128)}, /*index=5*/bf16[272,1024]{1,0:T(8,128)(2,1)}) custom-call(bf16[512,1024]{1,0:T(8,128)(2,1)} %tok_ref.7, ...), custom_call_target="tpu_custom_call", output_to_operand_aliasing={{0}: (9, {}), {1}: (10, {}), {2}: (11, {}), {3}: (12, {}), ... | custom-call | flops 115000000 | bytes 100000 | tf_op jit(solution)/shard_map/attn_second/pallas_call | solution.py:100
  32.2 7.4 %collective-permute-done.2.refs_2_.refs_6_ = bf16[272,1024]{1,0:T(8,128)(2,1)S(1)} collective-permute-done((bf16[272,1024]{1,0:T(8,128)(2,1)}, bf16[272,1024]{1,0:T(8,128)(2,1)S(1)}, u32[]{:S(2)}, u32[]{:S(2)}) %collective-permute-start.2) | collective-permute-done | bytes 557088 | tf_op jit(solution)/shard_map/rows_a0_2/ppermute | solution.py:1018
  44.3 16.7 %cot_hidden.1 = (bf16[1280,2816]{1,0:T(8,128)(2,1)}, bf16[1280,1024]{1,0:T(8,128)(2,1)}) custom-call(s32[1]{0:T(128)} %bitcast.9.me_ref.refs_0_, bf16[272,1024]{1,0:T(8,128)(2,1)} %get-tuple-element.549.refs_0_.refs_2_, bf16[272,1024]{1,0:T(8,128)(2,1)} %copy-done.2, bf16[272,1024]{1,0:T(8,128)(2,1)} %copy-done.3, bf16[272,1024]{1,0:T(8,128)(2,1)} %copy-done.4, ...), custom_call_target="tpu_custom_call" | custom-call | flops 115000000 | bytes 100000 | tf_op jit(solution)/shard_map/cot_hidden/pallas_call | solution.py:100
  63.8 33.0 %expert_grads.2 = (bf16[1280,1024]{1,0:T(8,128)(2,1)}, bf16[1024,1280]{1,0:T(8,128)(2,1)}, f32[1280,128]{1,0:T(8,128)}, bf16[1280,1024]{1,0:T(8,128)(2,1)}, bf16...) custom-call(s32[1]{0:T(128)} %bitcast.9.me_ref.refs_0_, ...), custom_call_target="tpu_custom_call" | custom-call | flops 115000000 | bytes 100000 | tf_op jit(solution)/shard_map/expert_grads/pallas_call | solution.py:100
  102.4 25.3 %expert_grads.3 = (bf16[512,1280]{1,0:T(8,128)(2,1)}, bf16[512,1280]{1,0:T(8,128)(2,1)}, bf16[512,1280]{1,0:T(8,128)(2,1)}, bf16[512,1280]{1,0:T(8,128)(2,1)}, f...) custom-call(bf16[1280,1024]{1,0:T(8,128)(2,1)} %get-tuple-element.58, ...), custom_call_target="tpu_custom_call", output_to_operand_aliasing={{5}: (6, {}), {6}: (7, {}), {7}: (8, {}), {8}: (9, {})} | custom-call | flops 115000000 | bytes 100000 | tf_op jit(solution)/shard_map/expert_grads/pallas_call | solution.py:100
  128.5 26.0 %expert_input_grad.1 = (bf16[1,336,1024]{2,1,0:T(8,128)(2,1)}, bf16[1,336,1024]{2,1,0:T(8,128)(2,1)}, bf16[2,336,1024]{2,1,0:T(8,128)(2,1)}) custom-call(bf16[1280,2816]{1,0:T(8,128)(2,1)} %get-tuple-element.609.gg_ref, bf16[1280,2816]{1,0:T(8,128)(2,1)} %get-tuple-element.610.gu_ref, f32[1280,128]{1,0:T(8,128)} %get-tuple-element.611.refs_0_, ...), custom_call_target="tpu_custom_call" | custom-call | flops 115000000 | bytes 100000 | tf_op jit(solution)/shard_map/expert_input_grad/pallas_call | solution.py:100
  157.5 4.6 %fold.6 = (bf16[256,1536]{1,0:T(8,128)(2,1)}, bf16[256,1536]{1,0:T(8,128)(2,1)}, bf16[256,1536]{1,0:T(8,128)(2,1)}, bf16[256,1536]{1,0:T(8,128)(2,1)}) custom-call(bf16[512,1536]{1,0:T(8,128)(2,1)} %get-tuple-element.626.refs_0_, bf16[512,1536]{1,0:T(8,128)(2,1)} %copy-done.5, bf16[512,1536]{1,0:T(8,128)(2,1)} %get-tuple-element.628.refs_2_, ...), custom_call_target="tpu_custom_call" | custom-call | flops 115000000 | bytes 100000 | tf_op jit(solution)/shard_map/fold/pallas_call | solution.py:100
  165.3 16.7 %down_grads.1 = (bf16[1408,512]{1,0:T(8,128)(2,1)}, bf16[1408,512]{1,0:T(8,128)(2,1)}, bf16[1408,512]{1,0:T(8,128)(2,1)}, bf16[1408,512]{1,0:T(8,128)(2,1)}) custom-call(s32[8]{0:T(128)} %get-tuple-element.1013.place_a_ref, s32[8]{0:T(128)} %get-tuple-element.548.refs_1_.place_b_ref, bf16[2816,1280]{1,0:T(8,128)(2,1)} %get-tuple-element.640.hidt_ref, ...), custom_call_target="tpu_custom_call" | custom-call | flops 11500000256 | bytes 100000 | tf_op jit(solution)/shard_map/down_grads/pallas_call | solution.py:100
  184.7 5.5 %fold.7 = (bf16[256,1280]{1,0:T(8,128)(2,1)}, bf16[256,1280]{1,0:T(8,128)(2,1)}, bf16[256,1280]{1,0:T(8,128)(2,1)}, bf16[256,1280]{1,0:T(8,128)(2,1)}, bf16[2,12...) custom-call(bf16[512,1280]{1,0:T(8,128)(2,1)} %get-tuple-element.662.refs_0_, bf16[512,1280]{1,0:T(8,128)(2,1)} %copy-done.34, ...), custom_call_target="tpu_custom_call" | custom-call | flops 2300000000 | bytes 100000 | tf_op jit(solution)/shard_map/fold/pallas_call | solution.py:100
  192.4 4.7 %sorted_rows.1 = (bf16[1024,512]{1,0:T(8,128)(2,1)}, bf16[2,1024,512]{2,1,0:T(8,128)(2,1)}) custom-call(s32[32]{0:T(128)} %get-tuple-element.1012.pq_ref.place_ref, s32[32]{0:T(128)} %get-tuple-element.1011.pk_ref, bf16[512,1024]{1,0:T(8,128)(2,1)} %tok_ref.7, f32[1,1024]{1,0:T(1,128)} %bitcast.46, bf16[512,1024]{1,0:T(8,128)(2,1)} %get-tuple-element.697.att_ref), custom_call_target="tpu_custom_call" | custom-call | flops 115000000 | bytes 100000 | tf_op jit(solution)/shard_map/sorted_rows/pallas_call | solution.py:100
  202.7 10.0 %moe_bwd.1 = (f32[512,1024]{1,0:T(8,128)}, bf16[512,1024]{1,0:T(8,128)(2,1)}, bf16[512,1024]{1,0:T(8,128)(2,1)}, f32[1,1024]{1,0:T(1,128)}, f32[16,1024]{1,0:T(8,128)}) custom-call(bf16[512,1024]{1,0:T(8,128)(2,1)} %cot_ref.1, f32[512,1024]{1,0:T(8,128)} %get-tuple-element.508.mid_ref, f32[1,1024]{1,0:T(1,128)} %bitcast.44, ...), custom_call_target="tpu_custom_call" | custom-call | flops 115000000 | bytes 100000 | tf_op jit(solution)/shard_map/moe_bwd/pallas_call | solution.py:100
  212.7 16.2 %attn_bwd.1 = (bf16[512,1024]{1,0:T(8,128)(2,1)}, bf16[512,1024]{1,0:T(8,128)(2,1)}, bf16[512,1024]{1,0:T(8,128)(2,1)}, f32[4,4,512]{2,1,0:T(4,128)}) custom-call(bf16[512,1024]{1,0:T(8,128)(2,1)} %get-tuple-element.492.qs_ref, bf16[512,1024]{1,0:T(8,128)(2,1)} %get-tuple-element.493.k_ref, bf16[512,1024]{1,0:T(8,128)(2,1)} %get-tuple-element.494.v_ref, ...), custom_call_target="tpu_custom_call" | custom-call | flops 115000000 | bytes 100000 | tf_op jit(solution)/shard_map/attn_bwd/pallas_call | solution.py:100
  229.0 9.4 %dense_terms.1 = (bf16[4,512,1024]{2,1,0:T(8,128)(2,1)}, bf16[4,512,1024]{2,1,0:T(8,128)(2,1)}) custom-call(bf16[1024,512]{1,0:T(8,128)(2,1)} %get-tuple-element.704.att_ref, bf16[2,1024,512]{2,1,0:T(8,128)(2,1)} %get-tuple-element.705.rows_ref, bf16[512,1024]{1,0:T(8,128)(2,1)} %get-tuple-element.719.branch_ref, ...), custom_call_target="tpu_custom_call" | custom-call | flops 15064999936 | bytes 100000 | tf_op jit(solution)/shard_map/dense_terms/pallas_call | solution.py:100
  239.0 2.6 collective-permute-start.24
  241.6 5.5 %fold.8 = (bf16[704,512]{1,0:T(8,128)(2,1)}, bf16[704,512]{1,0:T(8,128)(2,1)}, bf16[704,512]{1,0:T(8,128)(2,1)}, bf16[704,512]{1,0:T(8,128)(2,1)}, bf16[2,128,12...) custom-call(bf16[1408,512]{1,0:T(8,128)(2,1)} %get-tuple-element.764.refs_0_, bf16[1408,512]{1,0:T(8,128)(2,1)} %copy-done.6, ...), custom_call_target="tpu_custom_call" | custom-call | flops 115000000 | bytes 100000 | tf_op jit(solution)/shard_map/fold/pallas_call | solution.py:100
  251.2 10.9 %norm_bwd.1 = (f32[512,1024]{1,0:T(8,128)}, bf16[512,128]{1,0:T(8,128)(2,1)}, bf16[512,128]{1,0:T(8,128)(2,1)}) custom-call(s32[32]{0:T(128)} %get-tuple-element.1012.pq_ref.place_ref, bf16[512,1024]{1,0:T(8,128)(2,1)} %tok_ref.7, f32[1,1024]{1,0:T(1,128)} %bitcast.47, f32[512,1024]{1,0:T(8,128)} %get-tuple-element.782.gmid_ref, ...), custom_call_target="tpu_custom_call" | custom-call | flops 115000000 | bytes 100000 | tf_op jit(solution)/shard_map/norm_bwd/pallas_call | solution.py:100
  264.5 5.8 %fold_first.1 = (bf16[2,256,1152]{2,1,0:T(8,128)(2,1)}, bf16[2,256,1152]{2,1,0:T(8,128)(2,1)}, bf16[2,256,1024]{2,1,0:T(8,128)(2,1)}, bf16[2,256,1024]{2,1,0:T(8,128)(2,1)}) custom-call(bf16[4,512,1024]{2,1,0:T(8,128)(2,1)} %get-tuple-element.800.keep_ref, bf16[4,512,1024]{2,1,0:T(8,128)(2,1)} %collective-permute-done.22.got_ref, ...), custom_call_target="tpu_custom_call" | custom-call | flops 115000000 | bytes 100000 | tf_op jit(solution)/shard_map/fold_first/pallas_call | solution.py:100
  270.3 6.6 %collective-permute-done.24.refs_9_ = bf16[2,128,1536]{2,1,0:T(8,128)(2,1)} collective-permute-done((bf16[2,128,1536]{2,1,0:T(8,128)(2,1)}, bf16[2,128,1536]{2,1,0:T(8,128)(2,1)}, u32[]{:S(2)}, u32[]{:S(2)}) %collective-permute-start.24) | collective-permute-done | bytes 786464 | tf_op jit(solution)/shard_map/gate0_dp4/ppermute | solution.py:1018
  278.8 3.1 collective-permute-start.30
  282.0 12.9 %produced_rows.1 = (bf16[2,320,1024]{2,1,0:T(8,128)(2,1)}, bf16[2,320,1024]{2,1,0:T(8,128)(2,1)}) custom-call(bf16[1280,2816]{1,0:T(8,128)(2,1)} %get-tuple-element.821.hid_ref, bf16[1,2816,1024]{2,1,0:T(8,128)(2,1)} %wd_ref.1), custom_call_target="tpu_custom_call" | custom-call | flops 115000000 | bytes 100000 | tf_op jit(solution)/shard_map/produced_rows/pallas_call | solution.py:100
  297.7 4.6 %collective-permute-done.27.refs_1_ = bf16[2,256,1024]{2,1,0:T(8,128)(2,1)S(1)} collective-permute-done((bf16[2,256,1024]{2,1,0:T(8,128)(2,1)}, bf16[2,256,1024]{2,1,0:T(8,128)(2,1)S(1)}, u32[]{:S(2)}, u32[]{:S(2)}) %collective-permute-start.27) | collective-permute-done | bytes 1048608 | tf_op jit(solution)/shard_map/k_v_dp1/ppermute | solution.py:1018
  302.3 3.7 collective-permute-done.28.refs_3_
  306.0 4.4 %collective-permute-done.29.refs_7_ = bf16[704,512]{1,0:T(8,128)(2,1)S(1)} collective-permute-done((bf16[704,512]{1,0:T(8,128)(2,1)S(1)}, bf16[704,512]{1,0:T(8,128)(2,1)S(1)}, u32[]{:S(2)}, u32[]{:S(2)}) %collective-permute-start.29) | collective-permute-done | bytes 720928 | tf_op jit(solution)/shard_map/down1_dp2/ppermute | solution.py:1018
  312.2 6.8 %fold.9 = (bf16[2,128,1024]{2,1,0:T(8,128)(2,1)}, bf16[2,128,1024]{2,1,0:T(8,128)(2,1)}, bf16[2,128,1152]{2,1,0:T(8,128)(2,1)}, bf16[2,128,1152]{2,1,0:T(8,128)(...) custom-call(bf16[2,256,1024]{2,1,0:T(8,128)(2,1)} %get-tuple-element, ...), custom_call_target="tpu_custom_call" | custom-call | flops 115000000 | bytes 100000 | tf_op jit(solution)/shard_map/fold/pallas_call | solution.py:100
  321.2 2.7 collective-permute-start.37
  326.4 15.3 %collective-permute-done.31.refs_1_ = bf16[2,128,1024]{2,1,0:T(8,128)(2,1)S(1)} collective-permute-done((bf16[2,128,1024]{2,1,0:T(8,128)(2,1)}, bf16[2,128,1024]{2,1,0:T(8,128)(2,1)S(1)}, u32[]{:S(2)}, u32[]{:S(2)}) %collective-permute-start.31) | collective-permute-done | bytes 524320 | tf_op jit(solution)/shard_map/k_v_dp2/ppermute | solution.py:1018
  343.3 2.7 fold.10
  350.0 6.3 %layer_output.1 = bf16[512,1024]{1,0:T(8,128)(2,1)} custom-call(f32[512,1024]{1,0:T(8,128)} %get-tuple-element.508.mid_ref, f32[16,512]{1,0:T(8,128)} %select_maximum_fusion.3.ch_ref, s32[512,4]{1,0:T(8,128)} %bitcast.39, bf16[2,320,1024]{2,1,0:T(8,128)(2,1)} %get-tuple-element.825.refs_0_, bf16[1,320,1024]{2,1,0:T(8,128)(2,1)} %copy-done.19, ...), custom_call_target="tpu_custom_call" | custom-call | flops 115000000 | bytes 100000 | tf_op jit(solution)/shard_map/layer_output/pallas_call | solution.py:100
  356.2 4.4 %collective-permute-done.35.refs_1_ = bf16[2,64,1152]{2,1,0:T(8,128)(2,1)S(1)} collective-permute-done((bf16[2,64,1152]{2,1,0:T(8,128)(2,1)}, bf16[2,64,1152]{2,1,0:T(8,128)(2,1)S(1)}, u32[]{:S(2)}, u32[]{:S(2)}) %collective-permute-start.35) | collective-permute-done | bytes 294944 | tf_op jit(solution)/shard_map/out_q_dp2/ppermute | solution.py:1018
  362.3 3.0 fold.11
  368.5 12.2 %collective-permute-done.38.got_ref = bf16[2,32,2176]{2,1,0:T(8,128)(2,1)S(1)} collective-permute-done((bf16[2,32,2176]{2,1,0:T(8,128)(2,1)}, bf16[2,32,2176]{2,1,0:T(8,128)(2,1)S(1)}, u32[]{:S(2)}, u32[]{:S(2)}) %collective-permute-start.38) | collective-permute-done | bytes 278560 | tf_op jit(solution)/shard_map/out_q_dp4/ppermute | solution.py:1018
  (178 shorter events, 66.3 us)
Async XLA Ops:
  0.6 31.5 %collective-permute-start.1 = (bf16[512,1024]{1,0:T(8,128)(2,1)}, bf16[512,1024]{1,0:T(8,128)(2,1)S(1)}, u32[]{:S(2)}, u32[]{:S(2)}) collective-permute-start(bf16[512,1024]{1,0:T(8,128)(2,1)} %cot_ref.1), channel_id=1, source_target_pairs={{0,1},{1,0},{2,3},{3,2},{4,5},{5,4},{6,7},{7,6},{8,9},{9,8},{10,11... | collective-permute-start | bytes 3145736 | tf_op jit(solution)/shard_map/cot0_1/ppermute | solution.py:1018
  1.2 38.5 %collective-permute-start.4 = (bf16[512,1024]{1,0:T(8,128)(2,1)}, bf16[512,1024]{1,0:T(8,128)(2,1)}, u32[]{:S(2)}, u32[]{:S(2)}) collective-permute-start(bf16[512,1024]{1,0:T(8,128)(2,1)} %cot_ref.1), channel_id=1, source_target_pairs={{0,2},{1,3},{2,0},{3,1},{4,6},{5,7},{6,4},{7,5},{8,10},{9,11},{10,... | collective-permute-start | bytes 3145736 | tf_op jit(solution)/shard_map/cot0_2/ppermute | solution.py:1018
  19.3 12.9 %collective-permute-start = (bf16[272,1024]{1,0:T(8,128)(2,1)}, bf16[272,1024]{1,0:T(8,128)(2,1)S(1)}, u32[]{:S(2)}, u32[]{:S(2)}) collective-permute-start(bf16[272,1024]{1,0:T(8,128)(2,1)} %get-tuple-element.549.refs_0_.refs_2_), channel_id=1, source_target_pairs={{0,1},{1,0},{2,3},{3,2},{4,5},{5,4},{6,7},{7,6},{8,9},{9,8},{10,11... | collective-permute-start | bytes 1671176 | tf_op jit(solution)/shard_map/rows_a0_1/ppermute | solution.py:1018
  19.6 20.1 %collective-permute-start.2 = (bf16[272,1024]{1,0:T(8,128)(2,1)}, bf16[272,1024]{1,0:T(8,128)(2,1)S(1)}, u32[]{:S(2)}, u32[]{:S(2)}) collective-permute-start(bf16[272,1024]{1,0:T(8,128)(2,1)} %get-tuple-element.549.refs_0_.refs_2_), channel_id=1, source_target_pairs={{0,2},{1,3},{2,0},{3,1},{4,6},{5,7},{6,4},{7,5},{8,10},{9,11},{10,... | collective-permute-start | bytes 1671176 | tf_op jit(solution)/shard_map/rows_a0_2/ppermute | solution.py:1018
  40.2 20.8 %collective-permute-start.7 = (bf16[272,1024]{1,0:T(8,128)(2,1)}, bf16[272,1024]{1,0:T(8,128)(2,1)S(1)}, u32[]{:S(2)}, u32[]{:S(2)}) collective-permute-start(bf16[272,1024]{1,0:T(8,128)(2,1)} %get-tuple-element.550.refs_3_), channel_id=1, source_target_pairs={{0,2},{1,3},{2,0},{3,1},{4,6},{5,7},{6,4},{7,5},{8,10},{9,11},{10,... | collective-permute-start | bytes 1671176 | tf_op jit(solution)/shard_map/rows_b0_2/ppermute | solution.py:1018
  41.9 19.8 %collective-permute-start.6 = (bf16[272,1024]{1,0:T(8,128)(2,1)}, bf16[272,1024]{1,0:T(8,128)(2,1)}, u32[]{:S(2)}, u32[]{:S(2)}) collective-permute-start(bf16[272,1024]{1,0:T(8,128)(2,1)} %get-tuple-element.550.refs_3_), channel_id=1, source_target_pairs={{0,1},{1,0},{2,3},{3,2},{4,5},{5,4},{6,7},{7,6},{8,9},{9,8},{10,11... | collective-permute-start | bytes 1671176 | tf_op jit(solution)/shard_map/rows_b0_1/ppermute | solution.py:1018
  96.8 59.6 %collective-permute-start.10 = (bf16[512,1536]{1,0:T(8,128)(2,1)}, bf16[512,1536]{1,0:T(8,128)(2,1)S(1)}, u32[]{:S(2)}, u32[]{:S(2)}) collective-permute-start(bf16[512,1536]{1,0:T(8,128)(2,1)} %get-tuple-element.604), channel_id=1, source_target_pairs={{0,8},{4,12},{8,0},{12,4},{16,24},{20,28},{24,16},{28,20},{1,9},{5... | collective-permute-start | bytes 4718600 | tf_op jit(solution)/shard_map/gate0_dp2/ppermute | solution.py:1018
  98.7 57.7 %collective-permute-start.11 = (bf16[512,1536]{1,0:T(8,128)(2,1)}, bf16[512,1536]{1,0:T(8,128)(2,1)}, u32[]{:S(2)}, u32[]{:S(2)}) collective-permute-start(bf16[512,1536]{1,0:T(8,128)(2,1)} %get-tuple-element.622), channel_id=1, source_target_pairs={{0,4},{4,0},{8,12},{12,8},{16,20},{20,16},{24,28},{28,24},{1,5},{5... | collective-permute-start | bytes 4718600 | tf_op jit(solution)/shard_map/up0_dp1/ppermute | solution.py:1018
  127.6 54.4 %collective-permute-start.9 = (bf16[512,1280]{1,0:T(8,128)(2,1)}, bf16[512,1280]{1,0:T(8,128)(2,1)S(1)}, u32[]{:S(2)}, u32[]{:S(2)}) collective-permute-start(bf16[512,1280]{1,0:T(8,128)(2,1)} %get-tuple-element.601), channel_id=1, source_target_pairs={{0,8},{4,12},{8,0},{12,4},{16,24},{20,28},{24,16},{28,20},{1,9},{5... | collective-permute-start | bytes 3932168 | tf_op jit(solution)/shard_map/gate1_dp2/ppermute | solution.py:1018
  128.1 53.9 %collective-permute-start.12 = (bf16[512,1280]{1,0:T(8,128)(2,1)}, bf16[512,1280]{1,0:T(8,128)(2,1)S(1)}, u32[]{:S(2)}, u32[]{:S(2)}) collective-permute-start(bf16[512,1280]{1,0:T(8,128)(2,1)} %get-tuple-element.650), channel_id=1, source_target_pairs={{0,4},{4,0},{8,12},{12,8},{16,20},{20,16},{24,28},{28,24},{1,5},{5... | collective-permute-start | bytes 3932168 | tf_op jit(solution)/shard_map/up1_dp1/ppermute | solution.py:1018
  154.4 35.8 %collective-permute-start.15 = (bf16[2,336,1024]{2,1,0:T(8,128)(2,1)}, bf16[2,336,1024]{2,1,0:T(8,128)(2,1)S(1)}, u32[]{:S(2)}, u32[]{:S(2)}) collective-permute-start(bf16[2,336,1024]{2,1,0:T(8,128)(2,1)} %get-tuple-element.688), channel_id=1, source_target_pairs={{0,2},{1,3},{2,0},{3,1},{4,6},{5,7},{6,4},{7,5},{8,10},{9,11},{10,... | collective-permute-start | bytes 4128776 | tf_op jit(solution)/shard_map/grad_rows2/ppermute | solution.py:1018
  162.2 19.8 %collective-permute-start.13 = (bf16[256,1536]{1,0:T(8,128)(2,1)}, bf16[256,1536]{1,0:T(8,128)(2,1)S(1)}, u32[]{:S(2)}, u32[]{:S(2)}) collective-permute-start(bf16[256,1536]{1,0:T(8,128)(2,1)} %get-tuple-element.654), channel_id=1, source_target_pairs={{0,4},{4,0},{8,12},{12,8},{16,20},{20,16},{24,28},{28,24},{1,5},{5... | collective-permute-start | bytes 2359304 | tf_op jit(solution)/shard_map/gate0_dp1/ppermute | solution.py:1018
  163.7 18.4 %collective-permute-start.14 = (bf16[256,1536]{1,0:T(8,128)(2,1)}, bf16[256,1536]{1,0:T(8,128)(2,1)S(1)}, u32[]{:S(2)}, u32[]{:S(2)}) collective-permute-start(bf16[256,1536]{1,0:T(8,128)(2,1)} %get-tuple-element.658), channel_id=1, source_target_pairs={{0,8},{4,12},{8,0},{12,4},{16,24},{20,28},{24,16},{28,20},{1,9},{5... | collective-permute-start | bytes 2359304 | tf_op jit(solution)/shard_map/up0_dp2/ppermute | solution.py:1018
  190.3 6.8 %collective-permute-start.17 = (bf16[1,336,1024]{2,1,0:T(8,128)(2,1)S(1)}, bf16[1,336,1024]{2,1,0:T(8,128)(2,1)S(1)}, u32[]{:S(2)}, u32[]{:S(2)}) collective-permute-start(bf16[1,336,1024]{2,1,0:T(8,128)(2,1)S(1)} %slice.27), channel_id=1, source_target_pairs={{0,1},{1,0},{2,3},{3,2},{4,5},{5,4},{6,7},{7,6},{8,9},{9,8},{10,11... | collective-permute-start | bytes 2064392 | tf_op jit(solution)/shard_map/grad_rows1_3/ppermute | solution.py:1018
  190.8 38.1 %collective-permute-start.20 = (bf16[256,1280]{1,0:T(8,128)(2,1)}, bf16[256,1280]{1,0:T(8,128)(2,1)}, u32[]{:S(2)}, u32[]{:S(2)}) collective-permute-start(bf16[256,1280]{1,0:T(8,128)(2,1)} %get-tuple-element.731), channel_id=1, source_target_pairs={{0,4},{4,0},{8,12},{12,8},{16,20},{20,16},{24,28},{28,24},{1,5},{5... | collective-permute-start | bytes 1966088 | tf_op jit(solution)/shard_map/gate1_dp1/ppermute | solution.py:1018
  191.4 37.6 %collective-permute-start.19 = (bf16[256,1280]{1,0:T(8,128)(2,1)}, bf16[256,1280]{1,0:T(8,128)(2,1)}, u32[]{:S(2)}, u32[]{:S(2)}) collective-permute-start(bf16[256,1280]{1,0:T(8,128)(2,1)} %get-tuple-element.730), channel_id=1, source_target_pairs={{0,8},{4,12},{8,0},{12,4},{16,24},{20,28},{24,16},{28,20},{1,9},{5... | collective-permute-start | bytes 1966088 | tf_op jit(solution)/shard_map/up1_dp2/ppermute | solution.py:1018
  198.8 40.1 %collective-permute-start.18 = (bf16[1408,512]{1,0:T(8,128)(2,1)}, bf16[1408,512]{1,0:T(8,128)(2,1)S(1)}, u32[]{:S(2)}, u32[]{:S(2)}) collective-permute-start(bf16[1408,512]{1,0:T(8,128)(2,1)} %get-tuple-element.703), channel_id=1, source_target_pairs={{0,8},{4,12},{8,0},{12,4},{16,24},{20,28},{24,16},{28,20},{1,9},{5... | collective-permute-start | bytes 4325384 | tf_op jit(solution)/shard_map/down0_dp2/ppermute | solution.py:1018
  200.3 38.6 %collective-permute-start.21 = (bf16[1408,512]{1,0:T(8,128)(2,1)}, bf16[1408,512]{1,0:T(8,128)(2,1)S(1)}, u32[]{:S(2)}, u32[]{:S(2)}) collective-permute-start(bf16[1408,512]{1,0:T(8,128)(2,1)} %get-tuple-element.745), channel_id=1, source_target_pairs={{0,4},{4,0},{8,12},{12,8},{16,20},{20,16},{24,28},{28,24},{1,5},{5... | collective-permute-start | bytes 4325384 | tf_op jit(solution)/shard_map/down1_dp1/ppermute | solution.py:1018
  238.9 23.3 %collective-permute-start.22 = (bf16[4,512,1024]{2,1,0:T(8,128)(2,1)}, bf16[4,512,1024]{2,1,0:T(8,128)(2,1)}, u32[]{:S(2)}, u32[]{:S(2)}) collective-permute-start(bf16[4,512,1024]{2,1,0:T(8,128)(2,1)} %get-tuple-element.781), channel_id=1, source_target_pairs={{0,1},{1,0},{2,3},{3,2},{4,5},{5,4},{6,7},{7,6},{8,9},{9,8},{10,11... | collective-permute-start | bytes 12582920 | tf_op jit(solution)/shard_map/dense_expert1/ppermute | solution.py:1018
  239.0 37.9 %collective-permute-start.24 = (bf16[2,128,1536]{2,1,0:T(8,128)(2,1)}, bf16[2,128,1536]{2,1,0:T(8,128)(2,1)}, u32[]{:S(2)}, u32[]{:S(2)}) collective-permute-start(bf16[2,128,1536]{2,1,0:T(8,128)(2,1)} %get-tuple-element.813), channel_id=1, source_target_pairs={{0,16},{4,20},{8,24},{12,28},{16,0},{20,4},{24,8},{28,12},{1,17},{... | collective-permute-start | bytes 2359304 | tf_op jit(solution)/shard_map/gate0_dp4/ppermute | solution.py:1018
  247.2 23.2 %collective-permute-start.25 = (bf16[704,512]{1,0:T(8,128)(2,1)}, bf16[704,512]{1,0:T(8,128)(2,1)S(1)}, u32[]{:S(2)}, u32[]{:S(2)}) collective-permute-start(bf16[704,512]{1,0:T(8,128)(2,1)} %get-tuple-element.814), channel_id=1, source_target_pairs={{0,4},{4,0},{8,12},{12,8},{16,20},{20,16},{24,28},{28,24},{1,5},{5... | collective-permute-start | bytes 2162696 | tf_op jit(solution)/shard_map/down0_dp1/ppermute | solution.py:1018
  276.9 29.0 %collective-permute-start.28 = (bf16[2,256,1152]{2,1,0:T(8,128)(2,1)}, bf16[2,256,1152]{2,1,0:T(8,128)(2,1)S(1)}, u32[]{:S(2)}, u32[]{:S(2)}) collective-permute-start(bf16[2,256,1152]{2,1,0:T(8,128)(2,1)} %get-tuple-element.834), channel_id=1, source_target_pairs={{0,2},{1,3},{2,0},{3,1},{4,6},{5,7},{6,4},{7,5},{8,10},{9,11},{10,... | collective-permute-start | bytes 3538952 | tf_op jit(solution)/shard_map/out_q_expert2/ppermute | solution.py:1018
  277.2 25.1 %collective-permute-start.27 = (bf16[2,256,1024]{2,1,0:T(8,128)(2,1)}, bf16[2,256,1024]{2,1,0:T(8,128)(2,1)S(1)}, u32[]{:S(2)}, u32[]{:S(2)}) collective-permute-start(bf16[2,256,1024]{2,1,0:T(8,128)(2,1)} %get-tuple-element.830), channel_id=1, source_target_pairs={{0,4},{4,0},{8,12},{12,8},{16,20},{20,16},{24,28},{28,24},{1,5},{5... | collective-permute-start | bytes 3145736 | tf_op jit(solution)/shard_map/k_v_dp1/ppermute | solution.py:1018
  278.8 31.6 %collective-permute-start.29 = (bf16[704,512]{1,0:T(8,128)(2,1)S(1)}, bf16[704,512]{1,0:T(8,128)(2,1)S(1)}, u32[]{:S(2)}, u32[]{:S(2)}) collective-permute-start(bf16[704,512]{1,0:T(8,128)(2,1)S(1)} %copy-done.38), channel_id=1, source_target_pairs={{0,8},{4,12},{8,0},{12,4},{16,24},{20,28},{24,16},{28,20},{1,9},{5... | collective-permute-start | bytes 2162696 | tf_op jit(solution)/shard_map/down1_dp2/ppermute | solution.py:1018
  278.8 31.6 %collective-permute-start.30 = (bf16[2,128,1280]{2,1,0:T(8,128)(2,1)S(1)}, bf16[2,128,1280]{2,1,0:T(8,128)(2,1)S(1)}, u32[]{:S(2)}, u32[]{:S(2)}) collective-permute-start(bf16[2,128,1280]{2,1,0:T(8,128)(2,1)S(1)} %copy-done.40), channel_id=1, source_target_pairs={{0,16},{4,20},{8,24},{12,28},{16,0},{20,4},{24,8},{28,12},{1,17},{... | collective-permute-start | bytes 1966088 | tf_op jit(solution)/shard_map/gate1_dp4/ppermute | solution.py:1018
  294.9 51.1 %collective-permute-start.26 = (bf16[2,320,1024]{2,1,0:T(8,128)(2,1)}, bf16[2,320,1024]{2,1,0:T(8,128)(2,1)S(1)}, u32[]{:S(2)}, u32[]{:S(2)}) collective-permute-start(bf16[2,320,1024]{2,1,0:T(8,128)(2,1)} %get-tuple-element.828), channel_id=1, source_target_pairs={{0,2},{1,3},{2,0},{3,1},{4,6},{5,7},{6,4},{7,5},{8,10},{9,11},{10,... | collective-permute-start | bytes 3932168 | tf_op jit(solution)/shard_map/produced_rows2/ppermute | solution.py:1018
  319.0 22.7 %collective-permute-start.32 = (bf16[2,128,1152]{2,1,0:T(8,128)(2,1)}, bf16[2,128,1152]{2,1,0:T(8,128)(2,1)S(1)}, u32[]{:S(2)}, u32[]{:S(2)}) collective-permute-start(bf16[2,128,1152]{2,1,0:T(8,128)(2,1)} %get-tuple-element.888), channel_id=1, source_target_pairs={{0,4},{4,0},{8,12},{12,8},{16,20},{20,16},{24,28},{28,24},{1,5},{5... | collective-permute-start | bytes 1769480 | tf_op jit(solution)/shard_map/out_q_dp1/ppermute | solution.py:1018
  319.5 22.1 %collective-permute-start.31 = (bf16[2,128,1024]{2,1,0:T(8,128)(2,1)}, bf16[2,128,1024]{2,1,0:T(8,128)(2,1)S(1)}, u32[]{:S(2)}, u32[]{:S(2)}) collective-permute-start(bf16[2,128,1024]{2,1,0:T(8,128)(2,1)} %get-tuple-element.880), channel_id=1, source_target_pairs={{0,8},{4,12},{8,0},{12,4},{16,24},{20,28},{24,16},{28,20},{1,9},{5... | collective-permute-start | bytes 1572872 | tf_op jit(solution)/shard_map/k_v_dp2/ppermute | solution.py:1018
  321.2 39.5 %collective-permute-start.37 = (bf16[2,352,512]{2,1,0:T(8,128)(2,1)S(1)}, bf16[2,352,512]{2,1,0:T(8,128)(2,1)S(1)}, u32[]{:S(2)}, u32[]{:S(2)}) collective-permute-start(bf16[2,352,512]{2,1,0:T(8,128)(2,1)S(1)} %copy-done.39), channel_id=1, source_target_pairs={{0,16},{4,20},{8,24},{12,28},{16,0},{20,4},{24,8},{28,12},{1,17},{... | collective-permute-start | bytes 2162696 | tf_op jit(solution)/shard_map/down0_dp4/ppermute | solution.py:1018
  346.6 14.1 %collective-permute-start.35 = (bf16[2,64,1152]{2,1,0:T(8,128)(2,1)}, bf16[2,64,1152]{2,1,0:T(8,128)(2,1)S(1)}, u32[]{:S(2)}, u32[]{:S(2)}) collective-permute-start(bf16[2,64,1152]{2,1,0:T(8,128)(2,1)} %get-tuple-element.920), channel_id=1, source_target_pairs={{0,8},{4,12},{8,0},{12,4},{16,24},{20,28},{24,16},{28,20},{1,9},{5... | collective-permute-start | bytes 884744 | tf_op jit(solution)/shard_map/out_q_dp2/ppermute | solution.py:1018
  346.6 14.1 %collective-permute-start.36 = (bf16[2,64,1024]{2,1,0:T(8,128)(2,1)}, bf16[2,64,1024]{2,1,0:T(8,128)(2,1)S(1)}, u32[]{:S(2)}, u32[]{:S(2)}) collective-permute-start(bf16[2,64,1024]{2,1,0:T(8,128)(2,1)} %get-tuple-element.924), channel_id=1, source_target_pairs={{0,2},{1,3},{2,0},{3,1},{4,6},{5,7},{6,4},{7,5},{8,10},{9,11},{10,... | collective-permute-start | bytes 786440 | tf_op jit(solution)/shard_map/k_v_expert2/ppermute | solution.py:1018
  365.4 15.3 %collective-permute-start.38 = (bf16[2,32,2176]{2,1,0:T(8,128)(2,1)}, bf16[2,32,2176]{2,1,0:T(8,128)(2,1)S(1)}, u32[]{:S(2)}, u32[]{:S(2)}) collective-permute-start(bf16[2,32,2176]{2,1,0:T(8,128)(2,1)} %get-tuple-element.945), channel_id=1, source_target_pairs={{0,16},{4,20},{8,24},{12,28},{16,0},{20,4},{24,8},{28,12},{1,17},{... | collective-permute-start | bytes 835592 | tf_op jit(solution)/shard_map/out_q_dp4/ppermute | solution.py:1018
  (48 other events, 304.1 us)
